TPU v7x, 512 devices: a whole 4x8x8 slice. The times are simulated.
512 devices in a mesh: fsdp: 8 (over y_hi, core), replica: 64 (over y_lo, x, z).
Axes of the slice: x: 4, y: 8 (y_hi: 4, y_lo: 2; y = y_hi * 2 + y_lo), z: 8, core: 2. Of those that a mesh axis runs over, the one named last changes fastest.
Arguments:
- tokens: bfloat16 [64, 1024, 4096], P('replica', 'fsdp'), may hold values from -6 to 6
- cotangent: bfloat16 [64, 1024, 4096], P('replica', 'fsdp'), may hold values from -0.1796875 to 0.1796875
- w_gate: bfloat16 [4096, 256], P('fsdp'), may hold values from -0.09375 to 0.09375
- w_up: bfloat16 [4096, 256], P('fsdp'), may hold values from -0.09375 to 0.09375
- w_down: bfloat16 [256, 4096], P(None, 'fsdp'), may hold values from -0.375 to 0.375
- delta: float32 [64, 128, 4096], P('replica', 'fsdp'), may hold values from -6 to 6
- anchor: float32 [128, 4096], P('fsdp'), may hold values from -3 to 3
- momentum: float32 [128, 4096], P('fsdp'), may hold values from -1.8 to 1.8
Outputs:
- grad_gate: bfloat16 [64, 4096, 256], P('replica', 'fsdp')
- grad_up: bfloat16 [64, 4096, 256], P('replica', 'fsdp')
- grad_down: bfloat16 [64, 256, 4096], P('replica', None, 'fsdp')
- new_anchor: float32 [128, 4096], P('fsdp')
- new_momentum: float32 [128, 4096], P('fsdp')
All inputs are finite; a program needn't handle non-finite values.
Results may differ from a plain program's by a relative error of at most 0.0049.
Values may be sent and summed in bfloat16 or wider, within the bound.
No kernel may reach another device: no remote copies, remote signals or barrier semaphores. Data moves between devices by JAX's collectives and lax.ppermute only.
A program may use at most 64 MiB of HBM per device.

v0:
```python
import jax
import jax.numpy as jnp
from jax import lax
from jax.sharding import PartitionSpec as P


def contract_rows(left, right):
    return lax.dot_general(
        left, right, (((0,), (0,)), ((), ())), preferred_element_type=jnp.float32
    )


def contract_cols(left, right):
    return lax.dot_general(
        left, right, (((1,), (1,)), ((), ())), preferred_element_type=jnp.float32
    )


def outer_update(pseudo, anchor_part, moment_part):
    new_moment = 0.9 * moment_part + pseudo
    new_params = anchor_part - 0.7 * (pseudo + 0.9 * new_moment)
    return (new_params, new_moment)


def on_device(tokens, cotangent, w_gate, w_up, w_down, delta, anchor, momentum):
    inputs = tokens[0]
    out_grad = cotangent[0]
    inputs_block, out_block = (
        lax.all_to_all(inputs, "fsdp", split_axis=1, concat_axis=0, tiled=True),
        lax.all_to_all(out_grad, "fsdp", split_axis=1, concat_axis=0, tiled=True),
    )
    pieces = (
        lax.all_gather(w_gate, "fsdp", axis=0, tiled=True),
        lax.all_gather(w_up, "fsdp", axis=0, tiled=True),
    )
    columns = inputs
    first = jnp.dot(columns, pieces[0], preferred_element_type=jnp.float32)
    second = jnp.dot(columns, pieces[1], preferred_element_type=jnp.float32)
    columns = out_grad
    d_hidden = contract_cols(columns, lax.all_gather(w_down, "fsdp", axis=1, tiled=True))
    sig = jax.nn.sigmoid(first)
    active = first * sig
    slope = sig * (1.0 + first * (1.0 - sig))
    hidden = (active * second).astype(jnp.bfloat16)
    d_up = (d_hidden * active).astype(jnp.bfloat16)
    d_gate = (d_hidden * second * slope).astype(jnp.bfloat16)
    pieces = (
        lax.all_gather(d_gate, "fsdp", axis=0, tiled=True),
        lax.all_gather(d_up, "fsdp", axis=0, tiled=True),
        lax.all_gather(hidden, "fsdp", axis=0, tiled=True),
    )
    grad_g = contract_rows(inputs_block, pieces[0])
    grad_u = contract_rows(inputs_block, pieces[1])
    grad_d = contract_rows(pieces[2], out_block)
    grad_g, grad_u, grad_d = (grad_g, grad_u, grad_d)
    replicas = lax.axis_size("replica")
    total = lax.psum(delta[0], "replica")
    pseudo = total / replicas
    new_anchor, new_momentum = outer_update(pseudo, anchor, momentum)
    grad_gate = grad_g.astype(jnp.bfloat16)[None]
    grad_up = grad_u.astype(jnp.bfloat16)[None]
    grad_down = grad_d.astype(jnp.bfloat16)[None]
    return (grad_gate, grad_up, grad_down, new_anchor, new_momentum)


def solution(mesh):
    placed = (
        P("replica", "fsdp", None),
        P("replica", "fsdp", None),
        P("fsdp", None),
        P("fsdp", None),
        P(None, "fsdp"),
        P("replica", "fsdp", None),
        P("fsdp", None),
        P("fsdp", None),
    )
    return jax.shard_map(
        on_device,
        mesh=mesh,
        in_specs=placed,
        out_specs=(
            P("replica", "fsdp", None),
            P("replica", "fsdp", None),
            P("replica", None, "fsdp"),
            P("fsdp", None),
            P("fsdp", None),
        ),
        check_vma=False,
    )
```

profile of v0, /device:TPU:1, one launch (start us, length us, event | category | flops | bytes accessed | tf_op | source)
XLA Modules:
  0.0 673.8 jit_solution(1601940122410706110)
XLA Ops:
  8.0 0.0 all-reduce.2.cloned.1.call-start
  8.0 0.7 all-reduce.2.cloned.1.call-update
  8.7 0.0 all-gather.8.cloned.1.call-start
  8.8 0.5 all-gather.8.cloned.1.call-update
  9.3 0.0 all-gather.4.cloned.1.call-start
  9.4 0.5 all-gather.4.cloned.1.call-update
  9.9 0.0 copy-start.1
  9.9 2.4 copy.17
  12.3 10.3 %all-to-all-start = ((bf16[128,8,512]{0,2,1:T(8,128)(2,1)}), bf16[128,8,512]{0,2,1:T(8,128)(2,1)S(1)}, u32[]{:S(2)}, u32[]{:S(2)}) async-start(bf16[128,8,512]{0,2,1:T(8,128)(2,1)} %bitcast.2), calls=%async_computation | async-start | bytes 2097152 | tf_op jit(solution)/shard_map/all_to_all | solution.py:29
  22.7 0.0 all-gather.6.cloned.1.call-start
  22.7 0.6 all-gather.6.cloned.1.call-update
  23.2 0.0 copy-done.1
  23.2 0.0 copy-start.3
  23.3 0.0 copy-start.4
  23.3 1.3 copy.19
  24.6 32.1 %all-to-all-done = bf16[128,8,512]{0,2,1:T(8,128)(2,1)S(1)} async-done(((bf16[128,8,512]{0,2,1:T(8,128)(2,1)}), bf16[128,8,512]{0,2,1:T(8,128)(2,1)S(1)}, u32[]{:S(2)}, u32[]{:S(2)}) %all-to-all-start) | async-done | bytes 1048608 | tf_op jit(solution)/shard_map/all_to_all | solution.py:29
  56.7 6.8 %all-to-all-start.1 = ((bf16[128,8,512]{0,2,1:T(8,128)(2,1)}), bf16[128,8,512]{0,2,1:T(8,128)(2,1)}, u32[]{:S(2)}, u32[]{:S(2)}) async-start(bf16[128,8,512]{0,2,1:T(8,128)(2,1)} %bitcast.9), calls=%async_computation.1 | async-start | bytes 2097152 | tf_op jit(solution)/shard_map/all_to_all | solution.py:30
  63.5 513.0 %all-reduce.2.cloned.1.call-done = f32[16,4096]{1,0:T(8,128)} async-done(((f32[16,4096]{1,0:T(8,128)}), f32[16,4096]{1,0:T(8,128)}) %all-reduce.2.cloned.1.call-update) | async-done | bytes 262160 | tf_op jit(solution)/shard_map/psum | solution.py:57
  576.5 0.0 copy-done.3
  576.5 0.0 copy-done.4
  576.5 1.8 multiply_subtract_fusion
  578.3 0.0 copy-start
  578.3 1.3 copy.18
  579.6 0.0 all-to-all-done.1
  579.6 1.5 copy.20
  581.1 0.0 all-gather.8.cloned.1.call-done
  581.1 0.0 copy-done
  581.1 2.0 fusion.3
  583.2 0.0 all-gather.4.cloned.1.call-done
  583.2 2.4 fusion.7
  585.6 0.0 copy-start.2
  585.7 0.0 all-gather.6.cloned.1.call-done
  585.7 2.1 multiply_convert_fusion
  587.8 44.5 %all_gather.21 = bf16[1024,256]{1,0:T(8,128)(2,1)S(1)} all-gather(bf16[128,256]{1,0:T(8,128)(2,1)S(1)} %get-tuple-element.23), channel_id=1, replica_groups=mesh['fsdp'=8,'replica'=64] {'fsdp'}, dimensions={0}, use_global_device_ids=true | all-gather | bytes 589824 | tf_op jit(solution)/shard_map/all_gather | solution.py:48
  632.4 0.0 copy-done.2
  632.4 0.5 fusion
  632.8 0.8 copy.21
  633.7 15.1 %all_gather.22 = bf16[1024,256]{1,0:T(8,128)(2,1)S(1)} all-gather(bf16[128,256]{1,0:T(8,128)(2,1)S(1)} %get-tuple-element.24), channel_id=1, replica_groups=mesh['fsdp'=8,'replica'=64] {'fsdp'}, dimensions={0}, use_global_device_ids=true | all-gather | bytes 589824 | tf_op jit(solution)/shard_map/all_gather | solution.py:49
  648.8 0.5 fusion.1
  649.2 0.8 copy.22
  650.1 15.0 %all_gather.23 = bf16[1024,256]{1,0:T(8,128)(2,1)S(1)} all-gather(bf16[128,256]{1,0:T(8,128)(2,1)S(1)} %get-tuple-element.22), channel_id=1, replica_groups=mesh['fsdp'=8,'replica'=64] {'fsdp'}, dimensions={0}, use_global_device_ids=true | all-gather | bytes 589824 | tf_op jit(solution)/shard_map/all_gather | solution.py:50
  665.0 1.2 fusion.2
Async XLA Ops:
  8.0 568.5 %all-reduce.2.cloned.1.call-start = ((), (), s32[]{:S(2)}) async-start(), calls=%async_computation.5 | async-start | bytes 524288 | tf_op jit(solution)/shard_map/psum | solution.py:57
  8.7 572.4 %all-gather.8.cloned.1.call-start = ((), (), s32[]{:S(2)}) async-start(), calls=%async_computation.4 | async-start | bytes 2359296 | tf_op jit(solution)/shard_map/all_gather | solution.py:33
  9.3 573.9 %all-gather.4.cloned.1.call-start = ((), (), s32[]{:S(2)}) async-start(), calls=%async_computation.2 | async-start | bytes 2359296 | tf_op jit(solution)/shard_map/all_gather | solution.py:40
  9.9 13.3 %copy-start.1 = (bf16[1,128,4096]{2,1,0:T(8,128)(2,1)S(1)}, bf16[1,128,4096]{2,1,0:T(8,128)(2,1)}, u32[]{:S(2)}) copy-start(bf16[1,128,4096]{2,1,0:T(8,128)(2,1)} %param.9) | copy-start | bytes 3145732
  12.3 44.3 %all-to-all-start = ((bf16[128,8,512]{0,2,1:T(8,128)(2,1)}), bf16[128,8,512]{0,2,1:T(8,128)(2,1)S(1)}, u32[]{:S(2)}, u32[]{:S(2)}) async-start(bf16[128,8,512]{0,2,1:T(8,128)(2,1)} %bitcast.2), calls=%async_computation | async-start | bytes 2097152 | tf_op jit(solution)/shard_map/all_to_all | solution.py:29
  22.7 563.0 %all-gather.6.cloned.1.call-start = ((), (), s32[]{:S(2)}) async-start(), calls=%async_computation.3 | async-start | bytes 2359296 | tf_op jit(solution)/shard_map/all_gather | solution.py:34
  23.2 553.2 %copy-start.3 = (f32[16,4096]{1,0:T(8,128)S(1)}, f32[16,4096]{1,0:T(8,128)}, u32[]{:S(2)}) copy-start(f32[16,4096]{1,0:T(8,128)} %param.14) | copy-start | bytes 786436
  23.3 553.2 %copy-start.4 = (f32[16,4096]{1,0:T(8,128)S(1)}, f32[16,4096]{1,0:T(8,128)}, u32[]{:S(2)}) copy-start(f32[16,4096]{1,0:T(8,128)} %param.15) | copy-start | bytes 786436
  56.7 522.9 %all-to-all-start.1 = ((bf16[128,8,512]{0,2,1:T(8,128)(2,1)}), bf16[128,8,512]{0,2,1:T(8,128)(2,1)}, u32[]{:S(2)}, u32[]{:S(2)}) async-start(bf16[128,8,512]{0,2,1:T(8,128)(2,1)} %bitcast.9), calls=%async_computation.1 | async-start | bytes 2097152 | tf_op jit(solution)/shard_map/all_to_all | solution.py:30
  578.3 2.8 copy-start
  585.6 46.7 %copy-start.2 = (bf16[8,128,512]{2,1,0:T(8,128)(2,1)S(1)}, bf16[8,128,512]{2,1,0:T(8,128)(2,1)}, u32[]{:S(2)}) copy-start(bf16[8,128,512]{2,1,0:T(8,128)(2,1)} %copy.18) | copy-start | bytes 3145732
Sparse Core Ops, SparseCore 0:
  11.7 564.6 all-reduce.1
Sparse Core Ops, SparseCore 1:
  11.4 56.5 all-gather.7
  70.0 55.5 all-gather.3
  127.5 36.6 all-gather.5
where the time goes:
time: 674 us
  waiting for transfers between devices  547 us (81%)
  blocking collectives  74.6 us (11%)
  starting transfers between devices  17.3 us (3%)
  between operations  15.8 us (2%)
  matrix products  8.64 us (1%)
  local copies, waits for them, and re-layouts  8.27 us (1%)
    psum x1, waiting for transfers between devices, on_device(): total = lax.psum(delta[0], 'replica')  513 us
    all_gather x1, blocking collectives, on_device(): lax.all_gather(d_gate, 'fsdp', axis=0, tiled=True)  44.5 us
    all_to_all x1, waiting for transfers between devices, on_device(): lax.all_to_all(inputs, 'fsdp', split_axis=1, concat_axis=0, tiled=True)  32.1 us
    all_gather x1, blocking collectives, on_device(): lax.all_gather(d_up, 'fsdp', axis=0, tiled=True)  15.1 us
    all_gather x1, blocking collectives, on_device(): lax.all_gather(hidden, 'fsdp', axis=0, tiled=True)  15 us
  transfers between devices with their start and end apart: 6, of which 2 were waited for; matrix products, arithmetic and copies ran while one was open for 2% of the time, Pallas kernels for 0%

commit v1 on v0

v1 whole, which is shorter than its diff:
```python
import functools

import jax
import jax.numpy as jnp
from jax import lax
from jax.experimental import pallas as pl
from jax.experimental.pallas import tpu as pltpu
from jax.sharding import Mesh
from jax.sharding import PartitionSpec as P

CHIPS = 4
ROWS = 128
WIDE = 1024
HALF = 512
HID = 256
VMEM_LIMIT = 48 * 1024 * 1024

F32 = jnp.float32
BF16 = jnp.bfloat16
ANY = pl.BlockSpec(memory_space=pl.ANY)
VMEM = pl.BlockSpec(memory_space=pltpu.VMEM)
SMEM = pl.BlockSpec(memory_space=pltpu.SMEM)


def run_copies(copies, sems):
    started = [pltpu.make_async_copy(src, dst, sems.at[i]) for i, (src, dst) in enumerate(copies)]
    for copy in started:
        copy.start()
    return started


def columns(base, width):
    return pl.ds(pl.multiple_of(base, HALF), width)


def pack_kernel(place, x, dy, one, two, three, beside, sems):
    chip, core = place[0], place[1]
    copies = []
    for shift in range(CHIPS):
        block = lax.rem(chip + shift, CHIPS) * WIDE
        if shift:
            target = (one, two, three)[shift - 1]
            copies += [(x.at[:, columns(block, WIDE)], target.at[0]), (dy.at[:, columns(block, WIDE)], target.at[1])]
        other = columns(block + (1 - core) * HALF, HALF)
        copies += [(x.at[:, other], beside.at[shift, 0]), (dy.at[:, other], beside.at[shift, 1])]
    for copy in run_copies(copies, sems):
        copy.wait()


def pack(place, x, dy):
    wide = jax.ShapeDtypeStruct((2, ROWS, WIDE), BF16)
    return pl.pallas_call(
        pack_kernel,
        out_shape=(wide, wide, wide, jax.ShapeDtypeStruct((CHIPS, 2, ROWS, HALF), BF16)),
        in_specs=[SMEM, ANY, ANY],
        out_specs=(ANY,) * 4,
        scratch_shapes=[pltpu.SemaphoreType.DMA((14,))],
        cost_estimate=pl.CostEstimate(flops=0, bytes_accessed=6 << 20, transcendentals=0),
        name="pack_tokens",
    )(place, x, dy)


def repack_kernel(place, one, two, three, out, sems):
    other = columns((1 - place[1]) * HALF, HALF)
    copies = [(ref.at[:, :, other], out.at[i]) for i, ref in enumerate((one, two, three))]
    for copy in run_copies(copies, sems):
        copy.wait()


def repack(place, one, two, three):
    return pl.pallas_call(
        repack_kernel,
        out_shape=jax.ShapeDtypeStruct((3, 2, ROWS, HALF), BF16),
        in_specs=[SMEM] + [ANY] * 3,
        out_specs=ANY,
        scratch_shapes=[pltpu.SemaphoreType.DMA((3,))],
        cost_estimate=pl.CostEstimate(flops=0, bytes_accessed=2 << 20, transcendentals=0),
        name="repack_tokens",
    )(place, one, two, three)


def hidden_kernel(place, x, dy, beside, ups, downs, mine, theirs, xs, dys, sems):
    chip, core = place[0], place[1]
    copies = []
    for shift in range(CHIPS):
        own = columns(lax.rem(chip + shift, CHIPS) * WIDE + core * HALF, HALF)
        copies += [
            (x.at[:, own], xs.at[shift, :ROWS]),
            (dy.at[:, own], dys.at[shift, :ROWS]),
            (beside.at[shift, 0], xs.at[shift, ROWS:]),
            (beside.at[shift, 1], dys.at[shift, ROWS:]),
        ]
    for copy in run_copies(copies, sems):
        copy.wait()
    gate = up = dh = None
    for shift in range(CHIPS):
        a, b = xs[shift], dys[shift]
        g = jnp.dot(a, ups[:, shift, 0].reshape(HALF, HID), preferred_element_type=F32)
        u = jnp.dot(a, ups[:, shift, 1].reshape(HALF, HID), preferred_element_type=F32)
        d = sum(
            lax.dot_general(
                b[:, 256 * h : 256 * (h + 1)],
                downs[:, shift, h].reshape(HID, 256),
                (((1,), (1,)), ((), ())),
                preferred_element_type=F32,
            )
            for h in range(2)
        )
        gate, up, dh = (g, u, d) if gate is None else (gate + g, up + u, dh + d)
    for i, value in enumerate((gate, up, dh)):
        mine[i] = value[:ROWS]
        theirs[i] = value[ROWS:]


def hidden_sums(place, x, dy, beside, ups, downs):
    out = jax.ShapeDtypeStruct((3, ROWS, HID), F32)
    return pl.pallas_call(
        hidden_kernel,
        out_shape=(out, out),
        in_specs=[SMEM, ANY, ANY, ANY, VMEM, VMEM],
        out_specs=(VMEM, VMEM),
        scratch_shapes=[
            pltpu.VMEM((CHIPS, 2 * ROWS, HALF), BF16),
            pltpu.VMEM((CHIPS, 2 * ROWS, HALF), BF16),
            pltpu.SemaphoreType.DMA((16,)),
        ],
        compiler_params=pltpu.CompilerParams(vmem_limit_bytes=VMEM_LIMIT),
        cost_estimate=pl.CostEstimate(flops=6 * 256 * 2048 * 256, bytes_accessed=6 << 20, transcendentals=0),
        name="hidden_sums",
    )(place, x, dy, beside, ups, downs)


def activation_kernel(mine, arrived, out):
    gate = mine[0] + arrived[0]
    up = mine[1] + arrived[1]
    dh = mine[2] + arrived[2]
    sig = jax.nn.sigmoid(gate)
    active = gate * sig
    slope = sig * (1.0 + gate * (1.0 - sig))
    out[0] = (dh * up * slope).astype(BF16)
    out[1] = (dh * active).astype(BF16)
    out[2] = (active * up).astype(BF16)


def activation(mine, arrived):
    return pl.pallas_call(
        activation_kernel,
        out_shape=jax.ShapeDtypeStruct((3, ROWS, HID), BF16),
        in_specs=[VMEM, VMEM],
        out_specs=VMEM,
        cost_estimate=pl.CostEstimate(flops=20 * ROWS * HID, bytes_accessed=1 << 20, transcendentals=ROWS * HID),
        name="activation",
    )(mine, arrived)


def grads_kernel(place, x, dy, beside, one, two, three, swapped, *rest):
    acts, (gg, gu, gd, xs, dys, hs, sems) = rest[:8], rest[8:]
    chip, core = place[0], place[1]
    own = columns(chip * WIDE + core * HALF, HALF)
    half = columns(core * HALF, HALF)
    sources = [(x.at[:, own], dy.at[:, own])]
    sources += [(ref.at[0, :, half], ref.at[1, :, half]) for ref in (one, two, three)]
    sources += [(beside.at[0, 0], beside.at[0, 1])]
    sources += [(swapped.at[i, 0], swapped.at[i, 1]) for i in range(3)]
    copies = []
    for i, (a, b) in enumerate(sources):
        rows = pl.ds(i * ROWS, ROWS)
        copies += [(a, xs.at[rows]), (b, dys.at[rows]), (acts[i], hs.at[:, rows])]
    for copy in run_copies(copies, sems):
        copy.wait()
    tall = (((0,), (0,)), ((), ()))
    gg[0] = lax.dot_general(xs[...], hs[0], tall, preferred_element_type=F32).astype(BF16)
    gu[0] = lax.dot_general(xs[...], hs[1], tall, preferred_element_type=F32).astype(BF16)
    gd[0] = lax.dot_general(hs[2], dys[...], tall, preferred_element_type=F32).astype(BF16)


def grads(place, x, dy, beside, arrived, swapped, acts):
    tokens = 8 * ROWS
    return pl.pallas_call(
        grads_kernel,
        out_shape=(
            jax.ShapeDtypeStruct((1, HALF, HID), BF16),
            jax.ShapeDtypeStruct((1, HALF, HID), BF16),
            jax.ShapeDtypeStruct((1, HID, HALF), BF16),
        ),
        in_specs=[SMEM] + [ANY] * 15,
        out_specs=(VMEM,) * 3,
        scratch_shapes=[
            pltpu.VMEM((tokens, HALF), BF16),
            pltpu.VMEM((tokens, HALF), BF16),
            pltpu.VMEM((3, tokens, HID), BF16),
            pltpu.SemaphoreType.DMA((24,)),
        ],
        compiler_params=pltpu.CompilerParams(vmem_limit_bytes=VMEM_LIMIT),
        cost_estimate=pl.CostEstimate(flops=6 * 1024 * 512 * 256, bytes_accessed=5 << 20, transcendentals=0),
        name="weight_grads",
    )(place, x, dy, beside, *arrived, swapped, *acts)


def from_shift(value, shift):
    return lax.ppermute(value, "yh", [(i, (i - shift) % CHIPS) for i in range(CHIPS)])


def to_shift(value, shift):
    return lax.ppermute(value, "yh", [(i, (i + shift) % CHIPS) for i in range(CHIPS)])


def other_core(value):
    return lax.ppermute(value, "core", [(0, 1), (1, 0)])


def mean_of_replicas(delta):
    everyone = ("yl", "x", "z")
    count = lax.axis_size(everyone)
    rows, cols = delta.shape
    tiles = delta.reshape(rows // 8, 8, cols // 128, 128).transpose(0, 2, 1, 3).reshape(count, 8, 128)
    parts = lax.all_to_all(tiles, everyone, 0, 0, tiled=True)
    mean = jnp.sum(parts, axis=0, keepdims=True) / count
    whole = lax.all_to_all(jnp.broadcast_to(mean, (count, 8, 128)), everyone, 0, 0, tiled=True)
    return whole.reshape(rows // 8, cols // 128, 8, 128).transpose(0, 2, 1, 3).reshape(rows, cols)


def on_device(tokens, cotangent, w_gate, w_up, w_down, delta, anchor, momentum):
    x, dy = tokens[0], cotangent[0]
    place = jnp.stack([lax.axis_index("yh"), lax.axis_index("core")]).astype(jnp.int32)
    nx, nz = lax.axis_size("x"), lax.axis_size("z")
    gate_rows, down_rows = HALF // nx, HID // nz
    at_x, at_z = lax.axis_index("x") * gate_rows, lax.axis_index("z") * down_rows

    down = lax.dynamic_slice_in_dim(w_down, at_z, down_rows, 0)
    share = jnp.concatenate(
        [
            lax.dynamic_slice_in_dim(w_gate, at_x, gate_rows, 0),
            lax.dynamic_slice_in_dim(w_up, at_x, gate_rows, 0),
            down[:, :HID],
            down[:, HID:],
        ]
    )
    shares = [share] + [from_shift(share, s) for s in (1, 3, 2)]
    shares = [shares[i] for i in (0, 1, 3, 2)]
    cut = 2 * gate_rows
    ups = lax.all_gather(jnp.concatenate([s[:cut] for s in shares]), "x", axis=0, tiled=True)
    downs = lax.all_gather(jnp.concatenate([s[cut:] for s in shares]), "z", axis=0, tiled=True)
    ups = ups.reshape(nx, CHIPS, 2, gate_rows, HID)
    downs = downs.reshape(nz, CHIPS, 2, down_rows, HID)

    one, two, three, beside = pack(place, x, dy)
    one, three, two = to_shift(one, 1), to_shift(three, 3), to_shift(two, 2)
    beside = other_core(beside)
    swapped = other_core(repack(place, one, two, three))

    pseudo = mean_of_replicas(delta[0])
    new_momentum = 0.9 * momentum + pseudo
    new_anchor = anchor - 0.7 * (pseudo + 0.9 * new_momentum)

    mine, theirs = hidden_sums(place, x, dy, beside, ups, downs)
    acts = activation(mine, other_core(theirs))
    spread = [acts, to_shift(acts, 1), to_shift(acts, 2), to_shift(acts, 3)]
    spread += [other_core(a) for a in spread]
    grad_gate, grad_up, grad_down = grads(place, x, dy, beside, (one, two, three), swapped, spread)
    return grad_gate, grad_up, grad_down, new_anchor, new_momentum


def solution(mesh):
    fine = Mesh(mesh.devices.reshape(4, 2, 2, 4, 8), ("yh", "core", "yl", "x", "z"))
    fsdp, replica = ("yh", "core"), ("yl", "x", "z")
    placed = (
        P(replica, fsdp, None),
        P(replica, fsdp, None),
        P(fsdp, None),
        P(fsdp, None),
        P(None, fsdp),
        P(replica, fsdp, None),
        P(fsdp, None),
        P(fsdp, None),
    )
    return jax.shard_map(
        on_device,
        mesh=fine,
        in_specs=placed,
        out_specs=(
            P(replica, fsdp, None),
            P(replica, fsdp, None),
            P(replica, None, fsdp),
            P(fsdp, None),
            P(fsdp, None),
        ),
        check_vma=False,
    )
```

time: 674 us -> 256 us (0.38)
  waiting for transfers between devices: 547 us -> 21 us
  Pallas kernels: 0 us -> 119 us
  blocking collectives: 74.6 us -> 0 us
  starting transfers between devices: 17.3 us -> 89.8 us
  matrix products: 8.64 us -> 0 us
    psum x1 -> x0, waiting for transfers between devices: 513 us -> none  [on_device(): total = lax.psum(delta[0], 'replica')]
    pallas_call x0 -> x5, Pallas kernels: none -> 119 us  [the longest x1 81.4 us: pack(): pl.pallas_call(pack_kernel, out_shape=(wide, wide, wide, jax.ShapeDtypeSt...]
    all_gather x3 -> x0, blocking collectives: 74.6 us -> none  [the longest x1 44.5 us: on_device(): lax.all_gather(d_gate, 'fsdp', axis=0, tiled=True)]
    ppermute x0 -> x16, starting transfers between devices: none -> 63.3 us  [the longest x6 28 us: to_shift(): lax.ppermute(value, 'yh', [(i, (i + shift) % CHIPS) for i in range(CHIPS)])]
    all_to_all x2, waiting for transfers between devices: 32.1 us -> 0.01 us  [the longest x1 0.01 us: mean_of_replicas(): parts = lax.all_to_all(tiles, everyone, 0, 0, tiled=True)]
    all_gather x3 -> x2, waiting for transfers between devices: 0.08 us -> 15.4 us  [the longest x1 15.4 us: on_device(): lax.all_gather(jnp.concatenate([s[:cut] for s in shares]), 'x', axis=0, t...]
    all_to_all x2, starting transfers between devices: 17.2 us -> 26.4 us  [the longest x1 16 us: mean_of_replicas(): parts = lax.all_to_all(tiles, everyone, 0, 0, tiled=True)]
    dot_general x6 -> x0, matrix products: 8.64 us -> none  [the longest x1 2.42 us: contract_cols(): lax.dot_general(left, right, (((1,), (1,)), ((), ())), preferred_element_...]
  transfers between devices with their start and end apart: 6 -> 20, of which waited for: 2 -> 3; matrix products, arithmetic and copies ran while one was open for 2% -> 1% of each run, Pallas kernels for 0% -> 45%
where the time goes in v1:
time: 256 us; the launch traced here: 255 us
  Pallas kernels  119 us (46%)
  starting transfers between devices  89.8 us (35%)
  waiting for transfers between devices  21 us (8%)
  between operations  14.5 us (6%)
  local copies, waits for them, and re-layouts  8.15 us (3%)
  other arithmetic  2.63 us (1%)
    pallas_call x1, Pallas kernels, pack(): pl.pallas_call(pack_kernel, out_shape=(wide, wide, wide, jax.ShapeDtypeSt...  81.4 us
    ppermute x6, starting transfers between devices, to_shift(): lax.ppermute(value, 'yh', [(i, (i + shift) % CHIPS) for i in range(CHIPS)])  28 us
    pallas_call x1, Pallas kernels, repack(): pl.pallas_call(repack_kernel, out_shape=jax.ShapeDtypeStruct((3, 2, ROWS,...  25.6 us
    ppermute x7, starting transfers between devices, other_core(): return lax.ppermute(value, 'core', [(0, 1), (1, 0)])  20.8 us
    all_to_all x1, starting transfers between devices, mean_of_replicas(): parts = lax.all_to_all(tiles, everyone, 0, 0, tiled=True)  16 us
    all_gather x1, waiting for transfers between devices, on_device(): lax.all_gather(jnp.concatenate([s[:cut] for s in shares]), 'x', axis=0, t...  15.4 us
    ppermute x3, starting transfers between devices, from_shift(): lax.ppermute(value, 'yh', [(i, (i - shift) % CHIPS) for i in range(CHIPS)])  14.5 us
    all_to_all x1, starting transfers between devices, mean_of_replicas(): lax.all_to_all(jnp.broadcast_to(mean, (count, 8, 128)), everyone, 0, 0, t...  10.4 us
  transfers between devices with their start and end apart: 20, of which 3 were waited for; matrix products, arithmetic and copies ran while one was open for 1% of the time, Pallas kernels for 45%

profile of v1, /device:TPU:1, one launch (start us, length us, event | category | flops | bytes accessed | tf_op | source)
XLA Modules:
  0.0 254.8 jit_solution(15111933607028381809)
XLA Ops:
  7.2 0.0 all-gather.5.cloned.1.call-start
  7.2 0.9 constant_dynamic-update-slice_fusion.1
  8.1 0.9 constant_dynamic-update-slice_fusion
  8.9 0.7 constant_dynamic-update-slice_fusion.3
  9.7 0.7 constant_dynamic-update-slice_fusion.2
  10.4 6.7 %collective-permute-start.5 = (bf16[320,256]{1,0:T(8,128)(2,1)S(1)}, bf16[320,256]{1,0:T(8,128)(2,1)S(1)}, u32[]{:S(2)}, u32[]{:S(2)}) collective-permute-start(bf16[320,256]{1,0:T(8,128)(2,1)S(1)} %pad_maximum_fusion), channel_id=1, source_target_pairs={{0,384},{128,0},{256,128},{384,256},{1,385},{129,1},{257,129},{385... | collective-permute-start | bytes 491528 | tf_op jit(solution)/shard_map/ppermute | solution.py:201
  17.1 3.5 %collective-permute-start.6 = (bf16[320,256]{1,0:T(8,128)(2,1)S(1)}, bf16[320,256]{1,0:T(8,128)(2,1)S(1)}, u32[]{:S(2)}, u32[]{:S(2)}) collective-permute-start(bf16[320,256]{1,0:T(8,128)(2,1)S(1)} %pad_maximum_fusion), channel_id=1, source_target_pairs={{0,256},{128,384},{256,0},{384,128},{1,257},{129,385},{257,1},{385... | collective-permute-start | bytes 491528 | tf_op jit(solution)/shard_map/ppermute | solution.py:201
  20.7 4.2 %collective-permute-start.7 = (bf16[320,256]{1,0:T(8,128)(2,1)S(1)}, bf16[320,256]{1,0:T(8,128)(2,1)S(1)}, u32[]{:S(2)}, u32[]{:S(2)}) collective-permute-start(bf16[320,256]{1,0:T(8,128)(2,1)S(1)} %pad_maximum_fusion), channel_id=1, source_target_pairs={{0,128},{128,256},{256,384},{384,0},{1,129},{129,257},{257,385},{3... | collective-permute-start | bytes 491528 | tf_op jit(solution)/shard_map/ppermute | solution.py:201
  24.9 0.0 collective-permute-done.5
  24.9 4.1 %collective-permute-done.6 = bf16[320,256]{1,0:T(8,128)(2,1)S(1)} collective-permute-done((bf16[320,256]{1,0:T(8,128)(2,1)S(1)}, bf16[320,256]{1,0:T(8,128)(2,1)S(1)}, u32[]{:S(2)}, u32[]{:S(2)}) %collective-permute-start.6) | collective-permute-done | bytes 163872 | tf_op jit(solution)/shard_map/ppermute | solution.py:201
  29.0 1.4 collective-permute-done.7
  30.4 0.7 copy-done.10
  31.1 0.0 all-gather.5.cloned.1.call-update
  31.1 0.0 all-gather.3.cloned.1.call-start
  31.1 0.0 copy-start
  31.1 0.0 copy-start.1
  31.2 0.8 copy-done.8
  32.1 0.0 all-gather.3.cloned.1.call-update
  32.1 0.6 pad_add_fusion.place
  32.7 81.4 %pack_tokens.1 = (bf16[2,128,1024]{2,1,0:T(8,128)(2,1)}, bf16[2,128,1024]{2,1,0:T(8,128)(2,1)}, bf16[2,128,1024]{2,1,0:T(8,128)(2,1)}, bf16[4,2,128,512]{3,2,1,0:T(8,128)(2,1)}) custom-call(s32[2]{0:T(128)} %pad_add_fusion.place, bf16[128,4096]{1,0:T(8,128)(2,1)} %bitcast.16, bf16[128,4096]{1,0:T(8,128)(2,1)} %bitcast.19), custom_call_target="tpu_custom_call" | custom-call | bytes 6291456 | tf_op jit(solution)/shard_map/pack_tokens/pallas_call | solution.py:52
  114.1 6.5 %collective-permute-start = (bf16[4,2,128,512]{3,2,1,0:T(8,128)(2,1)}, bf16[4,2,128,512]{3,2,1,0:T(8,128)(2,1)S(1)}, u32[]{:S(2)}, u32[]{:S(2)}) collective-permute-start(bf16[4,2,128,512]{3,2,1,0:T(8,128)(2,1)} %get-tuple-element.14), channel_id=1, source_target_pairs={{0,64},{64,0},{1,65},{65,1},{2,66},{66,2},{3,67},{67,3},{4,68},{68... | collective-permute-start | bytes 3145736 | tf_op jit(solution)/shard_map/ppermute | solution.py:209
  120.7 16.0 %all-to-all-start = ((f32[64,8,128]{2,1,0:T(8,128)}), f32[64,8,128]{2,1,0:T(8,128)S(1)}, u32[]{:S(2)}, u32[]{:S(2)}) async-start(f32[64,8,128]{2,1,0:T(8,128)} %bitcast.24), calls=%async_computation | async-start | bytes 524288 | tf_op jit(solution)/shard_map/all_to_all | solution.py:217
  136.7 3.9 %collective-permute-start.1 = (bf16[2,128,1024]{2,1,0:T(8,128)(2,1)}, bf16[2,128,1024]{2,1,0:T(8,128)(2,1)}, u32[]{:S(2)}, u32[]{:S(2)}) collective-permute-start(bf16[2,128,1024]{2,1,0:T(8,128)(2,1)} %get-tuple-element.15), channel_id=1, source_target_pairs={{0,128},{128,256},{256,384},{384,0},{1,129},{129,257},{257,385},{3... | collective-permute-start | bytes 1572872 | tf_op jit(solution)/shard_map/ppermute | solution.py:205
  140.7 5.7 %collective-permute-start.2 = (bf16[2,128,1024]{2,1,0:T(8,128)(2,1)}, bf16[2,128,1024]{2,1,0:T(8,128)(2,1)}, u32[]{:S(2)}, u32[]{:S(2)}) collective-permute-start(bf16[2,128,1024]{2,1,0:T(8,128)(2,1)} %get-tuple-element.16), channel_id=1, source_target_pairs={{0,256},{128,384},{256,0},{384,128},{1,257},{129,385},{257,1},{385... | collective-permute-start | bytes 1572872 | tf_op jit(solution)/shard_map/ppermute | solution.py:205
  146.3 4.7 %collective-permute-start.3 = (bf16[2,128,1024]{2,1,0:T(8,128)(2,1)}, bf16[2,128,1024]{2,1,0:T(8,128)(2,1)}, u32[]{:S(2)}, u32[]{:S(2)}) collective-permute-start(bf16[2,128,1024]{2,1,0:T(8,128)(2,1)} %get-tuple-element.17), channel_id=1, source_target_pairs={{0,384},{128,0},{256,128},{384,256},{1,385},{129,1},{257,129},{385... | collective-permute-start | bytes 1572872 | tf_op jit(solution)/shard_map/ppermute | solution.py:205
  151.1 0.0 all-to-all-done
  151.1 0.1 reduce_sum.9
  151.2 0.0 all-gather.5.cloned.1.call-done
  151.2 15.4 %all-gather.3.cloned.1.call-done = bf16[4096,256]{1,0:T(8,128)(2,1)} async-done(((bf16[1024,256]{1,0:T(8,128)(2,1)}), bf16[4096,256]{1,0:T(8,128)(2,1)}) %all-gather.3.cloned.1.call-update) | async-done | bytes 2097168 | tf_op jit(solution)/shard_map/all_gather | solution.py:242
  166.6 1.2 copy-done.3
  167.8 5.0 %hidden_sums.1 = (f32[3,128,256]{2,1,0:T(8,128)S(1)}, f32[3,128,256]{2,1,0:T(8,128)}) custom-call(s32[2]{0:T(128)S(1)} %copy-done.6, bf16[128,4096]{1,0:T(8,128)(2,1)S(1)} %bitcast.17, bf16[128,4096]{1,0:T(8,128)(2,1)S(1)} %bitcast.20, bf16[4,2,128,512]{3,2,1,0:T(8,128)(2,1)S(1)} %collective-permute-done.beside, bf16[4,4,2,128,256]{4,3,2,1,0:T(8,128)(2,1)} %bitcast.23, ...), custom_call_target="tpu_custom_call" | custom-call | flops 805306368 | bytes 6291456 | tf_op jit(solution)/shard_map/hidden_sums/pallas_call | solution.py:117
  172.9 0.7 copy-done.5
  173.6 2.5 collective-permute-start.8
  176.2 0.7 broadcast_in_dim.2
  176.9 10.4 %all-to-all-start.1 = ((f32[64,8,128]{2,1,0:T(8,128)}), f32[64,8,128]{2,1,0:T(8,128)}, u32[]{:S(2)}, u32[]{:S(2)}) async-start(f32[64,8,128]{2,1,0:T(8,128)} %broadcast_in_dim.2), calls=%async_computation.1 | async-start | bytes 524288 | tf_op jit(solution)/shard_map/all_to_all | solution.py:219
  187.3 0.7 copy-done.9
  188.1 1.9 activation.1.rest_0_
  189.9 4.2 %collective-permute-start.9 = (bf16[3,128,256]{2,1,0:T(8,128)(2,1)}, bf16[3,128,256]{2,1,0:T(8,128)(2,1)S(1)}, u32[]{:S(2)}, u32[]{:S(2)}) collective-permute-start(bf16[3,128,256]{2,1,0:T(8,128)(2,1)} %activation.1.rest_0_), channel_id=1, source_target_pairs={{0,128},{128,256},{256,384},{384,0},{1,129},{129,257},{257,385},{3... | collective-permute-start | bytes 589832 | tf_op jit(solution)/shard_map/ppermute | solution.py:205
  194.1 4.4 %collective-permute-start.10 = (bf16[3,128,256]{2,1,0:T(8,128)(2,1)}, bf16[3,128,256]{2,1,0:T(8,128)(2,1)S(1)}, u32[]{:S(2)}, u32[]{:S(2)}) collective-permute-start(bf16[3,128,256]{2,1,0:T(8,128)(2,1)} %activation.1.rest_0_), channel_id=1, source_target_pairs={{0,256},{128,384},{256,0},{384,128},{1,257},{129,385},{257,1},{385... | collective-permute-start | bytes 589832 | tf_op jit(solution)/shard_map/ppermute | solution.py:205
  198.5 5.2 %collective-permute-start.11 = (bf16[3,128,256]{2,1,0:T(8,128)(2,1)}, bf16[3,128,256]{2,1,0:T(8,128)(2,1)}, u32[]{:S(2)}, u32[]{:S(2)}) collective-permute-start(bf16[3,128,256]{2,1,0:T(8,128)(2,1)} %activation.1.rest_0_), channel_id=1, source_target_pairs={{0,384},{128,0},{256,128},{384,256},{1,385},{129,1},{257,129},{385... | collective-permute-start | bytes 589832 | tf_op jit(solution)/shard_map/ppermute | solution.py:205
  203.7 25.6 %repack_tokens.1 = bf16[3,2,128,512]{3,2,1,0:T(8,128)(2,1)} custom-call(s32[2]{0:T(128)} %pad_add_fusion.place, bf16[2,128,1024]{2,1,0:T(8,128)(2,1)} %collective-permute-done.1.one, bf16[2,128,1024]{2,1,0:T(8,128)(2,1)} %collective-permute-done.2.two, bf16[2,128,1024]{2,1,0:T(8,128)(2,1)} %collective-permute-done.3.three), custom_call_target="tpu_custom_call" | custom-call | bytes 2097152 | tf_op jit(solution)/shard_map/repack_tokens/pallas_call | solution.py:71
  229.3 3.0 %collective-permute-start.4 = (bf16[3,2,128,512]{3,2,1,0:T(8,128)(2,1)}, bf16[3,2,128,512]{3,2,1,0:T(8,128)(2,1)S(1)}, u32[]{:S(2)}, u32[]{:S(2)}) collective-permute-start(bf16[3,2,128,512]{3,2,1,0:T(8,128)(2,1)} %repack_tokens.1), channel_id=1, source_target_pairs={{0,64},{64,0},{1,65},{65,1},{2,66},{66,2},{3,67},{67,3},{4,68},{68... | collective-permute-start | bytes 2359304 | tf_op jit(solution)/shard_map/ppermute | solution.py:209
  232.4 1.9 collective-permute-start.12
  234.3 2.4 collective-permute-start.13
  236.8 1.9 collective-permute-start.14
  238.7 2.4 collective-permute-start.15
  241.1 2.0 multiply_subtract_fusion
  243.1 4.8 %weight_grads.1 = (bf16[1,512,256]{2,1,0:T(8,128)(2,1)}, bf16[1,512,256]{2,1,0:T(8,128)(2,1)}, bf16[1,256,512]{2,1,0:T(8,128)(2,1)}) custom-call(s32[2]{0:T(128)S(1)} %copy-done.7, bf16[128,4096]{1,0:T(8,128)(2,1)S(1)} %bitcast.18, bf16[128,4096]{1,0:T(8,128)(2,1)S(1)} %bitcast.21, bf16[4,2,128,512]{3,2,1,0:T(8,128)(2,1)} %copy-done.2, ...), custom_call_target="tpu_custom_call" | custom-call | flops 805306368 | bytes 5242880 | tf_op jit(solution)/shard_map/weight_grads/pallas_call | solution.py:179
  (37 shorter events, 0.1 us)
Async XLA Ops:
  7.2 144.0 %all-gather.5.cloned.1.call-start = ((), (), s32[]{:S(2)}) async-start(), calls=%async_computation.3 | async-start | bytes 1179648 | tf_op jit(solution)/shard_map/all_gather | solution.py:243
  10.4 14.5 %collective-permute-start.5 = (bf16[320,256]{1,0:T(8,128)(2,1)S(1)}, bf16[320,256]{1,0:T(8,128)(2,1)S(1)}, u32[]{:S(2)}, u32[]{:S(2)}) collective-permute-start(bf16[320,256]{1,0:T(8,128)(2,1)S(1)} %pad_maximum_fusion), channel_id=1, source_target_pairs={{0,384},{128,0},{256,128},{384,256},{1,385},{129,1},{257,129},{385... | collective-permute-start | bytes 491528 | tf_op jit(solution)/shard_map/ppermute | solution.py:201
  17.1 11.9 %collective-permute-start.6 = (bf16[320,256]{1,0:T(8,128)(2,1)S(1)}, bf16[320,256]{1,0:T(8,128)(2,1)S(1)}, u32[]{:S(2)}, u32[]{:S(2)}) collective-permute-start(bf16[320,256]{1,0:T(8,128)(2,1)S(1)} %pad_maximum_fusion), channel_id=1, source_target_pairs={{0,256},{128,384},{256,0},{384,128},{1,257},{129,385},{257,1},{385... | collective-permute-start | bytes 491528 | tf_op jit(solution)/shard_map/ppermute | solution.py:201
  20.7 9.7 %collective-permute-start.7 = (bf16[320,256]{1,0:T(8,128)(2,1)S(1)}, bf16[320,256]{1,0:T(8,128)(2,1)S(1)}, u32[]{:S(2)}, u32[]{:S(2)}) collective-permute-start(bf16[320,256]{1,0:T(8,128)(2,1)S(1)} %pad_maximum_fusion), channel_id=1, source_target_pairs={{0,128},{128,256},{256,384},{384,0},{1,129},{129,257},{257,385},{3... | collective-permute-start | bytes 491528 | tf_op jit(solution)/shard_map/ppermute | solution.py:201
  30.4 0.7 copy-start.10
  31.1 135.5 %all-gather.3.cloned.1.call-start = ((), (), s32[]{:S(2)}) async-start(), calls=%async_computation.2 | async-start | bytes 2621440 | tf_op jit(solution)/shard_map/all_gather | solution.py:242
  31.1 135.5 %copy-start = (bf16[1,128,4096]{2,1,0:T(8,128)(2,1)S(1)}, bf16[1,128,4096]{2,1,0:T(8,128)(2,1)}, u32[]{:S(2)}) copy-start(bf16[1,128,4096]{2,1,0:T(8,128)(2,1)} %param.8) | copy-start | bytes 3145732
  31.1 135.5 %copy-start.1 = (bf16[1,128,4096]{2,1,0:T(8,128)(2,1)S(1)}, bf16[1,128,4096]{2,1,0:T(8,128)(2,1)}, u32[]{:S(2)}) copy-start(bf16[1,128,4096]{2,1,0:T(8,128)(2,1)} %param.9) | copy-start | bytes 3145732
  31.2 0.9 copy-start.8
  32.7 133.9 %copy-start.6 = (s32[2]{0:T(128)S(1)}, s32[2]{0:T(128)}, u32[]{:S(2)}) copy-start(s32[2]{0:T(128)} %pad_add_fusion.place) | copy-start | bytes 28
  114.1 37.1 %collective-permute-start = (bf16[4,2,128,512]{3,2,1,0:T(8,128)(2,1)}, bf16[4,2,128,512]{3,2,1,0:T(8,128)(2,1)S(1)}, u32[]{:S(2)}, u32[]{:S(2)}) collective-permute-start(bf16[4,2,128,512]{3,2,1,0:T(8,128)(2,1)} %get-tuple-element.14), channel_id=1, source_target_pairs={{0,64},{64,0},{1,65},{65,1},{2,66},{66,2},{3,67},{67,3},{4,68},{68... | collective-permute-start | bytes 3145736 | tf_op jit(solution)/shard_map/ppermute | solution.py:209
  120.7 30.4 %all-to-all-start = ((f32[64,8,128]{2,1,0:T(8,128)}), f32[64,8,128]{2,1,0:T(8,128)S(1)}, u32[]{:S(2)}, u32[]{:S(2)}) async-start(f32[64,8,128]{2,1,0:T(8,128)} %bitcast.24), calls=%async_computation | async-start | bytes 524288 | tf_op jit(solution)/shard_map/all_to_all | solution.py:217
  136.7 61.8 %collective-permute-start.1 = (bf16[2,128,1024]{2,1,0:T(8,128)(2,1)}, bf16[2,128,1024]{2,1,0:T(8,128)(2,1)}, u32[]{:S(2)}, u32[]{:S(2)}) collective-permute-start(bf16[2,128,1024]{2,1,0:T(8,128)(2,1)} %get-tuple-element.15), channel_id=1, source_target_pairs={{0,128},{128,256},{256,384},{384,0},{1,129},{129,257},{257,385},{3... | collective-permute-start | bytes 1572872 | tf_op jit(solution)/shard_map/ppermute | solution.py:205
  140.7 63.0 %collective-permute-start.2 = (bf16[2,128,1024]{2,1,0:T(8,128)(2,1)}, bf16[2,128,1024]{2,1,0:T(8,128)(2,1)}, u32[]{:S(2)}, u32[]{:S(2)}) collective-permute-start(bf16[2,128,1024]{2,1,0:T(8,128)(2,1)} %get-tuple-element.16), channel_id=1, source_target_pairs={{0,256},{128,384},{256,0},{384,128},{1,257},{129,385},{257,1},{385... | collective-permute-start | bytes 1572872 | tf_op jit(solution)/shard_map/ppermute | solution.py:205
  146.3 57.4 %collective-permute-start.3 = (bf16[2,128,1024]{2,1,0:T(8,128)(2,1)}, bf16[2,128,1024]{2,1,0:T(8,128)(2,1)}, u32[]{:S(2)}, u32[]{:S(2)}) collective-permute-start(bf16[2,128,1024]{2,1,0:T(8,128)(2,1)} %get-tuple-element.17), channel_id=1, source_target_pairs={{0,384},{128,0},{256,128},{384,256},{1,385},{129,1},{257,129},{385... | collective-permute-start | bytes 1572872 | tf_op jit(solution)/shard_map/ppermute | solution.py:205
  151.2 21.7 %copy-start.2 = (bf16[4,2,128,512]{3,2,1,0:T(8,128)(2,1)}, bf16[4,2,128,512]{3,2,1,0:T(8,128)(2,1)S(1)}, u32[]{:S(2)}) copy-start(bf16[4,2,128,512]{3,2,1,0:T(8,128)(2,1)S(1)} %collective-permute-done.beside) | copy-start | bytes 3145732
  166.6 1.2 copy-start.3
  172.9 0.7 copy-start.5
  173.6 13.7 %collective-permute-start.8 = (f32[3,128,256]{2,1,0:T(8,128)}, f32[3,128,256]{2,1,0:T(8,128)S(1)}, u32[]{:S(2)}, u32[]{:S(2)}) collective-permute-start(f32[3,128,256]{2,1,0:T(8,128)} %get-tuple-element.19), channel_id=1, source_target_pairs={{0,64},{64,0},{1,65},{65,1},{2,66},{66,2},{3,67},{67,3},{4,68},{68... | collective-permute-start | bytes 1179656 | tf_op jit(solution)/shard_map/ppermute | solution.py:209
  176.9 64.2 %all-to-all-start.1 = ((f32[64,8,128]{2,1,0:T(8,128)}), f32[64,8,128]{2,1,0:T(8,128)}, u32[]{:S(2)}, u32[]{:S(2)}) async-start(f32[64,8,128]{2,1,0:T(8,128)} %broadcast_in_dim.2), calls=%async_computation.1 | async-start | bytes 524288 | tf_op jit(solution)/shard_map/all_to_all | solution.py:219
  187.3 0.8 copy-start.9
  188.1 55.1 %copy-start.7 = (s32[2]{0:T(128)S(1)}, s32[2]{0:T(128)}, u32[]{:S(2)}) copy-start(s32[2]{0:T(128)} %pad_add_fusion.place) | copy-start | bytes 28
  189.9 42.4 %copy-start.4 = (bf16[3,128,256]{2,1,0:T(8,128)(2,1)S(1)}, bf16[3,128,256]{2,1,0:T(8,128)(2,1)}, u32[]{:S(2)}) copy-start(bf16[3,128,256]{2,1,0:T(8,128)(2,1)} %activation.1.rest_0_) | copy-start | bytes 589828
  189.9 44.4 %collective-permute-start.9 = (bf16[3,128,256]{2,1,0:T(8,128)(2,1)}, bf16[3,128,256]{2,1,0:T(8,128)(2,1)S(1)}, u32[]{:S(2)}, u32[]{:S(2)}) collective-permute-start(bf16[3,128,256]{2,1,0:T(8,128)(2,1)} %activation.1.rest_0_), channel_id=1, source_target_pairs={{0,128},{128,256},{256,384},{384,0},{1,129},{129,257},{257,385},{3... | collective-permute-start | bytes 589832 | tf_op jit(solution)/shard_map/ppermute | solution.py:205
  194.1 42.6 %collective-permute-start.10 = (bf16[3,128,256]{2,1,0:T(8,128)(2,1)}, bf16[3,128,256]{2,1,0:T(8,128)(2,1)S(1)}, u32[]{:S(2)}, u32[]{:S(2)}) collective-permute-start(bf16[3,128,256]{2,1,0:T(8,128)(2,1)} %activation.1.rest_0_), channel_id=1, source_target_pairs={{0,256},{128,384},{256,0},{384,128},{1,257},{129,385},{257,1},{385... | collective-permute-start | bytes 589832 | tf_op jit(solution)/shard_map/ppermute | solution.py:205
  198.5 40.2 %collective-permute-start.11 = (bf16[3,128,256]{2,1,0:T(8,128)(2,1)}, bf16[3,128,256]{2,1,0:T(8,128)(2,1)}, u32[]{:S(2)}, u32[]{:S(2)}) collective-permute-start(bf16[3,128,256]{2,1,0:T(8,128)(2,1)} %activation.1.rest_0_), channel_id=1, source_target_pairs={{0,384},{128,0},{256,128},{384,256},{1,385},{129,1},{257,129},{385... | collective-permute-start | bytes 589832 | tf_op jit(solution)/shard_map/ppermute | solution.py:205
  229.3 13.8 %collective-permute-start.4 = (bf16[3,2,128,512]{3,2,1,0:T(8,128)(2,1)}, bf16[3,2,128,512]{3,2,1,0:T(8,128)(2,1)S(1)}, u32[]{:S(2)}, u32[]{:S(2)}) collective-permute-start(bf16[3,2,128,512]{3,2,1,0:T(8,128)(2,1)} %repack_tokens.1), channel_id=1, source_target_pairs={{0,64},{64,0},{1,65},{65,1},{2,66},{66,2},{3,67},{67,3},{4,68},{68... | collective-permute-start | bytes 2359304 | tf_op jit(solution)/shard_map/ppermute | solution.py:209
  232.4 10.7 %collective-permute-start.12 = (bf16[3,128,256]{2,1,0:T(8,128)(2,1)S(1)}, bf16[3,128,256]{2,1,0:T(8,128)(2,1)}, u32[]{:S(2)}, u32[]{:S(2)}) collective-permute-start(bf16[3,128,256]{2,1,0:T(8,128)(2,1)S(1)} %copy-done.4), channel_id=1, source_target_pairs={{0,64},{64,0},{1,65},{65,1},{2,66},{66,2},{3,67},{67,3},{4,68},{68... | collective-permute-start | bytes 589832 | tf_op jit(solution)/shard_map/ppermute | solution.py:209
  234.3 8.8 %collective-permute-start.13 = (bf16[3,128,256]{2,1,0:T(8,128)(2,1)S(1)}, bf16[3,128,256]{2,1,0:T(8,128)(2,1)}, u32[]{:S(2)}, u32[]{:S(2)}) collective-permute-start(bf16[3,128,256]{2,1,0:T(8,128)(2,1)S(1)} %collective-permute-done.9.rest_1_), channel_id=1, source_target_pairs={{0,64},{64,0},{1,65},{65,1},{2,66},{66,2},{3,67},{67,3},{4,68},{68... | collective-permute-start | bytes 589832 | tf_op jit(solution)/shard_map/ppermute | solution.py:209
  236.8 6.3 %collective-permute-start.14 = (bf16[3,128,256]{2,1,0:T(8,128)(2,1)S(1)}, bf16[3,128,256]{2,1,0:T(8,128)(2,1)}, u32[]{:S(2)}, u32[]{:S(2)}) collective-permute-start(bf16[3,128,256]{2,1,0:T(8,128)(2,1)S(1)} %collective-permute-done.10.rest_2_), channel_id=1, source_target_pairs={{0,64},{64,0},{1,65},{65,1},{2,66},{66,2},{3,67},{67,3},{4,68},{68... | collective-permute-start | bytes 589832 | tf_op jit(solution)/shard_map/ppermute | solution.py:209
  238.7 4.4 %collective-permute-start.15 = (bf16[3,128,256]{2,1,0:T(8,128)(2,1)}, bf16[3,128,256]{2,1,0:T(8,128)(2,1)}, u32[]{:S(2)}, u32[]{:S(2)}) collective-permute-start(bf16[3,128,256]{2,1,0:T(8,128)(2,1)} %collective-permute-done.11.rest_3_), channel_id=1, source_target_pairs={{0,64},{64,0},{1,65},{65,1},{2,66},{66,2},{3,67},{67,3},{4,68},{68... | collective-permute-start | bytes 589832 | tf_op jit(solution)/shard_map/ppermute | solution.py:209
Sparse Core Ops, SparseCore 0:
  31.2 86.9 all-gather.4
  120.3 46.2 all-gather.2

commit v2 on v1

v2 whole, which is shorter than its diff:
```python
import functools

import jax
import jax.numpy as jnp
from jax import lax
from jax.experimental import pallas as pl
from jax.experimental.pallas import tpu as pltpu
from jax.sharding import Mesh
from jax.sharding import PartitionSpec as P

CHIPS = 4
ROWS = 128
WIDE = 1024
HALF = 512
HID = 256
VMEM_LIMIT = 48 * 1024 * 1024

F32 = jnp.float32
BF16 = jnp.bfloat16
ANY = pl.BlockSpec(memory_space=pl.ANY)
VMEM = pl.BlockSpec(memory_space=pltpu.VMEM)
SMEM = pl.BlockSpec(memory_space=pltpu.SMEM)


def run_copies(copies, sems):
    started = [pltpu.make_async_copy(src, dst, sems.at[i]) for i, (src, dst) in enumerate(copies)]
    for copy in started:
        copy.start()
    for copy in started:
        copy.wait()


def columns(base):
    return pl.ds(pl.multiple_of(base, HALF), HALF)


def wide_columns(chip):
    return pl.ds(pl.multiple_of(chip * WIDE, WIDE), WIDE)


def share_kernel(parts, place, gate, up, down, out, sems):
    gate_rows, down_rows = HALF // parts, HID // parts
    at_gate = pl.ds(pl.multiple_of(place[1] * gate_rows, gate_rows), gate_rows)
    at_down = pl.ds(pl.multiple_of(place[1] * down_rows, down_rows), down_rows)
    copies = []
    for chip in range(CHIPS):
        to = out.at[chip]
        copies += [
            (gate.at[at_gate], to.at[pl.ds(0, gate_rows)]),
            (up.at[at_gate], to.at[pl.ds(gate_rows, gate_rows)]),
            (down.at[at_down, :HID], to.at[pl.ds(2 * gate_rows, down_rows)]),
            (down.at[at_down, HID:], to.at[pl.ds(2 * gate_rows + down_rows, down_rows)]),
        ]
    run_copies(copies, sems)


def own_share(place, gate, up, down, parts):
    rows = 2 * (HALF + HID) // parts
    return pl.pallas_call(
        functools.partial(share_kernel, parts),
        out_shape=jax.ShapeDtypeStruct((CHIPS, rows, HID), BF16),
        in_specs=[SMEM, ANY, ANY, ANY],
        out_specs=VMEM,
        scratch_shapes=[pltpu.SemaphoreType.DMA((16,))],
        cost_estimate=pl.CostEstimate(flops=0, bytes_accessed=2 << 20, transcendentals=0),
        name="weight_share",
    )(place, gate, up, down)


def pack_kernel(shifts, place, x, dy, after, *rest):
    outs, sems = rest[:-1], rest[-1]
    del after
    copies = []
    for shift, out in zip(shifts, outs):
        block = wide_columns(lax.rem(place[2] + shift, CHIPS))
        copies += [(x.at[:, block], out.at[0]), (dy.at[:, block], out.at[1])]
    if len(outs) > len(shifts):
        for chip in range(CHIPS):
            other = columns(chip * WIDE + (1 - place[0]) * HALF)
            copies += [(x.at[:, other], outs[-1].at[chip, 0]), (dy.at[:, other], outs[-1].at[chip, 1])]
    run_copies(copies, sems)


def pack(place, x, dy, after, shifts, with_beside):
    outs = [jax.ShapeDtypeStruct((2, ROWS, WIDE), BF16)] * len(shifts)
    if with_beside:
        outs.append(jax.ShapeDtypeStruct((CHIPS, 2, ROWS, HALF), BF16))
    return pl.pallas_call(
        functools.partial(pack_kernel, shifts),
        out_shape=tuple(outs),
        in_specs=[SMEM, ANY, ANY, ANY],
        out_specs=(VMEM,) * len(outs),
        scratch_shapes=[pltpu.SemaphoreType.DMA((2 * len(shifts) + 8 * with_beside,))],
        compiler_params=pltpu.CompilerParams(vmem_limit_bytes=VMEM_LIMIT),
        cost_estimate=pl.CostEstimate(flops=0, bytes_accessed=len(outs) << 20, transcendentals=0),
        name="pack_tokens",
    )(place, x, dy, after)


def repack_kernel(place, one, two, three, out, sems):
    other = columns((1 - place[0]) * HALF)
    run_copies([(ref.at[:, :, other], out.at[i]) for i, ref in enumerate((one, two, three))], sems)


def repack(place, arrived):
    return pl.pallas_call(
        repack_kernel,
        out_shape=jax.ShapeDtypeStruct((CHIPS - 1, 2, ROWS, HALF), BF16),
        in_specs=[SMEM] + [ANY] * 3,
        out_specs=VMEM,
        scratch_shapes=[pltpu.SemaphoreType.DMA((CHIPS - 1,))],
        compiler_params=pltpu.CompilerParams(vmem_limit_bytes=VMEM_LIMIT),
        cost_estimate=pl.CostEstimate(flops=0, bytes_accessed=2 << 20, transcendentals=0),
        name="repack_tokens",
    )(place, *arrived)


def tiles_kernel(delta, after, out, sems):
    del after
    rows, cols = delta.shape
    copies = []
    for i in range(rows // 8):
        for j in range(cols // 128):
            copies.append((delta.at[8 * i : 8 * i + 8, 128 * j : 128 * j + 128], out.at[i * (cols // 128) + j]))
    run_copies(copies, sems)


def tiles_of(delta, after):
    count = delta.size // 1024
    return pl.pallas_call(
        tiles_kernel,
        out_shape=jax.ShapeDtypeStruct((count, 8, 128), F32),
        in_specs=[ANY, ANY],
        out_specs=VMEM,
        scratch_shapes=[pltpu.SemaphoreType.DMA((count,))],
        cost_estimate=pl.CostEstimate(flops=0, bytes_accessed=1 << 19, transcendentals=0),
        name="delta_tiles",
    )(delta, after)


def hidden_kernel(waited, place, x, dy, beside, *rest):
    rest = rest[waited:]
    weights, (mine, theirs, xs, dys, gates, ups, downs, sems) = rest[:-8], rest[-8:]
    parts = len(weights)
    gate_rows, down_rows = HALF // parts, HID // parts
    core, at = place[0], place[1]
    copies = []
    for shift, ref in enumerate(weights):
        part = lax.rem(at + shift, parts)
        to_gate = pl.ds(pl.multiple_of(part * gate_rows, gate_rows), gate_rows)
        to_down = pl.ds(pl.multiple_of(part * down_rows, down_rows), down_rows)
        copies += [
            (ref.at[:, pl.ds(0, gate_rows)], gates.at[:, to_gate]),
            (ref.at[:, pl.ds(gate_rows, gate_rows)], ups.at[:, to_gate]),
            (ref.at[:, pl.ds(2 * gate_rows, down_rows)], downs.at[:, 0, to_down]),
            (ref.at[:, pl.ds(2 * gate_rows + down_rows, down_rows)], downs.at[:, 1, to_down]),
        ]
    for chip in range(CHIPS):
        own = columns(chip * WIDE + core * HALF)
        copies += [
            (x.at[:, own], xs.at[chip, :ROWS]),
            (dy.at[:, own], dys.at[chip, :ROWS]),
            (beside.at[chip, 0], xs.at[chip, ROWS:]),
            (beside.at[chip, 1], dys.at[chip, ROWS:]),
        ]
    run_copies(copies, sems)
    gate = up = dh = 0.0
    for chip in range(CHIPS):
        a, b = xs[chip], dys[chip]
        gate += jnp.dot(a, gates[chip], preferred_element_type=F32)
        up += jnp.dot(a, ups[chip], preferred_element_type=F32)
        for h in range(2):
            dh += lax.dot_general(
                b[:, HID * h : HID * (h + 1)],
                downs[chip, h],
                (((1,), (1,)), ((), ())),
                preferred_element_type=F32,
            )
    for i, value in enumerate((gate, up, dh)):
        mine[i] = value[:ROWS]
        theirs[i] = value[ROWS:]


def hidden_sums(place, x, dy, beside, weights, after):
    out = jax.ShapeDtypeStruct((3, ROWS, HID), F32)
    return pl.pallas_call(
        functools.partial(hidden_kernel, len(after)),
        out_shape=(out, out),
        in_specs=[SMEM] + [ANY] * (3 + len(after) + len(weights)),
        out_specs=(VMEM, VMEM),
        scratch_shapes=[
            pltpu.VMEM((CHIPS, 2 * ROWS, HALF), BF16),
            pltpu.VMEM((CHIPS, 2 * ROWS, HALF), BF16),
            pltpu.VMEM((CHIPS, HALF, HID), BF16),
            pltpu.VMEM((CHIPS, HALF, HID), BF16),
            pltpu.VMEM((CHIPS, 2, HID, HID), BF16),
            pltpu.SemaphoreType.DMA((4 * len(weights) + 16,)),
        ],
        compiler_params=pltpu.CompilerParams(vmem_limit_bytes=VMEM_LIMIT),
        cost_estimate=pl.CostEstimate(flops=6 * 256 * 2048 * 256, bytes_accessed=6 << 20, transcendentals=0),
        name="hidden_sums",
    )(place, x, dy, beside, *after, *weights)


def activation_kernel(mine, arrived, out):
    gate = mine[0] + arrived[0]
    up = mine[1] + arrived[1]
    dh = mine[2] + arrived[2]
    sig = jax.nn.sigmoid(gate)
    active = gate * sig
    slope = sig * (1.0 + gate * (1.0 - sig))
    for i, value in enumerate((dh * up * slope, dh * active, active * up)):
        for chip in range(CHIPS):
            out[chip, i] = value.astype(BF16)


def activation(mine, arrived):
    return pl.pallas_call(
        activation_kernel,
        out_shape=jax.ShapeDtypeStruct((CHIPS, 3, ROWS, HID), BF16),
        in_specs=[VMEM, VMEM],
        out_specs=VMEM,
        cost_estimate=pl.CostEstimate(flops=20 * ROWS * HID, bytes_accessed=1 << 20, transcendentals=ROWS * HID),
        name="activation",
    )(mine, arrived)


def grads_kernel(place, x, dy, beside, one, two, three, swapped, acts, acts_beside, gg, gu, gd, xs, dys, hs, sems):
    core, chip = place[0], place[2]
    half, own = columns(core * HALF), columns(chip * WIDE + core * HALF)
    copies = []
    for i, ref in enumerate((None, one, two, three)):
        source = lax.rem(chip + CHIPS - i, CHIPS)
        near = pl.ds(pl.multiple_of(source * ROWS, ROWS), ROWS)
        far = pl.ds(pl.multiple_of((CHIPS + source) * ROWS, ROWS), ROWS)
        if i:
            copies += [(ref.at[0, :, half], xs.at[near]), (ref.at[1, :, half], dys.at[near])]
            copies += [(swapped.at[i - 1, 0], xs.at[far]), (swapped.at[i - 1, 1], dys.at[far])]
        else:
            copies += [(x.at[:, own], xs.at[near]), (dy.at[:, own], dys.at[near])]
            copies += [(beside.at[chip, 0], xs.at[far]), (beside.at[chip, 1], dys.at[far])]
        near, far = pl.ds(i * ROWS, ROWS), pl.ds((CHIPS + i) * ROWS, ROWS)
        copies += [(acts.at[i], hs.at[:, near]), (acts_beside.at[i], hs.at[:, far])]
    run_copies(copies, sems)
    tall = (((0,), (0,)), ((), ()))
    gg[0] = lax.dot_general(xs[...], hs[0], tall, preferred_element_type=F32).astype(BF16)
    gu[0] = lax.dot_general(xs[...], hs[1], tall, preferred_element_type=F32).astype(BF16)
    gd[0] = lax.dot_general(hs[2], dys[...], tall, preferred_element_type=F32).astype(BF16)


def grads(place, x, dy, beside, arrived, swapped, acts, acts_beside):
    tokens = 2 * CHIPS * ROWS
    return pl.pallas_call(
        grads_kernel,
        out_shape=(
            jax.ShapeDtypeStruct((1, HALF, HID), BF16),
            jax.ShapeDtypeStruct((1, HALF, HID), BF16),
            jax.ShapeDtypeStruct((1, HID, HALF), BF16),
        ),
        in_specs=[SMEM] + [ANY] * 9,
        out_specs=(VMEM,) * 3,
        scratch_shapes=[
            pltpu.VMEM((tokens, HALF), BF16),
            pltpu.VMEM((tokens, HALF), BF16),
            pltpu.VMEM((3, tokens, HID), BF16),
            pltpu.SemaphoreType.DMA((24,)),
        ],
        compiler_params=pltpu.CompilerParams(vmem_limit_bytes=VMEM_LIMIT),
        cost_estimate=pl.CostEstimate(flops=6 * 1024 * 512 * 256, bytes_accessed=5 << 20, transcendentals=0),
        name="weight_grads",
    )(place, x, dy, beside, *arrived, swapped, acts, acts_beside)


def to_chips(value):
    return lax.all_to_all(value, "yh", 0, 0, tiled=True)


def to_shift(value, shift):
    return lax.ppermute(value, "yh", [(i, (i + shift) % CHIPS) for i in range(CHIPS)])


def other_core(value):
    return lax.ppermute(value, "core", [(0, 1), (1, 0)])


def from_x(value, shift, size):
    return lax.ppermute(value, "x", [(i, (i - shift) % size) for i in range(size)])


def mean_of_replicas(delta, after):
    everyone = ("yl", "x", "z")
    count = lax.axis_size(everyone)
    rows, cols = delta.shape
    parts = lax.all_to_all(tiles_of(delta, after), everyone, 0, 0, tiled=True)
    mean = jnp.sum(parts, axis=0, keepdims=True) / count
    whole = lax.all_to_all(jnp.broadcast_to(mean, (count, 8, 128)), everyone, 0, 0, tiled=True)
    return whole.reshape(rows // 8, cols // 128, 8, 128).transpose(0, 2, 1, 3).reshape(rows, cols)


def on_device(tokens, cotangent, w_gate, w_up, w_down, delta, anchor, momentum):
    x, dy = tokens[0], cotangent[0]
    place = jnp.stack([lax.axis_index(name) for name in ("core", "x", "yh")]).astype(jnp.int32)
    parts = lax.axis_size("x")

    outgoing = own_share(place, w_gate, w_up, w_down, parts)
    share = to_chips(outgoing)
    weights = [share] + [from_x(share, shift, parts) for shift in range(1, parts)]

    (two,) = pack(place, x, dy, outgoing, (2,), False)
    one, three, beside = pack(place, x, dy, share, (1, 3), True)
    arrived = [to_shift(one, 1), to_shift(two, 2), to_shift(three, 3)]
    beside = other_core(beside)
    swapped = other_core(repack(place, arrived))

    pseudo = mean_of_replicas(delta[0], beside)
    new_momentum = 0.9 * momentum + pseudo
    new_anchor = anchor - 0.7 * (pseudo + 0.9 * new_momentum)

    mine, theirs = hidden_sums(place, x, dy, beside, weights, (*arrived, pseudo))
    acts = to_chips(activation(mine, other_core(theirs)))
    grad_gate, grad_up, grad_down = grads(place, x, dy, beside, arrived, swapped, acts, other_core(acts))
    return grad_gate, grad_up, grad_down, new_anchor, new_momentum


def solution(mesh):
    fine = Mesh(mesh.devices.reshape(4, 2, 2, 4, 8), ("yh", "core", "yl", "x", "z"))
    fsdp, replica = ("yh", "core"), ("yl", "x", "z")
    placed = (
        P(replica, fsdp, None),
        P(replica, fsdp, None),
        P(fsdp, None),
        P(fsdp, None),
        P(None, fsdp),
        P(replica, fsdp, None),
        P(fsdp, None),
        P(fsdp, None),
    )
    return jax.shard_map(
        on_device,
        mesh=fine,
        in_specs=placed,
        out_specs=(
            P(replica, fsdp, None),
            P(replica, fsdp, None),
            P(replica, None, fsdp),
            P(fsdp, None),
            P(fsdp, None),
        ),
        check_vma=False,
    )
```

time: 256 us -> 168 us (0.66)
  Pallas kernels: 119 us -> 20.4 us
  blocking collectives: 0 us -> 28.2 us
  starting transfers between devices: 89.8 us -> 68.5 us
  waiting for transfers between devices: 21 us -> 41.5 us
  between operations: 14.5 us -> 0.94 us
  local copies, waits for them, and re-layouts: 8.15 us -> 4.93 us
    pallas_call x4 -> x7, Pallas kernels: 114 us -> 16.2 us  [the longest x1 4.16 us: hidden_sums(): pl.pallas_call(functools.partial(hidden_kernel, len(after)), out_shape=(o...]
    all_to_all x0 -> x1, blocking collectives: none -> 28.2 us  [to_chips(): return lax.all_to_all(value, 'yh', 0, 0, tiled=True)]
    all_to_all x1 -> x2, waiting for transfers between devices: 0.01 us -> 22.6 us  [the longest x1 15 us: to_chips(): return lax.all_to_all(value, 'yh', 0, 0, tiled=True)]
    ppermute x6 -> x3, starting transfers between devices: 28 us -> 11.1 us  [to_shift(): lax.ppermute(value, 'yh', [(i, (i + shift) % CHIPS) for i in range(CHIPS)])]
    all_gather x2 -> x0, waiting for transfers between devices: 15.4 us -> none  [the longest x1 15.4 us: on_device(): lax.all_gather(jnp.concatenate([s[:cut] for s in shares]), 'x', axis=0, t...]
    all_to_all x1, waiting for transfers between devices: 0.01 us -> 15 us  [mean_of_replicas(): lax.all_to_all(jnp.broadcast_to(mean, (count, 8, 128)), everyone, 0, 0, t...]
    ppermute x7 -> x4, starting transfers between devices: 20.8 us -> 12.7 us  [other_core(): return lax.ppermute(value, 'core', [(0, 1), (1, 0)])]
    all_to_all x1, starting transfers between devices: 10.4 us -> 17.4 us  [mean_of_replicas(): lax.all_to_all(jnp.broadcast_to(mean, (count, 8, 128)), everyone, 0, 0, t...]
  transfers between devices with their start and end apart: 20 -> 13, of which waited for: 3 -> 6; matrix products, arithmetic and copies ran while one was open for 1% -> 2% of each run, Pallas kernels for 45% -> 3%
where the time goes in v2:
time: 168 us; the launch traced here: 167 us
  starting transfers between devices  68.5 us (41%)
  waiting for transfers between devices  41.5 us (25%)
  blocking collectives  28.2 us (17%)
  Pallas kernels  20.4 us (12%)
  local copies, waits for them, and re-layouts  4.93 us (3%)
  other arithmetic  2.54 us (2%)
    all_to_all x1, blocking collectives, to_chips(): return lax.all_to_all(value, 'yh', 0, 0, tiled=True)  28.2 us
    all_to_all x1, starting transfers between devices, mean_of_replicas(): lax.all_to_all(jnp.broadcast_to(mean, (count, 8, 128)), everyone, 0, 0, t...  17.4 us
    all_to_all x1, waiting for transfers between devices, mean_of_replicas(): lax.all_to_all(jnp.broadcast_to(mean, (count, 8, 128)), everyone, 0, 0, t...  15 us
    all_to_all x1, waiting for transfers between devices, to_chips(): return lax.all_to_all(value, 'yh', 0, 0, tiled=True)  15 us
    all_to_all x1, starting transfers between devices, mean_of_replicas(): parts = lax.all_to_all(tiles_of(delta, after), everyone, 0, 0, tiled=True)  14 us
    ppermute x4, starting transfers between devices, other_core(): return lax.ppermute(value, 'core', [(0, 1), (1, 0)])  12.7 us
    ppermute x3, starting transfers between devices, to_shift(): lax.ppermute(value, 'yh', [(i, (i + shift) % CHIPS) for i in range(CHIPS)])  11.1 us
    ppermute x3, starting transfers between devices, from_x(): lax.ppermute(value, 'x', [(i, (i - shift) % size) for i in range(size)])  9.11 us
  transfers between devices with their start and end apart: 13, of which 6 were waited for; matrix products, arithmetic and copies ran while one was open for 2% of the time, Pallas kernels for 3%

profile of v2, /device:TPU:1, one launch (start us, length us, event | category | flops | bytes accessed | tf_op | source)
XLA Modules:
  0.0 167.1 jit_solution(18138782120764513263)
XLA Ops:
  0.6 0.6 pad_add_fusion.place
  1.2 3.1 %weight_share.1.after = bf16[4,384,256]{2,1,0:T(8,128)(2,1)} custom-call(s32[3]{0:T(128)} %pad_add_fusion.place, bf16[512,256]{1,0:T(8,128)(2,1)} %gate.1, bf16[512,256]{1,0:T(8,128)(2,1)} %up.1, bf16[256,512]{1,0:T(8,128)(2,1)} %down.1), custom_call_target="tpu_custom_call" | custom-call | bytes 2097152 | tf_op jit(solution)/shard_map/weight_share/pallas_call | solution.py:59
  4.3 0.0 copy-start
  4.3 28.2 %all_to_all.20.after.rest_4_ = bf16[4,384,256]{2,1,0:T(8,128)(2,1)S(1)} all-to-all(bf16[4,384,256]{2,1,0:T(8,128)(2,1)} %weight_share.1.after), channel_id=1, replica_groups=mesh['yh'=4,'core'=2,'yl'=2,'x'=4,'z'=8] {'yh'}, dimensions={0} | all-to-all | bytes 1572864 | tf_op jit(solution)/shard_map/all_to_all | solution.py:275
  32.5 0.6 copy-done.8
  33.2 1.7 %pack_tokens.2 = (bf16[2,128,1024]{2,1,0:T(8,128)(2,1)}, bf16[2,128,1024]{2,1,0:T(8,128)(2,1)S(1)}, bf16[4,2,128,512]{3,2,1,0:T(8,128)(2,1)S(1)}) custom-call(s32[3]{0:T(128)S(1)} %copy-done.8, bf16[128,4096]{1,0:T(8,128)(2,1)S(1)} %bitcast.12, bf16[128,4096]{1,0:T(8,128)(2,1)S(1)} %bitcast.16, bf16[4,384,256]{2,1,0:T(8,128)(2,1)S(1)} %all_to_all.20.after.rest_4_), custom_call_target="tpu_custom_call" | custom-call | bytes 3145728 | tf_op jit(solution)/shard_map/pack_tokens/pallas_call | solution.py:88
  34.9 4.4 %collective-permute-start = (bf16[4,2,128,512]{3,2,1,0:T(8,128)(2,1)S(1)}, bf16[4,2,128,512]{3,2,1,0:T(8,128)(2,1)S(1)}, u32[]{:S(2)}, u32[]{:S(2)}) collective-permute-start(bf16[4,2,128,512]{3,2,1,0:T(8,128)(2,1)S(1)} %get-tuple-element.13), channel_id=1, source_target_pairs={{0,64},{64,0},{1,65},{65,1},{2,66},{66,2},{3,67},{67,3},{4,68},{68... | collective-permute-start | bytes 3145736 | tf_op jit(solution)/shard_map/ppermute | solution.py:283
  39.3 1.4 pack_tokens.3
  40.7 3.1 %collective-permute-start.2 = (bf16[2,128,1024]{2,1,0:T(8,128)(2,1)}, bf16[2,128,1024]{2,1,0:T(8,128)(2,1)S(1)}, u32[]{:S(2)}, u32[]{:S(2)}) collective-permute-start(bf16[2,128,1024]{2,1,0:T(8,128)(2,1)} %pack_tokens.3), channel_id=1, source_target_pairs={{0,256},{128,384},{256,0},{384,128},{1,257},{129,385},{257,1},{385... | collective-permute-start | bytes 1572872 | tf_op jit(solution)/shard_map/ppermute | solution.py:279
  43.9 0.0 collective-permute-done.after.beside
  43.9 0.0 copy-start.11
  43.9 1.0 copy-done.11
  44.9 2.3 %delta_tiles.1 = f32[64,8,128]{2,1,0:T(8,128)} custom-call(f32[16,4096]{1,0:T(8,128)} %bitcast.21, bf16[4,2,128,512]{3,2,1,0:T(8,128)(2,1)} %copy-done.11), custom_call_target="tpu_custom_call" | custom-call | bytes 524288 | tf_op jit(solution)/shard_map/delta_tiles/pallas_call | solution.py:130
  47.2 14.0 %all-to-all-start.1 = ((f32[64,8,128]{2,1,0:T(8,128)}), f32[64,8,128]{2,1,0:T(8,128)S(1)}, u32[]{:S(2)}, u32[]{:S(2)}) async-start(f32[64,8,128]{2,1,0:T(8,128)} %delta_tiles.1), calls=%async_computation.1 | async-start | bytes 524288 | tf_op jit(solution)/shard_map/all_to_all | solution.py:294
  61.2 4.2 %collective-permute-start.5 = (bf16[4,384,256]{2,1,0:T(8,128)(2,1)S(1)}, bf16[4,384,256]{2,1,0:T(8,128)(2,1)}, u32[]{:S(2)}, u32[]{:S(2)}) collective-permute-start(bf16[4,384,256]{2,1,0:T(8,128)(2,1)S(1)} %all_to_all.20.after.rest_4_), channel_id=1, source_target_pairs={{0,24},{8,0},{16,8},{24,16},{1,25},{9,1},{17,9},{25,17},{2,26},{10... | collective-permute-start | bytes 2359304 | tf_op jit(solution)/shard_map/ppermute | solution.py:287
  65.4 2.4 %collective-permute-start.6 = (bf16[4,384,256]{2,1,0:T(8,128)(2,1)S(1)}, bf16[4,384,256]{2,1,0:T(8,128)(2,1)}, u32[]{:S(2)}, u32[]{:S(2)}) collective-permute-start(bf16[4,384,256]{2,1,0:T(8,128)(2,1)S(1)} %all_to_all.20.after.rest_4_), channel_id=1, source_target_pairs={{0,16},{8,24},{16,0},{24,8},{1,17},{9,25},{17,1},{25,9},{2,18},{10... | collective-permute-start | bytes 2359304 | tf_op jit(solution)/shard_map/ppermute | solution.py:287
  67.8 2.5 %collective-permute-start.7 = (bf16[4,384,256]{2,1,0:T(8,128)(2,1)S(1)}, bf16[4,384,256]{2,1,0:T(8,128)(2,1)}, u32[]{:S(2)}, u32[]{:S(2)}) collective-permute-start(bf16[4,384,256]{2,1,0:T(8,128)(2,1)S(1)} %all_to_all.20.after.rest_4_), channel_id=1, source_target_pairs={{0,8},{8,16},{16,24},{24,0},{1,9},{9,17},{17,25},{25,1},{2,10},{10... | collective-permute-start | bytes 2359304 | tf_op jit(solution)/shard_map/ppermute | solution.py:287
  70.3 3.1 %collective-permute-start.1 = (bf16[2,128,1024]{2,1,0:T(8,128)(2,1)}, bf16[2,128,1024]{2,1,0:T(8,128)(2,1)S(1)}, u32[]{:S(2)}, u32[]{:S(2)}) collective-permute-start(bf16[2,128,1024]{2,1,0:T(8,128)(2,1)} %get-tuple-element.14), channel_id=1, source_target_pairs={{0,128},{128,256},{256,384},{384,0},{1,129},{129,257},{257,385},{3... | collective-permute-start | bytes 1572872 | tf_op jit(solution)/shard_map/ppermute | solution.py:279
  73.4 7.6 %all-to-all-done.1 = f32[64,8,128]{2,1,0:T(8,128)S(1)} async-done(((f32[64,8,128]{2,1,0:T(8,128)}), f32[64,8,128]{2,1,0:T(8,128)S(1)}, u32[]{:S(2)}, u32[]{:S(2)}) %all-to-all-start.1) | async-done | bytes 262176 | tf_op jit(solution)/shard_map/all_to_all | solution.py:294
  81.0 0.1 reduce_sum.9
  81.1 0.0 collective-permute-done.2.two.rest_1_
  81.1 4.9 %collective-permute-start.3 = (bf16[2,128,1024]{2,1,0:T(8,128)(2,1)S(1)}, bf16[2,128,1024]{2,1,0:T(8,128)(2,1)S(1)}, u32[]{:S(2)}, u32[]{:S(2)}) collective-permute-start(bf16[2,128,1024]{2,1,0:T(8,128)(2,1)S(1)} %copy-done.10), channel_id=1, source_target_pairs={{0,384},{128,0},{256,128},{384,256},{1,385},{129,1},{257,129},{385... | collective-permute-start | bytes 1572872 | tf_op jit(solution)/shard_map/ppermute | solution.py:279
  86.0 0.7 broadcast_in_dim.2
  86.8 17.4 %all-to-all-start.2 = ((f32[64,8,128]{2,1,0:T(8,128)}), f32[64,8,128]{2,1,0:T(8,128)S(1)}, u32[]{:S(2)}, u32[]{:S(2)}) async-start(f32[64,8,128]{2,1,0:T(8,128)} %broadcast_in_dim.2), calls=%async_computation.2 | async-start | bytes 524288 | tf_op jit(solution)/shard_map/all_to_all | solution.py:296
  104.2 0.0 collective-permute-done.1.one.rest_0_
  104.2 0.0 collective-permute-done.3.three.rest_2_
  104.2 0.0 collective-permute-done.5.rest_5_
  104.2 0.0 collective-permute-done.6.rest_6_
  104.2 2.3 %collective-permute-done.7.rest_7_ = bf16[4,384,256]{2,1,0:T(8,128)(2,1)} collective-permute-done((bf16[4,384,256]{2,1,0:T(8,128)(2,1)S(1)}, bf16[4,384,256]{2,1,0:T(8,128)(2,1)}, u32[]{:S(2)}, u32[]{:S(2)}) %collective-permute-start.7) | collective-permute-done | bytes 786464 | tf_op jit(solution)/shard_map/ppermute | solution.py:287
  106.6 15.0 %all-to-all-done.2 = f32[64,8,128]{2,1,0:T(8,128)S(1)} async-done(((f32[64,8,128]{2,1,0:T(8,128)}), f32[64,8,128]{2,1,0:T(8,128)S(1)}, u32[]{:S(2)}, u32[]{:S(2)}) %all-to-all-start.2) | async-done | bytes 262176 | tf_op jit(solution)/shard_map/all_to_all | solution.py:296
  121.6 4.2 %hidden_sums.1 = (f32[3,128,256]{2,1,0:T(8,128)S(1)}, f32[3,128,256]{2,1,0:T(8,128)S(1)}) custom-call(s32[3]{0:T(128)S(1)} %copy-done.8, bf16[128,4096]{1,0:T(8,128)(2,1)} %bitcast.11, bf16[128,4096]{1,0:T(8,128)(2,1)} %bitcast.15, bf16[4,2,128,512]{3,2,1,0:T(8,128)(2,1)} %copy-done.11, bf16[2,128,1024]{2,1,0:T(8,128)(2,1)S(1)} %collective-permute-done.1.one.rest_0_, ...), custom_call_target="tpu_custom_call" | custom-call | flops 805306368 | bytes 6291456 | tf_op jit(solution)/shard_map/hidden_sums/pallas_call | solution.py:186
  125.8 0.7 copy-done.7
  126.5 2.8 %collective-permute-start.8 = (f32[3,128,256]{2,1,0:T(8,128)S(1)}, f32[3,128,256]{2,1,0:T(8,128)S(1)}, u32[]{:S(2)}, u32[]{:S(2)}) collective-permute-start(f32[3,128,256]{2,1,0:T(8,128)S(1)} %get-tuple-element.17), channel_id=1, source_target_pairs={{0,64},{64,0},{1,65},{65,1},{2,66},{66,2},{3,67},{67,3},{4,68},{68... | collective-permute-start | bytes 1179656 | tf_op jit(solution)/shard_map/ppermute | solution.py:283
  129.3 1.3 collective-permute-done.8.arrived
  130.6 0.8 copy-done.12
  131.4 2.1 %activation.1 = bf16[4,3,128,256]{3,2,1,0:T(8,128)(2,1)} custom-call(f32[3,128,256]{2,1,0:T(8,128)} %copy-done.7, f32[3,128,256]{2,1,0:T(8,128)} %copy-done.12), custom_call_target="tpu_custom_call" | custom-call | flops 655360 | bytes 1048576 | tf_op jit(solution)/shard_map/activation/pallas_call | solution.py:218
  133.5 4.2 %all-to-all-start.3 = ((bf16[4,3,128,256]{3,2,1,0:T(8,128)(2,1)}), bf16[4,3,128,256]{3,2,1,0:T(8,128)(2,1)}, u32[]{:S(2)}, u32[]{:S(2)}) async-start(bf16[4,3,128,256]{3,2,1,0:T(8,128)(2,1)} %activation.1), calls=%async_computation.3 | async-start | bytes 1572864 | tf_op jit(solution)/shard_map/all_to_all | solution.py:275
  137.7 0.0 copy-start.3
  137.7 1.5 repack_tokens.1
  139.2 0.0 copy-start.1
  139.3 2.4 %collective-permute-start.4 = (bf16[3,2,128,512]{3,2,1,0:T(8,128)(2,1)}, bf16[3,2,128,512]{3,2,1,0:T(8,128)(2,1)}, u32[]{:S(2)}, u32[]{:S(2)}) collective-permute-start(bf16[3,2,128,512]{3,2,1,0:T(8,128)(2,1)} %repack_tokens.1), channel_id=1, source_target_pairs={{0,64},{64,0},{1,65},{65,1},{2,66},{66,2},{3,67},{67,3},{4,68},{68... | collective-permute-start | bytes 2359304 | tf_op jit(solution)/shard_map/ppermute | solution.py:283
  141.7 15.0 %all-to-all-done.3.acts = bf16[4,3,128,256]{3,2,1,0:T(8,128)(2,1)} async-done(((bf16[4,3,128,256]{3,2,1,0:T(8,128)(2,1)}), bf16[4,3,128,256]{3,2,1,0:T(8,128)(2,1)}, u32[]{:S(2)}, u32[]{:S(2)}) %all-to-all-start.3) | async-done | bytes 786464 | tf_op jit(solution)/shard_map/all_to_all | solution.py:275
  156.7 3.1 %collective-permute-start.9 = (bf16[4,3,128,256]{3,2,1,0:T(8,128)(2,1)}, bf16[4,3,128,256]{3,2,1,0:T(8,128)(2,1)S(1)}, u32[]{:S(2)}, u32[]{:S(2)}) collective-permute-start(bf16[4,3,128,256]{3,2,1,0:T(8,128)(2,1)} %all-to-all-done.3.acts), channel_id=1, source_target_pairs={{0,64},{64,0},{1,65},{65,1},{2,66},{66,2},{3,67},{67,3},{4,68},{68... | collective-permute-start | bytes 2359304 | tf_op jit(solution)/shard_map/ppermute | solution.py:283
  159.7 1.9 %multiply_subtract_fusion = (f32[16,4096]{1,0:T(8,128)}, f32[16,4096]{1,0:T(8,128)}) fusion(f32[16,4096]{1,0:T(8,128)} %param.14, f32[16,4096]{1,0:T(8,128)S(1)} %bitcast.20, f32[16,4096]{1,0:T(8,128)} %param.15), kind=kLoop, calls=%fused_computation | loop fusion | flops 393216 | bytes 1310720 | tf_op jit(solution)/shard_map/sub | solution.py:317
  161.6 0.0 collective-permute-done.4.swapped
  161.6 0.2 collective-permute-done.9.acts_beside
  161.9 1.0 copy-done.6
  162.9 4.2 %weight_grads.1 = (bf16[1,512,256]{2,1,0:T(8,128)(2,1)}, bf16[1,512,256]{2,1,0:T(8,128)(2,1)}, bf16[1,256,512]{2,1,0:T(8,128)(2,1)}) custom-call(s32[3]{0:T(128)S(1)} %copy-done.8, bf16[128,4096]{1,0:T(8,128)(2,1)S(1)} %bitcast.14, bf16[128,4096]{1,0:T(8,128)(2,1)S(1)} %bitcast.18, bf16[4,2,128,512]{3,2,1,0:T(8,128)(2,1)} %copy-done.11, ...), custom_call_target="tpu_custom_call" | custom-call | flops 805306368 | bytes 5242880 | tf_op jit(solution)/shard_map/weight_grads/pallas_call | solution.py:253
  (18 shorter events, 0.0 us)
Async XLA Ops:
  1.2 31.3 %copy-start.2 = (bf16[1,128,4096]{2,1,0:T(8,128)(2,1)S(1)}, bf16[1,128,4096]{2,1,0:T(8,128)(2,1)}, u32[]{:S(2)}) copy-start(bf16[1,128,4096]{2,1,0:T(8,128)(2,1)} %param.9) | copy-start | bytes 3145732
  4.3 28.3 %copy-start = (bf16[1,128,4096]{2,1,0:T(8,128)(2,1)S(1)}, bf16[1,128,4096]{2,1,0:T(8,128)(2,1)}, u32[]{:S(2)}) copy-start(bf16[1,128,4096]{2,1,0:T(8,128)(2,1)} %param.8) | copy-start | bytes 3145732
  32.5 0.7 copy-start.8
  33.2 6.1 %copy-start.4 = (bf16[4,384,256]{2,1,0:T(8,128)(2,1)S(1)}, bf16[4,384,256]{2,1,0:T(8,128)(2,1)}, u32[]{:S(2)}) copy-start(bf16[4,384,256]{2,1,0:T(8,128)(2,1)} %weight_share.1.after) | copy-start | bytes 2359300
  34.9 5.8 %copy-start.9 = (bf16[2,128,1024]{2,1,0:T(8,128)(2,1)}, bf16[2,128,1024]{2,1,0:T(8,128)(2,1)S(1)}, u32[]{:S(2)}) copy-start(bf16[2,128,1024]{2,1,0:T(8,128)(2,1)S(1)} %get-tuple-element.15) | copy-start | bytes 1572868
  34.9 9.0 %collective-permute-start = (bf16[4,2,128,512]{3,2,1,0:T(8,128)(2,1)S(1)}, bf16[4,2,128,512]{3,2,1,0:T(8,128)(2,1)S(1)}, u32[]{:S(2)}, u32[]{:S(2)}) collective-permute-start(bf16[4,2,128,512]{3,2,1,0:T(8,128)(2,1)S(1)} %get-tuple-element.13), channel_id=1, source_target_pairs={{0,64},{64,0},{1,65},{65,1},{2,66},{66,2},{3,67},{67,3},{4,68},{68... | collective-permute-start | bytes 3145736 | tf_op jit(solution)/shard_map/ppermute | solution.py:283
  40.7 40.3 %collective-permute-start.2 = (bf16[2,128,1024]{2,1,0:T(8,128)(2,1)}, bf16[2,128,1024]{2,1,0:T(8,128)(2,1)S(1)}, u32[]{:S(2)}, u32[]{:S(2)}) collective-permute-start(bf16[2,128,1024]{2,1,0:T(8,128)(2,1)} %pack_tokens.3), channel_id=1, source_target_pairs={{0,256},{128,384},{256,0},{384,128},{1,257},{129,385},{257,1},{385... | collective-permute-start | bytes 1572872 | tf_op jit(solution)/shard_map/ppermute | solution.py:279
  43.9 1.0 copy-start.11
  47.2 33.9 %copy-start.10 = (bf16[2,128,1024]{2,1,0:T(8,128)(2,1)S(1)}, bf16[2,128,1024]{2,1,0:T(8,128)(2,1)}, u32[]{:S(2)}) copy-start(bf16[2,128,1024]{2,1,0:T(8,128)(2,1)} %copy-done.9) | copy-start | bytes 1572868
  47.2 33.8 %all-to-all-start.1 = ((f32[64,8,128]{2,1,0:T(8,128)}), f32[64,8,128]{2,1,0:T(8,128)S(1)}, u32[]{:S(2)}, u32[]{:S(2)}) async-start(f32[64,8,128]{2,1,0:T(8,128)} %delta_tiles.1), calls=%async_computation.1 | async-start | bytes 524288 | tf_op jit(solution)/shard_map/all_to_all | solution.py:294
  61.2 43.0 %collective-permute-start.5 = (bf16[4,384,256]{2,1,0:T(8,128)(2,1)S(1)}, bf16[4,384,256]{2,1,0:T(8,128)(2,1)}, u32[]{:S(2)}, u32[]{:S(2)}) collective-permute-start(bf16[4,384,256]{2,1,0:T(8,128)(2,1)S(1)} %all_to_all.20.after.rest_4_), channel_id=1, source_target_pairs={{0,24},{8,0},{16,8},{24,16},{1,25},{9,1},{17,9},{25,17},{2,26},{10... | collective-permute-start | bytes 2359304 | tf_op jit(solution)/shard_map/ppermute | solution.py:287
  65.4 38.9 %collective-permute-start.6 = (bf16[4,384,256]{2,1,0:T(8,128)(2,1)S(1)}, bf16[4,384,256]{2,1,0:T(8,128)(2,1)}, u32[]{:S(2)}, u32[]{:S(2)}) collective-permute-start(bf16[4,384,256]{2,1,0:T(8,128)(2,1)S(1)} %all_to_all.20.after.rest_4_), channel_id=1, source_target_pairs={{0,16},{8,24},{16,0},{24,8},{1,17},{9,25},{17,1},{25,9},{2,18},{10... | collective-permute-start | bytes 2359304 | tf_op jit(solution)/shard_map/ppermute | solution.py:287
  67.8 38.7 %collective-permute-start.7 = (bf16[4,384,256]{2,1,0:T(8,128)(2,1)S(1)}, bf16[4,384,256]{2,1,0:T(8,128)(2,1)}, u32[]{:S(2)}, u32[]{:S(2)}) collective-permute-start(bf16[4,384,256]{2,1,0:T(8,128)(2,1)S(1)} %all_to_all.20.after.rest_4_), channel_id=1, source_target_pairs={{0,8},{8,16},{16,24},{24,0},{1,9},{9,17},{17,25},{25,1},{2,10},{10... | collective-permute-start | bytes 2359304 | tf_op jit(solution)/shard_map/ppermute | solution.py:287
  70.3 33.9 %collective-permute-start.1 = (bf16[2,128,1024]{2,1,0:T(8,128)(2,1)}, bf16[2,128,1024]{2,1,0:T(8,128)(2,1)S(1)}, u32[]{:S(2)}, u32[]{:S(2)}) collective-permute-start(bf16[2,128,1024]{2,1,0:T(8,128)(2,1)} %get-tuple-element.14), channel_id=1, source_target_pairs={{0,128},{128,256},{256,384},{384,0},{1,129},{129,257},{257,385},{3... | collective-permute-start | bytes 1572872 | tf_op jit(solution)/shard_map/ppermute | solution.py:279
  81.1 23.1 %collective-permute-start.3 = (bf16[2,128,1024]{2,1,0:T(8,128)(2,1)S(1)}, bf16[2,128,1024]{2,1,0:T(8,128)(2,1)S(1)}, u32[]{:S(2)}, u32[]{:S(2)}) collective-permute-start(bf16[2,128,1024]{2,1,0:T(8,128)(2,1)S(1)} %copy-done.10), channel_id=1, source_target_pairs={{0,384},{128,0},{256,128},{384,256},{1,385},{129,1},{257,129},{385... | collective-permute-start | bytes 1572872 | tf_op jit(solution)/shard_map/ppermute | solution.py:279
  86.8 34.8 %all-to-all-start.2 = ((f32[64,8,128]{2,1,0:T(8,128)}), f32[64,8,128]{2,1,0:T(8,128)S(1)}, u32[]{:S(2)}, u32[]{:S(2)}) async-start(f32[64,8,128]{2,1,0:T(8,128)} %broadcast_in_dim.2), calls=%async_computation.2 | async-start | bytes 524288 | tf_op jit(solution)/shard_map/all_to_all | solution.py:296
  104.2 33.5 %copy-start.5 = (bf16[2,128,1024]{2,1,0:T(8,128)(2,1)}, bf16[2,128,1024]{2,1,0:T(8,128)(2,1)S(1)}, u32[]{:S(2)}) copy-start(bf16[2,128,1024]{2,1,0:T(8,128)(2,1)S(1)} %collective-permute-done.3.three.rest_2_) | copy-start | bytes 1572868
  125.8 0.8 copy-start.7
  126.5 4.1 %collective-permute-start.8 = (f32[3,128,256]{2,1,0:T(8,128)S(1)}, f32[3,128,256]{2,1,0:T(8,128)S(1)}, u32[]{:S(2)}, u32[]{:S(2)}) collective-permute-start(f32[3,128,256]{2,1,0:T(8,128)S(1)} %get-tuple-element.17), channel_id=1, source_target_pairs={{0,64},{64,0},{1,65},{65,1},{2,66},{66,2},{3,67},{67,3},{4,68},{68... | collective-permute-start | bytes 1179656 | tf_op jit(solution)/shard_map/ppermute | solution.py:283
  130.6 0.8 copy-start.12
  133.5 23.2 %all-to-all-start.3 = ((bf16[4,3,128,256]{3,2,1,0:T(8,128)(2,1)}), bf16[4,3,128,256]{3,2,1,0:T(8,128)(2,1)}, u32[]{:S(2)}, u32[]{:S(2)}) async-start(bf16[4,3,128,256]{3,2,1,0:T(8,128)(2,1)} %activation.1), calls=%async_computation.3 | async-start | bytes 1572864 | tf_op jit(solution)/shard_map/all_to_all | solution.py:275
  137.7 24.1 %copy-start.3 = (bf16[1,128,4096]{2,1,0:T(8,128)(2,1)S(1)}, bf16[1,128,4096]{2,1,0:T(8,128)(2,1)}, u32[]{:S(2)}) copy-start(bf16[1,128,4096]{2,1,0:T(8,128)(2,1)} %param.9) | copy-start | bytes 3145732
  139.2 22.6 %copy-start.1 = (bf16[1,128,4096]{2,1,0:T(8,128)(2,1)S(1)}, bf16[1,128,4096]{2,1,0:T(8,128)(2,1)}, u32[]{:S(2)}) copy-start(bf16[1,128,4096]{2,1,0:T(8,128)(2,1)} %param.8) | copy-start | bytes 3145732
  139.3 22.4 %collective-permute-start.4 = (bf16[3,2,128,512]{3,2,1,0:T(8,128)(2,1)}, bf16[3,2,128,512]{3,2,1,0:T(8,128)(2,1)}, u32[]{:S(2)}, u32[]{:S(2)}) collective-permute-start(bf16[3,2,128,512]{3,2,1,0:T(8,128)(2,1)} %repack_tokens.1), channel_id=1, source_target_pairs={{0,64},{64,0},{1,65},{65,1},{2,66},{66,2},{3,67},{67,3},{4,68},{68... | collective-permute-start | bytes 2359304 | tf_op jit(solution)/shard_map/ppermute | solution.py:283
  156.7 5.2 %collective-permute-start.9 = (bf16[4,3,128,256]{3,2,1,0:T(8,128)(2,1)}, bf16[4,3,128,256]{3,2,1,0:T(8,128)(2,1)S(1)}, u32[]{:S(2)}, u32[]{:S(2)}) collective-permute-start(bf16[4,3,128,256]{3,2,1,0:T(8,128)(2,1)} %all-to-all-done.3.acts), channel_id=1, source_target_pairs={{0,64},{64,0},{1,65},{65,1},{2,66},{66,2},{3,67},{67,3},{4,68},{68... | collective-permute-start | bytes 2359304 | tf_op jit(solution)/shard_map/ppermute | solution.py:283
  161.9 1.0 copy-start.6

commit v3 on v2

--- a/solution.py
+++ b/solution.py
@@ -40,29 +40,26 @@
 
 def share_kernel(parts, place, gate, up, down, out, sems):
     gate_rows, down_rows = HALF // parts, HID // parts
+    cut = 2 * gate_rows
     at_gate = pl.ds(pl.multiple_of(place[1] * gate_rows, gate_rows), gate_rows)
     at_down = pl.ds(pl.multiple_of(place[1] * down_rows, down_rows), down_rows)
-    copies = []
-    for chip in range(CHIPS):
-        to = out.at[chip]
-        copies += [
-            (gate.at[at_gate], to.at[pl.ds(0, gate_rows)]),
-            (up.at[at_gate], to.at[pl.ds(gate_rows, gate_rows)]),
-            (down.at[at_down, :HID], to.at[pl.ds(2 * gate_rows, down_rows)]),
-            (down.at[at_down, HID:], to.at[pl.ds(2 * gate_rows + down_rows, down_rows)]),
-        ]
+    copies = [
+        (gate.at[at_gate], out.at[pl.ds(0, gate_rows)]),
+        (up.at[at_gate], out.at[pl.ds(gate_rows, gate_rows)]),
+        (down.at[at_down, :HID], out.at[pl.ds(cut, down_rows)]),
+        (down.at[at_down, HID:], out.at[pl.ds(cut + down_rows, down_rows)]),
+    ]
     run_copies(copies, sems)
 
 
 def own_share(place, gate, up, down, parts):
-    rows = 2 * (HALF + HID) // parts
     return pl.pallas_call(
         functools.partial(share_kernel, parts),
-        out_shape=jax.ShapeDtypeStruct((CHIPS, rows, HID), BF16),
+        out_shape=jax.ShapeDtypeStruct((2 * (HALF + HID) // parts, HID), BF16),
         in_specs=[SMEM, ANY, ANY, ANY],
         out_specs=VMEM,
-        scratch_shapes=[pltpu.SemaphoreType.DMA((16,))],
-        cost_estimate=pl.CostEstimate(flops=0, bytes_accessed=2 << 20, transcendentals=0),
+        scratch_shapes=[pltpu.SemaphoreType.DMA((4,))],
+        cost_estimate=pl.CostEstimate(flops=0, bytes_accessed=1 << 18, transcendentals=0),
         name="weight_share",
     )(place, gate, up, down)
 
@@ -138,30 +135,29 @@
     )(delta, after)
 
 
-def hidden_kernel(waited, place, x, dy, beside, *rest):
-    rest = rest[waited:]
-    weights, (mine, theirs, xs, dys, gates, ups, downs, sems) = rest[:-8], rest[-8:]
-    parts = len(weights)
+def hidden_kernel(waited, place, x, dy, beside, weights, *rest):
+    mine, theirs, xs, dys, gates, ups, downs, sems = rest[waited:]
+    parts = weights.shape[0]
     gate_rows, down_rows = HALF // parts, HID // parts
-    core, at = place[0], place[1]
+    cut = 2 * gate_rows
     copies = []
-    for shift, ref in enumerate(weights):
-        part = lax.rem(at + shift, parts)
-        to_gate = pl.ds(pl.multiple_of(part * gate_rows, gate_rows), gate_rows)
-        to_down = pl.ds(pl.multiple_of(part * down_rows, down_rows), down_rows)
+    for shift in range(CHIPS):
+        chip = lax.rem(place[2] + shift, CHIPS)
+        own = columns(chip * WIDE + place[0] * HALF)
+        copies += [
+            (x.at[:, own], xs.at[shift, :ROWS]),
+            (dy.at[:, own], dys.at[shift, :ROWS]),
+            (beside.at[chip, 0], xs.at[shift, ROWS:]),
+            (beside.at[chip, 1], dys.at[shift, ROWS:]),
+        ]
+    for part in range(parts):
+        ref = weights.at[part]
+        to_gate, to_down = pl.ds(part * gate_rows, gate_rows), pl.ds(part * down_rows, down_rows)
         copies += [
             (ref.at[:, pl.ds(0, gate_rows)], gates.at[:, to_gate]),
             (ref.at[:, pl.ds(gate_rows, gate_rows)], ups.at[:, to_gate]),
-            (ref.at[:, pl.ds(2 * gate_rows, down_rows)], downs.at[:, 0, to_down]),
-            (ref.at[:, pl.ds(2 * gate_rows + down_rows, down_rows)], downs.at[:, 1, to_down]),
-        ]
-    for chip in range(CHIPS):
-        own = columns(chip * WIDE + core * HALF)
-        copies += [
-            (x.at[:, own], xs.at[chip, :ROWS]),
-            (dy.at[:, own], dys.at[chip, :ROWS]),
-            (beside.at[chip, 0], xs.at[chip, ROWS:]),
-            (beside.at[chip, 1], dys.at[chip, ROWS:]),
+            (ref.at[:, pl.ds(cut, down_rows)], downs.at[:, 0, to_down]),
+            (ref.at[:, pl.ds(cut + down_rows, down_rows)], downs.at[:, 1, to_down]),
         ]
     run_copies(copies, sems)
     gate = up = dh = 0.0
@@ -186,7 +182,7 @@
     return pl.pallas_call(
         functools.partial(hidden_kernel, len(after)),
         out_shape=(out, out),
-        in_specs=[SMEM] + [ANY] * (3 + len(after) + len(weights)),
+        in_specs=[SMEM] + [ANY] * (4 + len(after)),
         out_specs=(VMEM, VMEM),
         scratch_shapes=[
             pltpu.VMEM((CHIPS, 2 * ROWS, HALF), BF16),
@@ -194,15 +190,17 @@
             pltpu.VMEM((CHIPS, HALF, HID), BF16),
             pltpu.VMEM((CHIPS, HALF, HID), BF16),
             pltpu.VMEM((CHIPS, 2, HID, HID), BF16),
-            pltpu.SemaphoreType.DMA((4 * len(weights) + 16,)),
+            pltpu.SemaphoreType.DMA((4 * weights.shape[0] + 16,)),
         ],
         compiler_params=pltpu.CompilerParams(vmem_limit_bytes=VMEM_LIMIT),
         cost_estimate=pl.CostEstimate(flops=6 * 256 * 2048 * 256, bytes_accessed=6 << 20, transcendentals=0),
         name="hidden_sums",
-    )(place, x, dy, beside, *after, *weights)
-
-
-def activation_kernel(mine, arrived, out):
+    )(place, x, dy, beside, weights, *after)
+
+
+def activation_kernel(mine_ref, arrived_ref, after, out, mine, arrived, sems):
+    del after
+    run_copies([(mine_ref, mine), (arrived_ref, arrived)], sems)
     gate = mine[0] + arrived[0]
     up = mine[1] + arrived[1]
     dh = mine[2] + arrived[2]
@@ -214,15 +212,20 @@
             out[chip, i] = value.astype(BF16)
 
 
-def activation(mine, arrived):
+def activation(mine, arrived, after):
     return pl.pallas_call(
         activation_kernel,
         out_shape=jax.ShapeDtypeStruct((CHIPS, 3, ROWS, HID), BF16),
-        in_specs=[VMEM, VMEM],
+        in_specs=[ANY] * 3,
         out_specs=VMEM,
+        scratch_shapes=[
+            pltpu.VMEM((3, ROWS, HID), F32),
+            pltpu.VMEM((3, ROWS, HID), F32),
+            pltpu.SemaphoreType.DMA((2,)),
+        ],
         cost_estimate=pl.CostEstimate(flops=20 * ROWS * HID, bytes_accessed=1 << 20, transcendentals=ROWS * HID),
         name="activation",
-    )(mine, arrived)
+    )(mine, arrived, after)
 
 
 def grads_kernel(place, x, dy, beside, one, two, three, swapped, acts, acts_beside, gg, gu, gd, xs, dys, hs, sems):
@@ -279,12 +282,12 @@
     return lax.ppermute(value, "yh", [(i, (i + shift) % CHIPS) for i in range(CHIPS)])
 
 
+def from_shift(value, shift):
+    return lax.ppermute(value, "yh", [(i, (i - shift) % CHIPS) for i in range(CHIPS)])
+
+
 def other_core(value):
     return lax.ppermute(value, "core", [(0, 1), (1, 0)])
-
-
-def from_x(value, shift, size):
-    return lax.ppermute(value, "x", [(i, (i - shift) % size) for i in range(size)])
 
 
 def mean_of_replicas(delta, after):
@@ -299,25 +302,26 @@
 
 def on_device(tokens, cotangent, w_gate, w_up, w_down, delta, anchor, momentum):
     x, dy = tokens[0], cotangent[0]
-    place = jnp.stack([lax.axis_index(name) for name in ("core", "x", "yh")]).astype(jnp.int32)
-    parts = lax.axis_size("x")
-
-    outgoing = own_share(place, w_gate, w_up, w_down, parts)
-    share = to_chips(outgoing)
-    weights = [share] + [from_x(share, shift, parts) for shift in range(1, parts)]
-
-    (two,) = pack(place, x, dy, outgoing, (2,), False)
-    one, three, beside = pack(place, x, dy, share, (1, 3), True)
+    place = jnp.stack([lax.axis_index(name) for name in ("core", "z", "yh")]).astype(jnp.int32)
+    parts = lax.axis_size("z")
+
+    share = own_share(place, w_gate, w_up, w_down, parts)
+    shares = {shift: from_shift(share, shift) for shift in (2, 1, 3)}
+    first = shares[2]
+    shares = jnp.stack([share] + [shares[shift] for shift in (1, 2, 3)])
+    weights = lax.all_gather(shares, "z", axis=0, tiled=False)
+
+    one, two, three, beside = pack(place, x, dy, shares, (1, 2, 3), True)
     arrived = [to_shift(one, 1), to_shift(two, 2), to_shift(three, 3)]
     beside = other_core(beside)
     swapped = other_core(repack(place, arrived))
 
-    pseudo = mean_of_replicas(delta[0], beside)
+    pseudo = mean_of_replicas(delta[0], first)
     new_momentum = 0.9 * momentum + pseudo
     new_anchor = anchor - 0.7 * (pseudo + 0.9 * new_momentum)
 
-    mine, theirs = hidden_sums(place, x, dy, beside, weights, (*arrived, pseudo))
-    acts = to_chips(activation(mine, other_core(theirs)))
+    mine, theirs = hidden_sums(place, x, dy, beside, weights, arrived)
+    acts = to_chips(activation(mine, other_core(theirs), new_anchor))
     grad_gate, grad_up, grad_down = grads(place, x, dy, beside, arrived, swapped, acts, other_core(acts))
     return grad_gate, grad_up, grad_down, new_anchor, new_momentum
 

time: 168 us -> 164 us (0.976)
  blocking collectives: 28.2 us -> 0 us
  between operations: 0.94 us -> 14.3 us
  waiting for transfers between devices: 41.5 us -> 51.4 us
  local copies, waits for them, and re-layouts: 4.93 us -> 2.52 us
  starting transfers between devices: 68.5 us -> 70.9 us
  other arithmetic: 2.54 us -> 4.32 us
    ppermute x3, waiting for transfers between devices: 0.01 us -> 32.6 us  [to_shift(): lax.ppermute(value, 'yh', [(i, (i + shift) % CHIPS) for i in range(CHIPS)])]
    all_to_all x1 -> x0, blocking collectives: 28.2 us -> none  [to_chips(): return lax.all_to_all(value, 'yh', 0, 0, tiled=True)]
    all_to_all x1, waiting for transfers between devices: 15 us -> 0.01 us  [mean_of_replicas(): lax.all_to_all(jnp.broadcast_to(mean, (count, 8, 128)), everyone, 0, 0, t...]
    all_to_all x1, waiting for transfers between devices: 7.59 us -> 0.01 us  [mean_of_replicas(): parts = lax.all_to_all(tiles_of(delta, after), everyone, 0, 0, tiled=True)]
    all_to_all x1, starting transfers between devices: 17.4 us -> 11.3 us  [mean_of_replicas(): lax.all_to_all(jnp.broadcast_to(mean, (count, 8, 128)), everyone, 0, 0, t...]
    ppermute x3, starting transfers between devices: 9.11 us -> 14.5 us  [from_shift(): lax.ppermute(value, 'yh', [(i, (i - shift) % CHIPS) for i in range(CHIPS)])]
    all_to_all x1, waiting for transfers between devices: 15 us -> 12.5 us  [to_chips(): return lax.all_to_all(value, 'yh', 0, 0, tiled=True)]
    all_to_all x1, starting transfers between devices: 14 us -> 16.4 us  [mean_of_replicas(): parts = lax.all_to_all(tiles_of(delta, after), everyone, 0, 0, tiled=True)]
  transfers between devices with their start and end apart: 13 -> 14, of which waited for: 6 -> 5; matrix products, arithmetic and copies ran while one was open for 2% -> 2% of each run, Pallas kernels for 3% -> 7%
where the time goes in v3:
time: 164 us
  starting transfers between devices  70.9 us (43%)
  waiting for transfers between devices  51.4 us (31%)
  Pallas kernels  20 us (12%)
  between operations  14.3 us (9%)
  other arithmetic  4.32 us (3%)
  local copies, waits for them, and re-layouts  2.52 us (2%)
    ppermute x3, waiting for transfers between devices, to_shift(): lax.ppermute(value, 'yh', [(i, (i + shift) % CHIPS) for i in range(CHIPS)])  32.6 us
    all_to_all x1, starting transfers between devices, mean_of_replicas(): parts = lax.all_to_all(tiles_of(delta, after), everyone, 0, 0, tiled=True)  16.4 us
    ppermute x3, starting transfers between devices, from_shift(): lax.ppermute(value, 'yh', [(i, (i - shift) % CHIPS) for i in range(CHIPS)])  14.5 us
    all_to_all x1, waiting for transfers between devices, to_chips(): return lax.all_to_all(value, 'yh', 0, 0, tiled=True)  12.5 us
    ppermute x4, starting transfers between devices, other_core(): return lax.ppermute(value, 'core', [(0, 1), (1, 0)])  12.5 us
    ppermute x3, starting transfers between devices, to_shift(): lax.ppermute(value, 'yh', [(i, (i + shift) % CHIPS) for i in range(CHIPS)])  12 us
    all_to_all x1, starting transfers between devices, mean_of_replicas(): lax.all_to_all(jnp.broadcast_to(mean, (count, 8, 128)), everyone, 0, 0, t...  11.3 us
    pallas_call x1, Pallas kernels, hidden_sums(): pl.pallas_call(functools.partial(hidden_kernel, len(after)), out_shape=(o...  4.24 us
  transfers between devices with their start and end apart: 14, of which 5 were waited for; matrix products, arithmetic and copies ran while one was open for 2% of the time, Pallas kernels for 7%

profile of v3, /device:TPU:1, one launch (start us, length us, event | category | flops | bytes accessed | tf_op | source)
XLA Modules:
  0.0 163.5 jit_solution(12973802544877987756)
XLA Ops:
  7.2 0.0 copy-start
  7.2 0.0 copy-start.1
  7.2 0.0 all-gather.3.cloned.1.call-start
  7.2 0.6 pad_add_fusion.place
  7.8 2.2 %weight_share.1 = bf16[192,256]{1,0:T(8,128)(2,1)} custom-call(s32[3]{0:T(128)} %pad_add_fusion.place, bf16[512,256]{1,0:T(8,128)(2,1)} %gate.1, bf16[512,256]{1,0:T(8,128)(2,1)} %up.1, bf16[256,512]{1,0:T(8,128)(2,1)} %down.1), custom_call_target="tpu_custom_call" | custom-call | bytes 262144 | tf_op jit(solution)/shard_map/weight_share/pallas_call | solution.py:56
  10.1 8.3 %collective-permute-start.1 = (bf16[192,256]{1,0:T(8,128)(2,1)}, bf16[192,256]{1,0:T(8,128)(2,1)S(1)}, u32[]{:S(2)}, u32[]{:S(2)}) collective-permute-start(bf16[192,256]{1,0:T(8,128)(2,1)} %weight_share.1), channel_id=1, source_target_pairs={{0,256},{128,384},{256,0},{384,128},{1,257},{129,385},{257,1},{385... | collective-permute-start | bytes 294920 | tf_op jit(solution)/shard_map/ppermute | solution.py:286
  18.4 2.0 %collective-permute-start = (bf16[192,256]{1,0:T(8,128)(2,1)}, bf16[192,256]{1,0:T(8,128)(2,1)S(1)}, u32[]{:S(2)}, u32[]{:S(2)}) collective-permute-start(bf16[192,256]{1,0:T(8,128)(2,1)} %weight_share.1), channel_id=1, source_target_pairs={{0,384},{128,0},{256,128},{384,256},{1,385},{129,1},{257,129},{385... | collective-permute-start | bytes 294920 | tf_op jit(solution)/shard_map/ppermute | solution.py:286
  20.3 4.2 %collective-permute-start.2 = (bf16[192,256]{1,0:T(8,128)(2,1)}, bf16[192,256]{1,0:T(8,128)(2,1)S(1)}, u32[]{:S(2)}, u32[]{:S(2)}) collective-permute-start(bf16[192,256]{1,0:T(8,128)(2,1)} %weight_share.1), channel_id=1, source_target_pairs={{0,128},{128,256},{256,384},{384,0},{1,129},{129,257},{257,385},{3... | collective-permute-start | bytes 294920 | tf_op jit(solution)/shard_map/ppermute | solution.py:286
  24.6 0.0 collective-permute-done.1.after
  24.6 0.0 copy-start.5
  24.6 4.2 %collective-permute-done = bf16[192,256]{1,0:T(8,128)(2,1)S(1)} collective-permute-done((bf16[192,256]{1,0:T(8,128)(2,1)}, bf16[192,256]{1,0:T(8,128)(2,1)S(1)}, u32[]{:S(2)}, u32[]{:S(2)}) %collective-permute-start) | collective-permute-done | bytes 98336 | tf_op jit(solution)/shard_map/ppermute | solution.py:286
  28.8 0.0 collective-permute-done.2
  28.8 1.7 %pad_maximum_fusion.after = bf16[4,192,256]{2,1,0:T(8,128)(2,1)} fusion(bf16[1,192,256]{2,1,0:T(8,128)(2,1)S(1)} %bitcast.27, bf16[1,192,256]{2,1,0:T(8,128)(2,1)S(1)} %bitcast.23, bf16[1,192,256]{2,1,0:T(8,128)(2,1)S(1)} %bitcast.26, bf16[1,192,256]{2,1,0:T(8,128)(2,1)} %bitcast.24), kind=kLoop, calls=%fused_computation | loop fusion | flops 589824 | bytes 786432 | tf_op jit(solution)/shard_map/stack | solution.py:311
  30.5 0.0 all-gather.3.cloned.1.call-update
  30.5 0.0 copy-done.5
  30.5 2.3 %delta_tiles.1 = f32[64,8,128]{2,1,0:T(8,128)} custom-call(f32[16,4096]{1,0:T(8,128)} %bitcast.25, bf16[192,256]{1,0:T(8,128)(2,1)} %copy-done.5), custom_call_target="tpu_custom_call" | custom-call | bytes 524288 | tf_op jit(solution)/shard_map/delta_tiles/pallas_call | solution.py:127
  32.8 16.4 %all-to-all-start = ((f32[64,8,128]{2,1,0:T(8,128)}), f32[64,8,128]{2,1,0:T(8,128)S(1)}, u32[]{:S(2)}, u32[]{:S(2)}) async-start(f32[64,8,128]{2,1,0:T(8,128)} %delta_tiles.1), calls=%async_computation | async-start | bytes 524288 | tf_op jit(solution)/shard_map/all_to_all | solution.py:297
  49.2 0.0 copy-done
  49.3 1.0 copy-done.2
  50.3 2.5 %pack_tokens.1 = (bf16[2,128,1024]{2,1,0:T(8,128)(2,1)}, bf16[2,128,1024]{2,1,0:T(8,128)(2,1)}, bf16[2,128,1024]{2,1,0:T(8,128)(2,1)}, bf16[4,2,128,512]{3,2,1,0:T(8,128)(2,1)}) custom-call(s32[3]{0:T(128)S(1)} %copy-done.4, bf16[128,4096]{1,0:T(8,128)(2,1)S(1)} %bitcast.16, bf16[128,4096]{1,0:T(8,128)(2,1)S(1)} %bitcast.19, bf16[4,192,256]{2,1,0:T(8,128)(2,1)S(1)} %copy-done.2), custom_call_target="tpu_custom_call" | custom-call | bytes 4194304 | tf_op jit(solution)/shard_map/pack_tokens/pallas_call | solution.py:85
  52.8 3.3 %collective-permute-start.3 = (bf16[4,2,128,512]{3,2,1,0:T(8,128)(2,1)}, bf16[4,2,128,512]{3,2,1,0:T(8,128)(2,1)}, u32[]{:S(2)}, u32[]{:S(2)}) collective-permute-start(bf16[4,2,128,512]{3,2,1,0:T(8,128)(2,1)} %get-tuple-element.14), channel_id=1, source_target_pairs={{0,64},{64,0},{1,65},{65,1},{2,66},{66,2},{3,67},{67,3},{4,68},{68... | collective-permute-start | bytes 3145736 | tf_op jit(solution)/shard_map/ppermute | solution.py:290
  56.1 1.9 %collective-permute-start.4 = (bf16[2,128,1024]{2,1,0:T(8,128)(2,1)}, bf16[2,128,1024]{2,1,0:T(8,128)(2,1)S(1)}, u32[]{:S(2)}, u32[]{:S(2)}) collective-permute-start(bf16[2,128,1024]{2,1,0:T(8,128)(2,1)} %get-tuple-element.15), channel_id=1, source_target_pairs={{0,128},{128,256},{256,384},{384,0},{1,129},{129,257},{257,385},{3... | collective-permute-start | bytes 1572872 | tf_op jit(solution)/shard_map/ppermute | solution.py:282
  58.0 4.6 %collective-permute-start.5 = (bf16[2,128,1024]{2,1,0:T(8,128)(2,1)}, bf16[2,128,1024]{2,1,0:T(8,128)(2,1)S(1)}, u32[]{:S(2)}, u32[]{:S(2)}) collective-permute-start(bf16[2,128,1024]{2,1,0:T(8,128)(2,1)} %get-tuple-element.16), channel_id=1, source_target_pairs={{0,256},{128,384},{256,0},{384,128},{1,257},{129,385},{257,1},{385... | collective-permute-start | bytes 1572872 | tf_op jit(solution)/shard_map/ppermute | solution.py:282
  62.6 5.5 %collective-permute-start.6 = (bf16[2,128,1024]{2,1,0:T(8,128)(2,1)}, bf16[2,128,1024]{2,1,0:T(8,128)(2,1)}, u32[]{:S(2)}, u32[]{:S(2)}) collective-permute-start(bf16[2,128,1024]{2,1,0:T(8,128)(2,1)} %get-tuple-element.17), channel_id=1, source_target_pairs={{0,384},{128,0},{256,128},{384,256},{1,385},{129,1},{257,129},{385... | collective-permute-start | bytes 1572872 | tf_op jit(solution)/shard_map/ppermute | solution.py:282
  68.1 0.0 all-to-all-done
  68.1 0.1 reduce_sum.9
  68.2 0.7 broadcast_in_dim.2
  68.9 11.3 %all-to-all-start.1 = ((f32[64,8,128]{2,1,0:T(8,128)}), f32[64,8,128]{2,1,0:T(8,128)}, u32[]{:S(2)}, u32[]{:S(2)}) async-start(f32[64,8,128]{2,1,0:T(8,128)} %broadcast_in_dim.2), calls=%async_computation.1 | async-start | bytes 524288 | tf_op jit(solution)/shard_map/all_to_all | solution.py:299
  80.2 16.1 %collective-permute-done.4.one.rest_0_ = bf16[2,128,1024]{2,1,0:T(8,128)(2,1)S(1)} collective-permute-done((bf16[2,128,1024]{2,1,0:T(8,128)(2,1)}, bf16[2,128,1024]{2,1,0:T(8,128)(2,1)S(1)}, u32[]{:S(2)}, u32[]{:S(2)}) %collective-permute-start.4) | collective-permute-done | bytes 524320 | tf_op jit(solution)/shard_map/ppermute | solution.py:282
  96.3 0.0 collective-permute-done.5.two.rest_1_
  96.3 16.5 %collective-permute-done.6.three.rest_2_ = bf16[2,128,1024]{2,1,0:T(8,128)(2,1)} collective-permute-done((bf16[2,128,1024]{2,1,0:T(8,128)(2,1)}, bf16[2,128,1024]{2,1,0:T(8,128)(2,1)}, u32[]{:S(2)}, u32[]{:S(2)}) %collective-permute-start.6) | collective-permute-done | bytes 524320 | tf_op jit(solution)/shard_map/ppermute | solution.py:282
  112.8 0.0 collective-permute-done.3.beside
  112.8 4.2 %hidden_sums.1 = (f32[3,128,256]{2,1,0:T(8,128)S(1)}, f32[3,128,256]{2,1,0:T(8,128)S(1)}) custom-call(s32[3]{0:T(128)S(1)} %copy-done.4, bf16[128,4096]{1,0:T(8,128)(2,1)S(1)} %bitcast.17, bf16[128,4096]{1,0:T(8,128)(2,1)S(1)} %bitcast.20, bf16[4,2,128,512]{3,2,1,0:T(8,128)(2,1)} %collective-permute-done.3.beside, bf16[8,4,192,256]{3,2,1,0:T(8,128)(2,1)} %bitcast.22, ...), custom_call_target="tpu_custom_call" | custom-call | flops 805306368 | bytes 6291456 | tf_op jit(solution)/shard_map/hidden_sums/pallas_call | solution.py:182
  117.0 0.0 copy-start.3
  117.0 0.7 copy-done.3
  117.8 2.4 %collective-permute-start.8 = (f32[3,128,256]{2,1,0:T(8,128)S(1)}, f32[3,128,256]{2,1,0:T(8,128)}, u32[]{:S(2)}, u32[]{:S(2)}) collective-permute-start(f32[3,128,256]{2,1,0:T(8,128)S(1)} %get-tuple-element.19), channel_id=1, source_target_pairs={{0,64},{64,0},{1,65},{65,1},{2,66},{66,2},{3,67},{67,3},{4,68},{68... | collective-permute-start | bytes 1179656 | tf_op jit(solution)/shard_map/ppermute | solution.py:290
  120.2 0.0 all-to-all-done.1
  120.2 2.0 %multiply_subtract_fusion = (f32[16,4096]{1,0:T(8,128)}, f32[16,4096]{1,0:T(8,128)}) fusion(f32[16,4096]{1,0:T(8,128)} %param.14, f32[16,4096]{1,0:T(8,128)} %bitcast.13, f32[16,4096]{1,0:T(8,128)} %param.15), kind=kLoop, calls=%fused_computation.1 | loop fusion | flops 393216 | bytes 1310720 | tf_op jit(solution)/shard_map/sub | solution.py:321
  122.2 0.0 collective-permute-done.8.arrived_ref
  122.2 2.1 %activation.1 = bf16[4,3,128,256]{3,2,1,0:T(8,128)(2,1)} custom-call(f32[3,128,256]{2,1,0:T(8,128)} %copy-done.3, f32[3,128,256]{2,1,0:T(8,128)} %collective-permute-done.8.arrived_ref, f32[16,4096]{1,0:T(8,128)} %get-tuple-element.23.after), custom_call_target="tpu_custom_call" | custom-call | flops 655360 | bytes 1048576 | tf_op jit(solution)/shard_map/activation/pallas_call | solution.py:216
  124.3 4.2 %all-to-all-start.2 = ((bf16[4,3,128,256]{3,2,1,0:T(8,128)(2,1)}), bf16[4,3,128,256]{3,2,1,0:T(8,128)(2,1)}, u32[]{:S(2)}, u32[]{:S(2)}) async-start(bf16[4,3,128,256]{3,2,1,0:T(8,128)(2,1)} %activation.1), calls=%async_computation.2 | async-start | bytes 1572864 | tf_op jit(solution)/shard_map/all_to_all | solution.py:278
  128.5 2.5 %repack_tokens.1 = bf16[3,2,128,512]{3,2,1,0:T(8,128)(2,1)} custom-call(s32[3]{0:T(128)S(1)} %copy-done.4, bf16[2,128,1024]{2,1,0:T(8,128)(2,1)S(1)} %collective-permute-done.4.one.rest_0_, bf16[2,128,1024]{2,1,0:T(8,128)(2,1)S(1)} %collective-permute-done.5.two.rest_1_, bf16[2,128,1024]{2,1,0:T(8,128)(2,1)} %collective-permute-done.6.three.rest_2_), custom_call_target="tpu_custom_call" | custom-call | bytes 2097152 | tf_op jit(solution)/shard_map/repack_tokens/pallas_call | solution.py:103
  131.0 2.8 %collective-permute-start.7 = (bf16[3,2,128,512]{3,2,1,0:T(8,128)(2,1)}, bf16[3,2,128,512]{3,2,1,0:T(8,128)(2,1)}, u32[]{:S(2)}, u32[]{:S(2)}) collective-permute-start(bf16[3,2,128,512]{3,2,1,0:T(8,128)(2,1)} %repack_tokens.1), channel_id=1, source_target_pairs={{0,64},{64,0},{1,65},{65,1},{2,66},{66,2},{3,67},{67,3},{4,68},{68... | collective-permute-start | bytes 2359304 | tf_op jit(solution)/shard_map/ppermute | solution.py:290
  133.7 12.5 %all-to-all-done.2.acts = bf16[4,3,128,256]{3,2,1,0:T(8,128)(2,1)} async-done(((bf16[4,3,128,256]{3,2,1,0:T(8,128)(2,1)}), bf16[4,3,128,256]{3,2,1,0:T(8,128)(2,1)}, u32[]{:S(2)}, u32[]{:S(2)}) %all-to-all-start.2) | async-done | bytes 786464 | tf_op jit(solution)/shard_map/all_to_all | solution.py:278
  146.3 4.0 %collective-permute-start.9 = (bf16[4,3,128,256]{3,2,1,0:T(8,128)(2,1)}, bf16[4,3,128,256]{3,2,1,0:T(8,128)(2,1)S(1)}, u32[]{:S(2)}, u32[]{:S(2)}) collective-permute-start(bf16[4,3,128,256]{3,2,1,0:T(8,128)(2,1)} %all-to-all-done.2.acts), channel_id=1, source_target_pairs={{0,64},{64,0},{1,65},{65,1},{2,66},{66,2},{3,67},{67,3},{4,68},{68... | collective-permute-start | bytes 2359304 | tf_op jit(solution)/shard_map/ppermute | solution.py:290
  150.3 0.0 collective-permute-done.7.swapped
  150.3 2.1 %collective-permute-done.9.acts_beside = bf16[4,3,128,256]{3,2,1,0:T(8,128)(2,1)S(1)} collective-permute-done((bf16[4,3,128,256]{3,2,1,0:T(8,128)(2,1)}, bf16[4,3,128,256]{3,2,1,0:T(8,128)(2,1)S(1)}, u32[]{:S(2)}, u32[]{:S(2)}) %collective-permute-start.9) | collective-permute-done | bytes 786464 | tf_op jit(solution)/shard_map/ppermute | solution.py:290
  152.4 4.2 %weight_grads.1 = (bf16[1,512,256]{2,1,0:T(8,128)(2,1)}, bf16[1,512,256]{2,1,0:T(8,128)(2,1)}, bf16[1,256,512]{2,1,0:T(8,128)(2,1)}) custom-call(s32[3]{0:T(128)S(1)} %copy-done.4, bf16[128,4096]{1,0:T(8,128)(2,1)S(1)} %bitcast.18, bf16[128,4096]{1,0:T(8,128)(2,1)S(1)} %bitcast.21, bf16[4,2,128,512]{3,2,1,0:T(8,128)(2,1)} %collective-permute-done.3.beside, ...), custom_call_target="tpu_custom_call" | custom-call | flops 805306368 | bytes 5242880 | tf_op jit(solution)/shard_map/weight_grads/pallas_call | solution.py:256
  (6 shorter events, 0.0 us)
Async XLA Ops:
  7.2 42.1 %copy-start = (bf16[1,128,4096]{2,1,0:T(8,128)(2,1)S(1)}, bf16[1,128,4096]{2,1,0:T(8,128)(2,1)}, u32[]{:S(2)}) copy-start(bf16[1,128,4096]{2,1,0:T(8,128)(2,1)} %param.8) | copy-start | bytes 3145732
  7.2 42.1 %copy-start.1 = (bf16[1,128,4096]{2,1,0:T(8,128)(2,1)S(1)}, bf16[1,128,4096]{2,1,0:T(8,128)(2,1)}, u32[]{:S(2)}) copy-start(bf16[1,128,4096]{2,1,0:T(8,128)(2,1)} %param.9) | copy-start | bytes 3145732
  7.2 105.6 %all-gather.3.cloned.1.call-start = ((), (), s32[]{:S(2)}) async-start(), calls=%async_computation.3 | async-start | bytes 3538944 | tf_op jit(solution)/shard_map/all_gather | solution.py:312
  7.8 41.4 %copy-start.4 = (s32[3]{0:T(128)S(1)}, s32[3]{0:T(128)}, u32[]{:S(2)}) copy-start(s32[3]{0:T(128)} %pad_add_fusion.place) | copy-start | bytes 40
  10.1 14.5 %collective-permute-start.1 = (bf16[192,256]{1,0:T(8,128)(2,1)}, bf16[192,256]{1,0:T(8,128)(2,1)S(1)}, u32[]{:S(2)}, u32[]{:S(2)}) collective-permute-start(bf16[192,256]{1,0:T(8,128)(2,1)} %weight_share.1), channel_id=1, source_target_pairs={{0,256},{128,384},{256,0},{384,128},{1,257},{129,385},{257,1},{385... | collective-permute-start | bytes 294920 | tf_op jit(solution)/shard_map/ppermute | solution.py:286
  18.4 10.4 %collective-permute-start = (bf16[192,256]{1,0:T(8,128)(2,1)}, bf16[192,256]{1,0:T(8,128)(2,1)S(1)}, u32[]{:S(2)}, u32[]{:S(2)}) collective-permute-start(bf16[192,256]{1,0:T(8,128)(2,1)} %weight_share.1), channel_id=1, source_target_pairs={{0,384},{128,0},{256,128},{384,256},{1,385},{129,1},{257,129},{385... | collective-permute-start | bytes 294920 | tf_op jit(solution)/shard_map/ppermute | solution.py:286
  20.3 8.4 %collective-permute-start.2 = (bf16[192,256]{1,0:T(8,128)(2,1)}, bf16[192,256]{1,0:T(8,128)(2,1)S(1)}, u32[]{:S(2)}, u32[]{:S(2)}) collective-permute-start(bf16[192,256]{1,0:T(8,128)(2,1)} %weight_share.1), channel_id=1, source_target_pairs={{0,128},{128,256},{256,384},{384,0},{1,129},{129,257},{257,385},{3... | collective-permute-start | bytes 294920 | tf_op jit(solution)/shard_map/ppermute | solution.py:286
  24.6 5.9 %copy-start.5 = (bf16[192,256]{1,0:T(8,128)(2,1)}, bf16[192,256]{1,0:T(8,128)(2,1)S(1)}, u32[]{:S(2)}) copy-start(bf16[192,256]{1,0:T(8,128)(2,1)S(1)} %collective-permute-done.1.after) | copy-start | bytes 294916
  32.8 35.3 %all-to-all-start = ((f32[64,8,128]{2,1,0:T(8,128)}), f32[64,8,128]{2,1,0:T(8,128)S(1)}, u32[]{:S(2)}, u32[]{:S(2)}) async-start(f32[64,8,128]{2,1,0:T(8,128)} %delta_tiles.1), calls=%async_computation | async-start | bytes 524288 | tf_op jit(solution)/shard_map/all_to_all | solution.py:297
  49.3 1.0 copy-start.2
  52.8 60.0 %collective-permute-start.3 = (bf16[4,2,128,512]{3,2,1,0:T(8,128)(2,1)}, bf16[4,2,128,512]{3,2,1,0:T(8,128)(2,1)}, u32[]{:S(2)}, u32[]{:S(2)}) collective-permute-start(bf16[4,2,128,512]{3,2,1,0:T(8,128)(2,1)} %get-tuple-element.14), channel_id=1, source_target_pairs={{0,64},{64,0},{1,65},{65,1},{2,66},{66,2},{3,67},{67,3},{4,68},{68... | collective-permute-start | bytes 3145736 | tf_op jit(solution)/shard_map/ppermute | solution.py:290
  56.1 40.2 %collective-permute-start.4 = (bf16[2,128,1024]{2,1,0:T(8,128)(2,1)}, bf16[2,128,1024]{2,1,0:T(8,128)(2,1)S(1)}, u32[]{:S(2)}, u32[]{:S(2)}) collective-permute-start(bf16[2,128,1024]{2,1,0:T(8,128)(2,1)} %get-tuple-element.15), channel_id=1, source_target_pairs={{0,128},{128,256},{256,384},{384,0},{1,129},{129,257},{257,385},{3... | collective-permute-start | bytes 1572872 | tf_op jit(solution)/shard_map/ppermute | solution.py:282
  58.0 38.3 %collective-permute-start.5 = (bf16[2,128,1024]{2,1,0:T(8,128)(2,1)}, bf16[2,128,1024]{2,1,0:T(8,128)(2,1)S(1)}, u32[]{:S(2)}, u32[]{:S(2)}) collective-permute-start(bf16[2,128,1024]{2,1,0:T(8,128)(2,1)} %get-tuple-element.16), channel_id=1, source_target_pairs={{0,256},{128,384},{256,0},{384,128},{1,257},{129,385},{257,1},{385... | collective-permute-start | bytes 1572872 | tf_op jit(solution)/shard_map/ppermute | solution.py:282
  62.6 50.2 %collective-permute-start.6 = (bf16[2,128,1024]{2,1,0:T(8,128)(2,1)}, bf16[2,128,1024]{2,1,0:T(8,128)(2,1)}, u32[]{:S(2)}, u32[]{:S(2)}) collective-permute-start(bf16[2,128,1024]{2,1,0:T(8,128)(2,1)} %get-tuple-element.17), channel_id=1, source_target_pairs={{0,384},{128,0},{256,128},{384,256},{1,385},{129,1},{257,129},{385... | collective-permute-start | bytes 1572872 | tf_op jit(solution)/shard_map/ppermute | solution.py:282
  68.9 51.3 %all-to-all-start.1 = ((f32[64,8,128]{2,1,0:T(8,128)}), f32[64,8,128]{2,1,0:T(8,128)}, u32[]{:S(2)}, u32[]{:S(2)}) async-start(f32[64,8,128]{2,1,0:T(8,128)} %broadcast_in_dim.2), calls=%async_computation.1 | async-start | bytes 524288 | tf_op jit(solution)/shard_map/all_to_all | solution.py:299
  117.0 0.8 copy-start.3
  117.8 4.4 %collective-permute-start.8 = (f32[3,128,256]{2,1,0:T(8,128)S(1)}, f32[3,128,256]{2,1,0:T(8,128)}, u32[]{:S(2)}, u32[]{:S(2)}) collective-permute-start(f32[3,128,256]{2,1,0:T(8,128)S(1)} %get-tuple-element.19), channel_id=1, source_target_pairs={{0,64},{64,0},{1,65},{65,1},{2,66},{66,2},{3,67},{67,3},{4,68},{68... | collective-permute-start | bytes 1179656 | tf_op jit(solution)/shard_map/ppermute | solution.py:290
  124.3 22.0 %all-to-all-start.2 = ((bf16[4,3,128,256]{3,2,1,0:T(8,128)(2,1)}), bf16[4,3,128,256]{3,2,1,0:T(8,128)(2,1)}, u32[]{:S(2)}, u32[]{:S(2)}) async-start(bf16[4,3,128,256]{3,2,1,0:T(8,128)(2,1)} %activation.1), calls=%async_computation.2 | async-start | bytes 1572864 | tf_op jit(solution)/shard_map/all_to_all | solution.py:278
  131.0 19.4 %collective-permute-start.7 = (bf16[3,2,128,512]{3,2,1,0:T(8,128)(2,1)}, bf16[3,2,128,512]{3,2,1,0:T(8,128)(2,1)}, u32[]{:S(2)}, u32[]{:S(2)}) collective-permute-start(bf16[3,2,128,512]{3,2,1,0:T(8,128)(2,1)} %repack_tokens.1), channel_id=1, source_target_pairs={{0,64},{64,0},{1,65},{65,1},{2,66},{66,2},{3,67},{67,3},{4,68},{68... | collective-permute-start | bytes 2359304 | tf_op jit(solution)/shard_map/ppermute | solution.py:290
  146.3 6.1 %collective-permute-start.9 = (bf16[4,3,128,256]{3,2,1,0:T(8,128)(2,1)}, bf16[4,3,128,256]{3,2,1,0:T(8,128)(2,1)S(1)}, u32[]{:S(2)}, u32[]{:S(2)}) collective-permute-start(bf16[4,3,128,256]{3,2,1,0:T(8,128)(2,1)} %all-to-all-done.2.acts), channel_id=1, source_target_pairs={{0,64},{64,0},{1,65},{65,1},{2,66},{66,2},{3,67},{67,3},{4,68},{68... | collective-permute-start | bytes 2359304 | tf_op jit(solution)/shard_map/ppermute | solution.py:290
Sparse Core Ops, SparseCore 0:
  30.6 60.4 all-gather.2

commit v4 on v3

v4 whole, which is shorter than its diff:
```python
import functools

import jax
import jax.numpy as jnp
from jax import lax
from jax.experimental import pallas as pl
from jax.experimental.pallas import tpu as pltpu
from jax.sharding import Mesh
from jax.sharding import PartitionSpec as P

CHIPS = 4
ROWS = 128
WIDE = 1024
HALF = 512
HID = 256
VMEM_LIMIT = 48 * 1024 * 1024

F32 = jnp.float32
BF16 = jnp.bfloat16
ANY = pl.BlockSpec(memory_space=pl.ANY)
VMEM = pl.BlockSpec(memory_space=pltpu.VMEM)
SMEM = pl.BlockSpec(memory_space=pltpu.SMEM)


def run_copies(copies, sems):
    started = [pltpu.make_async_copy(src, dst, sems.at[i]) for i, (src, dst) in enumerate(copies)]
    for copy in started:
        copy.start()
    for copy in started:
        copy.wait()


def columns(base):
    return pl.ds(pl.multiple_of(base, HALF), HALF)


def share_kernel(parts, place, gate, up, down, out, sems):
    gate_rows, down_rows = HALF // parts, HID // parts
    cut = 2 * gate_rows
    at_gate = pl.ds(pl.multiple_of(place[1] * gate_rows, gate_rows), gate_rows)
    at_down = pl.ds(pl.multiple_of(place[1] * down_rows, down_rows), down_rows)
    copies = [
        (gate.at[at_gate], out.at[pl.ds(0, gate_rows)]),
        (up.at[at_gate], out.at[pl.ds(gate_rows, gate_rows)]),
        (down.at[at_down, :HID], out.at[pl.ds(cut, down_rows)]),
        (down.at[at_down, HID:], out.at[pl.ds(cut + down_rows, down_rows)]),
    ]
    run_copies(copies, sems)


def own_share(place, gate, up, down, parts):
    return pl.pallas_call(
        functools.partial(share_kernel, parts),
        out_shape=jax.ShapeDtypeStruct((2 * (HALF + HID) // parts, HID), BF16),
        in_specs=[SMEM, ANY, ANY, ANY],
        out_specs=VMEM,
        scratch_shapes=[pltpu.SemaphoreType.DMA((4,))],
        cost_estimate=pl.CostEstimate(flops=0, bytes_accessed=1 << 18, transcendentals=0),
        name="weight_share",
    )(place, gate, up, down)


def pack_kernel(place, x, dy, after, also_after, out, beside, sems):
    del after, also_after
    other = (1 - place[0]) * HALF
    copies = []
    for chip in range(CHIPS):
        for i, ref in enumerate((x, dy)):
            copies += [
                (ref.at[:, pl.ds(chip * WIDE, WIDE)], out.at[chip, i]),
                (ref.at[:, columns(chip * WIDE + other)], beside.at[chip, i]),
            ]
    run_copies(copies, sems)


def pack(place, x, dy, after, also_after):
    return pl.pallas_call(
        pack_kernel,
        out_shape=(
            jax.ShapeDtypeStruct((CHIPS, 2, ROWS, WIDE), BF16),
            jax.ShapeDtypeStruct((CHIPS, 2, ROWS, HALF), BF16),
        ),
        in_specs=[SMEM] + [ANY] * 4,
        out_specs=(VMEM,) * 2,
        scratch_shapes=[pltpu.SemaphoreType.DMA((16,))],
        compiler_params=pltpu.CompilerParams(vmem_limit_bytes=VMEM_LIMIT),
        cost_estimate=pl.CostEstimate(flops=0, bytes_accessed=6 << 20, transcendentals=0),
        name="pack_tokens",
    )(place, x, dy, after, also_after)


def repack_kernel(place, arrived, out, sems):
    other = columns((1 - place[0]) * HALF)
    run_copies([(arrived.at[i, :, :, other], out.at[i]) for i in range(CHIPS)], sems)


def repack(place, arrived):
    return pl.pallas_call(
        repack_kernel,
        out_shape=jax.ShapeDtypeStruct((CHIPS, 2, ROWS, HALF), BF16),
        in_specs=[SMEM, ANY],
        out_specs=VMEM,
        scratch_shapes=[pltpu.SemaphoreType.DMA((CHIPS,))],
        compiler_params=pltpu.CompilerParams(vmem_limit_bytes=VMEM_LIMIT),
        cost_estimate=pl.CostEstimate(flops=0, bytes_accessed=2 << 20, transcendentals=0),
        name="repack_tokens",
    )(place, arrived)


def hidden_kernel(parts, waited, place, x, dy, beside, *rest):
    weights = rest[:parts]
    mine, theirs, xs, dys, gates, ups, downs, sems = rest[parts + waited :]
    gate_rows, down_rows = HALF // parts, HID // parts
    cut = 2 * gate_rows
    copies = []
    for shift in range(CHIPS):
        chip = lax.rem(place[2] + shift, CHIPS)
        own = columns(chip * WIDE + place[0] * HALF)
        copies += [
            (x.at[:, own], xs.at[shift, :ROWS]),
            (dy.at[:, own], dys.at[shift, :ROWS]),
            (beside.at[chip, 0], xs.at[shift, ROWS:]),
            (beside.at[chip, 1], dys.at[shift, ROWS:]),
        ]
    for shift, ref in enumerate(weights):
        part = lax.rem(place[1] + shift, parts)
        to_gate = pl.ds(pl.multiple_of(part * gate_rows, gate_rows), gate_rows)
        to_down = pl.ds(pl.multiple_of(part * down_rows, down_rows), down_rows)
        copies += [
            (ref.at[:, pl.ds(0, gate_rows)], gates.at[:, to_gate]),
            (ref.at[:, pl.ds(gate_rows, gate_rows)], ups.at[:, to_gate]),
            (ref.at[:, pl.ds(cut, down_rows)], downs.at[:, 0, to_down]),
            (ref.at[:, pl.ds(cut + down_rows, down_rows)], downs.at[:, 1, to_down]),
        ]
    run_copies(copies, sems)
    gate = up = dh = 0.0
    for chip in range(CHIPS):
        a, b = xs[chip], dys[chip]
        gate += jnp.dot(a, gates[chip], preferred_element_type=F32)
        up += jnp.dot(a, ups[chip], preferred_element_type=F32)
        for h in range(2):
            dh += lax.dot_general(
                b[:, HID * h : HID * (h + 1)],
                downs[chip, h],
                (((1,), (1,)), ((), ())),
                preferred_element_type=F32,
            )
    for i, value in enumerate((gate, up, dh)):
        mine[i] = value[:ROWS]
        theirs[i] = value[ROWS:]


def hidden_sums(place, x, dy, beside, weights, after):
    out = jax.ShapeDtypeStruct((3, ROWS, HID), F32)
    return pl.pallas_call(
        functools.partial(hidden_kernel, len(weights), len(after)),
        out_shape=(out, out),
        in_specs=[SMEM] + [ANY] * (3 + len(weights) + len(after)),
        out_specs=(VMEM, VMEM),
        scratch_shapes=[
            pltpu.VMEM((CHIPS, 2 * ROWS, HALF), BF16),
            pltpu.VMEM((CHIPS, 2 * ROWS, HALF), BF16),
            pltpu.VMEM((CHIPS, HALF, HID), BF16),
            pltpu.VMEM((CHIPS, HALF, HID), BF16),
            pltpu.VMEM((CHIPS, 2, HID, HID), BF16),
            pltpu.SemaphoreType.DMA((4 * len(weights) + 16,)),
        ],
        compiler_params=pltpu.CompilerParams(vmem_limit_bytes=VMEM_LIMIT),
        cost_estimate=pl.CostEstimate(flops=6 * 256 * 2048 * 256, bytes_accessed=6 << 20, transcendentals=0),
        name="hidden_sums",
    )(place, x, dy, beside, *weights, *after)


def activation_kernel(mine_ref, arrived_ref, after, out, mine, arrived, sems):
    del after
    run_copies([(mine_ref, mine), (arrived_ref, arrived)], sems)
    gate = mine[0] + arrived[0]
    up = mine[1] + arrived[1]
    dh = mine[2] + arrived[2]
    sig = jax.nn.sigmoid(gate)
    active = gate * sig
    slope = sig * (1.0 + gate * (1.0 - sig))
    for i, value in enumerate((dh * up * slope, dh * active, active * up)):
        out[i] = value.astype(BF16)


def activation(mine, arrived, after):
    return pl.pallas_call(
        activation_kernel,
        out_shape=jax.ShapeDtypeStruct((3, ROWS, HID), BF16),
        in_specs=[ANY] * 3,
        out_specs=VMEM,
        scratch_shapes=[
            pltpu.VMEM((3, ROWS, HID), F32),
            pltpu.VMEM((3, ROWS, HID), F32),
            pltpu.SemaphoreType.DMA((2,)),
        ],
        cost_estimate=pl.CostEstimate(flops=20 * ROWS * HID, bytes_accessed=1 << 20, transcendentals=ROWS * HID),
        name="activation",
    )(mine, arrived, after)


def grads_kernel(place, arrived, swapped, *rest):
    acts, (gg, gu, gd, xs, dys, hs, sems) = rest[: 2 * CHIPS], rest[2 * CHIPS :]
    half = columns(place[0] * HALF)
    copies = []
    for i in range(CHIPS):
        near, far = pl.ds(i * ROWS, ROWS), pl.ds((CHIPS + i) * ROWS, ROWS)
        copies += [
            (arrived.at[i, 0, :, half], xs.at[near]),
            (arrived.at[i, 1, :, half], dys.at[near]),
            (swapped.at[i, 0], xs.at[far]),
            (swapped.at[i, 1], dys.at[far]),
        ]
    for shift in range(CHIPS):
        chip = lax.rem(place[2] + CHIPS - shift, CHIPS)
        near = pl.ds(pl.multiple_of(chip * ROWS, ROWS), ROWS)
        far = pl.ds(pl.multiple_of((CHIPS + chip) * ROWS, ROWS), ROWS)
        copies += [(acts[shift], hs.at[:, near]), (acts[CHIPS + shift], hs.at[:, far])]
    run_copies(copies, sems)
    tall = (((0,), (0,)), ((), ()))
    gg[0] = lax.dot_general(xs[...], hs[0], tall, preferred_element_type=F32).astype(BF16)
    gu[0] = lax.dot_general(xs[...], hs[1], tall, preferred_element_type=F32).astype(BF16)
    gd[0] = lax.dot_general(hs[2], dys[...], tall, preferred_element_type=F32).astype(BF16)


def grads(place, arrived, swapped, acts):
    tokens = 2 * CHIPS * ROWS
    return pl.pallas_call(
        grads_kernel,
        out_shape=(
            jax.ShapeDtypeStruct((1, HALF, HID), BF16),
            jax.ShapeDtypeStruct((1, HALF, HID), BF16),
            jax.ShapeDtypeStruct((1, HID, HALF), BF16),
        ),
        in_specs=[SMEM] + [ANY] * (2 + len(acts)),
        out_specs=(VMEM,) * 3,
        scratch_shapes=[
            pltpu.VMEM((tokens, HALF), BF16),
            pltpu.VMEM((tokens, HALF), BF16),
            pltpu.VMEM((3, tokens, HID), BF16),
            pltpu.SemaphoreType.DMA((24,)),
        ],
        compiler_params=pltpu.CompilerParams(vmem_limit_bytes=VMEM_LIMIT),
        cost_estimate=pl.CostEstimate(flops=6 * 1024 * 512 * 256, bytes_accessed=5 << 20, transcendentals=0),
        name="weight_grads",
    )(place, arrived, swapped, *acts)


def to_shift(value, shift):
    return lax.ppermute(value, "yh", [(i, (i + shift) % CHIPS) for i in range(CHIPS)])


def from_shift(value, shift):
    return lax.ppermute(value, "yh", [(i, (i - shift) % CHIPS) for i in range(CHIPS)])


def from_x(value, shift, size):
    return lax.ppermute(value, "x", [(i, (i - shift) % size) for i in range(size)])


def other_core(value):
    return lax.ppermute(value, "core", [(0, 1), (1, 0)])


def sum_over(total, names):
    for name in names:
        size = lax.axis_size(name)
        step = 1
        while step < size:
            total += lax.ppermute(total, name, [(i, i ^ step) for i in range(size)])
            step *= 2
    return total


def on_device(tokens, cotangent, w_gate, w_up, w_down, delta, anchor, momentum):
    x, dy = tokens[0], cotangent[0]
    place = jnp.stack([lax.axis_index(name) for name in ("core", "x", "yh")]).astype(jnp.int32)
    parts = lax.axis_size("x")

    share = own_share(place, w_gate, w_up, w_down, parts)
    shares = {shift: from_shift(share, shift) for shift in (1, 2, 3)}
    shares = jnp.stack([share] + [shares[shift] for shift in (1, 2, 3)])
    weights = [shares] + [from_x(shares, shift, parts) for shift in range(1, parts)]

    partial = sum_over(delta[0], ("yl", "x"))
    packed, beside = pack(place, x, dy, shares, partial)
    arrived = lax.all_to_all(packed, "yh", 0, 0, tiled=True)
    beside = other_core(beside)
    swapped = other_core(repack(place, arrived))

    pseudo = sum_over(partial, ("z",)) / lax.axis_size(("yl", "x", "z"))
    new_momentum = 0.9 * momentum + pseudo
    new_anchor = anchor - 0.7 * (pseudo + 0.9 * new_momentum)

    mine, theirs = hidden_sums(place, x, dy, beside, weights, ())
    acts = activation(mine, other_core(theirs), new_anchor)
    acts = [acts] + [to_shift(acts, shift) for shift in (1, 2, 3)]
    acts += [other_core(value) for value in acts]
    grad_gate, grad_up, grad_down = grads(place, arrived, swapped, acts)
    return grad_gate, grad_up, grad_down, new_anchor, new_momentum


def solution(mesh):
    fine = Mesh(mesh.devices.reshape(4, 2, 2, 4, 8), ("yh", "core", "yl", "x", "z"))
    fsdp, replica = ("yh", "core"), ("yl", "x", "z")
    placed = (
        P(replica, fsdp, None),
        P(replica, fsdp, None),
        P(fsdp, None),
        P(fsdp, None),
        P(None, fsdp),
        P(replica, fsdp, None),
        P(fsdp, None),
        P(fsdp, None),
    )
    return jax.shard_map(
        on_device,
        mesh=fine,
        in_specs=placed,
        out_specs=(
            P(replica, fsdp, None),
            P(replica, fsdp, None),
            P(replica, None, fsdp),
            P(fsdp, None),
            P(fsdp, None),
        ),
        check_vma=False,
    )
```

time: 164 us -> 162 us (0.988)
  starting transfers between devices: 70.9 us -> 100 us
  waiting for transfers between devices: 51.4 us -> 32.8 us
  between operations: 14.3 us -> 1.05 us
  Pallas kernels: 20 us -> 16.2 us
  local copies, waits for them, and re-layouts: 2.52 us -> 4.89 us
    ppermute x0 -> x9, starting transfers between devices: none -> 41.5 us  [the longest x6 31.6 us: sum_over(): total += lax.ppermute(total, name, [(i, i ^ step) for i in range(size)])]
    ppermute x3, waiting for transfers between devices: 32.6 us -> 5.42 us  [to_shift(): lax.ppermute(value, 'yh', [(i, (i + shift) % CHIPS) for i in range(CHIPS)])]
    all_to_all x3 -> x1, starting transfers between devices: 31.9 us -> 5.3 us  [on_device(): arrived = lax.all_to_all(packed, 'yh', 0, 0, tiled=True)]
    ppermute x0 -> x9, waiting for transfers between devices: none -> 21.2 us  [the longest x6 21.2 us: sum_over(): total += lax.ppermute(total, name, [(i, i ^ step) for i in range(size)])]
    all_to_all x3 -> x1, waiting for transfers between devices: 12.6 us -> 0.01 us  [on_device(): arrived = lax.all_to_all(packed, 'yh', 0, 0, tiled=True)]
    ppermute x4 -> x7, starting transfers between devices: 12.5 us -> 24.9 us  [other_core(): return lax.ppermute(value, 'core', [(0, 1), (1, 0)])]
    pallas_call x5 -> x4, Pallas kernels: 13.6 us -> 9.09 us  [the longest x1 3.2 us: hidden_sums(): pl.pallas_call(functools.partial(hidden_kernel, len(weights), len(after))...]
    unnamed x12 -> x18, local copies, waits for them, and re-layouts: 1.8 us -> 4.89 us
  transfers between devices with their start and end apart: 14 -> 23, of which waited for: 5 -> 8; matrix products, arithmetic and copies ran while one was open for 2% -> 3% of each run, Pallas kernels for 7% -> 6%
where the time goes in v4:
time: 162 us; the launch traced here: 161 us
  starting transfers between devices  100 us (62%)
  waiting for transfers between devices  32.8 us (20%)
  Pallas kernels  16.2 us (10%)
  other arithmetic  5.48 us (3%)
  local copies, waits for them, and re-layouts  4.89 us (3%)
    ppermute x6, starting transfers between devices, sum_over(): total += lax.ppermute(total, name, [(i, i ^ step) for i in range(size)])  31.6 us
    ppermute x7, starting transfers between devices, other_core(): return lax.ppermute(value, 'core', [(0, 1), (1, 0)])  24.9 us
    ppermute x6, waiting for transfers between devices, sum_over(): total += lax.ppermute(total, name, [(i, i ^ step) for i in range(size)])  21.2 us
    ppermute x3, starting transfers between devices, to_shift(): lax.ppermute(value, 'yh', [(i, (i + shift) % CHIPS) for i in range(CHIPS)])  14.9 us
    ppermute x3, starting transfers between devices, from_shift(): lax.ppermute(value, 'yh', [(i, (i - shift) % CHIPS) for i in range(CHIPS)])  13.6 us
    ppermute x3, starting transfers between devices, from_x(): lax.ppermute(value, 'x', [(i, (i - shift) % size) for i in range(size)])  9.84 us
    ppermute x3, waiting for transfers between devices, to_shift(): lax.ppermute(value, 'yh', [(i, (i + shift) % CHIPS) for i in range(CHIPS)])  5.42 us
    all_to_all x1, starting transfers between devices, on_device(): arrived = lax.all_to_all(packed, 'yh', 0, 0, tiled=True)  5.3 us
  transfers between devices with their start and end apart: 23, of which 8 were waited for; matrix products, arithmetic and copies ran while one was open for 3% of the time, Pallas kernels for 6%

profile of v4, /device:TPU:1, one launch (start us, length us, event | category | flops | bytes accessed | tf_op | source)
XLA Modules:
  0.0 160.6 jit_solution(4873480488756936530)
XLA Ops:
  0.6 4.0 %collective-permute-start.3 = (f32[16,4096]{1,0:T(8,128)}, f32[16,4096]{1,0:T(8,128)S(1)}, u32[]{:S(2)}, u32[]{:S(2)}) collective-permute-start(f32[16,4096]{1,0:T(8,128)} %bitcast.16), channel_id=1, source_target_pairs={{0,32},{32,0},{1,33},{33,1},{2,34},{34,2},{3,35},{35,3},{4,36},{36... | collective-permute-start | bytes 786440 | tf_op jit(solution)/shard_map/ppermute | solution.py:271
  4.7 4.0 %collective-permute-done.3 = f32[16,4096]{1,0:T(8,128)S(1)} collective-permute-done((f32[16,4096]{1,0:T(8,128)}, f32[16,4096]{1,0:T(8,128)S(1)}, u32[]{:S(2)}, u32[]{:S(2)}) %collective-permute-start.3) | collective-permute-done | bytes 262176 | tf_op jit(solution)/shard_map/ppermute | solution.py:271
  8.6 1.0 bitcast_add_fusion
  9.6 0.0 copy-start.2
  9.6 5.4 %collective-permute-start.4 = (f32[16,4096]{1,0:T(8,128)S(1)}, f32[16,4096]{1,0:T(8,128)S(1)}, u32[]{:S(2)}, u32[]{:S(2)}) collective-permute-start(f32[16,4096]{1,0:T(8,128)S(1)} %bitcast_add_fusion), channel_id=1, source_target_pairs={{0,8},{8,0},{16,24},{24,16},{1,9},{9,1},{17,25},{25,17},{2,10},{10... | collective-permute-start | bytes 786440 | tf_op jit(solution)/shard_map/ppermute | solution.py:271
  15.0 0.6 pad_add_fusion.place
  15.6 2.4 %weight_share.1 = bf16[384,256]{1,0:T(8,128)(2,1)} custom-call(s32[3]{0:T(128)} %pad_add_fusion.place, bf16[512,256]{1,0:T(8,128)(2,1)} %gate.1, bf16[512,256]{1,0:T(8,128)(2,1)} %up.1, bf16[256,512]{1,0:T(8,128)(2,1)} %down.1), custom_call_target="tpu_custom_call" | custom-call | bytes 262144 | tf_op jit(solution)/shard_map/weight_share/pallas_call | solution.py:52
  18.0 5.9 %collective-permute-start = (bf16[384,256]{1,0:T(8,128)(2,1)}, bf16[384,256]{1,0:T(8,128)(2,1)S(1)}, u32[]{:S(2)}, u32[]{:S(2)}) collective-permute-start(bf16[384,256]{1,0:T(8,128)(2,1)} %weight_share.1), channel_id=1, source_target_pairs={{0,384},{128,0},{256,128},{384,256},{1,385},{129,1},{257,129},{385... | collective-permute-start | bytes 589832 | tf_op jit(solution)/shard_map/ppermute | solution.py:255
  23.9 3.5 %collective-permute-start.1 = (bf16[384,256]{1,0:T(8,128)(2,1)}, bf16[384,256]{1,0:T(8,128)(2,1)S(1)}, u32[]{:S(2)}, u32[]{:S(2)}) collective-permute-start(bf16[384,256]{1,0:T(8,128)(2,1)} %weight_share.1), channel_id=1, source_target_pairs={{0,256},{128,384},{256,0},{384,128},{1,257},{129,385},{257,1},{385... | collective-permute-start | bytes 589832 | tf_op jit(solution)/shard_map/ppermute | solution.py:255
  27.4 4.2 %collective-permute-start.2 = (bf16[384,256]{1,0:T(8,128)(2,1)}, bf16[384,256]{1,0:T(8,128)(2,1)S(1)}, u32[]{:S(2)}, u32[]{:S(2)}) collective-permute-start(bf16[384,256]{1,0:T(8,128)(2,1)} %weight_share.1), channel_id=1, source_target_pairs={{0,128},{128,256},{256,384},{384,0},{1,129},{129,257},{257,385},{3... | collective-permute-start | bytes 589832 | tf_op jit(solution)/shard_map/ppermute | solution.py:255
  31.7 4.4 %collective-permute-start.5 = (f32[16,4096]{1,0:T(8,128)S(1)}, f32[16,4096]{1,0:T(8,128)S(1)}, u32[]{:S(2)}, u32[]{:S(2)}) collective-permute-start(f32[16,4096]{1,0:T(8,128)S(1)} %add.25), channel_id=1, source_target_pairs={{0,16},{8,24},{16,0},{24,8},{1,17},{9,25},{17,1},{25,9},{2,18},{10... | collective-permute-start | bytes 786440 | tf_op jit(solution)/shard_map/ppermute | solution.py:271
  36.1 1.0 collective-permute-done.1
  37.0 4.2 %collective-permute-done.2 = bf16[384,256]{1,0:T(8,128)(2,1)S(1)} collective-permute-done((bf16[384,256]{1,0:T(8,128)(2,1)}, bf16[384,256]{1,0:T(8,128)(2,1)S(1)}, u32[]{:S(2)}, u32[]{:S(2)}) %collective-permute-start.2) | collective-permute-done | bytes 196640 | tf_op jit(solution)/shard_map/ppermute | solution.py:255
  41.2 1.0 pad_maximum_fusion.after.rest_0_
  42.3 2.4 %pack_tokens.1 = (bf16[4,2,128,1024]{3,2,1,0:T(8,128)(2,1)}, bf16[4,2,128,512]{3,2,1,0:T(8,128)(2,1)S(1)}) custom-call(s32[3]{0:T(128)S(1)} %copy-done.6, bf16[128,4096]{1,0:T(8,128)(2,1)S(1)} %bitcast.11, bf16[128,4096]{1,0:T(8,128)(2,1)S(1)} %bitcast.13, bf16[4,384,256]{2,1,0:T(8,128)(2,1)S(1)} %pad_maximum_fusion.after.rest_0_, f32[16,4096]{1,0:T(8,128)S(1)} %add.26.also_after), custom_call_target="tpu_custom_call" | custom-call | bytes 6291456 | tf_op jit(solution)/shard_map/pack_tokens/pallas_call | solution.py:77
  44.7 1.0 copy-done.7
  45.7 5.3 %all-to-all-start = ((bf16[4,2,128,1024]{3,2,1,0:T(8,128)(2,1)}), bf16[4,2,128,1024]{3,2,1,0:T(8,128)(2,1)S(1)}, u32[]{:S(2)}, u32[]{:S(2)}) async-start(bf16[4,2,128,1024]{3,2,1,0:T(8,128)(2,1)} %get-tuple-element.12), calls=%async_computation | async-start | bytes 4194304 | tf_op jit(solution)/shard_map/all_to_all | solution.py:288
  51.0 8.8 %collective-permute-start.7 = (bf16[4,2,128,512]{3,2,1,0:T(8,128)(2,1)}, bf16[4,2,128,512]{3,2,1,0:T(8,128)(2,1)S(1)}, u32[]{:S(2)}, u32[]{:S(2)}) collective-permute-start(bf16[4,2,128,512]{3,2,1,0:T(8,128)(2,1)} %copy-done.7), channel_id=1, source_target_pairs={{0,64},{64,0},{1,65},{65,1},{2,66},{66,2},{3,67},{67,3},{4,68},{68... | collective-permute-start | bytes 3145736 | tf_op jit(solution)/shard_map/ppermute | solution.py:263
  59.7 2.2 %collective-permute-start.10 = (bf16[4,384,256]{2,1,0:T(8,128)(2,1)S(1)}, bf16[4,384,256]{2,1,0:T(8,128)(2,1)S(1)}, u32[]{:S(2)}, u32[]{:S(2)}) collective-permute-start(bf16[4,384,256]{2,1,0:T(8,128)(2,1)S(1)} %pad_maximum_fusion.after.rest_0_), channel_id=1, source_target_pairs={{0,8},{8,16},{16,24},{24,0},{1,9},{9,17},{17,25},{25,1},{2,10},{10... | collective-permute-start | bytes 2359304 | tf_op jit(solution)/shard_map/ppermute | solution.py:259
  61.9 4.3 %collective-permute-start.8 = (bf16[4,384,256]{2,1,0:T(8,128)(2,1)S(1)}, bf16[4,384,256]{2,1,0:T(8,128)(2,1)S(1)}, u32[]{:S(2)}, u32[]{:S(2)}) collective-permute-start(bf16[4,384,256]{2,1,0:T(8,128)(2,1)S(1)} %pad_maximum_fusion.after.rest_0_), channel_id=1, source_target_pairs={{0,24},{8,0},{16,8},{24,16},{1,25},{9,1},{17,9},{25,17},{2,26},{10... | collective-permute-start | bytes 2359304 | tf_op jit(solution)/shard_map/ppermute | solution.py:259
  66.3 3.3 %collective-permute-start.9 = (bf16[4,384,256]{2,1,0:T(8,128)(2,1)S(1)}, bf16[4,384,256]{2,1,0:T(8,128)(2,1)S(1)}, u32[]{:S(2)}, u32[]{:S(2)}) collective-permute-start(bf16[4,384,256]{2,1,0:T(8,128)(2,1)S(1)} %pad_maximum_fusion.after.rest_0_), channel_id=1, source_target_pairs={{0,16},{8,24},{16,0},{24,8},{1,17},{9,25},{17,1},{25,9},{2,18},{10... | collective-permute-start | bytes 2359304 | tf_op jit(solution)/shard_map/ppermute | solution.py:259
  69.6 4.0 %collective-permute-start.12 = (f32[16,4096]{1,0:T(8,128)S(1)}, f32[16,4096]{1,0:T(8,128)S(1)}, u32[]{:S(2)}, u32[]{:S(2)}) collective-permute-start(f32[16,4096]{1,0:T(8,128)S(1)} %add.26.also_after), channel_id=1, source_target_pairs={{0,1},{1,0},{2,3},{3,2},{4,5},{5,4},{6,7},{7,6},{8,9},{9,8},{10,11... | collective-permute-start | bytes 786440 | tf_op jit(solution)/shard_map/ppermute | solution.py:271
  73.6 5.8 %collective-permute-done.12 = f32[16,4096]{1,0:T(8,128)S(1)} collective-permute-done((f32[16,4096]{1,0:T(8,128)S(1)}, f32[16,4096]{1,0:T(8,128)S(1)}, u32[]{:S(2)}, u32[]{:S(2)}) %collective-permute-start.12) | collective-permute-done | bytes 262176 | tf_op jit(solution)/shard_map/ppermute | solution.py:271
  79.5 5.8 %collective-permute-start.13 = (f32[16,4096]{1,0:T(8,128)S(1)}, f32[16,4096]{1,0:T(8,128)S(1)}, u32[]{:S(2)}, u32[]{:S(2)}) collective-permute-start(f32[16,4096]{1,0:T(8,128)S(1)} %add.27), channel_id=1, source_target_pairs={{0,2},{1,3},{2,0},{3,1},{4,6},{5,7},{6,4},{7,5},{8,10},{9,11},{10,... | collective-permute-start | bytes 786440 | tf_op jit(solution)/shard_map/ppermute | solution.py:271
  85.3 11.5 %collective-permute-done.13 = f32[16,4096]{1,0:T(8,128)S(1)} collective-permute-done((f32[16,4096]{1,0:T(8,128)S(1)}, f32[16,4096]{1,0:T(8,128)S(1)}, u32[]{:S(2)}, u32[]{:S(2)}) %collective-permute-start.13) | collective-permute-done | bytes 262176 | tf_op jit(solution)/shard_map/ppermute | solution.py:271
  96.7 0.7 add.28
  97.5 8.1 %collective-permute-start.14 = (f32[16,4096]{1,0:T(8,128)}, f32[16,4096]{1,0:T(8,128)}, u32[]{:S(2)}, u32[]{:S(2)}) collective-permute-start(f32[16,4096]{1,0:T(8,128)} %add.28), channel_id=1, source_target_pairs={{0,4},{1,5},{2,6},{3,7},{4,0},{5,1},{6,2},{7,3},{8,12},{9,13},{10,... | collective-permute-start | bytes 786440 | tf_op jit(solution)/shard_map/ppermute | solution.py:271
  105.6 1.0 copy-done.8
  106.6 1.2 copy-done.3
  107.8 3.2 %hidden_sums.1 = (f32[3,128,256]{2,1,0:T(8,128)S(1)}, f32[3,128,256]{2,1,0:T(8,128)S(1)}) custom-call(s32[3]{0:T(128)S(1)} %copy-done.6, bf16[128,4096]{1,0:T(8,128)(2,1)S(1)} %bitcast.12, bf16[128,4096]{1,0:T(8,128)(2,1)S(1)} %bitcast.14, bf16[4,2,128,512]{3,2,1,0:T(8,128)(2,1)} %copy-done.8, bf16[4,384,256]{2,1,0:T(8,128)(2,1)S(1)} %pad_maximum_fusion.after.rest_0_, ...), custom_call_target="tpu_custom_call" | custom-call | flops 805306368 | bytes 6291456 | tf_op jit(solution)/shard_map/hidden_sums/pallas_call | solution.py:155
  111.0 0.8 copy-done.5
  111.8 3.7 %collective-permute-start.11 = (f32[3,128,256]{2,1,0:T(8,128)S(1)}, f32[3,128,256]{2,1,0:T(8,128)}, u32[]{:S(2)}, u32[]{:S(2)}) collective-permute-start(f32[3,128,256]{2,1,0:T(8,128)S(1)} %get-tuple-element.15), channel_id=1, source_target_pairs={{0,64},{64,0},{1,65},{65,1},{2,66},{66,2},{3,67},{67,3},{4,68},{68... | collective-permute-start | bytes 1179656 | tf_op jit(solution)/shard_map/ppermute | solution.py:263
  115.4 1.6 %repack_tokens.1 = bf16[4,2,128,512]{3,2,1,0:T(8,128)(2,1)} custom-call(s32[3]{0:T(128)S(1)} %copy-done.6, bf16[4,2,128,1024]{3,2,1,0:T(8,128)(2,1)S(1)} %all-to-all-done.arrived), custom_call_target="tpu_custom_call" | custom-call | bytes 2097152 | tf_op jit(solution)/shard_map/repack_tokens/pallas_call | solution.py:98
  117.1 1.9 %collective-permute-start.6 = (bf16[4,2,128,512]{3,2,1,0:T(8,128)(2,1)}, bf16[4,2,128,512]{3,2,1,0:T(8,128)(2,1)S(1)}, u32[]{:S(2)}, u32[]{:S(2)}) collective-permute-start(bf16[4,2,128,512]{3,2,1,0:T(8,128)(2,1)} %repack_tokens.1), channel_id=1, source_target_pairs={{0,64},{64,0},{1,65},{65,1},{2,66},{66,2},{3,67},{67,3},{4,68},{68... | collective-permute-start | bytes 3145736 | tf_op jit(solution)/shard_map/ppermute | solution.py:263
  119.0 2.1 %multiply_subtract_fusion = (f32[16,4096]{1,0:T(8,128)}, f32[16,4096]{1,0:T(8,128)}) fusion(f32[16,4096]{1,0:T(8,128)} %param.14, f32[16,4096]{1,0:T(8,128)} %add.28, f32[16,4096]{1,0:T(8,128)} %collective-permute-done.14, f32[16,4096]{1,0:T(8,128)} %param.15), kind=kLoop, calls=%fused_computation.1 | loop fusion | flops 524288 | bytes 1572864 | tf_op jit(solution)/shard_map/sub | solution.py:294
  121.1 1.9 %activation.1.rest_0_ = bf16[3,128,256]{2,1,0:T(8,128)(2,1)} custom-call(f32[3,128,256]{2,1,0:T(8,128)} %copy-done.5, f32[3,128,256]{2,1,0:T(8,128)} %collective-permute-done.11.arrived_ref, f32[16,4096]{1,0:T(8,128)} %get-tuple-element.19.after), custom_call_target="tpu_custom_call" | custom-call | flops 655360 | bytes 1048576 | tf_op jit(solution)/shard_map/activation/pallas_call | solution.py:188
  123.0 4.5 %collective-permute-start.15 = (bf16[3,128,256]{2,1,0:T(8,128)(2,1)}, bf16[3,128,256]{2,1,0:T(8,128)(2,1)S(1)}, u32[]{:S(2)}, u32[]{:S(2)}) collective-permute-start(bf16[3,128,256]{2,1,0:T(8,128)(2,1)} %activation.1.rest_0_), channel_id=1, source_target_pairs={{0,128},{128,256},{256,384},{384,0},{1,129},{129,257},{257,385},{3... | collective-permute-start | bytes 589832 | tf_op jit(solution)/shard_map/ppermute | solution.py:251
  127.5 5.2 %collective-permute-start.16 = (bf16[3,128,256]{2,1,0:T(8,128)(2,1)}, bf16[3,128,256]{2,1,0:T(8,128)(2,1)S(1)}, u32[]{:S(2)}, u32[]{:S(2)}) collective-permute-start(bf16[3,128,256]{2,1,0:T(8,128)(2,1)} %activation.1.rest_0_), channel_id=1, source_target_pairs={{0,256},{128,384},{256,0},{384,128},{1,257},{129,385},{257,1},{385... | collective-permute-start | bytes 589832 | tf_op jit(solution)/shard_map/ppermute | solution.py:251
  132.7 5.2 %collective-permute-start.17 = (bf16[3,128,256]{2,1,0:T(8,128)(2,1)}, bf16[3,128,256]{2,1,0:T(8,128)(2,1)S(1)}, u32[]{:S(2)}, u32[]{:S(2)}) collective-permute-start(bf16[3,128,256]{2,1,0:T(8,128)(2,1)} %activation.1.rest_0_), channel_id=1, source_target_pairs={{0,384},{128,0},{256,128},{384,256},{1,385},{129,1},{257,129},{385... | collective-permute-start | bytes 589832 | tf_op jit(solution)/shard_map/ppermute | solution.py:251
  137.9 3.2 %collective-permute-start.18 = (bf16[3,128,256]{2,1,0:T(8,128)(2,1)}, bf16[3,128,256]{2,1,0:T(8,128)(2,1)S(1)}, u32[]{:S(2)}, u32[]{:S(2)}) collective-permute-start(bf16[3,128,256]{2,1,0:T(8,128)(2,1)} %activation.1.rest_0_), channel_id=1, source_target_pairs={{0,64},{64,0},{1,65},{65,1},{2,66},{66,2},{3,67},{67,3},{4,68},{68... | collective-permute-start | bytes 589832 | tf_op jit(solution)/shard_map/ppermute | solution.py:263
  141.2 1.9 %collective-permute-start.19 = (bf16[3,128,256]{2,1,0:T(8,128)(2,1)S(1)}, bf16[3,128,256]{2,1,0:T(8,128)(2,1)S(1)}, u32[]{:S(2)}, u32[]{:S(2)}) collective-permute-start(bf16[3,128,256]{2,1,0:T(8,128)(2,1)S(1)} %collective-permute-done.15.rest_1_), channel_id=1, source_target_pairs={{0,64},{64,0},{1,65},{65,1},{2,66},{66,2},{3,67},{67,3},{4,68},{68... | collective-permute-start | bytes 589832 | tf_op jit(solution)/shard_map/ppermute | solution.py:263
  143.1 0.4 collective-permute-done.16.rest_2_
  143.6 3.0 %collective-permute-start.20 = (bf16[3,128,256]{2,1,0:T(8,128)(2,1)S(1)}, bf16[3,128,256]{2,1,0:T(8,128)(2,1)S(1)}, u32[]{:S(2)}, u32[]{:S(2)}) collective-permute-start(bf16[3,128,256]{2,1,0:T(8,128)(2,1)S(1)} %collective-permute-done.16.rest_2_), channel_id=1, source_target_pairs={{0,64},{64,0},{1,65},{65,1},{2,66},{66,2},{3,67},{67,3},{4,68},{68... | collective-permute-start | bytes 589832 | tf_op jit(solution)/shard_map/ppermute | solution.py:263
  146.5 5.0 %collective-permute-done.17.rest_3_ = bf16[3,128,256]{2,1,0:T(8,128)(2,1)S(1)} collective-permute-done((bf16[3,128,256]{2,1,0:T(8,128)(2,1)}, bf16[3,128,256]{2,1,0:T(8,128)(2,1)S(1)}, u32[]{:S(2)}, u32[]{:S(2)}) %collective-permute-start.17) | collective-permute-done | bytes 196640 | tf_op jit(solution)/shard_map/ppermute | solution.py:251
  151.5 2.4 %collective-permute-start.21 = (bf16[3,128,256]{2,1,0:T(8,128)(2,1)S(1)}, bf16[3,128,256]{2,1,0:T(8,128)(2,1)S(1)}, u32[]{:S(2)}, u32[]{:S(2)}) collective-permute-start(bf16[3,128,256]{2,1,0:T(8,128)(2,1)S(1)} %collective-permute-done.17.rest_3_), channel_id=1, source_target_pairs={{0,64},{64,0},{1,65},{65,1},{2,66},{66,2},{3,67},{67,3},{4,68},{68... | collective-permute-start | bytes 589832 | tf_op jit(solution)/shard_map/ppermute | solution.py:263
  154.0 1.0 collective-permute-done.21.rest_7_
  155.0 0.9 copy-done.4
  155.9 4.7 %weight_grads.1 = (bf16[1,512,256]{2,1,0:T(8,128)(2,1)}, bf16[1,512,256]{2,1,0:T(8,128)(2,1)}, bf16[1,256,512]{2,1,0:T(8,128)(2,1)}) custom-call(s32[3]{0:T(128)S(1)} %copy-done.6, bf16[4,2,128,1024]{3,2,1,0:T(8,128)(2,1)S(1)} %all-to-all-done.arrived, bf16[4,2,128,512]{3,2,1,0:T(8,128)(2,1)S(1)} %collective-permute-done.6.swapped, ...), custom_call_target="tpu_custom_call" | custom-call | flops 805306368 | bytes 5242880 | tf_op jit(solution)/shard_map/weight_grads/pallas_call | solution.py:229
  (30 shorter events, 0.2 us)
Async XLA Ops:
  0.6 8.0 %collective-permute-start.3 = (f32[16,4096]{1,0:T(8,128)}, f32[16,4096]{1,0:T(8,128)S(1)}, u32[]{:S(2)}, u32[]{:S(2)}) collective-permute-start(f32[16,4096]{1,0:T(8,128)} %bitcast.16), channel_id=1, source_target_pairs={{0,32},{32,0},{1,33},{33,1},{2,34},{34,2},{3,35},{35,3},{4,36},{36... | collective-permute-start | bytes 786440 | tf_op jit(solution)/shard_map/ppermute | solution.py:271
  9.6 32.6 %copy-start = (bf16[1,128,4096]{2,1,0:T(8,128)(2,1)S(1)}, bf16[1,128,4096]{2,1,0:T(8,128)(2,1)}, u32[]{:S(2)}) copy-start(bf16[1,128,4096]{2,1,0:T(8,128)(2,1)} %param.8) | copy-start | bytes 3145732
  9.6 32.6 %copy-start.2 = (bf16[1,128,4096]{2,1,0:T(8,128)(2,1)S(1)}, bf16[1,128,4096]{2,1,0:T(8,128)(2,1)}, u32[]{:S(2)}) copy-start(bf16[1,128,4096]{2,1,0:T(8,128)(2,1)} %param.9) | copy-start | bytes 3145732
  9.6 22.0 %collective-permute-start.4 = (f32[16,4096]{1,0:T(8,128)S(1)}, f32[16,4096]{1,0:T(8,128)S(1)}, u32[]{:S(2)}, u32[]{:S(2)}) collective-permute-start(f32[16,4096]{1,0:T(8,128)S(1)} %bitcast_add_fusion), channel_id=1, source_target_pairs={{0,8},{8,0},{16,24},{24,16},{1,9},{9,1},{17,25},{25,17},{2,10},{10... | collective-permute-start | bytes 786440 | tf_op jit(solution)/shard_map/ppermute | solution.py:271
  15.6 26.7 %copy-start.6 = (s32[3]{0:T(128)S(1)}, s32[3]{0:T(128)}, u32[]{:S(2)}) copy-start(s32[3]{0:T(128)} %pad_add_fusion.place) | copy-start | bytes 40
  18.0 18.1 %collective-permute-start = (bf16[384,256]{1,0:T(8,128)(2,1)}, bf16[384,256]{1,0:T(8,128)(2,1)S(1)}, u32[]{:S(2)}, u32[]{:S(2)}) collective-permute-start(bf16[384,256]{1,0:T(8,128)(2,1)} %weight_share.1), channel_id=1, source_target_pairs={{0,384},{128,0},{256,128},{384,256},{1,385},{129,1},{257,129},{385... | collective-permute-start | bytes 589832 | tf_op jit(solution)/shard_map/ppermute | solution.py:255
  23.9 13.1 %collective-permute-start.1 = (bf16[384,256]{1,0:T(8,128)(2,1)}, bf16[384,256]{1,0:T(8,128)(2,1)S(1)}, u32[]{:S(2)}, u32[]{:S(2)}) collective-permute-start(bf16[384,256]{1,0:T(8,128)(2,1)} %weight_share.1), channel_id=1, source_target_pairs={{0,256},{128,384},{256,0},{384,128},{1,257},{129,385},{257,1},{385... | collective-permute-start | bytes 589832 | tf_op jit(solution)/shard_map/ppermute | solution.py:255
  27.4 13.8 %collective-permute-start.2 = (bf16[384,256]{1,0:T(8,128)(2,1)}, bf16[384,256]{1,0:T(8,128)(2,1)S(1)}, u32[]{:S(2)}, u32[]{:S(2)}) collective-permute-start(bf16[384,256]{1,0:T(8,128)(2,1)} %weight_share.1), channel_id=1, source_target_pairs={{0,128},{128,256},{256,384},{384,0},{1,129},{129,257},{257,385},{3... | collective-permute-start | bytes 589832 | tf_op jit(solution)/shard_map/ppermute | solution.py:255
  31.7 10.5 %collective-permute-start.5 = (f32[16,4096]{1,0:T(8,128)S(1)}, f32[16,4096]{1,0:T(8,128)S(1)}, u32[]{:S(2)}, u32[]{:S(2)}) collective-permute-start(f32[16,4096]{1,0:T(8,128)S(1)} %add.25), channel_id=1, source_target_pairs={{0,16},{8,24},{16,0},{24,8},{1,17},{9,25},{17,1},{25,9},{2,18},{10... | collective-permute-start | bytes 786440 | tf_op jit(solution)/shard_map/ppermute | solution.py:271
  44.7 1.0 copy-start.7
  45.7 69.8 %all-to-all-start = ((bf16[4,2,128,1024]{3,2,1,0:T(8,128)(2,1)}), bf16[4,2,128,1024]{3,2,1,0:T(8,128)(2,1)S(1)}, u32[]{:S(2)}, u32[]{:S(2)}) async-start(bf16[4,2,128,1024]{3,2,1,0:T(8,128)(2,1)} %get-tuple-element.12), calls=%async_computation | async-start | bytes 4194304 | tf_op jit(solution)/shard_map/all_to_all | solution.py:288
  51.0 55.6 %copy-start.1 = (bf16[1,128,4096]{2,1,0:T(8,128)(2,1)S(1)}, bf16[1,128,4096]{2,1,0:T(8,128)(2,1)}, u32[]{:S(2)}) copy-start(bf16[1,128,4096]{2,1,0:T(8,128)(2,1)} %param.8) | copy-start | bytes 3145732
  51.0 54.6 %collective-permute-start.7 = (bf16[4,2,128,512]{3,2,1,0:T(8,128)(2,1)}, bf16[4,2,128,512]{3,2,1,0:T(8,128)(2,1)S(1)}, u32[]{:S(2)}, u32[]{:S(2)}) collective-permute-start(bf16[4,2,128,512]{3,2,1,0:T(8,128)(2,1)} %copy-done.7), channel_id=1, source_target_pairs={{0,64},{64,0},{1,65},{65,1},{2,66},{66,2},{3,67},{67,3},{4,68},{68... | collective-permute-start | bytes 3145736 | tf_op jit(solution)/shard_map/ppermute | solution.py:263
  59.7 45.8 %collective-permute-start.10 = (bf16[4,384,256]{2,1,0:T(8,128)(2,1)S(1)}, bf16[4,384,256]{2,1,0:T(8,128)(2,1)S(1)}, u32[]{:S(2)}, u32[]{:S(2)}) collective-permute-start(bf16[4,384,256]{2,1,0:T(8,128)(2,1)S(1)} %pad_maximum_fusion.after.rest_0_), channel_id=1, source_target_pairs={{0,8},{8,16},{16,24},{24,0},{1,9},{9,17},{17,25},{25,1},{2,10},{10... | collective-permute-start | bytes 2359304 | tf_op jit(solution)/shard_map/ppermute | solution.py:259
  61.9 43.6 %collective-permute-start.8 = (bf16[4,384,256]{2,1,0:T(8,128)(2,1)S(1)}, bf16[4,384,256]{2,1,0:T(8,128)(2,1)S(1)}, u32[]{:S(2)}, u32[]{:S(2)}) collective-permute-start(bf16[4,384,256]{2,1,0:T(8,128)(2,1)S(1)} %pad_maximum_fusion.after.rest_0_), channel_id=1, source_target_pairs={{0,24},{8,0},{16,8},{24,16},{1,25},{9,1},{17,9},{25,17},{2,26},{10... | collective-permute-start | bytes 2359304 | tf_op jit(solution)/shard_map/ppermute | solution.py:259
  66.3 39.3 %collective-permute-start.9 = (bf16[4,384,256]{2,1,0:T(8,128)(2,1)S(1)}, bf16[4,384,256]{2,1,0:T(8,128)(2,1)S(1)}, u32[]{:S(2)}, u32[]{:S(2)}) collective-permute-start(bf16[4,384,256]{2,1,0:T(8,128)(2,1)S(1)} %pad_maximum_fusion.after.rest_0_), channel_id=1, source_target_pairs={{0,16},{8,24},{16,0},{24,8},{1,17},{9,25},{17,1},{25,9},{2,18},{10... | collective-permute-start | bytes 2359304 | tf_op jit(solution)/shard_map/ppermute | solution.py:259
  69.6 9.8 %collective-permute-start.12 = (f32[16,4096]{1,0:T(8,128)S(1)}, f32[16,4096]{1,0:T(8,128)S(1)}, u32[]{:S(2)}, u32[]{:S(2)}) collective-permute-start(f32[16,4096]{1,0:T(8,128)S(1)} %add.26.also_after), channel_id=1, source_target_pairs={{0,1},{1,0},{2,3},{3,2},{4,5},{5,4},{6,7},{7,6},{8,9},{9,8},{10,11... | collective-permute-start | bytes 786440 | tf_op jit(solution)/shard_map/ppermute | solution.py:271
  79.5 17.3 %collective-permute-start.13 = (f32[16,4096]{1,0:T(8,128)S(1)}, f32[16,4096]{1,0:T(8,128)S(1)}, u32[]{:S(2)}, u32[]{:S(2)}) collective-permute-start(f32[16,4096]{1,0:T(8,128)S(1)} %add.27), channel_id=1, source_target_pairs={{0,2},{1,3},{2,0},{3,1},{4,6},{5,7},{6,4},{7,5},{8,10},{9,11},{10,... | collective-permute-start | bytes 786440 | tf_op jit(solution)/shard_map/ppermute | solution.py:271
  97.5 21.6 %collective-permute-start.14 = (f32[16,4096]{1,0:T(8,128)}, f32[16,4096]{1,0:T(8,128)}, u32[]{:S(2)}, u32[]{:S(2)}) collective-permute-start(f32[16,4096]{1,0:T(8,128)} %add.28), channel_id=1, source_target_pairs={{0,4},{1,5},{2,6},{3,7},{4,0},{5,1},{6,2},{7,3},{8,12},{9,13},{10,... | collective-permute-start | bytes 786440 | tf_op jit(solution)/shard_map/ppermute | solution.py:271
  105.6 1.0 copy-start.8
  106.6 1.2 copy-start.3
  111.0 0.8 copy-start.5
  111.8 9.3 %collective-permute-start.11 = (f32[3,128,256]{2,1,0:T(8,128)S(1)}, f32[3,128,256]{2,1,0:T(8,128)}, u32[]{:S(2)}, u32[]{:S(2)}) collective-permute-start(f32[3,128,256]{2,1,0:T(8,128)S(1)} %get-tuple-element.15), channel_id=1, source_target_pairs={{0,64},{64,0},{1,65},{65,1},{2,66},{66,2},{3,67},{67,3},{4,68},{68... | collective-permute-start | bytes 1179656 | tf_op jit(solution)/shard_map/ppermute | solution.py:263
  117.1 37.9 %collective-permute-start.6 = (bf16[4,2,128,512]{3,2,1,0:T(8,128)(2,1)}, bf16[4,2,128,512]{3,2,1,0:T(8,128)(2,1)S(1)}, u32[]{:S(2)}, u32[]{:S(2)}) collective-permute-start(bf16[4,2,128,512]{3,2,1,0:T(8,128)(2,1)} %repack_tokens.1), channel_id=1, source_target_pairs={{0,64},{64,0},{1,65},{65,1},{2,66},{66,2},{3,67},{67,3},{4,68},{68... | collective-permute-start | bytes 3145736 | tf_op jit(solution)/shard_map/ppermute | solution.py:263
  123.0 18.2 %collective-permute-start.15 = (bf16[3,128,256]{2,1,0:T(8,128)(2,1)}, bf16[3,128,256]{2,1,0:T(8,128)(2,1)S(1)}, u32[]{:S(2)}, u32[]{:S(2)}) collective-permute-start(bf16[3,128,256]{2,1,0:T(8,128)(2,1)} %activation.1.rest_0_), channel_id=1, source_target_pairs={{0,128},{128,256},{256,384},{384,0},{1,129},{129,257},{257,385},{3... | collective-permute-start | bytes 589832 | tf_op jit(solution)/shard_map/ppermute | solution.py:251
  127.5 16.0 %collective-permute-start.16 = (bf16[3,128,256]{2,1,0:T(8,128)(2,1)}, bf16[3,128,256]{2,1,0:T(8,128)(2,1)S(1)}, u32[]{:S(2)}, u32[]{:S(2)}) collective-permute-start(bf16[3,128,256]{2,1,0:T(8,128)(2,1)} %activation.1.rest_0_), channel_id=1, source_target_pairs={{0,256},{128,384},{256,0},{384,128},{1,257},{129,385},{257,1},{385... | collective-permute-start | bytes 589832 | tf_op jit(solution)/shard_map/ppermute | solution.py:251
  132.7 18.8 %collective-permute-start.17 = (bf16[3,128,256]{2,1,0:T(8,128)(2,1)}, bf16[3,128,256]{2,1,0:T(8,128)(2,1)S(1)}, u32[]{:S(2)}, u32[]{:S(2)}) collective-permute-start(bf16[3,128,256]{2,1,0:T(8,128)(2,1)} %activation.1.rest_0_), channel_id=1, source_target_pairs={{0,384},{128,0},{256,128},{384,256},{1,385},{129,1},{257,129},{385... | collective-permute-start | bytes 589832 | tf_op jit(solution)/shard_map/ppermute | solution.py:251
  137.9 16.0 %collective-permute-start.18 = (bf16[3,128,256]{2,1,0:T(8,128)(2,1)}, bf16[3,128,256]{2,1,0:T(8,128)(2,1)S(1)}, u32[]{:S(2)}, u32[]{:S(2)}) collective-permute-start(bf16[3,128,256]{2,1,0:T(8,128)(2,1)} %activation.1.rest_0_), channel_id=1, source_target_pairs={{0,64},{64,0},{1,65},{65,1},{2,66},{66,2},{3,67},{67,3},{4,68},{68... | collective-permute-start | bytes 589832 | tf_op jit(solution)/shard_map/ppermute | solution.py:263
  141.2 12.7 %collective-permute-start.19 = (bf16[3,128,256]{2,1,0:T(8,128)(2,1)S(1)}, bf16[3,128,256]{2,1,0:T(8,128)(2,1)S(1)}, u32[]{:S(2)}, u32[]{:S(2)}) collective-permute-start(bf16[3,128,256]{2,1,0:T(8,128)(2,1)S(1)} %collective-permute-done.15.rest_1_), channel_id=1, source_target_pairs={{0,64},{64,0},{1,65},{65,1},{2,66},{66,2},{3,67},{67,3},{4,68},{68... | collective-permute-start | bytes 589832 | tf_op jit(solution)/shard_map/ppermute | solution.py:263
  143.6 10.4 %collective-permute-start.20 = (bf16[3,128,256]{2,1,0:T(8,128)(2,1)S(1)}, bf16[3,128,256]{2,1,0:T(8,128)(2,1)S(1)}, u32[]{:S(2)}, u32[]{:S(2)}) collective-permute-start(bf16[3,128,256]{2,1,0:T(8,128)(2,1)S(1)} %collective-permute-done.16.rest_2_), channel_id=1, source_target_pairs={{0,64},{64,0},{1,65},{65,1},{2,66},{66,2},{3,67},{67,3},{4,68},{68... | collective-permute-start | bytes 589832 | tf_op jit(solution)/shard_map/ppermute | solution.py:263
  151.5 3.5 %collective-permute-start.21 = (bf16[3,128,256]{2,1,0:T(8,128)(2,1)S(1)}, bf16[3,128,256]{2,1,0:T(8,128)(2,1)S(1)}, u32[]{:S(2)}, u32[]{:S(2)}) collective-permute-start(bf16[3,128,256]{2,1,0:T(8,128)(2,1)S(1)} %collective-permute-done.17.rest_3_), channel_id=1, source_target_pairs={{0,64},{64,0},{1,65},{65,1},{2,66},{66,2},{3,67},{67,3},{4,68},{68... | collective-permute-start | bytes 589832 | tf_op jit(solution)/shard_map/ppermute | solution.py:263
  155.0 0.9 copy-start.4

commit v5 on v4

--- a/solution.py
+++ b/solution.py
@@ -13,6 +13,7 @@
 WIDE = 1024
 HALF = 512
 HID = 256
+DEAR = 100
 VMEM_LIMIT = 48 * 1024 * 1024
 
 F32 = jnp.float32
@@ -32,6 +33,10 @@
 
 def columns(base):
     return pl.ds(pl.multiple_of(base, HALF), HALF)
+
+
+def wide_columns(chip):
+    return pl.ds(pl.multiple_of(chip * WIDE, WIDE), WIDE)
 
 
 def share_kernel(parts, place, gate, up, down, out, sems):
@@ -60,51 +65,110 @@
     )(place, gate, up, down)
 
 
-def pack_kernel(place, x, dy, after, also_after, out, beside, sems):
-    del after, also_after
-    other = (1 - place[0]) * HALF
+def beside_kernel(place, x, dy, after, out, sems):
+    del after
     copies = []
-    for chip in range(CHIPS):
-        for i, ref in enumerate((x, dy)):
-            copies += [
-                (ref.at[:, pl.ds(chip * WIDE, WIDE)], out.at[chip, i]),
-                (ref.at[:, columns(chip * WIDE + other)], beside.at[chip, i]),
-            ]
-    run_copies(copies, sems)
-
-
-def pack(place, x, dy, after, also_after):
-    return pl.pallas_call(
-        pack_kernel,
-        out_shape=(
-            jax.ShapeDtypeStruct((CHIPS, 2, ROWS, WIDE), BF16),
-            jax.ShapeDtypeStruct((CHIPS, 2, ROWS, HALF), BF16),
-        ),
-        in_specs=[SMEM] + [ANY] * 4,
-        out_specs=(VMEM,) * 2,
-        scratch_shapes=[pltpu.SemaphoreType.DMA((16,))],
-        compiler_params=pltpu.CompilerParams(vmem_limit_bytes=VMEM_LIMIT),
-        cost_estimate=pl.CostEstimate(flops=0, bytes_accessed=6 << 20, transcendentals=0),
-        name="pack_tokens",
-    )(place, x, dy, after, also_after)
-
-
-def repack_kernel(place, arrived, out, sems):
-    other = columns((1 - place[0]) * HALF)
-    run_copies([(arrived.at[i, :, :, other], out.at[i]) for i in range(CHIPS)], sems)
-
-
-def repack(place, arrived):
-    return pl.pallas_call(
-        repack_kernel,
+    for i in range(CHIPS):
+        other = columns(i * WIDE + (1 - place[0]) * HALF)
+        copies += [(x.at[:, other], out.at[i, 0]), (dy.at[:, other], out.at[i, 1])]
+    run_copies(copies, sems)
+
+
+def for_beside(place, x, dy, after):
+    return pl.pallas_call(
+        beside_kernel,
         out_shape=jax.ShapeDtypeStruct((CHIPS, 2, ROWS, HALF), BF16),
-        in_specs=[SMEM, ANY],
+        in_specs=[SMEM] + [ANY] * 3,
         out_specs=VMEM,
-        scratch_shapes=[pltpu.SemaphoreType.DMA((CHIPS,))],
+        scratch_shapes=[pltpu.SemaphoreType.DMA((8,))],
         compiler_params=pltpu.CompilerParams(vmem_limit_bytes=VMEM_LIMIT),
         cost_estimate=pl.CostEstimate(flops=0, bytes_accessed=2 << 20, transcendentals=0),
+        name="tokens_beside",
+    )(place, x, dy, after)
+
+
+def pack_kernel(waited, place, x, dy, *rest):
+    ahead, back, sems = rest[waited:]
+    chip = place[2]
+    near, far, last = (wide_columns(lax.rem(chip + shift, CHIPS)) for shift in (1, 2, 3))
+    copies = [
+        (x.at[:, near], ahead.at[0]),
+        (dy.at[:, near], ahead.at[1]),
+        (x.at[:, far], ahead.at[2]),
+        (x.at[:, last], back.at[0]),
+        (dy.at[:, last], back.at[1]),
+        (dy.at[:, far], back.at[2]),
+    ]
+    run_copies(copies, sems)
+
+
+def pack(place, x, dy, after):
+    wide = jax.ShapeDtypeStruct((3, ROWS, WIDE), BF16)
+    return pl.pallas_call(
+        functools.partial(pack_kernel, len(after)),
+        out_shape=(wide, wide),
+        in_specs=[SMEM] + [ANY] * (2 + len(after)),
+        out_specs=(VMEM, VMEM),
+        scratch_shapes=[pltpu.SemaphoreType.DMA((6,))],
+        compiler_params=pltpu.CompilerParams(vmem_limit_bytes=VMEM_LIMIT),
+        cost_estimate=pl.CostEstimate(flops=0, bytes_accessed=4 << 20, transcendentals=0),
+        name="pack_tokens",
+    )(place, x, dy, *after)
+
+
+def onward_kernel(ahead, back, far_x, far_dy, sems):
+    run_copies([(ahead.at[2], far_x.at[0]), (back.at[2], far_dy.at[0])], sems)
+
+
+def onward(ahead, back):
+    one = jax.ShapeDtypeStruct((1, ROWS, WIDE), BF16)
+    return pl.pallas_call(
+        onward_kernel,
+        out_shape=(one, one),
+        in_specs=[ANY, ANY],
+        out_specs=(VMEM, VMEM),
+        scratch_shapes=[pltpu.SemaphoreType.DMA((2,))],
+        cost_estimate=pl.CostEstimate(flops=0, bytes_accessed=DEAR << 20, transcendentals=0),
+        name="onward",
+    )(ahead, back)
+
+
+def repack_kernel(place, ahead, back, far_x, far_dy, out, sems):
+    other = columns((1 - place[0]) * HALF)
+    copies = []
+    for i, (a, b) in enumerate(((ahead.at[0], ahead.at[1]), (far_x.at[0], far_dy.at[0]), (back.at[0], back.at[1]))):
+        copies += [(a.at[:, other], out.at[i, 0]), (b.at[:, other], out.at[i, 1])]
+    run_copies(copies, sems)
+
+
+def repack(place, arrived):
+    return pl.pallas_call(
+        repack_kernel,
+        out_shape=jax.ShapeDtypeStruct((CHIPS - 1, 2, ROWS, HALF), BF16),
+        in_specs=[SMEM] + [ANY] * 4,
+        out_specs=VMEM,
+        scratch_shapes=[pltpu.SemaphoreType.DMA((6,))],
+        compiler_params=pltpu.CompilerParams(vmem_limit_bytes=VMEM_LIMIT),
+        cost_estimate=pl.CostEstimate(flops=0, bytes_accessed=DEAR * 2 << 20, transcendentals=0),
         name="repack_tokens",
-    )(place, arrived)
+    )(place, *arrived)
+
+
+def staged_kernel(delta, after, out, sem):
+    del after
+    run_copies([(delta, out)], sem)
+
+
+def staged(delta, after):
+    return pl.pallas_call(
+        staged_kernel,
+        out_shape=jax.ShapeDtypeStruct(delta.shape, delta.dtype),
+        in_specs=[ANY, ANY],
+        out_specs=VMEM,
+        scratch_shapes=[pltpu.SemaphoreType.DMA((1,))],
+        cost_estimate=pl.CostEstimate(flops=0, bytes_accessed=1 << 19, transcendentals=0),
+        name="delta_staged",
+    )(delta, after)
 
 
 def hidden_kernel(parts, waited, place, x, dy, beside, *rest):
@@ -181,13 +245,14 @@
     active = gate * sig
     slope = sig * (1.0 + gate * (1.0 - sig))
     for i, value in enumerate((dh * up * slope, dh * active, active * up)):
-        out[i] = value.astype(BF16)
+        for chip in range(CHIPS):
+            out[chip, i] = value.astype(BF16)
 
 
 def activation(mine, arrived, after):
     return pl.pallas_call(
         activation_kernel,
-        out_shape=jax.ShapeDtypeStruct((3, ROWS, HID), BF16),
+        out_shape=jax.ShapeDtypeStruct((CHIPS, 3, ROWS, HID), BF16),
         in_specs=[ANY] * 3,
         out_specs=VMEM,
         scratch_shapes=[
@@ -200,23 +265,22 @@
     )(mine, arrived, after)
 
 
-def grads_kernel(place, arrived, swapped, *rest):
-    acts, (gg, gu, gd, xs, dys, hs, sems) = rest[: 2 * CHIPS], rest[2 * CHIPS :]
-    half = columns(place[0] * HALF)
+def grads_kernel(place, x, dy, beside, ahead, back, far_x, far_dy, swapped, *rest):
+    acts, (gg, gu, gd, xs, dys, hs, sems) = rest[:2], rest[2:]
+    core, chip = place[0], place[2]
+    half, own = columns(core * HALF), columns(chip * WIDE + core * HALF)
+    here = [(x.at[:, own], dy.at[:, own])]
+    here += [
+        (a.at[:, half], b.at[:, half])
+        for a, b in ((ahead.at[0], ahead.at[1]), (far_x.at[0], far_dy.at[0]), (back.at[0], back.at[1]))
+    ]
+    there = [(beside.at[chip, 0], beside.at[chip, 1])]
+    there += [(swapped.at[i, 0], swapped.at[i, 1]) for i in range(CHIPS - 1)]
     copies = []
-    for i in range(CHIPS):
-        near, far = pl.ds(i * ROWS, ROWS), pl.ds((CHIPS + i) * ROWS, ROWS)
-        copies += [
-            (arrived.at[i, 0, :, half], xs.at[near]),
-            (arrived.at[i, 1, :, half], dys.at[near]),
-            (swapped.at[i, 0], xs.at[far]),
-            (swapped.at[i, 1], dys.at[far]),
-        ]
-    for shift in range(CHIPS):
-        chip = lax.rem(place[2] + CHIPS - shift, CHIPS)
-        near = pl.ds(pl.multiple_of(chip * ROWS, ROWS), ROWS)
-        far = pl.ds(pl.multiple_of((CHIPS + chip) * ROWS, ROWS), ROWS)
-        copies += [(acts[shift], hs.at[:, near]), (acts[CHIPS + shift], hs.at[:, far])]
+    for i, (a, b) in enumerate(here + there):
+        rows = pl.ds(i * ROWS, ROWS)
+        source = lax.rem(chip + 2 * CHIPS - i, CHIPS)
+        copies += [(a, xs.at[rows]), (b, dys.at[rows]), (acts[i // CHIPS].at[source], hs.at[:, rows])]
     run_copies(copies, sems)
     tall = (((0,), (0,)), ((), ()))
     gg[0] = lax.dot_general(xs[...], hs[0], tall, preferred_element_type=F32).astype(BF16)
@@ -224,7 +288,7 @@
     gd[0] = lax.dot_general(hs[2], dys[...], tall, preferred_element_type=F32).astype(BF16)
 
 
-def grads(place, arrived, swapped, acts):
+def grads(place, x, dy, beside, arrived, swapped, acts):
     tokens = 2 * CHIPS * ROWS
     return pl.pallas_call(
         grads_kernel,
@@ -233,7 +297,7 @@
             jax.ShapeDtypeStruct((1, HALF, HID), BF16),
             jax.ShapeDtypeStruct((1, HID, HALF), BF16),
         ),
-        in_specs=[SMEM] + [ANY] * (2 + len(acts)),
+        in_specs=[SMEM] + [ANY] * (8 + len(acts)),
         out_specs=(VMEM,) * 3,
         scratch_shapes=[
             pltpu.VMEM((tokens, HALF), BF16),
@@ -244,7 +308,7 @@
         compiler_params=pltpu.CompilerParams(vmem_limit_bytes=VMEM_LIMIT),
         cost_estimate=pl.CostEstimate(flops=6 * 1024 * 512 * 256, bytes_accessed=5 << 20, transcendentals=0),
         name="weight_grads",
-    )(place, arrived, swapped, *acts)
+    )(place, x, dy, beside, *arrived, swapped, *acts)
 
 
 def to_shift(value, shift):
@@ -263,14 +327,20 @@
     return lax.ppermute(value, "core", [(0, 1), (1, 0)])
 
 
-def sum_over(total, names):
-    for name in names:
-        size = lax.axis_size(name)
-        step = 1
-        while step < size:
-            total += lax.ppermute(total, name, [(i, i ^ step) for i in range(size)])
-            step *= 2
-    return total
+def share_of_sum(delta):
+    everyone = ("yl", "x", "z")
+    count = lax.axis_size(everyone)
+    rows, cols = delta.shape
+    tiles = delta.reshape(rows // 8, 8, cols // 128, 128).transpose(0, 2, 1, 3).reshape(count, 8, 128)
+    return jnp.sum(lax.all_to_all(tiles, everyone, 0, 0, tiled=True), axis=0, keepdims=True)
+
+
+def whole_mean(part, shape):
+    everyone = ("yl", "x", "z")
+    count = lax.axis_size(everyone)
+    rows, cols = shape
+    whole = lax.all_to_all(jnp.broadcast_to(part / count, (count, 8, 128)), everyone, 0, 0, tiled=True)
+    return whole.reshape(rows // 8, cols // 128, 8, 128).transpose(0, 2, 1, 3).reshape(rows, cols)
 
 
 def on_device(tokens, cotangent, w_gate, w_up, w_down, delta, anchor, momentum):
@@ -283,21 +353,24 @@
     shares = jnp.stack([share] + [shares[shift] for shift in (1, 2, 3)])
     weights = [shares] + [from_x(shares, shift, parts) for shift in range(1, parts)]
 
-    partial = sum_over(delta[0], ("yl", "x"))
-    packed, beside = pack(place, x, dy, shares, partial)
-    arrived = lax.all_to_all(packed, "yh", 0, 0, tiled=True)
-    beside = other_core(beside)
-    swapped = other_core(repack(place, arrived))
-
-    pseudo = sum_over(partial, ("z",)) / lax.axis_size(("yl", "x", "z"))
+    beside = other_core(for_beside(place, x, dy, share))
+    part = share_of_sum(staged(delta[0], beside))
+    ahead, back = pack(place, x, dy, (shares, beside))
+    ahead, back = to_shift(ahead, 1), to_shift(back, 3)
+    far_x, far_dy = onward(ahead, back)
+    arrived = [ahead, back, to_shift(far_x, 1), to_shift(far_dy, 3)]
+    repacked = repack(place, arrived)
+    swapped = other_core(repacked)
+
+    pseudo = whole_mean(part, anchor.shape)
     new_momentum = 0.9 * momentum + pseudo
     new_anchor = anchor - 0.7 * (pseudo + 0.9 * new_momentum)
 
-    mine, theirs = hidden_sums(place, x, dy, beside, weights, ())
+    mine, theirs = hidden_sums(place, x, dy, beside, weights, (repacked,))
     acts = activation(mine, other_core(theirs), new_anchor)
-    acts = [acts] + [to_shift(acts, shift) for shift in (1, 2, 3)]
-    acts += [other_core(value) for value in acts]
-    grad_gate, grad_up, grad_down = grads(place, arrived, swapped, acts)
+    acts = lax.all_to_all(acts, "yh", 0, 0, tiled=True)
+    acts = (acts, other_core(acts))
+    grad_gate, grad_up, grad_down = grads(place, x, dy, beside, arrived, swapped, acts)
     return grad_gate, grad_up, grad_down, new_anchor, new_momentum
 
 

time: 162 us -> 159 us (0.981)
  the two profiles are of different devices: /device:TPU:1 before, /device:TPU:397 now
where the time goes in v5:
time: 159 us; the launch traced here: 157 us
  starting transfers between devices  73.2 us (46%)
  waiting for transfers between devices  44.8 us (28%)
  Pallas kernels  19.7 us (12%)
  local copies, waits for them, and re-layouts  14.2 us (9%)
  other arithmetic  4.46 us (3%)
    ppermute x4, waiting for transfers between devices, to_shift(): lax.ppermute(value, 'yh', [(i, (i + shift) % CHIPS) for i in range(CHIPS)])  20.6 us
    all_to_all x1, waiting for transfers between devices, on_device(): acts = lax.all_to_all(acts, 'yh', 0, 0, tiled=True)  19.4 us
    ppermute x4, starting transfers between devices, to_shift(): lax.ppermute(value, 'yh', [(i, (i + shift) % CHIPS) for i in range(CHIPS)])  15.1 us
    unnamed x50, local copies, waits for them, and re-layouts  13.5 us
    ppermute x3, starting transfers between devices, from_shift(): lax.ppermute(value, 'yh', [(i, (i - shift) % CHIPS) for i in range(CHIPS)])  12.7 us
    ppermute x4, starting transfers between devices, other_core(): return lax.ppermute(value, 'core', [(0, 1), (1, 0)])  12.5 us
    all_to_all x1, starting transfers between devices, whole_mean(): lax.all_to_all(jnp.broadcast_to(part / count, (count, 8, 128)), everyone,...  10 us
    all_to_all x1, starting transfers between devices, share_of_sum(): lax.all_to_all(tiles, everyone, 0, 0, tiled=True)  9.3 us
  transfers between devices with their start and end apart: 17, of which 8 were waited for; matrix products, arithmetic and copies ran while one was open for 3% of the time, Pallas kernels for 6%

profile of v5, /device:TPU:397, one launch (start us, length us, event | category | flops | bytes accessed | tf_op | source)
XLA Modules:
  0.0 157.4 jit_solution(1555035931357605780)
XLA Ops:
  1.2 2.2 %weight_share.1.after = bf16[384,256]{1,0:T(8,128)(2,1)} custom-call(s32[3]{0:T(128)} %pad_add_fusion.place, bf16[512,256]{1,0:T(8,128)(2,1)} %gate.1, bf16[512,256]{1,0:T(8,128)(2,1)} %up.1, bf16[256,512]{1,0:T(8,128)(2,1)} %down.1), custom_call_target="tpu_custom_call" | custom-call | bytes 262144 | tf_op jit(solution)/shard_map/weight_share/pallas_call | solution.py:57
  4.1 1.2 copy-done
  5.4 1.2 copy-done.2
  6.6 0.9 copy-done.13
  7.5 0.8 tokens_beside.1
  8.3 2.6 %collective-permute-start = (bf16[4,2,128,512]{3,2,1,0:T(8,128)(2,1)S(1)}, bf16[4,2,128,512]{3,2,1,0:T(8,128)(2,1)S(1)}, u32[]{:S(2)}, u32[]{:S(2)}) collective-permute-start(bf16[4,2,128,512]{3,2,1,0:T(8,128)(2,1)S(1)} %tokens_beside.1), channel_id=1, source_target_pairs={{0,64},{64,0},{1,65},{65,1},{2,66},{66,2},{3,67},{67,3},{4,68},{68... | collective-permute-start | bytes 3145736 | tf_op jit(solution)/shard_map/ppermute | solution.py:327
  10.9 5.0 %collective-permute-start.1 = (bf16[384,256]{1,0:T(8,128)(2,1)S(1)}, bf16[384,256]{1,0:T(8,128)(2,1)S(1)}, u32[]{:S(2)}, u32[]{:S(2)}) collective-permute-start(bf16[384,256]{1,0:T(8,128)(2,1)S(1)} %copy-done.13), channel_id=1, source_target_pairs={{0,384},{128,0},{256,128},{384,256},{1,385},{129,1},{257,129},{385... | collective-permute-start | bytes 589832 | tf_op jit(solution)/shard_map/ppermute | solution.py:319
  15.9 4.4 %collective-permute-start.2 = (bf16[384,256]{1,0:T(8,128)(2,1)S(1)}, bf16[384,256]{1,0:T(8,128)(2,1)S(1)}, u32[]{:S(2)}, u32[]{:S(2)}) collective-permute-start(bf16[384,256]{1,0:T(8,128)(2,1)S(1)} %copy-done.13), channel_id=1, source_target_pairs={{0,256},{128,384},{256,0},{384,128},{1,257},{129,385},{257,1},{385... | collective-permute-start | bytes 589832 | tf_op jit(solution)/shard_map/ppermute | solution.py:319
  20.3 3.3 %collective-permute-start.3 = (bf16[384,256]{1,0:T(8,128)(2,1)S(1)}, bf16[384,256]{1,0:T(8,128)(2,1)S(1)}, u32[]{:S(2)}, u32[]{:S(2)}) collective-permute-start(bf16[384,256]{1,0:T(8,128)(2,1)S(1)} %copy-done.13), channel_id=1, source_target_pairs={{0,128},{128,256},{256,384},{384,0},{1,129},{129,257},{257,385},{3... | collective-permute-start | bytes 589832 | tf_op jit(solution)/shard_map/ppermute | solution.py:319
  23.7 1.0 copy-done.4
  24.7 1.7 %delta_staged.1 = f32[16,4096]{1,0:T(8,128)} custom-call(f32[16,4096]{1,0:T(8,128)} %bitcast.30, bf16[4,2,128,512]{3,2,1,0:T(8,128)(2,1)} %copy-done.4), custom_call_target="tpu_custom_call" | custom-call | bytes 524288 | tf_op jit(solution)/shard_map/delta_staged/pallas_call | solution.py:163
  26.4 9.3 %all-to-all-start = ((f32[64,8,128]{2,1,0:T(8,128)}), f32[64,8,128]{2,1,0:T(8,128)}, u32[]{:S(2)}, u32[]{:S(2)}) async-start(f32[64,8,128]{2,1,0:T(8,128)} %bitcast.29), calls=%async_computation | async-start | bytes 524288 | tf_op jit(solution)/shard_map/all_to_all | solution.py:335
  36.1 2.5 %collective-permute-done.3 = bf16[384,256]{1,0:T(8,128)(2,1)S(1)} collective-permute-done((bf16[384,256]{1,0:T(8,128)(2,1)S(1)}, bf16[384,256]{1,0:T(8,128)(2,1)S(1)}, u32[]{:S(2)}, u32[]{:S(2)}) %collective-permute-start.3) | collective-permute-done | bytes 196640 | tf_op jit(solution)/shard_map/ppermute | solution.py:319
  39.3 1.0 pad_maximum_fusion.rest_0_
  40.3 1.2 copy-done.5
  41.6 1.9 %pack_tokens.1 = (bf16[3,128,1024]{2,1,0:T(8,128)(2,1)}, bf16[3,128,1024]{2,1,0:T(8,128)(2,1)}) custom-call(s32[3]{0:T(128)S(1)} %copy-done.20, bf16[128,4096]{1,0:T(8,128)(2,1)S(1)} %bitcast.21, bf16[128,4096]{1,0:T(8,128)(2,1)S(1)} %bitcast.27, bf16[4,384,256]{2,1,0:T(8,128)(2,1)S(1)} %pad_maximum_fusion.rest_0_, bf16[4,2,128,512]{3,2,1,0:T(8,128)(2,1)S(1)} %copy-done.5), custom_call_target="tpu_custom_call" | custom-call | bytes 4194304 | tf_op jit(solution)/shard_map/pack_tokens/pallas_call | solution.py:107
  43.4 4.0 %collective-permute-start.4 = (bf16[3,128,1024]{2,1,0:T(8,128)(2,1)}, bf16[3,128,1024]{2,1,0:T(8,128)(2,1)S(1)}, u32[]{:S(2)}, u32[]{:S(2)}) collective-permute-start(bf16[3,128,1024]{2,1,0:T(8,128)(2,1)} %get-tuple-element.14), channel_id=1, source_target_pairs={{0,128},{128,256},{256,384},{384,0},{1,129},{129,257},{257,385},{3... | collective-permute-start | bytes 2359304 | tf_op jit(solution)/shard_map/ppermute | solution.py:315
  47.5 3.7 %collective-permute-start.5 = (bf16[3,128,1024]{2,1,0:T(8,128)(2,1)}, bf16[3,128,1024]{2,1,0:T(8,128)(2,1)S(1)}, u32[]{:S(2)}, u32[]{:S(2)}) collective-permute-start(bf16[3,128,1024]{2,1,0:T(8,128)(2,1)} %get-tuple-element.15), channel_id=1, source_target_pairs={{0,384},{128,0},{256,128},{384,256},{1,385},{129,1},{257,129},{385... | collective-permute-start | bytes 2359304 | tf_op jit(solution)/shard_map/ppermute | solution.py:315
  51.2 2.1 %collective-permute-start.10 = (bf16[4,384,256]{2,1,0:T(8,128)(2,1)S(1)}, bf16[4,384,256]{2,1,0:T(8,128)(2,1)}, u32[]{:S(2)}, u32[]{:S(2)}) collective-permute-start(bf16[4,384,256]{2,1,0:T(8,128)(2,1)S(1)} %pad_maximum_fusion.rest_0_), channel_id=1, source_target_pairs={{0,16},{8,24},{16,0},{24,8},{1,17},{9,25},{17,1},{25,9},{2,18},{10... | collective-permute-start | bytes 2359304 | tf_op jit(solution)/shard_map/ppermute | solution.py:323
  53.3 3.7 %collective-permute-start.11 = (bf16[4,384,256]{2,1,0:T(8,128)(2,1)S(1)}, bf16[4,384,256]{2,1,0:T(8,128)(2,1)}, u32[]{:S(2)}, u32[]{:S(2)}) collective-permute-start(bf16[4,384,256]{2,1,0:T(8,128)(2,1)S(1)} %pad_maximum_fusion.rest_0_), channel_id=1, source_target_pairs={{0,8},{8,16},{16,24},{24,0},{1,9},{9,17},{17,25},{25,1},{2,10},{10... | collective-permute-start | bytes 2359304 | tf_op jit(solution)/shard_map/ppermute | solution.py:323
  57.0 2.0 %collective-permute-start.9 = (bf16[4,384,256]{2,1,0:T(8,128)(2,1)S(1)}, bf16[4,384,256]{2,1,0:T(8,128)(2,1)}, u32[]{:S(2)}, u32[]{:S(2)}) collective-permute-start(bf16[4,384,256]{2,1,0:T(8,128)(2,1)S(1)} %pad_maximum_fusion.rest_0_), channel_id=1, source_target_pairs={{0,24},{8,0},{16,8},{24,16},{1,25},{9,1},{17,9},{25,17},{2,26},{10... | collective-permute-start | bytes 2359304 | tf_op jit(solution)/shard_map/ppermute | solution.py:323
  59.0 1.0 reduce_sum.9
  60.8 10.0 %all-to-all-start.1 = ((f32[64,8,128]{2,1,0:T(8,128)}), f32[64,8,128]{2,1,0:T(8,128)}, u32[]{:S(2)}, u32[]{:S(2)}) async-start(f32[64,8,128]{2,1,0:T(8,128)} %broadcast_in_dim.2), calls=%async_computation.1 | async-start | bytes 524288 | tf_op jit(solution)/shard_map/all_to_all | solution.py:342
  70.8 10.3 %collective-permute-done.4.ahead = bf16[3,128,1024]{2,1,0:T(8,128)(2,1)S(1)} collective-permute-done((bf16[3,128,1024]{2,1,0:T(8,128)(2,1)}, bf16[3,128,1024]{2,1,0:T(8,128)(2,1)S(1)}, u32[]{:S(2)}, u32[]{:S(2)}) %collective-permute-start.4) | collective-permute-done | bytes 786464 | tf_op jit(solution)/shard_map/ppermute | solution.py:315
  81.1 4.2 %collective-permute-done.5.back = bf16[3,128,1024]{2,1,0:T(8,128)(2,1)S(1)} collective-permute-done((bf16[3,128,1024]{2,1,0:T(8,128)(2,1)}, bf16[3,128,1024]{2,1,0:T(8,128)(2,1)S(1)}, u32[]{:S(2)}, u32[]{:S(2)}) %collective-permute-start.5) | collective-permute-done | bytes 786464 | tf_op jit(solution)/shard_map/ppermute | solution.py:315
  85.3 0.9 copy-done.9
  86.2 1.8 %onward.1 = (bf16[1,128,1024]{2,1,0:T(8,128)(2,1)}, bf16[1,128,1024]{2,1,0:T(8,128)(2,1)}) custom-call(bf16[3,128,1024]{2,1,0:T(8,128)(2,1)} %copy-done.6, bf16[3,128,1024]{2,1,0:T(8,128)(2,1)} %copy-done.9), custom_call_target="tpu_custom_call" | custom-call | bytes 104857600 | tf_op jit(solution)/shard_map/onward/pallas_call | solution.py:125
  88.1 2.2 %collective-permute-start.6 = (bf16[1,128,1024]{2,1,0:T(8,128)(2,1)}, bf16[1,128,1024]{2,1,0:T(8,128)(2,1)S(1)}, u32[]{:S(2)}, u32[]{:S(2)}) collective-permute-start(bf16[1,128,1024]{2,1,0:T(8,128)(2,1)} %get-tuple-element.16), channel_id=1, source_target_pairs={{0,128},{128,256},{256,384},{384,0},{1,129},{129,257},{257,385},{3... | collective-permute-start | bytes 786440 | tf_op jit(solution)/shard_map/ppermute | solution.py:315
  90.2 5.2 %collective-permute-start.7 = (bf16[1,128,1024]{2,1,0:T(8,128)(2,1)}, bf16[1,128,1024]{2,1,0:T(8,128)(2,1)S(1)}, u32[]{:S(2)}, u32[]{:S(2)}) collective-permute-start(bf16[1,128,1024]{2,1,0:T(8,128)(2,1)} %get-tuple-element.17), channel_id=1, source_target_pairs={{0,384},{128,0},{256,128},{384,256},{1,385},{129,1},{257,129},{385... | collective-permute-start | bytes 786440 | tf_op jit(solution)/shard_map/ppermute | solution.py:315
  95.5 4.2 %collective-permute-done.6.far_x = bf16[1,128,1024]{2,1,0:T(8,128)(2,1)S(1)} collective-permute-done((bf16[1,128,1024]{2,1,0:T(8,128)(2,1)}, bf16[1,128,1024]{2,1,0:T(8,128)(2,1)S(1)}, u32[]{:S(2)}, u32[]{:S(2)}) %collective-permute-start.6) | collective-permute-done | bytes 262176 | tf_op jit(solution)/shard_map/ppermute | solution.py:315
  99.7 1.9 %collective-permute-done.7.far_dy = bf16[1,128,1024]{2,1,0:T(8,128)(2,1)S(1)} collective-permute-done((bf16[1,128,1024]{2,1,0:T(8,128)(2,1)}, bf16[1,128,1024]{2,1,0:T(8,128)(2,1)S(1)}, u32[]{:S(2)}, u32[]{:S(2)}) %collective-permute-start.7) | collective-permute-done | bytes 262176 | tf_op jit(solution)/shard_map/ppermute | solution.py:315
  101.6 1.1 copy-done.7
  102.7 1.1 copy-done.10
  103.9 0.7 repack_tokens.1.rest_4_
  104.7 4.1 %hidden_sums.1 = (f32[3,128,256]{2,1,0:T(8,128)S(1)}, f32[3,128,256]{2,1,0:T(8,128)S(1)}) custom-call(s32[3]{0:T(128)S(1)} %copy-done.20, bf16[128,4096]{1,0:T(8,128)(2,1)S(1)} %bitcast.22, bf16[128,4096]{1,0:T(8,128)(2,1)} %bitcast.24, bf16[4,2,128,512]{3,2,1,0:T(8,128)(2,1)} %copy-done.4, bf16[4,384,256]{2,1,0:T(8,128)(2,1)S(1)} %pad_maximum_fusion.rest_0_, ...), custom_call_target="tpu_custom_call" | custom-call | flops 805306368 | bytes 6291456 | tf_op jit(solution)/shard_map/hidden_sums/pallas_call | solution.py:219
  108.8 0.7 copy-done.19
  109.5 5.4 %collective-permute-start.12 = (f32[3,128,256]{2,1,0:T(8,128)S(1)}, f32[3,128,256]{2,1,0:T(8,128)S(1)}, u32[]{:S(2)}, u32[]{:S(2)}) collective-permute-start(f32[3,128,256]{2,1,0:T(8,128)S(1)} %get-tuple-element.19), channel_id=1, source_target_pairs={{0,64},{64,0},{1,65},{65,1},{2,66},{66,2},{3,67},{67,3},{4,68},{68... | collective-permute-start | bytes 1179656 | tf_op jit(solution)/shard_map/ppermute | solution.py:327
  115.0 1.8 %multiply_subtract_fusion = (f32[16,4096]{1,0:T(8,128)}, f32[16,4096]{1,0:T(8,128)}) fusion(f32[16,4096]{1,0:T(8,128)S(1)} %copy-done.22, f32[16,4096]{1,0:T(8,128)} %bitcast.15, f32[16,4096]{1,0:T(8,128)S(1)} %copy-done.23), kind=kLoop, calls=%fused_computation.1 | loop fusion | flops 393216 | bytes 1310720 | tf_op jit(solution)/shard_map/sub | solution.py:367
  116.8 0.7 copy-done.21
  117.5 2.1 %activation.1 = bf16[4,3,128,256]{3,2,1,0:T(8,128)(2,1)} custom-call(f32[3,128,256]{2,1,0:T(8,128)} %copy-done.19, f32[3,128,256]{2,1,0:T(8,128)} %copy-done.21, f32[16,4096]{1,0:T(8,128)} %get-tuple-element.23.after), custom_call_target="tpu_custom_call" | custom-call | flops 655360 | bytes 1048576 | tf_op jit(solution)/shard_map/activation/pallas_call | solution.py:253
  119.7 5.6 %all-to-all-start.2 = ((bf16[4,3,128,256]{3,2,1,0:T(8,128)(2,1)}), bf16[4,3,128,256]{3,2,1,0:T(8,128)(2,1)S(1)}, u32[]{:S(2)}, u32[]{:S(2)}) async-start(bf16[4,3,128,256]{3,2,1,0:T(8,128)(2,1)} %activation.1), calls=%async_computation.2 | async-start | bytes 1572864 | tf_op jit(solution)/shard_map/all_to_all | solution.py:371
  125.3 2.2 %collective-permute-start.8 = (bf16[3,2,128,512]{3,2,1,0:T(8,128)(2,1)}, bf16[3,2,128,512]{3,2,1,0:T(8,128)(2,1)}, u32[]{:S(2)}, u32[]{:S(2)}) collective-permute-start(bf16[3,2,128,512]{3,2,1,0:T(8,128)(2,1)} %copy-done.12), channel_id=1, source_target_pairs={{0,64},{64,0},{1,65},{65,1},{2,66},{66,2},{3,67},{67,3},{4,68},{68... | collective-permute-start | bytes 2359304 | tf_op jit(solution)/shard_map/ppermute | solution.py:327
  127.5 19.4 %all-to-all-done.2.rest_0_ = bf16[4,3,128,256]{3,2,1,0:T(8,128)(2,1)S(1)} async-done(((bf16[4,3,128,256]{3,2,1,0:T(8,128)(2,1)}), bf16[4,3,128,256]{3,2,1,0:T(8,128)(2,1)S(1)}, u32[]{:S(2)}, u32[]{:S(2)}) %all-to-all-start.2) | async-done | bytes 786464 | tf_op jit(solution)/shard_map/all_to_all | solution.py:371
  146.9 2.4 %collective-permute-start.13 = (bf16[4,3,128,256]{3,2,1,0:T(8,128)(2,1)S(1)}, bf16[4,3,128,256]{3,2,1,0:T(8,128)(2,1)S(1)}, u32[]{:S(2)}, u32[]{:S(2)}) collective-permute-start(bf16[4,3,128,256]{3,2,1,0:T(8,128)(2,1)S(1)} %all-to-all-done.2.rest_0_), channel_id=1, source_target_pairs={{0,64},{64,0},{1,65},{65,1},{2,66},{66,2},{3,67},{67,3},{4,68},{68... | collective-permute-start | bytes 2359304 | tf_op jit(solution)/shard_map/ppermute | solution.py:327
  149.3 1.9 %collective-permute-done.13.rest_1_ = bf16[4,3,128,256]{3,2,1,0:T(8,128)(2,1)S(1)} collective-permute-done((bf16[4,3,128,256]{3,2,1,0:T(8,128)(2,1)S(1)}, bf16[4,3,128,256]{3,2,1,0:T(8,128)(2,1)S(1)}, u32[]{:S(2)}, u32[]{:S(2)}) %collective-permute-start.13) | collective-permute-done | bytes 786464 | tf_op jit(solution)/shard_map/ppermute | solution.py:327
  151.2 0.9 copy-done.16
  152.1 0.9 copy-done.18
  153.1 4.3 %weight_grads.1 = (bf16[1,512,256]{2,1,0:T(8,128)(2,1)}, bf16[1,512,256]{2,1,0:T(8,128)(2,1)}, bf16[1,256,512]{2,1,0:T(8,128)(2,1)}) custom-call(s32[3]{0:T(128)S(1)} %copy-done.20, bf16[128,4096]{1,0:T(8,128)(2,1)S(1)} %bitcast.23, bf16[128,4096]{1,0:T(8,128)(2,1)} %bitcast.25, bf16[4,2,128,512]{3,2,1,0:T(8,128)(2,1)} %copy-done.4, ...), custom_call_target="tpu_custom_call" | custom-call | flops 805306368 | bytes 5242880 | tf_op jit(solution)/shard_map/weight_grads/pallas_call | solution.py:293
  (51 shorter events, 3.1 us)
Async XLA Ops:
  3.5 0.7 copy-start.20
  4.1 1.2 copy-start
  5.4 1.2 copy-start.2
  6.6 0.9 copy-start.13
  8.3 15.4 %collective-permute-start = (bf16[4,2,128,512]{3,2,1,0:T(8,128)(2,1)S(1)}, bf16[4,2,128,512]{3,2,1,0:T(8,128)(2,1)S(1)}, u32[]{:S(2)}, u32[]{:S(2)}) collective-permute-start(bf16[4,2,128,512]{3,2,1,0:T(8,128)(2,1)S(1)} %tokens_beside.1), channel_id=1, source_target_pairs={{0,64},{64,0},{1,65},{65,1},{2,66},{66,2},{3,67},{67,3},{4,68},{68... | collective-permute-start | bytes 3145736 | tf_op jit(solution)/shard_map/ppermute | solution.py:327
  10.9 24.8 %collective-permute-start.1 = (bf16[384,256]{1,0:T(8,128)(2,1)S(1)}, bf16[384,256]{1,0:T(8,128)(2,1)S(1)}, u32[]{:S(2)}, u32[]{:S(2)}) collective-permute-start(bf16[384,256]{1,0:T(8,128)(2,1)S(1)} %copy-done.13), channel_id=1, source_target_pairs={{0,384},{128,0},{256,128},{384,256},{1,385},{129,1},{257,129},{385... | collective-permute-start | bytes 589832 | tf_op jit(solution)/shard_map/ppermute | solution.py:319
  15.9 20.2 %collective-permute-start.2 = (bf16[384,256]{1,0:T(8,128)(2,1)S(1)}, bf16[384,256]{1,0:T(8,128)(2,1)S(1)}, u32[]{:S(2)}, u32[]{:S(2)}) collective-permute-start(bf16[384,256]{1,0:T(8,128)(2,1)S(1)} %copy-done.13), channel_id=1, source_target_pairs={{0,256},{128,384},{256,0},{384,128},{1,257},{129,385},{257,1},{385... | collective-permute-start | bytes 589832 | tf_op jit(solution)/shard_map/ppermute | solution.py:319
  20.3 18.3 %collective-permute-start.3 = (bf16[384,256]{1,0:T(8,128)(2,1)S(1)}, bf16[384,256]{1,0:T(8,128)(2,1)S(1)}, u32[]{:S(2)}, u32[]{:S(2)}) collective-permute-start(bf16[384,256]{1,0:T(8,128)(2,1)S(1)} %copy-done.13), channel_id=1, source_target_pairs={{0,128},{128,256},{256,384},{384,0},{1,129},{129,257},{257,385},{3... | collective-permute-start | bytes 589832 | tf_op jit(solution)/shard_map/ppermute | solution.py:319
  23.7 1.0 copy-start.4
  24.7 14.6 %copy-start.14 = (bf16[384,256]{1,0:T(8,128)(2,1)S(1)}, bf16[384,256]{1,0:T(8,128)(2,1)}, u32[]{:S(2)}) copy-start(bf16[384,256]{1,0:T(8,128)(2,1)} %weight_share.1.after) | copy-start | bytes 589828
  26.4 13.9 %copy-start.1 = (bf16[1,128,4096]{2,1,0:T(8,128)(2,1)S(1)}, bf16[1,128,4096]{2,1,0:T(8,128)(2,1)}, u32[]{:S(2)}) copy-start(bf16[1,128,4096]{2,1,0:T(8,128)(2,1)} %param.8) | copy-start | bytes 3145732
  26.4 13.9 %copy-start.3 = (bf16[1,128,4096]{2,1,0:T(8,128)(2,1)S(1)}, bf16[1,128,4096]{2,1,0:T(8,128)(2,1)}, u32[]{:S(2)}) copy-start(bf16[1,128,4096]{2,1,0:T(8,128)(2,1)} %param.9) | copy-start | bytes 3145732
  26.4 32.6 %all-to-all-start = ((f32[64,8,128]{2,1,0:T(8,128)}), f32[64,8,128]{2,1,0:T(8,128)}, u32[]{:S(2)}, u32[]{:S(2)}) async-start(f32[64,8,128]{2,1,0:T(8,128)} %bitcast.29), calls=%async_computation | async-start | bytes 524288 | tf_op jit(solution)/shard_map/all_to_all | solution.py:335
  38.6 0.7 copy-start.24
  40.3 1.2 copy-start.5
  43.4 37.7 %collective-permute-start.4 = (bf16[3,128,1024]{2,1,0:T(8,128)(2,1)}, bf16[3,128,1024]{2,1,0:T(8,128)(2,1)S(1)}, u32[]{:S(2)}, u32[]{:S(2)}) collective-permute-start(bf16[3,128,1024]{2,1,0:T(8,128)(2,1)} %get-tuple-element.14), channel_id=1, source_target_pairs={{0,128},{128,256},{256,384},{384,0},{1,129},{129,257},{257,385},{3... | collective-permute-start | bytes 2359304 | tf_op jit(solution)/shard_map/ppermute | solution.py:315
  47.5 37.9 %collective-permute-start.5 = (bf16[3,128,1024]{2,1,0:T(8,128)(2,1)}, bf16[3,128,1024]{2,1,0:T(8,128)(2,1)S(1)}, u32[]{:S(2)}, u32[]{:S(2)}) collective-permute-start(bf16[3,128,1024]{2,1,0:T(8,128)(2,1)} %get-tuple-element.15), channel_id=1, source_target_pairs={{0,384},{128,0},{256,128},{384,256},{1,385},{129,1},{257,129},{385... | collective-permute-start | bytes 2359304 | tf_op jit(solution)/shard_map/ppermute | solution.py:315
  51.2 53.5 %collective-permute-start.10 = (bf16[4,384,256]{2,1,0:T(8,128)(2,1)S(1)}, bf16[4,384,256]{2,1,0:T(8,128)(2,1)}, u32[]{:S(2)}, u32[]{:S(2)}) collective-permute-start(bf16[4,384,256]{2,1,0:T(8,128)(2,1)S(1)} %pad_maximum_fusion.rest_0_), channel_id=1, source_target_pairs={{0,16},{8,24},{16,0},{24,8},{1,17},{9,25},{17,1},{25,9},{2,18},{10... | collective-permute-start | bytes 2359304 | tf_op jit(solution)/shard_map/ppermute | solution.py:323
  53.3 51.4 %collective-permute-start.11 = (bf16[4,384,256]{2,1,0:T(8,128)(2,1)S(1)}, bf16[4,384,256]{2,1,0:T(8,128)(2,1)}, u32[]{:S(2)}, u32[]{:S(2)}) collective-permute-start(bf16[4,384,256]{2,1,0:T(8,128)(2,1)S(1)} %pad_maximum_fusion.rest_0_), channel_id=1, source_target_pairs={{0,8},{8,16},{16,24},{24,0},{1,9},{9,17},{17,25},{25,1},{2,10},{10... | collective-permute-start | bytes 2359304 | tf_op jit(solution)/shard_map/ppermute | solution.py:323
  57.0 47.6 %collective-permute-start.9 = (bf16[4,384,256]{2,1,0:T(8,128)(2,1)S(1)}, bf16[4,384,256]{2,1,0:T(8,128)(2,1)}, u32[]{:S(2)}, u32[]{:S(2)}) collective-permute-start(bf16[4,384,256]{2,1,0:T(8,128)(2,1)S(1)} %pad_maximum_fusion.rest_0_), channel_id=1, source_target_pairs={{0,24},{8,0},{16,8},{24,16},{1,25},{9,1},{17,9},{25,17},{2,26},{10... | collective-permute-start | bytes 2359304 | tf_op jit(solution)/shard_map/ppermute | solution.py:323
  60.8 54.1 %all-to-all-start.1 = ((f32[64,8,128]{2,1,0:T(8,128)}), f32[64,8,128]{2,1,0:T(8,128)}, u32[]{:S(2)}, u32[]{:S(2)}) async-start(f32[64,8,128]{2,1,0:T(8,128)} %broadcast_in_dim.2), calls=%async_computation.1 | async-start | bytes 524288 | tf_op jit(solution)/shard_map/all_to_all | solution.py:342
  81.1 4.2 %copy-start.6 = (bf16[3,128,1024]{2,1,0:T(8,128)(2,1)}, bf16[3,128,1024]{2,1,0:T(8,128)(2,1)S(1)}, u32[]{:S(2)}) copy-start(bf16[3,128,1024]{2,1,0:T(8,128)(2,1)S(1)} %collective-permute-done.4.ahead) | copy-start | bytes 2359300
  85.3 0.9 copy-start.9
  88.1 11.6 %collective-permute-start.6 = (bf16[1,128,1024]{2,1,0:T(8,128)(2,1)}, bf16[1,128,1024]{2,1,0:T(8,128)(2,1)S(1)}, u32[]{:S(2)}, u32[]{:S(2)}) collective-permute-start(bf16[1,128,1024]{2,1,0:T(8,128)(2,1)} %get-tuple-element.16), channel_id=1, source_target_pairs={{0,128},{128,256},{256,384},{384,0},{1,129},{129,257},{257,385},{3... | collective-permute-start | bytes 786440 | tf_op jit(solution)/shard_map/ppermute | solution.py:315
  90.2 11.4 %collective-permute-start.7 = (bf16[1,128,1024]{2,1,0:T(8,128)(2,1)}, bf16[1,128,1024]{2,1,0:T(8,128)(2,1)S(1)}, u32[]{:S(2)}, u32[]{:S(2)}) collective-permute-start(bf16[1,128,1024]{2,1,0:T(8,128)(2,1)} %get-tuple-element.17), channel_id=1, source_target_pairs={{0,384},{128,0},{256,128},{384,256},{1,385},{129,1},{257,129},{385... | collective-permute-start | bytes 786440 | tf_op jit(solution)/shard_map/ppermute | solution.py:315
  99.7 4.9 %copy-start.15 = (bf16[1,128,1024]{2,1,0:T(8,128)(2,1)}, bf16[1,128,1024]{2,1,0:T(8,128)(2,1)S(1)}, u32[]{:S(2)}) copy-start(bf16[1,128,1024]{2,1,0:T(8,128)(2,1)S(1)} %collective-permute-done.6.far_x) | copy-start | bytes 786436
  101.6 1.1 copy-start.7
  102.7 1.1 copy-start.10
  103.9 0.7 copy-start.17
  104.6 4.1 %copy-start.12 = (bf16[3,2,128,512]{3,2,1,0:T(8,128)(2,1)}, bf16[3,2,128,512]{3,2,1,0:T(8,128)(2,1)S(1)}, u32[]{:S(2)}) copy-start(bf16[3,2,128,512]{3,2,1,0:T(8,128)(2,1)S(1)} %repack_tokens.1.rest_4_) | copy-start | bytes 2359300
  104.6 10.3 %copy-start.22 = (f32[16,4096]{1,0:T(8,128)S(1)}, f32[16,4096]{1,0:T(8,128)}, u32[]{:S(2)}) copy-start(f32[16,4096]{1,0:T(8,128)} %param.14) | copy-start | bytes 786436
  104.6 10.3 %copy-start.23 = (f32[16,4096]{1,0:T(8,128)S(1)}, f32[16,4096]{1,0:T(8,128)}, u32[]{:S(2)}) copy-start(f32[16,4096]{1,0:T(8,128)} %param.15) | copy-start | bytes 786436
  108.8 0.8 copy-start.19
  109.5 7.3 %collective-permute-start.12 = (f32[3,128,256]{2,1,0:T(8,128)S(1)}, f32[3,128,256]{2,1,0:T(8,128)S(1)}, u32[]{:S(2)}, u32[]{:S(2)}) collective-permute-start(f32[3,128,256]{2,1,0:T(8,128)S(1)} %get-tuple-element.19), channel_id=1, source_target_pairs={{0,64},{64,0},{1,65},{65,1},{2,66},{66,2},{3,67},{67,3},{4,68},{68... | collective-permute-start | bytes 1179656 | tf_op jit(solution)/shard_map/ppermute | solution.py:327
  116.8 0.8 copy-start.21
  119.7 31.5 %copy-start.8 = (bf16[3,128,1024]{2,1,0:T(8,128)(2,1)S(1)}, bf16[3,128,1024]{2,1,0:T(8,128)(2,1)}, u32[]{:S(2)}) copy-start(bf16[3,128,1024]{2,1,0:T(8,128)(2,1)} %copy-done.6) | copy-start | bytes 2359300
  119.7 31.5 %copy-start.11 = (bf16[3,128,1024]{2,1,0:T(8,128)(2,1)S(1)}, bf16[3,128,1024]{2,1,0:T(8,128)(2,1)}, u32[]{:S(2)}) copy-start(bf16[3,128,1024]{2,1,0:T(8,128)(2,1)} %copy-done.9) | copy-start | bytes 2359300
  119.7 27.2 %all-to-all-start.2 = ((bf16[4,3,128,256]{3,2,1,0:T(8,128)(2,1)}), bf16[4,3,128,256]{3,2,1,0:T(8,128)(2,1)S(1)}, u32[]{:S(2)}, u32[]{:S(2)}) async-start(bf16[4,3,128,256]{3,2,1,0:T(8,128)(2,1)} %activation.1), calls=%async_computation.2 | async-start | bytes 1572864 | tf_op jit(solution)/shard_map/all_to_all | solution.py:371
  125.3 24.0 %collective-permute-start.8 = (bf16[3,2,128,512]{3,2,1,0:T(8,128)(2,1)}, bf16[3,2,128,512]{3,2,1,0:T(8,128)(2,1)}, u32[]{:S(2)}, u32[]{:S(2)}) collective-permute-start(bf16[3,2,128,512]{3,2,1,0:T(8,128)(2,1)} %copy-done.12), channel_id=1, source_target_pairs={{0,64},{64,0},{1,65},{65,1},{2,66},{66,2},{3,67},{67,3},{4,68},{68... | collective-permute-start | bytes 2359304 | tf_op jit(solution)/shard_map/ppermute | solution.py:327
  146.9 4.3 %collective-permute-start.13 = (bf16[4,3,128,256]{3,2,1,0:T(8,128)(2,1)S(1)}, bf16[4,3,128,256]{3,2,1,0:T(8,128)(2,1)S(1)}, u32[]{:S(2)}, u32[]{:S(2)}) collective-permute-start(bf16[4,3,128,256]{3,2,1,0:T(8,128)(2,1)S(1)} %all-to-all-done.2.rest_0_), channel_id=1, source_target_pairs={{0,64},{64,0},{1,65},{65,1},{2,66},{66,2},{3,67},{67,3},{4,68},{68... | collective-permute-start | bytes 2359304 | tf_op jit(solution)/shard_map/ppermute | solution.py:327
  151.2 1.0 copy-start.16
  152.1 0.9 copy-start.18

commit v6 on v5

--- a/solution.py
+++ b/solution.py
@@ -14,7 +14,7 @@
 HALF = 512
 HID = 256
 DEAR = 100
-VMEM_LIMIT = 48 * 1024 * 1024
+VMEM_LIMIT = 63 * 1024 * 1024
 
 F32 = jnp.float32
 BF16 = jnp.bfloat16
@@ -60,6 +60,7 @@
         in_specs=[SMEM, ANY, ANY, ANY],
         out_specs=VMEM,
         scratch_shapes=[pltpu.SemaphoreType.DMA((4,))],
+        compiler_params=pltpu.CompilerParams(vmem_limit_bytes=VMEM_LIMIT),
         cost_estimate=pl.CostEstimate(flops=0, bytes_accessed=1 << 18, transcendentals=0),
         name="weight_share",
     )(place, gate, up, down)
@@ -128,6 +129,7 @@
         in_specs=[ANY, ANY],
         out_specs=(VMEM, VMEM),
         scratch_shapes=[pltpu.SemaphoreType.DMA((2,))],
+        compiler_params=pltpu.CompilerParams(vmem_limit_bytes=VMEM_LIMIT),
         cost_estimate=pl.CostEstimate(flops=0, bytes_accessed=DEAR << 20, transcendentals=0),
         name="onward",
     )(ahead, back)
@@ -166,6 +168,7 @@
         in_specs=[ANY, ANY],
         out_specs=VMEM,
         scratch_shapes=[pltpu.SemaphoreType.DMA((1,))],
+        compiler_params=pltpu.CompilerParams(vmem_limit_bytes=VMEM_LIMIT),
         cost_estimate=pl.CostEstimate(flops=0, bytes_accessed=1 << 19, transcendentals=0),
         name="delta_staged",
     )(delta, after)
@@ -260,6 +263,7 @@
             pltpu.VMEM((3, ROWS, HID), F32),
             pltpu.SemaphoreType.DMA((2,)),
         ],
+        compiler_params=pltpu.CompilerParams(vmem_limit_bytes=VMEM_LIMIT),
         cost_estimate=pl.CostEstimate(flops=20 * ROWS * HID, bytes_accessed=1 << 20, transcendentals=ROWS * HID),
         name="activation",
     )(mine, arrived, after)
@@ -358,7 +362,8 @@
     ahead, back = pack(place, x, dy, (shares, beside))
     ahead, back = to_shift(ahead, 1), to_shift(back, 3)
     far_x, far_dy = onward(ahead, back)
-    arrived = [ahead, back, to_shift(far_x, 1), to_shift(far_dy, 3)]
+    far_x, far_dy = to_shift(far_x, 1), to_shift(far_dy, 3)
+    arrived = [ahead, back, far_x, far_dy]
     repacked = repack(place, arrived)
     swapped = other_core(repacked)
 
@@ -366,7 +371,7 @@
     new_momentum = 0.9 * momentum + pseudo
     new_anchor = anchor - 0.7 * (pseudo + 0.9 * new_momentum)
 
-    mine, theirs = hidden_sums(place, x, dy, beside, weights, (repacked,))
+    mine, theirs = hidden_sums(place, x, dy, beside, weights, (far_x, far_dy))
     acts = activation(mine, other_core(theirs), new_anchor)
     acts = lax.all_to_all(acts, "yh", 0, 0, tiled=True)
     acts = (acts, other_core(acts))

time: 159 us -> 153 us (0.962)
  the two profiles are of different devices: /device:TPU:397 before, /device:TPU:459 now
where the time goes in v6:
time: 153 us; the launch traced here: 151 us
  starting transfers between devices  71.8 us (47%)
  waiting for transfers between devices  44.9 us (29%)
  Pallas kernels  27.1 us (18%)
  other arithmetic  4.51 us (3%)
  local copies, waits for them, and re-layouts  2.21 us (1%)
    ppermute x4, waiting for transfers between devices, to_shift(): lax.ppermute(value, 'yh', [(i, (i + shift) % CHIPS) for i in range(CHIPS)])  21.3 us
    all_to_all x1, waiting for transfers between devices, on_device(): acts = lax.all_to_all(acts, 'yh', 0, 0, tiled=True)  16.6 us
    ppermute x4, starting transfers between devices, to_shift(): lax.ppermute(value, 'yh', [(i, (i + shift) % CHIPS) for i in range(CHIPS)])  15.2 us
    ppermute x4, starting transfers between devices, other_core(): return lax.ppermute(value, 'core', [(0, 1), (1, 0)])  13.2 us
    ppermute x3, starting transfers between devices, from_shift(): lax.ppermute(value, 'yh', [(i, (i - shift) % CHIPS) for i in range(CHIPS)])  12.7 us
    ppermute x3, starting transfers between devices, from_x(): lax.ppermute(value, 'x', [(i, (i - shift) % size) for i in range(size)])  9.04 us
    all_to_all x1, starting transfers between devices, share_of_sum(): lax.all_to_all(tiles, everyone, 0, 0, tiled=True)  8.24 us
    all_to_all x1, starting transfers between devices, whole_mean(): lax.all_to_all(jnp.broadcast_to(part / count, (count, 8, 128)), everyone,...  7.88 us
  transfers between devices with their start and end apart: 17, of which 8 were waited for; matrix products, arithmetic and copies ran while one was open for 3% of the time, Pallas kernels for 10%

profile of v6, /device:TPU:459, one launch (start us, length us, event | category | flops | bytes accessed | tf_op | source)
XLA Modules:
  0.0 151.5 jit_solution(9971738125714018188)
XLA Ops:
  0.6 0.6 pad_add_fusion.place
  1.3 2.2 %weight_share.1.after = bf16[384,256]{1,0:T(8,128)(2,1)} custom-call(s32[3]{0:T(128)} %pad_add_fusion.place, bf16[512,256]{1,0:T(8,128)(2,1)} %gate.1, bf16[512,256]{1,0:T(8,128)(2,1)} %up.1, bf16[256,512]{1,0:T(8,128)(2,1)} %down.1), custom_call_target="tpu_custom_call" | custom-call | bytes 262144 | tf_op jit(solution)/shard_map/weight_share/pallas_call | solution.py:57
  3.5 0.0 copy-start.4
  3.5 3.1 %tokens_beside.1 = bf16[4,2,128,512]{3,2,1,0:T(8,128)(2,1)} custom-call(s32[3]{0:T(128)} %pad_add_fusion.place, bf16[128,4096]{1,0:T(8,128)(2,1)} %bitcast.20, bf16[128,4096]{1,0:T(8,128)(2,1)} %bitcast.24, bf16[384,256]{1,0:T(8,128)(2,1)} %weight_share.1.after), custom_call_target="tpu_custom_call" | custom-call | bytes 2097152 | tf_op jit(solution)/shard_map/tokens_beside/pallas_call | solution.py:79
  6.6 2.6 %collective-permute-start = (bf16[4,2,128,512]{3,2,1,0:T(8,128)(2,1)}, bf16[4,2,128,512]{3,2,1,0:T(8,128)(2,1)}, u32[]{:S(2)}, u32[]{:S(2)}) collective-permute-start(bf16[4,2,128,512]{3,2,1,0:T(8,128)(2,1)} %tokens_beside.1), channel_id=1, source_target_pairs={{0,64},{64,0},{1,65},{65,1},{2,66},{66,2},{3,67},{67,3},{4,68},{68... | collective-permute-start | bytes 3145736 | tf_op jit(solution)/shard_map/ppermute | solution.py:331
  9.2 5.0 %collective-permute-start.1 = (bf16[384,256]{1,0:T(8,128)(2,1)S(1)}, bf16[384,256]{1,0:T(8,128)(2,1)S(1)}, u32[]{:S(2)}, u32[]{:S(2)}) collective-permute-start(bf16[384,256]{1,0:T(8,128)(2,1)S(1)} %copy-done.4), channel_id=1, source_target_pairs={{0,384},{128,0},{256,128},{384,256},{1,385},{129,1},{257,129},{385... | collective-permute-start | bytes 589832 | tf_op jit(solution)/shard_map/ppermute | solution.py:323
  14.2 4.4 %collective-permute-start.2 = (bf16[384,256]{1,0:T(8,128)(2,1)S(1)}, bf16[384,256]{1,0:T(8,128)(2,1)S(1)}, u32[]{:S(2)}, u32[]{:S(2)}) collective-permute-start(bf16[384,256]{1,0:T(8,128)(2,1)S(1)} %copy-done.4), channel_id=1, source_target_pairs={{0,256},{128,384},{256,0},{384,128},{1,257},{129,385},{257,1},{385... | collective-permute-start | bytes 589832 | tf_op jit(solution)/shard_map/ppermute | solution.py:323
  18.7 3.3 %collective-permute-start.3 = (bf16[384,256]{1,0:T(8,128)(2,1)S(1)}, bf16[384,256]{1,0:T(8,128)(2,1)S(1)}, u32[]{:S(2)}, u32[]{:S(2)}) collective-permute-start(bf16[384,256]{1,0:T(8,128)(2,1)S(1)} %copy-done.4), channel_id=1, source_target_pairs={{0,128},{128,256},{256,384},{384,0},{1,129},{129,257},{257,385},{3... | collective-permute-start | bytes 589832 | tf_op jit(solution)/shard_map/ppermute | solution.py:323
  22.0 0.0 collective-permute-done.rest_1_.beside.after
  22.0 1.7 %delta_staged.1 = f32[16,4096]{1,0:T(8,128)} custom-call(f32[16,4096]{1,0:T(8,128)} %bitcast.30, bf16[4,2,128,512]{3,2,1,0:T(8,128)(2,1)} %collective-permute-done.rest_1_.beside.after), custom_call_target="tpu_custom_call" | custom-call | bytes 524288 | tf_op jit(solution)/shard_map/delta_staged/pallas_call | solution.py:165
  23.7 8.2 %all-to-all-start = ((f32[64,8,128]{2,1,0:T(8,128)}), f32[64,8,128]{2,1,0:T(8,128)}, u32[]{:S(2)}, u32[]{:S(2)}) async-start(f32[64,8,128]{2,1,0:T(8,128)} %bitcast.29), calls=%async_computation | async-start | bytes 524288 | tf_op jit(solution)/shard_map/all_to_all | solution.py:339
  31.9 2.5 %collective-permute-done.2 = bf16[384,256]{1,0:T(8,128)(2,1)S(1)} collective-permute-done((bf16[384,256]{1,0:T(8,128)(2,1)S(1)}, bf16[384,256]{1,0:T(8,128)(2,1)S(1)}, u32[]{:S(2)}, u32[]{:S(2)}) %collective-permute-start.2) | collective-permute-done | bytes 196640 | tf_op jit(solution)/shard_map/ppermute | solution.py:323
  34.5 2.5 %collective-permute-done.3 = bf16[384,256]{1,0:T(8,128)(2,1)S(1)} collective-permute-done((bf16[384,256]{1,0:T(8,128)(2,1)S(1)}, bf16[384,256]{1,0:T(8,128)(2,1)S(1)}, u32[]{:S(2)}, u32[]{:S(2)}) %collective-permute-start.3) | collective-permute-done | bytes 196640 | tf_op jit(solution)/shard_map/ppermute | solution.py:323
  37.0 1.0 pad_maximum_fusion.rest_0_
  38.0 3.2 %pack_tokens.1 = (bf16[3,128,1024]{2,1,0:T(8,128)(2,1)}, bf16[3,128,1024]{2,1,0:T(8,128)(2,1)}) custom-call(s32[3]{0:T(128)} %pad_add_fusion.place, bf16[128,4096]{1,0:T(8,128)(2,1)} %bitcast.21, bf16[128,4096]{1,0:T(8,128)(2,1)} %bitcast.25, bf16[4,384,256]{2,1,0:T(8,128)(2,1)} %pad_maximum_fusion.rest_0_, ...), custom_call_target="tpu_custom_call" | custom-call | bytes 4194304 | tf_op jit(solution)/shard_map/pack_tokens/pallas_call | solution.py:108
  41.2 4.0 %collective-permute-start.4 = (bf16[3,128,1024]{2,1,0:T(8,128)(2,1)}, bf16[3,128,1024]{2,1,0:T(8,128)(2,1)S(1)}, u32[]{:S(2)}, u32[]{:S(2)}) collective-permute-start(bf16[3,128,1024]{2,1,0:T(8,128)(2,1)} %get-tuple-element.14), channel_id=1, source_target_pairs={{0,128},{128,256},{256,384},{384,0},{1,129},{129,257},{257,385},{3... | collective-permute-start | bytes 2359304 | tf_op jit(solution)/shard_map/ppermute | solution.py:319
  45.2 3.7 %collective-permute-start.5 = (bf16[3,128,1024]{2,1,0:T(8,128)(2,1)}, bf16[3,128,1024]{2,1,0:T(8,128)(2,1)}, u32[]{:S(2)}, u32[]{:S(2)}) collective-permute-start(bf16[3,128,1024]{2,1,0:T(8,128)(2,1)} %get-tuple-element.15), channel_id=1, source_target_pairs={{0,384},{128,0},{256,128},{384,256},{1,385},{129,1},{257,129},{385... | collective-permute-start | bytes 2359304 | tf_op jit(solution)/shard_map/ppermute | solution.py:319
  48.9 3.8 %collective-permute-start.10 = (bf16[4,384,256]{2,1,0:T(8,128)(2,1)}, bf16[4,384,256]{2,1,0:T(8,128)(2,1)}, u32[]{:S(2)}, u32[]{:S(2)}) collective-permute-start(bf16[4,384,256]{2,1,0:T(8,128)(2,1)} %pad_maximum_fusion.rest_0_), channel_id=1, source_target_pairs={{0,16},{8,24},{16,0},{24,8},{1,17},{9,25},{17,1},{25,9},{2,18},{10... | collective-permute-start | bytes 2359304 | tf_op jit(solution)/shard_map/ppermute | solution.py:327
  52.7 1.9 %collective-permute-start.11 = (bf16[4,384,256]{2,1,0:T(8,128)(2,1)}, bf16[4,384,256]{2,1,0:T(8,128)(2,1)}, u32[]{:S(2)}, u32[]{:S(2)}) collective-permute-start(bf16[4,384,256]{2,1,0:T(8,128)(2,1)} %pad_maximum_fusion.rest_0_), channel_id=1, source_target_pairs={{0,8},{8,16},{16,24},{24,0},{1,9},{9,17},{17,25},{25,1},{2,10},{10... | collective-permute-start | bytes 2359304 | tf_op jit(solution)/shard_map/ppermute | solution.py:327
  54.6 3.4 %collective-permute-start.9 = (bf16[4,384,256]{2,1,0:T(8,128)(2,1)}, bf16[4,384,256]{2,1,0:T(8,128)(2,1)}, u32[]{:S(2)}, u32[]{:S(2)}) collective-permute-start(bf16[4,384,256]{2,1,0:T(8,128)(2,1)} %pad_maximum_fusion.rest_0_), channel_id=1, source_target_pairs={{0,24},{8,0},{16,8},{24,16},{1,25},{9,1},{17,9},{25,17},{2,26},{10... | collective-permute-start | bytes 2359304 | tf_op jit(solution)/shard_map/ppermute | solution.py:327
  58.0 0.0 all-to-all-done
  58.0 1.0 reduce_sum.9
  59.0 0.7 broadcast_in_dim.2
  59.7 7.9 %all-to-all-start.1 = ((f32[64,8,128]{2,1,0:T(8,128)}), f32[64,8,128]{2,1,0:T(8,128)}, u32[]{:S(2)}, u32[]{:S(2)}) async-start(f32[64,8,128]{2,1,0:T(8,128)} %broadcast_in_dim.2), calls=%async_computation.1 | async-start | bytes 524288 | tf_op jit(solution)/shard_map/all_to_all | solution.py:346
  67.6 10.2 %collective-permute-done.4.ahead = bf16[3,128,1024]{2,1,0:T(8,128)(2,1)S(1)} collective-permute-done((bf16[3,128,1024]{2,1,0:T(8,128)(2,1)}, bf16[3,128,1024]{2,1,0:T(8,128)(2,1)S(1)}, u32[]{:S(2)}, u32[]{:S(2)}) %collective-permute-start.4) | collective-permute-done | bytes 786464 | tf_op jit(solution)/shard_map/ppermute | solution.py:319
  77.8 5.3 %collective-permute-done.5.back = bf16[3,128,1024]{2,1,0:T(8,128)(2,1)} collective-permute-done((bf16[3,128,1024]{2,1,0:T(8,128)(2,1)}, bf16[3,128,1024]{2,1,0:T(8,128)(2,1)}, u32[]{:S(2)}, u32[]{:S(2)}) %collective-permute-start.5) | collective-permute-done | bytes 786464 | tf_op jit(solution)/shard_map/ppermute | solution.py:319
  83.2 1.8 %onward.1 = (bf16[1,128,1024]{2,1,0:T(8,128)(2,1)}, bf16[1,128,1024]{2,1,0:T(8,128)(2,1)}) custom-call(bf16[3,128,1024]{2,1,0:T(8,128)(2,1)} %copy-done, bf16[3,128,1024]{2,1,0:T(8,128)(2,1)} %collective-permute-done.5.back), custom_call_target="tpu_custom_call" | custom-call | bytes 104857600 | tf_op jit(solution)/shard_map/onward/pallas_call | solution.py:126
  85.0 2.2 %collective-permute-start.6 = (bf16[1,128,1024]{2,1,0:T(8,128)(2,1)}, bf16[1,128,1024]{2,1,0:T(8,128)(2,1)S(1)}, u32[]{:S(2)}, u32[]{:S(2)}) collective-permute-start(bf16[1,128,1024]{2,1,0:T(8,128)(2,1)} %get-tuple-element.16), channel_id=1, source_target_pairs={{0,128},{128,256},{256,384},{384,0},{1,129},{129,257},{257,385},{3... | collective-permute-start | bytes 786440 | tf_op jit(solution)/shard_map/ppermute | solution.py:319
  87.2 0.0 copy-start.6
  87.2 5.4 %collective-permute-start.7 = (bf16[1,128,1024]{2,1,0:T(8,128)(2,1)}, bf16[1,128,1024]{2,1,0:T(8,128)(2,1)S(1)}, u32[]{:S(2)}, u32[]{:S(2)}) collective-permute-start(bf16[1,128,1024]{2,1,0:T(8,128)(2,1)} %get-tuple-element.17), channel_id=1, source_target_pairs={{0,384},{128,0},{256,128},{384,256},{1,385},{129,1},{257,129},{385... | collective-permute-start | bytes 786440 | tf_op jit(solution)/shard_map/ppermute | solution.py:319
  92.6 0.0 collective-permute-done.11.rest_3_
  92.6 3.9 %collective-permute-done.6.far_x.rest_4_ = bf16[1,128,1024]{2,1,0:T(8,128)(2,1)S(1)} collective-permute-done((bf16[1,128,1024]{2,1,0:T(8,128)(2,1)}, bf16[1,128,1024]{2,1,0:T(8,128)(2,1)S(1)}, u32[]{:S(2)}, u32[]{:S(2)}) %collective-permute-start.6) | collective-permute-done | bytes 262176 | tf_op jit(solution)/shard_map/ppermute | solution.py:319
  96.4 1.9 %collective-permute-done.7.far_dy.rest_5_ = bf16[1,128,1024]{2,1,0:T(8,128)(2,1)S(1)} collective-permute-done((bf16[1,128,1024]{2,1,0:T(8,128)(2,1)}, bf16[1,128,1024]{2,1,0:T(8,128)(2,1)S(1)}, u32[]{:S(2)}, u32[]{:S(2)}) %collective-permute-start.7) | collective-permute-done | bytes 262176 | tf_op jit(solution)/shard_map/ppermute | solution.py:319
  98.3 0.7 copy-done.3
  99.0 5.4 %hidden_sums.1 = (f32[3,128,256]{2,1,0:T(8,128)}, f32[3,128,256]{2,1,0:T(8,128)}) custom-call(s32[3]{0:T(128)} %pad_add_fusion.place, bf16[128,4096]{1,0:T(8,128)(2,1)} %bitcast.22, bf16[128,4096]{1,0:T(8,128)(2,1)} %bitcast.26, bf16[4,2,128,512]{3,2,1,0:T(8,128)(2,1)} %collective-permute-done.rest_1_.beside.after, ...), custom_call_target="tpu_custom_call" | custom-call | flops 805306368 | bytes 6291456 | tf_op jit(solution)/shard_map/hidden_sums/pallas_call | solution.py:222
  104.4 5.8 %collective-permute-start.12 = (f32[3,128,256]{2,1,0:T(8,128)}, f32[3,128,256]{2,1,0:T(8,128)S(1)}, u32[]{:S(2)}, u32[]{:S(2)}) collective-permute-start(f32[3,128,256]{2,1,0:T(8,128)} %get-tuple-element.19), channel_id=1, source_target_pairs={{0,64},{64,0},{1,65},{65,1},{2,66},{66,2},{3,67},{67,3},{4,68},{68... | collective-permute-start | bytes 1179656 | tf_op jit(solution)/shard_map/ppermute | solution.py:331
  110.2 1.9 %multiply_subtract_fusion = (f32[16,4096]{1,0:T(8,128)}, f32[16,4096]{1,0:T(8,128)}) fusion(f32[16,4096]{1,0:T(8,128)S(1)} %copy-done.6, f32[16,4096]{1,0:T(8,128)} %bitcast.15, f32[16,4096]{1,0:T(8,128)} %param.15), kind=kLoop, calls=%fused_computation.1 | loop fusion | flops 393216 | bytes 1310720 | tf_op jit(solution)/shard_map/sub | solution.py:372
  112.1 0.0 collective-permute-done.12.arrived_ref
  112.1 0.8 copy-done.5
  112.9 2.1 %activation.1 = bf16[4,3,128,256]{3,2,1,0:T(8,128)(2,1)} custom-call(f32[3,128,256]{2,1,0:T(8,128)} %get-tuple-element.18.mine_ref, f32[3,128,256]{2,1,0:T(8,128)} %copy-done.5, f32[16,4096]{1,0:T(8,128)} %get-tuple-element.23.after), custom_call_target="tpu_custom_call" | custom-call | flops 655360 | bytes 1048576 | tf_op jit(solution)/shard_map/activation/pallas_call | solution.py:256
  115.0 5.5 %all-to-all-start.2 = ((bf16[4,3,128,256]{3,2,1,0:T(8,128)(2,1)}), bf16[4,3,128,256]{3,2,1,0:T(8,128)(2,1)S(1)}, u32[]{:S(2)}, u32[]{:S(2)}) async-start(bf16[4,3,128,256]{3,2,1,0:T(8,128)(2,1)} %activation.1), calls=%async_computation.2 | async-start | bytes 1572864 | tf_op jit(solution)/shard_map/all_to_all | solution.py:376
  120.5 2.8 %repack_tokens.1 = bf16[3,2,128,512]{3,2,1,0:T(8,128)(2,1)} custom-call(s32[3]{0:T(128)} %pad_add_fusion.place, bf16[3,128,1024]{2,1,0:T(8,128)(2,1)} %copy-done, bf16[3,128,1024]{2,1,0:T(8,128)(2,1)} %collective-permute-done.5.back, bf16[1,128,1024]{2,1,0:T(8,128)(2,1)} %copy-done.2, bf16[1,128,1024]{2,1,0:T(8,128)(2,1)} %copy-done.3), custom_call_target="tpu_custom_call" | custom-call | bytes 209715200 | tf_op jit(solution)/shard_map/repack_tokens/pallas_call | solution.py:147
  123.3 2.2 %collective-permute-start.8 = (bf16[3,2,128,512]{3,2,1,0:T(8,128)(2,1)}, bf16[3,2,128,512]{3,2,1,0:T(8,128)(2,1)}, u32[]{:S(2)}, u32[]{:S(2)}) collective-permute-start(bf16[3,2,128,512]{3,2,1,0:T(8,128)(2,1)} %repack_tokens.1), channel_id=1, source_target_pairs={{0,64},{64,0},{1,65},{65,1},{2,66},{66,2},{3,67},{67,3},{4,68},{68... | collective-permute-start | bytes 2359304 | tf_op jit(solution)/shard_map/ppermute | solution.py:331
  125.5 16.6 %all-to-all-done.2.rest_0_ = bf16[4,3,128,256]{3,2,1,0:T(8,128)(2,1)S(1)} async-done(((bf16[4,3,128,256]{3,2,1,0:T(8,128)(2,1)}), bf16[4,3,128,256]{3,2,1,0:T(8,128)(2,1)S(1)}, u32[]{:S(2)}, u32[]{:S(2)}) %all-to-all-start.2) | async-done | bytes 786464 | tf_op jit(solution)/shard_map/all_to_all | solution.py:376
  142.1 2.7 %collective-permute-start.13 = (bf16[4,3,128,256]{3,2,1,0:T(8,128)(2,1)S(1)}, bf16[4,3,128,256]{3,2,1,0:T(8,128)(2,1)}, u32[]{:S(2)}, u32[]{:S(2)}) collective-permute-start(bf16[4,3,128,256]{3,2,1,0:T(8,128)(2,1)S(1)} %all-to-all-done.2.rest_0_), channel_id=1, source_target_pairs={{0,64},{64,0},{1,65},{65,1},{2,66},{66,2},{3,67},{67,3},{4,68},{68... | collective-permute-start | bytes 2359304 | tf_op jit(solution)/shard_map/ppermute | solution.py:331
  144.8 0.0 collective-permute-done.8.swapped
  144.8 2.0 %collective-permute-done.13.rest_1_ = bf16[4,3,128,256]{3,2,1,0:T(8,128)(2,1)} collective-permute-done((bf16[4,3,128,256]{3,2,1,0:T(8,128)(2,1)S(1)}, bf16[4,3,128,256]{3,2,1,0:T(8,128)(2,1)}, u32[]{:S(2)}, u32[]{:S(2)}) %collective-permute-start.13) | collective-permute-done | bytes 786464 | tf_op jit(solution)/shard_map/ppermute | solution.py:331
  146.8 4.7 %weight_grads.1 = (bf16[1,512,256]{2,1,0:T(8,128)(2,1)}, bf16[1,512,256]{2,1,0:T(8,128)(2,1)}, bf16[1,256,512]{2,1,0:T(8,128)(2,1)}) custom-call(s32[3]{0:T(128)} %pad_add_fusion.place, bf16[128,4096]{1,0:T(8,128)(2,1)} %bitcast.23, bf16[128,4096]{1,0:T(8,128)(2,1)} %bitcast.27, bf16[4,2,128,512]{3,2,1,0:T(8,128)(2,1)} %collective-permute-done.rest_1_.beside.after, ...), custom_call_target="tpu_custom_call" | custom-call | flops 805306368 | bytes 5242880 | tf_op jit(solution)/shard_map/weight_grads/pallas_call | solution.py:297
  (15 shorter events, 0.0 us)
Async XLA Ops:
  3.5 5.7 %copy-start.4 = (bf16[384,256]{1,0:T(8,128)(2,1)S(1)}, bf16[384,256]{1,0:T(8,128)(2,1)}, u32[]{:S(2)}) copy-start(bf16[384,256]{1,0:T(8,128)(2,1)} %weight_share.1.after) | copy-start | bytes 589828
  6.6 15.4 %collective-permute-start = (bf16[4,2,128,512]{3,2,1,0:T(8,128)(2,1)}, bf16[4,2,128,512]{3,2,1,0:T(8,128)(2,1)}, u32[]{:S(2)}, u32[]{:S(2)}) collective-permute-start(bf16[4,2,128,512]{3,2,1,0:T(8,128)(2,1)} %tokens_beside.1), channel_id=1, source_target_pairs={{0,64},{64,0},{1,65},{65,1},{2,66},{66,2},{3,67},{67,3},{4,68},{68... | collective-permute-start | bytes 3145736 | tf_op jit(solution)/shard_map/ppermute | solution.py:331
  9.2 22.7 %collective-permute-start.1 = (bf16[384,256]{1,0:T(8,128)(2,1)S(1)}, bf16[384,256]{1,0:T(8,128)(2,1)S(1)}, u32[]{:S(2)}, u32[]{:S(2)}) collective-permute-start(bf16[384,256]{1,0:T(8,128)(2,1)S(1)} %copy-done.4), channel_id=1, source_target_pairs={{0,384},{128,0},{256,128},{384,256},{1,385},{129,1},{257,129},{385... | collective-permute-start | bytes 589832 | tf_op jit(solution)/shard_map/ppermute | solution.py:323
  14.2 20.2 %collective-permute-start.2 = (bf16[384,256]{1,0:T(8,128)(2,1)S(1)}, bf16[384,256]{1,0:T(8,128)(2,1)S(1)}, u32[]{:S(2)}, u32[]{:S(2)}) collective-permute-start(bf16[384,256]{1,0:T(8,128)(2,1)S(1)} %copy-done.4), channel_id=1, source_target_pairs={{0,256},{128,384},{256,0},{384,128},{1,257},{129,385},{257,1},{385... | collective-permute-start | bytes 589832 | tf_op jit(solution)/shard_map/ppermute | solution.py:323
  18.7 18.3 %collective-permute-start.3 = (bf16[384,256]{1,0:T(8,128)(2,1)S(1)}, bf16[384,256]{1,0:T(8,128)(2,1)S(1)}, u32[]{:S(2)}, u32[]{:S(2)}) collective-permute-start(bf16[384,256]{1,0:T(8,128)(2,1)S(1)} %copy-done.4), channel_id=1, source_target_pairs={{0,128},{128,256},{256,384},{384,0},{1,129},{129,257},{257,385},{3... | collective-permute-start | bytes 589832 | tf_op jit(solution)/shard_map/ppermute | solution.py:323
  23.7 34.3 %all-to-all-start = ((f32[64,8,128]{2,1,0:T(8,128)}), f32[64,8,128]{2,1,0:T(8,128)}, u32[]{:S(2)}, u32[]{:S(2)}) async-start(f32[64,8,128]{2,1,0:T(8,128)} %bitcast.29), calls=%async_computation | async-start | bytes 524288 | tf_op jit(solution)/shard_map/all_to_all | solution.py:339
  41.2 36.6 %collective-permute-start.4 = (bf16[3,128,1024]{2,1,0:T(8,128)(2,1)}, bf16[3,128,1024]{2,1,0:T(8,128)(2,1)S(1)}, u32[]{:S(2)}, u32[]{:S(2)}) collective-permute-start(bf16[3,128,1024]{2,1,0:T(8,128)(2,1)} %get-tuple-element.14), channel_id=1, source_target_pairs={{0,128},{128,256},{256,384},{384,0},{1,129},{129,257},{257,385},{3... | collective-permute-start | bytes 2359304 | tf_op jit(solution)/shard_map/ppermute | solution.py:319
  45.2 38.0 %collective-permute-start.5 = (bf16[3,128,1024]{2,1,0:T(8,128)(2,1)}, bf16[3,128,1024]{2,1,0:T(8,128)(2,1)}, u32[]{:S(2)}, u32[]{:S(2)}) collective-permute-start(bf16[3,128,1024]{2,1,0:T(8,128)(2,1)} %get-tuple-element.15), channel_id=1, source_target_pairs={{0,384},{128,0},{256,128},{384,256},{1,385},{129,1},{257,129},{385... | collective-permute-start | bytes 2359304 | tf_op jit(solution)/shard_map/ppermute | solution.py:319
  48.9 43.6 %collective-permute-start.10 = (bf16[4,384,256]{2,1,0:T(8,128)(2,1)}, bf16[4,384,256]{2,1,0:T(8,128)(2,1)}, u32[]{:S(2)}, u32[]{:S(2)}) collective-permute-start(bf16[4,384,256]{2,1,0:T(8,128)(2,1)} %pad_maximum_fusion.rest_0_), channel_id=1, source_target_pairs={{0,16},{8,24},{16,0},{24,8},{1,17},{9,25},{17,1},{25,9},{2,18},{10... | collective-permute-start | bytes 2359304 | tf_op jit(solution)/shard_map/ppermute | solution.py:327
  52.7 39.9 %collective-permute-start.11 = (bf16[4,384,256]{2,1,0:T(8,128)(2,1)}, bf16[4,384,256]{2,1,0:T(8,128)(2,1)}, u32[]{:S(2)}, u32[]{:S(2)}) collective-permute-start(bf16[4,384,256]{2,1,0:T(8,128)(2,1)} %pad_maximum_fusion.rest_0_), channel_id=1, source_target_pairs={{0,8},{8,16},{16,24},{24,0},{1,9},{9,17},{17,25},{25,1},{2,10},{10... | collective-permute-start | bytes 2359304 | tf_op jit(solution)/shard_map/ppermute | solution.py:327
  54.6 38.0 %collective-permute-start.9 = (bf16[4,384,256]{2,1,0:T(8,128)(2,1)}, bf16[4,384,256]{2,1,0:T(8,128)(2,1)}, u32[]{:S(2)}, u32[]{:S(2)}) collective-permute-start(bf16[4,384,256]{2,1,0:T(8,128)(2,1)} %pad_maximum_fusion.rest_0_), channel_id=1, source_target_pairs={{0,24},{8,0},{16,8},{24,16},{1,25},{9,1},{17,9},{25,17},{2,26},{10... | collective-permute-start | bytes 2359304 | tf_op jit(solution)/shard_map/ppermute | solution.py:327
  59.7 50.5 %all-to-all-start.1 = ((f32[64,8,128]{2,1,0:T(8,128)}), f32[64,8,128]{2,1,0:T(8,128)}, u32[]{:S(2)}, u32[]{:S(2)}) async-start(f32[64,8,128]{2,1,0:T(8,128)} %broadcast_in_dim.2), calls=%async_computation.1 | async-start | bytes 524288 | tf_op jit(solution)/shard_map/all_to_all | solution.py:346
  77.8 5.3 %copy-start = (bf16[3,128,1024]{2,1,0:T(8,128)(2,1)}, bf16[3,128,1024]{2,1,0:T(8,128)(2,1)S(1)}, u32[]{:S(2)}) copy-start(bf16[3,128,1024]{2,1,0:T(8,128)(2,1)S(1)} %collective-permute-done.4.ahead) | copy-start | bytes 2359300
  85.0 11.4 %collective-permute-start.6 = (bf16[1,128,1024]{2,1,0:T(8,128)(2,1)}, bf16[1,128,1024]{2,1,0:T(8,128)(2,1)S(1)}, u32[]{:S(2)}, u32[]{:S(2)}) collective-permute-start(bf16[1,128,1024]{2,1,0:T(8,128)(2,1)} %get-tuple-element.16), channel_id=1, source_target_pairs={{0,128},{128,256},{256,384},{384,0},{1,129},{129,257},{257,385},{3... | collective-permute-start | bytes 786440 | tf_op jit(solution)/shard_map/ppermute | solution.py:319
  87.2 23.1 %copy-start.6 = (f32[16,4096]{1,0:T(8,128)S(1)}, f32[16,4096]{1,0:T(8,128)}, u32[]{:S(2)}) copy-start(f32[16,4096]{1,0:T(8,128)} %param.14) | copy-start | bytes 786436
  87.2 11.2 %collective-permute-start.7 = (bf16[1,128,1024]{2,1,0:T(8,128)(2,1)}, bf16[1,128,1024]{2,1,0:T(8,128)(2,1)S(1)}, u32[]{:S(2)}, u32[]{:S(2)}) collective-permute-start(bf16[1,128,1024]{2,1,0:T(8,128)(2,1)} %get-tuple-element.17), channel_id=1, source_target_pairs={{0,384},{128,0},{256,128},{384,256},{1,385},{129,1},{257,129},{385... | collective-permute-start | bytes 786440 | tf_op jit(solution)/shard_map/ppermute | solution.py:319
  96.4 1.9 %copy-start.2 = (bf16[1,128,1024]{2,1,0:T(8,128)(2,1)}, bf16[1,128,1024]{2,1,0:T(8,128)(2,1)S(1)}, u32[]{:S(2)}) copy-start(bf16[1,128,1024]{2,1,0:T(8,128)(2,1)S(1)} %collective-permute-done.6.far_x.rest_4_) | copy-start | bytes 786436
  98.3 0.7 copy-start.3
  104.4 7.7 %collective-permute-start.12 = (f32[3,128,256]{2,1,0:T(8,128)}, f32[3,128,256]{2,1,0:T(8,128)S(1)}, u32[]{:S(2)}, u32[]{:S(2)}) collective-permute-start(f32[3,128,256]{2,1,0:T(8,128)} %get-tuple-element.19), channel_id=1, source_target_pairs={{0,64},{64,0},{1,65},{65,1},{2,66},{66,2},{3,67},{67,3},{4,68},{68... | collective-permute-start | bytes 1179656 | tf_op jit(solution)/shard_map/ppermute | solution.py:331
  112.1 0.8 copy-start.5
  115.0 27.1 %all-to-all-start.2 = ((bf16[4,3,128,256]{3,2,1,0:T(8,128)(2,1)}), bf16[4,3,128,256]{3,2,1,0:T(8,128)(2,1)S(1)}, u32[]{:S(2)}, u32[]{:S(2)}) async-start(bf16[4,3,128,256]{3,2,1,0:T(8,128)(2,1)} %activation.1), calls=%async_computation.2 | async-start | bytes 1572864 | tf_op jit(solution)/shard_map/all_to_all | solution.py:376
  123.3 21.4 %collective-permute-start.8 = (bf16[3,2,128,512]{3,2,1,0:T(8,128)(2,1)}, bf16[3,2,128,512]{3,2,1,0:T(8,128)(2,1)}, u32[]{:S(2)}, u32[]{:S(2)}) collective-permute-start(bf16[3,2,128,512]{3,2,1,0:T(8,128)(2,1)} %repack_tokens.1), channel_id=1, source_target_pairs={{0,64},{64,0},{1,65},{65,1},{2,66},{66,2},{3,67},{67,3},{4,68},{68... | collective-permute-start | bytes 2359304 | tf_op jit(solution)/shard_map/ppermute | solution.py:331
  142.1 4.7 %copy-start.1 = (bf16[4,3,128,256]{3,2,1,0:T(8,128)(2,1)}, bf16[4,3,128,256]{3,2,1,0:T(8,128)(2,1)S(1)}, u32[]{:S(2)}) copy-start(bf16[4,3,128,256]{3,2,1,0:T(8,128)(2,1)S(1)} %all-to-all-done.2.rest_0_) | copy-start | bytes 2359300
  142.1 4.7 %collective-permute-start.13 = (bf16[4,3,128,256]{3,2,1,0:T(8,128)(2,1)S(1)}, bf16[4,3,128,256]{3,2,1,0:T(8,128)(2,1)}, u32[]{:S(2)}, u32[]{:S(2)}) collective-permute-start(bf16[4,3,128,256]{3,2,1,0:T(8,128)(2,1)S(1)} %all-to-all-done.2.rest_0_), channel_id=1, source_target_pairs={{0,64},{64,0},{1,65},{65,1},{2,66},{66,2},{3,67},{67,3},{4,68},{68... | collective-permute-start | bytes 2359304 | tf_op jit(solution)/shard_map/ppermute | solution.py:331

commit v7 on v6

--- a/solution.py
+++ b/solution.py
@@ -238,8 +238,8 @@
     )(place, x, dy, beside, *weights, *after)
 
 
-def activation_kernel(mine_ref, arrived_ref, after, out, mine, arrived, sems):
-    del after
+def activation_kernel(waited, mine_ref, arrived_ref, *rest):
+    out, mine, arrived, sems = rest[waited:]
     run_copies([(mine_ref, mine), (arrived_ref, arrived)], sems)
     gate = mine[0] + arrived[0]
     up = mine[1] + arrived[1]
@@ -254,9 +254,9 @@
 
 def activation(mine, arrived, after):
     return pl.pallas_call(
-        activation_kernel,
+        functools.partial(activation_kernel, len(after)),
         out_shape=jax.ShapeDtypeStruct((CHIPS, 3, ROWS, HID), BF16),
-        in_specs=[ANY] * 3,
+        in_specs=[ANY] * (2 + len(after)),
         out_specs=VMEM,
         scratch_shapes=[
             pltpu.VMEM((3, ROWS, HID), F32),
@@ -266,7 +266,7 @@
         compiler_params=pltpu.CompilerParams(vmem_limit_bytes=VMEM_LIMIT),
         cost_estimate=pl.CostEstimate(flops=20 * ROWS * HID, bytes_accessed=1 << 20, transcendentals=ROWS * HID),
         name="activation",
-    )(mine, arrived, after)
+    )(mine, arrived, *after)
 
 
 def grads_kernel(place, x, dy, beside, ahead, back, far_x, far_dy, swapped, *rest):
@@ -359,7 +359,7 @@
 
     beside = other_core(for_beside(place, x, dy, share))
     part = share_of_sum(staged(delta[0], beside))
-    ahead, back = pack(place, x, dy, (shares, beside))
+    ahead, back = pack(place, x, dy, (beside,))
     ahead, back = to_shift(ahead, 1), to_shift(back, 3)
     far_x, far_dy = onward(ahead, back)
     far_x, far_dy = to_shift(far_x, 1), to_shift(far_dy, 3)
@@ -372,7 +372,7 @@
     new_anchor = anchor - 0.7 * (pseudo + 0.9 * new_momentum)
 
     mine, theirs = hidden_sums(place, x, dy, beside, weights, (far_x, far_dy))
-    acts = activation(mine, other_core(theirs), new_anchor)
+    acts = activation(mine, other_core(theirs), (pseudo,))
     acts = lax.all_to_all(acts, "yh", 0, 0, tiled=True)
     acts = (acts, other_core(acts))
     grad_gate, grad_up, grad_down = grads(place, x, dy, beside, arrived, swapped, acts)

time: 153 us -> 155 us (1.013)
  the two profiles are of different devices: /device:TPU:459 before, /device:TPU:11 now
where the time goes in v7:
time: 155 us; the launch traced here: 154 us
  starting transfers between devices  75.7 us (49%)
  waiting for transfers between devices  41.9 us (27%)
  Pallas kernels  27.1 us (17%)
  other arithmetic  4.74 us (3%)
  local copies, waits for them, and re-layouts  3.07 us (2%)
    all_to_all x1, waiting for transfers between devices, share_of_sum(): lax.all_to_all(tiles, everyone, 0, 0, tiled=True)  17.5 us
    all_to_all x1, waiting for transfers between devices, on_device(): acts = lax.all_to_all(acts, 'yh', 0, 0, tiled=True)  15.8 us
    ppermute x4, starting transfers between devices, to_shift(): lax.ppermute(value, 'yh', [(i, (i + shift) % CHIPS) for i in range(CHIPS)])  14.8 us
    all_to_all x1, starting transfers between devices, share_of_sum(): lax.all_to_all(tiles, everyone, 0, 0, tiled=True)  14.4 us
    ppermute x3, starting transfers between devices, from_shift(): lax.ppermute(value, 'yh', [(i, (i - shift) % CHIPS) for i in range(CHIPS)])  12.7 us
    ppermute x4, starting transfers between devices, other_core(): return lax.ppermute(value, 'core', [(0, 1), (1, 0)])  11.6 us
    ppermute x3, starting transfers between devices, from_x(): lax.ppermute(value, 'x', [(i, (i - shift) % size) for i in range(size)])  9.03 us
    all_to_all x1, starting transfers between devices, whole_mean(): lax.all_to_all(jnp.broadcast_to(part / count, (count, 8, 128)), everyone,...  8.03 us
  transfers between devices with their start and end apart: 17, of which 7 were waited for; matrix products, arithmetic and copies ran while one was open for 3% of the time, Pallas kernels for 10%

profile of v7, /device:TPU:11, one launch (start us, length us, event | category | flops | bytes accessed | tf_op | source)
XLA Modules:
  0.0 153.6 jit_solution(15270662602450346185)
XLA Ops:
  0.6 0.6 pad_add_fusion.place
  1.2 2.2 %weight_share.1.after = bf16[384,256]{1,0:T(8,128)(2,1)} custom-call(s32[3]{0:T(128)} %pad_add_fusion.place, bf16[512,256]{1,0:T(8,128)(2,1)} %gate.1, bf16[512,256]{1,0:T(8,128)(2,1)} %up.1, bf16[256,512]{1,0:T(8,128)(2,1)} %down.1), custom_call_target="tpu_custom_call" | custom-call | bytes 262144 | tf_op jit(solution)/shard_map/weight_share/pallas_call | solution.py:57
  3.5 0.0 copy-start.5
  3.5 3.1 %tokens_beside.1 = bf16[4,2,128,512]{3,2,1,0:T(8,128)(2,1)} custom-call(s32[3]{0:T(128)} %pad_add_fusion.place, bf16[128,4096]{1,0:T(8,128)(2,1)} %bitcast.20, bf16[128,4096]{1,0:T(8,128)(2,1)} %bitcast.24, bf16[384,256]{1,0:T(8,128)(2,1)} %weight_share.1.after), custom_call_target="tpu_custom_call" | custom-call | bytes 2097152 | tf_op jit(solution)/shard_map/tokens_beside/pallas_call | solution.py:79
  6.6 2.6 %collective-permute-start = (bf16[4,2,128,512]{3,2,1,0:T(8,128)(2,1)}, bf16[4,2,128,512]{3,2,1,0:T(8,128)(2,1)}, u32[]{:S(2)}, u32[]{:S(2)}) collective-permute-start(bf16[4,2,128,512]{3,2,1,0:T(8,128)(2,1)} %tokens_beside.1), channel_id=1, source_target_pairs={{0,64},{64,0},{1,65},{65,1},{2,66},{66,2},{3,67},{67,3},{4,68},{68... | collective-permute-start | bytes 3145736 | tf_op jit(solution)/shard_map/ppermute | solution.py:331
  9.3 5.0 %collective-permute-start.6 = (bf16[384,256]{1,0:T(8,128)(2,1)S(1)}, bf16[384,256]{1,0:T(8,128)(2,1)}, u32[]{:S(2)}, u32[]{:S(2)}) collective-permute-start(bf16[384,256]{1,0:T(8,128)(2,1)S(1)} %copy-done.5), channel_id=1, source_target_pairs={{0,384},{128,0},{256,128},{384,256},{1,385},{129,1},{257,129},{385... | collective-permute-start | bytes 589832 | tf_op jit(solution)/shard_map/ppermute | solution.py:323
  14.2 4.4 %collective-permute-start.7 = (bf16[384,256]{1,0:T(8,128)(2,1)S(1)}, bf16[384,256]{1,0:T(8,128)(2,1)}, u32[]{:S(2)}, u32[]{:S(2)}) collective-permute-start(bf16[384,256]{1,0:T(8,128)(2,1)S(1)} %copy-done.5), channel_id=1, source_target_pairs={{0,256},{128,384},{256,0},{384,128},{1,257},{129,385},{257,1},{385... | collective-permute-start | bytes 589832 | tf_op jit(solution)/shard_map/ppermute | solution.py:323
  18.7 3.3 %collective-permute-start.8 = (bf16[384,256]{1,0:T(8,128)(2,1)S(1)}, bf16[384,256]{1,0:T(8,128)(2,1)}, u32[]{:S(2)}, u32[]{:S(2)}) collective-permute-start(bf16[384,256]{1,0:T(8,128)(2,1)S(1)} %copy-done.5), channel_id=1, source_target_pairs={{0,128},{128,256},{256,384},{384,0},{1,129},{129,257},{257,385},{3... | collective-permute-start | bytes 589832 | tf_op jit(solution)/shard_map/ppermute | solution.py:323
  22.0 0.0 collective-permute-done.rest_0_.beside.after
  22.0 3.2 %pack_tokens.1 = (bf16[3,128,1024]{2,1,0:T(8,128)(2,1)}, bf16[3,128,1024]{2,1,0:T(8,128)(2,1)}) custom-call(s32[3]{0:T(128)} %pad_add_fusion.place, bf16[128,4096]{1,0:T(8,128)(2,1)} %bitcast.21, bf16[128,4096]{1,0:T(8,128)(2,1)} %bitcast.25, bf16[4,2,128,512]{3,2,1,0:T(8,128)(2,1)} %collective-permute-done.rest_0_.beside.after), custom_call_target="tpu_custom_call" | custom-call | bytes 4194304 | tf_op jit(solution)/shard_map/pack_tokens/pallas_call | solution.py:108
  25.3 3.6 %collective-permute-start.1 = (bf16[3,128,1024]{2,1,0:T(8,128)(2,1)}, bf16[3,128,1024]{2,1,0:T(8,128)(2,1)S(1)}, u32[]{:S(2)}, u32[]{:S(2)}) collective-permute-start(bf16[3,128,1024]{2,1,0:T(8,128)(2,1)} %get-tuple-element.14), channel_id=1, source_target_pairs={{0,128},{128,256},{256,384},{384,0},{1,129},{129,257},{257,385},{3... | collective-permute-start | bytes 2359304 | tf_op jit(solution)/shard_map/ppermute | solution.py:319
  28.9 3.8 %collective-permute-start.2 = (bf16[3,128,1024]{2,1,0:T(8,128)(2,1)}, bf16[3,128,1024]{2,1,0:T(8,128)(2,1)}, u32[]{:S(2)}, u32[]{:S(2)}) collective-permute-start(bf16[3,128,1024]{2,1,0:T(8,128)(2,1)} %get-tuple-element.15), channel_id=1, source_target_pairs={{0,384},{128,0},{256,128},{384,256},{1,385},{129,1},{257,129},{385... | collective-permute-start | bytes 2359304 | tf_op jit(solution)/shard_map/ppermute | solution.py:319
  32.7 1.7 %delta_staged.1 = f32[16,4096]{1,0:T(8,128)} custom-call(f32[16,4096]{1,0:T(8,128)} %bitcast.32, bf16[4,2,128,512]{3,2,1,0:T(8,128)(2,1)} %collective-permute-done.rest_0_.beside.after), custom_call_target="tpu_custom_call" | custom-call | bytes 524288 | tf_op jit(solution)/shard_map/delta_staged/pallas_call | solution.py:165
  34.3 14.4 %all-to-all-start = ((f32[64,8,128]{2,1,0:T(8,128)}), f32[64,8,128]{2,1,0:T(8,128)S(1)}, u32[]{:S(2)}, u32[]{:S(2)}) async-start(f32[64,8,128]{2,1,0:T(8,128)} %bitcast.31), calls=%async_computation | async-start | bytes 524288 | tf_op jit(solution)/shard_map/all_to_all | solution.py:339
  48.7 0.0 collective-permute-done.6
  48.7 5.1 %collective-permute-done.8 = bf16[384,256]{1,0:T(8,128)(2,1)} collective-permute-done((bf16[384,256]{1,0:T(8,128)(2,1)S(1)}, bf16[384,256]{1,0:T(8,128)(2,1)}, u32[]{:S(2)}, u32[]{:S(2)}) %collective-permute-start.8) | collective-permute-done | bytes 196640 | tf_op jit(solution)/shard_map/ppermute | solution.py:323
  53.9 2.1 %pad_maximum_fusion.rest_0_ = bf16[4,384,256]{2,1,0:T(8,128)(2,1)} fusion(bf16[1,384,256]{2,1,0:T(8,128)(2,1)} %bitcast.8, bf16[1,384,256]{2,1,0:T(8,128)(2,1)} %bitcast.7, bf16[1,384,256]{2,1,0:T(8,128)(2,1)} %bitcast.6, bf16[1,384,256]{2,1,0:T(8,128)(2,1)S(1)} %bitcast.30), kind=kLoop, calls=%fused_computation | loop fusion | flops 1179648 | bytes 1572864 | tf_op jit(solution)/shard_map/stack | solution.py:357
  55.9 3.7 %collective-permute-start.10 = (bf16[4,384,256]{2,1,0:T(8,128)(2,1)}, bf16[4,384,256]{2,1,0:T(8,128)(2,1)}, u32[]{:S(2)}, u32[]{:S(2)}) collective-permute-start(bf16[4,384,256]{2,1,0:T(8,128)(2,1)} %pad_maximum_fusion.rest_0_), channel_id=1, source_target_pairs={{0,16},{8,24},{16,0},{24,8},{1,17},{9,25},{17,1},{25,9},{2,18},{10... | collective-permute-start | bytes 2359304 | tf_op jit(solution)/shard_map/ppermute | solution.py:327
  59.7 2.1 %collective-permute-start.11 = (bf16[4,384,256]{2,1,0:T(8,128)(2,1)}, bf16[4,384,256]{2,1,0:T(8,128)(2,1)}, u32[]{:S(2)}, u32[]{:S(2)}) collective-permute-start(bf16[4,384,256]{2,1,0:T(8,128)(2,1)} %pad_maximum_fusion.rest_0_), channel_id=1, source_target_pairs={{0,8},{8,16},{16,24},{24,0},{1,9},{9,17},{17,25},{25,1},{2,10},{10... | collective-permute-start | bytes 2359304 | tf_op jit(solution)/shard_map/ppermute | solution.py:327
  61.8 3.2 %collective-permute-start.9 = (bf16[4,384,256]{2,1,0:T(8,128)(2,1)}, bf16[4,384,256]{2,1,0:T(8,128)(2,1)}, u32[]{:S(2)}, u32[]{:S(2)}) collective-permute-start(bf16[4,384,256]{2,1,0:T(8,128)(2,1)} %pad_maximum_fusion.rest_0_), channel_id=1, source_target_pairs={{0,24},{8,0},{16,8},{24,16},{1,25},{9,1},{17,9},{25,17},{2,26},{10... | collective-permute-start | bytes 2359304 | tf_op jit(solution)/shard_map/ppermute | solution.py:327
  65.0 17.5 %all-to-all-done = f32[64,8,128]{2,1,0:T(8,128)S(1)} async-done(((f32[64,8,128]{2,1,0:T(8,128)}), f32[64,8,128]{2,1,0:T(8,128)S(1)}, u32[]{:S(2)}, u32[]{:S(2)}) %all-to-all-start) | async-done | bytes 262176 | tf_op jit(solution)/shard_map/all_to_all | solution.py:339
  82.5 0.1 reduce_sum.9
  82.6 0.0 collective-permute-done.2.back
  82.6 0.9 copy-done
  83.5 1.8 %onward.1 = (bf16[1,128,1024]{2,1,0:T(8,128)(2,1)}, bf16[1,128,1024]{2,1,0:T(8,128)(2,1)}) custom-call(bf16[3,128,1024]{2,1,0:T(8,128)(2,1)} %copy-done, bf16[3,128,1024]{2,1,0:T(8,128)(2,1)} %collective-permute-done.2.back), custom_call_target="tpu_custom_call" | custom-call | bytes 104857600 | tf_op jit(solution)/shard_map/onward/pallas_call | solution.py:126
  85.3 3.8 %collective-permute-start.3 = (bf16[1,128,1024]{2,1,0:T(8,128)(2,1)}, bf16[1,128,1024]{2,1,0:T(8,128)(2,1)S(1)}, u32[]{:S(2)}, u32[]{:S(2)}) collective-permute-start(bf16[1,128,1024]{2,1,0:T(8,128)(2,1)} %get-tuple-element.16), channel_id=1, source_target_pairs={{0,128},{128,256},{256,384},{384,0},{1,129},{129,257},{257,385},{3... | collective-permute-start | bytes 786440 | tf_op jit(solution)/shard_map/ppermute | solution.py:319
  89.1 3.6 %collective-permute-start.4 = (bf16[1,128,1024]{2,1,0:T(8,128)(2,1)}, bf16[1,128,1024]{2,1,0:T(8,128)(2,1)S(1)}, u32[]{:S(2)}, u32[]{:S(2)}) collective-permute-start(bf16[1,128,1024]{2,1,0:T(8,128)(2,1)} %get-tuple-element.17), channel_id=1, source_target_pairs={{0,384},{128,0},{256,128},{384,256},{1,385},{129,1},{257,129},{385... | collective-permute-start | bytes 786440 | tf_op jit(solution)/shard_map/ppermute | solution.py:319
  92.7 0.7 broadcast_in_dim.2
  93.5 8.0 %all-to-all-start.1 = ((f32[64,8,128]{2,1,0:T(8,128)}), f32[64,8,128]{2,1,0:T(8,128)S(1)}, u32[]{:S(2)}, u32[]{:S(2)}) async-start(f32[64,8,128]{2,1,0:T(8,128)} %broadcast_in_dim.2), calls=%async_computation.1 | async-start | bytes 524288 | tf_op jit(solution)/shard_map/all_to_all | solution.py:346
  101.5 0.0 collective-permute-done.10.rest_2_
  101.5 0.0 collective-permute-done.9.rest_1_
  101.6 1.9 %collective-permute-done.4.far_dy.rest_5_ = bf16[1,128,1024]{2,1,0:T(8,128)(2,1)S(1)} collective-permute-done((bf16[1,128,1024]{2,1,0:T(8,128)(2,1)}, bf16[1,128,1024]{2,1,0:T(8,128)(2,1)S(1)}, u32[]{:S(2)}, u32[]{:S(2)}) %collective-permute-start.4) | collective-permute-done | bytes 262176 | tf_op jit(solution)/shard_map/ppermute | solution.py:319
  103.5 0.7 copy-done.3
  104.2 5.4 %hidden_sums.1 = (f32[3,128,256]{2,1,0:T(8,128)}, f32[3,128,256]{2,1,0:T(8,128)}) custom-call(s32[3]{0:T(128)} %pad_add_fusion.place, bf16[128,4096]{1,0:T(8,128)(2,1)} %bitcast.22, bf16[128,4096]{1,0:T(8,128)(2,1)} %bitcast.26, bf16[4,2,128,512]{3,2,1,0:T(8,128)(2,1)} %collective-permute-done.rest_0_.beside.after, ...), custom_call_target="tpu_custom_call" | custom-call | flops 805306368 | bytes 6291456 | tf_op jit(solution)/shard_map/hidden_sums/pallas_call | solution.py:222
  109.6 2.6 %collective-permute-start.12 = (f32[3,128,256]{2,1,0:T(8,128)}, f32[3,128,256]{2,1,0:T(8,128)S(1)}, u32[]{:S(2)}, u32[]{:S(2)}) collective-permute-start(f32[3,128,256]{2,1,0:T(8,128)} %get-tuple-element.19), channel_id=1, source_target_pairs={{0,64},{64,0},{1,65},{65,1},{2,66},{66,2},{3,67},{67,3},{4,68},{68... | collective-permute-start | bytes 1179656 | tf_op jit(solution)/shard_map/ppermute | solution.py:331
  112.2 0.9 all-to-all-done.1
  113.1 0.7 collective-permute-done.12.arrived_ref
  113.8 0.0 copy-done.4
  113.8 0.7 copy-done.6
  114.5 2.1 %activation.1 = bf16[4,3,128,256]{3,2,1,0:T(8,128)(2,1)} custom-call(f32[3,128,256]{2,1,0:T(8,128)} %get-tuple-element.18.mine_ref, f32[3,128,256]{2,1,0:T(8,128)} %copy-done.6, f32[16,4096]{1,0:T(8,128)} %bitcast.28), custom_call_target="tpu_custom_call" | custom-call | flops 655360 | bytes 1048576 | tf_op jit(solution)/shard_map/activation/pallas_call | solution.py:256
  116.7 5.2 %all-to-all-start.2 = ((bf16[4,3,128,256]{3,2,1,0:T(8,128)(2,1)}), bf16[4,3,128,256]{3,2,1,0:T(8,128)(2,1)S(1)}, u32[]{:S(2)}, u32[]{:S(2)}) async-start(bf16[4,3,128,256]{3,2,1,0:T(8,128)(2,1)} %activation.1), calls=%async_computation.2 | async-start | bytes 1572864 | tf_op jit(solution)/shard_map/all_to_all | solution.py:376
  121.9 2.8 %repack_tokens.1 = bf16[3,2,128,512]{3,2,1,0:T(8,128)(2,1)} custom-call(s32[3]{0:T(128)} %pad_add_fusion.place, bf16[3,128,1024]{2,1,0:T(8,128)(2,1)} %copy-done, bf16[3,128,1024]{2,1,0:T(8,128)(2,1)} %collective-permute-done.2.back, bf16[1,128,1024]{2,1,0:T(8,128)(2,1)} %copy-done.2, bf16[1,128,1024]{2,1,0:T(8,128)(2,1)} %copy-done.3), custom_call_target="tpu_custom_call" | custom-call | bytes 209715200 | tf_op jit(solution)/shard_map/repack_tokens/pallas_call | solution.py:147
  124.7 3.0 %collective-permute-start.5 = (bf16[3,2,128,512]{3,2,1,0:T(8,128)(2,1)}, bf16[3,2,128,512]{3,2,1,0:T(8,128)(2,1)}, u32[]{:S(2)}, u32[]{:S(2)}) collective-permute-start(bf16[3,2,128,512]{3,2,1,0:T(8,128)(2,1)} %repack_tokens.1), channel_id=1, source_target_pairs={{0,64},{64,0},{1,65},{65,1},{2,66},{66,2},{3,67},{67,3},{4,68},{68... | collective-permute-start | bytes 2359304 | tf_op jit(solution)/shard_map/ppermute | solution.py:331
  127.7 15.8 %all-to-all-done.2.rest_0_ = bf16[4,3,128,256]{3,2,1,0:T(8,128)(2,1)S(1)} async-done(((bf16[4,3,128,256]{3,2,1,0:T(8,128)(2,1)}), bf16[4,3,128,256]{3,2,1,0:T(8,128)(2,1)S(1)}, u32[]{:S(2)}, u32[]{:S(2)}) %all-to-all-start.2) | async-done | bytes 786464 | tf_op jit(solution)/shard_map/all_to_all | solution.py:376
  143.5 3.3 %collective-permute-start.13 = (bf16[4,3,128,256]{3,2,1,0:T(8,128)(2,1)S(1)}, bf16[4,3,128,256]{3,2,1,0:T(8,128)(2,1)}, u32[]{:S(2)}, u32[]{:S(2)}) collective-permute-start(bf16[4,3,128,256]{3,2,1,0:T(8,128)(2,1)S(1)} %all-to-all-done.2.rest_0_), channel_id=1, source_target_pairs={{0,64},{64,0},{1,65},{65,1},{2,66},{66,2},{3,67},{67,3},{4,68},{68... | collective-permute-start | bytes 2359304 | tf_op jit(solution)/shard_map/ppermute | solution.py:331
  146.9 2.0 %multiply_subtract_fusion = (f32[16,4096]{1,0:T(8,128)}, f32[16,4096]{1,0:T(8,128)}) fusion(f32[16,4096]{1,0:T(8,128)} %param.14, f32[16,4096]{1,0:T(8,128)} %bitcast.29, f32[16,4096]{1,0:T(8,128)} %param.15), kind=kLoop, calls=%fused_computation.1 | loop fusion | flops 393216 | bytes 1310720 | tf_op jit(solution)/shard_map/sub | solution.py:372
  148.8 0.1 collective-permute-done.13.rest_1_
  148.9 4.7 %weight_grads.1 = (bf16[1,512,256]{2,1,0:T(8,128)(2,1)}, bf16[1,512,256]{2,1,0:T(8,128)(2,1)}, bf16[1,256,512]{2,1,0:T(8,128)(2,1)}) custom-call(s32[3]{0:T(128)} %pad_add_fusion.place, bf16[128,4096]{1,0:T(8,128)(2,1)} %bitcast.23, bf16[128,4096]{1,0:T(8,128)(2,1)} %bitcast.27, bf16[4,2,128,512]{3,2,1,0:T(8,128)(2,1)} %collective-permute-done.rest_0_.beside.after, ...), custom_call_target="tpu_custom_call" | custom-call | flops 805306368 | bytes 5242880 | tf_op jit(solution)/shard_map/weight_grads/pallas_call | solution.py:297
  (15 shorter events, 0.0 us)
Async XLA Ops:
  3.5 5.7 %copy-start.5 = (bf16[384,256]{1,0:T(8,128)(2,1)S(1)}, bf16[384,256]{1,0:T(8,128)(2,1)}, u32[]{:S(2)}) copy-start(bf16[384,256]{1,0:T(8,128)(2,1)} %weight_share.1.after) | copy-start | bytes 589828
  6.6 15.4 %collective-permute-start = (bf16[4,2,128,512]{3,2,1,0:T(8,128)(2,1)}, bf16[4,2,128,512]{3,2,1,0:T(8,128)(2,1)}, u32[]{:S(2)}, u32[]{:S(2)}) collective-permute-start(bf16[4,2,128,512]{3,2,1,0:T(8,128)(2,1)} %tokens_beside.1), channel_id=1, source_target_pairs={{0,64},{64,0},{1,65},{65,1},{2,66},{66,2},{3,67},{67,3},{4,68},{68... | collective-permute-start | bytes 3145736 | tf_op jit(solution)/shard_map/ppermute | solution.py:331
  9.3 39.5 %collective-permute-start.6 = (bf16[384,256]{1,0:T(8,128)(2,1)S(1)}, bf16[384,256]{1,0:T(8,128)(2,1)}, u32[]{:S(2)}, u32[]{:S(2)}) collective-permute-start(bf16[384,256]{1,0:T(8,128)(2,1)S(1)} %copy-done.5), channel_id=1, source_target_pairs={{0,384},{128,0},{256,128},{384,256},{1,385},{129,1},{257,129},{385... | collective-permute-start | bytes 589832 | tf_op jit(solution)/shard_map/ppermute | solution.py:323
  14.2 34.5 %collective-permute-start.7 = (bf16[384,256]{1,0:T(8,128)(2,1)S(1)}, bf16[384,256]{1,0:T(8,128)(2,1)}, u32[]{:S(2)}, u32[]{:S(2)}) collective-permute-start(bf16[384,256]{1,0:T(8,128)(2,1)S(1)} %copy-done.5), channel_id=1, source_target_pairs={{0,256},{128,384},{256,0},{384,128},{1,257},{129,385},{257,1},{385... | collective-permute-start | bytes 589832 | tf_op jit(solution)/shard_map/ppermute | solution.py:323
  18.7 35.2 %collective-permute-start.8 = (bf16[384,256]{1,0:T(8,128)(2,1)S(1)}, bf16[384,256]{1,0:T(8,128)(2,1)}, u32[]{:S(2)}, u32[]{:S(2)}) collective-permute-start(bf16[384,256]{1,0:T(8,128)(2,1)S(1)} %copy-done.5), channel_id=1, source_target_pairs={{0,128},{128,256},{256,384},{384,0},{1,129},{129,257},{257,385},{3... | collective-permute-start | bytes 589832 | tf_op jit(solution)/shard_map/ppermute | solution.py:323
  25.3 57.3 %collective-permute-start.1 = (bf16[3,128,1024]{2,1,0:T(8,128)(2,1)}, bf16[3,128,1024]{2,1,0:T(8,128)(2,1)S(1)}, u32[]{:S(2)}, u32[]{:S(2)}) collective-permute-start(bf16[3,128,1024]{2,1,0:T(8,128)(2,1)} %get-tuple-element.14), channel_id=1, source_target_pairs={{0,128},{128,256},{256,384},{384,0},{1,129},{129,257},{257,385},{3... | collective-permute-start | bytes 2359304 | tf_op jit(solution)/shard_map/ppermute | solution.py:319
  28.9 53.7 %collective-permute-start.2 = (bf16[3,128,1024]{2,1,0:T(8,128)(2,1)}, bf16[3,128,1024]{2,1,0:T(8,128)(2,1)}, u32[]{:S(2)}, u32[]{:S(2)}) collective-permute-start(bf16[3,128,1024]{2,1,0:T(8,128)(2,1)} %get-tuple-element.15), channel_id=1, source_target_pairs={{0,384},{128,0},{256,128},{384,256},{1,385},{129,1},{257,129},{385... | collective-permute-start | bytes 2359304 | tf_op jit(solution)/shard_map/ppermute | solution.py:319
  34.3 48.2 %all-to-all-start = ((f32[64,8,128]{2,1,0:T(8,128)}), f32[64,8,128]{2,1,0:T(8,128)S(1)}, u32[]{:S(2)}, u32[]{:S(2)}) async-start(f32[64,8,128]{2,1,0:T(8,128)} %bitcast.31), calls=%async_computation | async-start | bytes 524288 | tf_op jit(solution)/shard_map/all_to_all | solution.py:339
  55.9 45.6 %collective-permute-start.10 = (bf16[4,384,256]{2,1,0:T(8,128)(2,1)}, bf16[4,384,256]{2,1,0:T(8,128)(2,1)}, u32[]{:S(2)}, u32[]{:S(2)}) collective-permute-start(bf16[4,384,256]{2,1,0:T(8,128)(2,1)} %pad_maximum_fusion.rest_0_), channel_id=1, source_target_pairs={{0,16},{8,24},{16,0},{24,8},{1,17},{9,25},{17,1},{25,9},{2,18},{10... | collective-permute-start | bytes 2359304 | tf_op jit(solution)/shard_map/ppermute | solution.py:327
  59.7 41.8 %collective-permute-start.11 = (bf16[4,384,256]{2,1,0:T(8,128)(2,1)}, bf16[4,384,256]{2,1,0:T(8,128)(2,1)}, u32[]{:S(2)}, u32[]{:S(2)}) collective-permute-start(bf16[4,384,256]{2,1,0:T(8,128)(2,1)} %pad_maximum_fusion.rest_0_), channel_id=1, source_target_pairs={{0,8},{8,16},{16,24},{24,0},{1,9},{9,17},{17,25},{25,1},{2,10},{10... | collective-permute-start | bytes 2359304 | tf_op jit(solution)/shard_map/ppermute | solution.py:327
  61.8 39.8 %collective-permute-start.9 = (bf16[4,384,256]{2,1,0:T(8,128)(2,1)}, bf16[4,384,256]{2,1,0:T(8,128)(2,1)}, u32[]{:S(2)}, u32[]{:S(2)}) collective-permute-start(bf16[4,384,256]{2,1,0:T(8,128)(2,1)} %pad_maximum_fusion.rest_0_), channel_id=1, source_target_pairs={{0,24},{8,0},{16,8},{24,16},{1,25},{9,1},{17,9},{25,17},{2,26},{10... | collective-permute-start | bytes 2359304 | tf_op jit(solution)/shard_map/ppermute | solution.py:327
  82.6 0.9 copy-start
  85.3 16.2 %collective-permute-start.3 = (bf16[1,128,1024]{2,1,0:T(8,128)(2,1)}, bf16[1,128,1024]{2,1,0:T(8,128)(2,1)S(1)}, u32[]{:S(2)}, u32[]{:S(2)}) collective-permute-start(bf16[1,128,1024]{2,1,0:T(8,128)(2,1)} %get-tuple-element.16), channel_id=1, source_target_pairs={{0,128},{128,256},{256,384},{384,0},{1,129},{129,257},{257,385},{3... | collective-permute-start | bytes 786440 | tf_op jit(solution)/shard_map/ppermute | solution.py:319
  89.1 14.3 %collective-permute-start.4 = (bf16[1,128,1024]{2,1,0:T(8,128)(2,1)}, bf16[1,128,1024]{2,1,0:T(8,128)(2,1)S(1)}, u32[]{:S(2)}, u32[]{:S(2)}) collective-permute-start(bf16[1,128,1024]{2,1,0:T(8,128)(2,1)} %get-tuple-element.17), channel_id=1, source_target_pairs={{0,384},{128,0},{256,128},{384,256},{1,385},{129,1},{257,129},{385... | collective-permute-start | bytes 786440 | tf_op jit(solution)/shard_map/ppermute | solution.py:319
  93.5 19.6 %all-to-all-start.1 = ((f32[64,8,128]{2,1,0:T(8,128)}), f32[64,8,128]{2,1,0:T(8,128)S(1)}, u32[]{:S(2)}, u32[]{:S(2)}) async-start(f32[64,8,128]{2,1,0:T(8,128)} %broadcast_in_dim.2), calls=%async_computation.1 | async-start | bytes 524288 | tf_op jit(solution)/shard_map/all_to_all | solution.py:346
  101.5 1.9 %copy-start.2 = (bf16[1,128,1024]{2,1,0:T(8,128)(2,1)}, bf16[1,128,1024]{2,1,0:T(8,128)(2,1)S(1)}, u32[]{:S(2)}) copy-start(bf16[1,128,1024]{2,1,0:T(8,128)(2,1)S(1)} %collective-permute-done.3.far_x.rest_4_) | copy-start | bytes 786436
  103.5 0.7 copy-start.3
  109.6 4.2 %collective-permute-start.12 = (f32[3,128,256]{2,1,0:T(8,128)}, f32[3,128,256]{2,1,0:T(8,128)S(1)}, u32[]{:S(2)}, u32[]{:S(2)}) collective-permute-start(f32[3,128,256]{2,1,0:T(8,128)} %get-tuple-element.19), channel_id=1, source_target_pairs={{0,64},{64,0},{1,65},{65,1},{2,66},{66,2},{3,67},{67,3},{4,68},{68... | collective-permute-start | bytes 1179656 | tf_op jit(solution)/shard_map/ppermute | solution.py:331
  113.1 0.7 copy-start.4
  113.8 0.8 copy-start.6
  116.7 26.8 %all-to-all-start.2 = ((bf16[4,3,128,256]{3,2,1,0:T(8,128)(2,1)}), bf16[4,3,128,256]{3,2,1,0:T(8,128)(2,1)S(1)}, u32[]{:S(2)}, u32[]{:S(2)}) async-start(bf16[4,3,128,256]{3,2,1,0:T(8,128)(2,1)} %activation.1), calls=%async_computation.2 | async-start | bytes 1572864 | tf_op jit(solution)/shard_map/all_to_all | solution.py:376
  124.7 24.1 %collective-permute-start.5 = (bf16[3,2,128,512]{3,2,1,0:T(8,128)(2,1)}, bf16[3,2,128,512]{3,2,1,0:T(8,128)(2,1)}, u32[]{:S(2)}, u32[]{:S(2)}) collective-permute-start(bf16[3,2,128,512]{3,2,1,0:T(8,128)(2,1)} %repack_tokens.1), channel_id=1, source_target_pairs={{0,64},{64,0},{1,65},{65,1},{2,66},{66,2},{3,67},{67,3},{4,68},{68... | collective-permute-start | bytes 2359304 | tf_op jit(solution)/shard_map/ppermute | solution.py:331
  143.5 5.4 %copy-start.1 = (bf16[4,3,128,256]{3,2,1,0:T(8,128)(2,1)}, bf16[4,3,128,256]{3,2,1,0:T(8,128)(2,1)S(1)}, u32[]{:S(2)}) copy-start(bf16[4,3,128,256]{3,2,1,0:T(8,128)(2,1)S(1)} %all-to-all-done.2.rest_0_) | copy-start | bytes 2359300
  143.5 5.4 %collective-permute-start.13 = (bf16[4,3,128,256]{3,2,1,0:T(8,128)(2,1)S(1)}, bf16[4,3,128,256]{3,2,1,0:T(8,128)(2,1)}, u32[]{:S(2)}, u32[]{:S(2)}) collective-permute-start(bf16[4,3,128,256]{3,2,1,0:T(8,128)(2,1)S(1)} %all-to-all-done.2.rest_0_), channel_id=1, source_target_pairs={{0,64},{64,0},{1,65},{65,1},{2,66},{66,2},{3,67},{67,3},{4,68},{68... | collective-permute-start | bytes 2359304 | tf_op jit(solution)/shard_map/ppermute | solution.py:331

commit v8 on v7

--- a/solution.py
+++ b/solution.py
@@ -331,19 +331,34 @@
     return lax.ppermute(value, "core", [(0, 1), (1, 0)])
 
 
-def share_of_sum(delta):
+def mean_kernel(waited, parts, *rest):
+    out, held, sems = rest[waited:]
+    run_copies([(parts, held)], sems)
+    count = parts.shape[0]
+    mean = jnp.sum(held[...], axis=0, keepdims=True) / count
+    out[...] = jnp.broadcast_to(mean, out.shape)
+
+
+def mean_tile(parts, after):
+    return pl.pallas_call(
+        functools.partial(mean_kernel, len(after)),
+        out_shape=jax.ShapeDtypeStruct(parts.shape, F32),
+        in_specs=[ANY] * (1 + len(after)),
+        out_specs=VMEM,
+        scratch_shapes=[pltpu.VMEM(parts.shape, F32), pltpu.SemaphoreType.DMA((1,))],
+        compiler_params=pltpu.CompilerParams(vmem_limit_bytes=VMEM_LIMIT),
+        cost_estimate=pl.CostEstimate(flops=1 << 16, bytes_accessed=1 << 19, transcendentals=0),
+        name="mean_tile",
+    )(parts, *after)
+
+
+def mean_of_replicas(delta, after):
     everyone = ("yl", "x", "z")
     count = lax.axis_size(everyone)
     rows, cols = delta.shape
     tiles = delta.reshape(rows // 8, 8, cols // 128, 128).transpose(0, 2, 1, 3).reshape(count, 8, 128)
-    return jnp.sum(lax.all_to_all(tiles, everyone, 0, 0, tiled=True), axis=0, keepdims=True)
-
-
-def whole_mean(part, shape):
-    everyone = ("yl", "x", "z")
-    count = lax.axis_size(everyone)
-    rows, cols = shape
-    whole = lax.all_to_all(jnp.broadcast_to(part / count, (count, 8, 128)), everyone, 0, 0, tiled=True)
+    mean = mean_tile(lax.all_to_all(tiles, everyone, 0, 0, tiled=True), after)
+    whole = lax.all_to_all(mean, everyone, 0, 0, tiled=True)
     return whole.reshape(rows // 8, cols // 128, 8, 128).transpose(0, 2, 1, 3).reshape(rows, cols)
 
 
@@ -358,16 +373,17 @@
     weights = [shares] + [from_x(shares, shift, parts) for shift in range(1, parts)]
 
     beside = other_core(for_beside(place, x, dy, share))
-    part = share_of_sum(staged(delta[0], beside))
-    ahead, back = pack(place, x, dy, (beside,))
+    held = staged(delta[0], beside)
+    ahead, back = pack(place, x, dy, (shares, beside))
     ahead, back = to_shift(ahead, 1), to_shift(back, 3)
-    far_x, far_dy = onward(ahead, back)
+    handed_on = onward(ahead, back)
+    far_x, far_dy = handed_on
     far_x, far_dy = to_shift(far_x, 1), to_shift(far_dy, 3)
     arrived = [ahead, back, far_x, far_dy]
     repacked = repack(place, arrived)
     swapped = other_core(repacked)
 
-    pseudo = whole_mean(part, anchor.shape)
+    pseudo = mean_of_replicas(held, handed_on)
     new_momentum = 0.9 * momentum + pseudo
     new_anchor = anchor - 0.7 * (pseudo + 0.9 * new_momentum)
 

time: 155 us -> 162 us (1.045)
  the two profiles are of different devices: /device:TPU:11 before, /device:TPU:15 now
where the time goes in v8:
time: 162 us; the launch traced here: 161 us
  starting transfers between devices  86.9 us (54%)
  waiting for transfers between devices  38.1 us (24%)
  Pallas kernels  28.9 us (18%)
  other arithmetic  3.6 us (2%)
  local copies, waits for them, and re-layouts  3.03 us (2%)
    all_to_all x1, starting transfers between devices, mean_of_replicas(): mean = mean_tile(lax.all_to_all(tiles, everyone, 0, 0, tiled=True), after)  19.4 us
    all_to_all x1, waiting for transfers between devices, on_device(): acts = lax.all_to_all(acts, 'yh', 0, 0, tiled=True)  16.2 us
    ppermute x4, starting transfers between devices, to_shift(): lax.ppermute(value, 'yh', [(i, (i + shift) % CHIPS) for i in range(CHIPS)])  14.8 us
    ppermute x3, starting transfers between devices, from_shift(): lax.ppermute(value, 'yh', [(i, (i - shift) % CHIPS) for i in range(CHIPS)])  13.9 us
    all_to_all x1, starting transfers between devices, mean_of_replicas(): whole = lax.all_to_all(mean, everyone, 0, 0, tiled=True)  12.9 us
    ppermute x4, starting transfers between devices, other_core(): return lax.ppermute(value, 'core', [(0, 1), (1, 0)])  11.9 us
    all_to_all x1, waiting for transfers between devices, mean_of_replicas(): mean = mean_tile(lax.all_to_all(tiles, everyone, 0, 0, tiled=True), after)  11.6 us
    ppermute x3, waiting for transfers between devices, from_shift(): lax.ppermute(value, 'yh', [(i, (i - shift) % CHIPS) for i in range(CHIPS)])  8.76 us
  transfers between devices with their start and end apart: 17, of which 8 were waited for; matrix products, arithmetic and copies ran while one was open for 2% of the time, Pallas kernels for 8%

profile of v8, /device:TPU:15, one launch (start us, length us, event | category | flops | bytes accessed | tf_op | source)
XLA Modules:
  0.0 161.5 jit_solution(6234643697555835171)
XLA Ops:
  0.6 0.7 pad_add_fusion.place
  1.3 2.2 %weight_share.1.after = bf16[384,256]{1,0:T(8,128)(2,1)} custom-call(s32[3]{0:T(128)} %pad_add_fusion.place, bf16[512,256]{1,0:T(8,128)(2,1)} %gate.1, bf16[512,256]{1,0:T(8,128)(2,1)} %up.1, bf16[256,512]{1,0:T(8,128)(2,1)} %down.1), custom_call_target="tpu_custom_call" | custom-call | bytes 262144 | tf_op jit(solution)/shard_map/weight_share/pallas_call | solution.py:57
  3.5 0.0 copy-start.5
  3.6 3.1 %tokens_beside.1 = bf16[4,2,128,512]{3,2,1,0:T(8,128)(2,1)} custom-call(s32[3]{0:T(128)} %pad_add_fusion.place, bf16[128,4096]{1,0:T(8,128)(2,1)} %bitcast.20, bf16[128,4096]{1,0:T(8,128)(2,1)} %bitcast.24, bf16[384,256]{1,0:T(8,128)(2,1)} %weight_share.1.after), custom_call_target="tpu_custom_call" | custom-call | bytes 2097152 | tf_op jit(solution)/shard_map/tokens_beside/pallas_call | solution.py:79
  6.7 2.6 %collective-permute-start = (bf16[4,2,128,512]{3,2,1,0:T(8,128)(2,1)}, bf16[4,2,128,512]{3,2,1,0:T(8,128)(2,1)}, u32[]{:S(2)}, u32[]{:S(2)}) collective-permute-start(bf16[4,2,128,512]{3,2,1,0:T(8,128)(2,1)} %tokens_beside.1), channel_id=1, source_target_pairs={{0,64},{64,0},{1,65},{65,1},{2,66},{66,2},{3,67},{67,3},{4,68},{68... | collective-permute-start | bytes 3145736 | tf_op jit(solution)/shard_map/ppermute | solution.py:331
  9.3 4.2 %collective-permute-start.3 = (bf16[384,256]{1,0:T(8,128)(2,1)S(1)}, bf16[384,256]{1,0:T(8,128)(2,1)S(1)}, u32[]{:S(2)}, u32[]{:S(2)}) collective-permute-start(bf16[384,256]{1,0:T(8,128)(2,1)S(1)} %copy-done.5), channel_id=1, source_target_pairs={{0,128},{128,256},{256,384},{384,0},{1,129},{129,257},{257,385},{3... | collective-permute-start | bytes 589832 | tf_op jit(solution)/shard_map/ppermute | solution.py:323
  13.5 4.8 %collective-permute-start.2 = (bf16[384,256]{1,0:T(8,128)(2,1)S(1)}, bf16[384,256]{1,0:T(8,128)(2,1)S(1)}, u32[]{:S(2)}, u32[]{:S(2)}) collective-permute-start(bf16[384,256]{1,0:T(8,128)(2,1)S(1)} %copy-done.5), channel_id=1, source_target_pairs={{0,256},{128,384},{256,0},{384,128},{1,257},{129,385},{257,1},{385... | collective-permute-start | bytes 589832 | tf_op jit(solution)/shard_map/ppermute | solution.py:323
  18.3 5.0 %collective-permute-start.1 = (bf16[384,256]{1,0:T(8,128)(2,1)S(1)}, bf16[384,256]{1,0:T(8,128)(2,1)S(1)}, u32[]{:S(2)}, u32[]{:S(2)}) collective-permute-start(bf16[384,256]{1,0:T(8,128)(2,1)S(1)} %copy-done.5), channel_id=1, source_target_pairs={{0,384},{128,0},{256,128},{384,256},{1,385},{129,1},{257,129},{385... | collective-permute-start | bytes 589832 | tf_op jit(solution)/shard_map/ppermute | solution.py:323
  23.3 2.7 %collective-permute-done.3 = bf16[384,256]{1,0:T(8,128)(2,1)S(1)} collective-permute-done((bf16[384,256]{1,0:T(8,128)(2,1)S(1)}, bf16[384,256]{1,0:T(8,128)(2,1)S(1)}, u32[]{:S(2)}, u32[]{:S(2)}) %collective-permute-start.3) | collective-permute-done | bytes 196640 | tf_op jit(solution)/shard_map/ppermute | solution.py:323
  26.0 2.1 %collective-permute-done.2 = bf16[384,256]{1,0:T(8,128)(2,1)S(1)} collective-permute-done((bf16[384,256]{1,0:T(8,128)(2,1)S(1)}, bf16[384,256]{1,0:T(8,128)(2,1)S(1)}, u32[]{:S(2)}, u32[]{:S(2)}) %collective-permute-start.2) | collective-permute-done | bytes 196640 | tf_op jit(solution)/shard_map/ppermute | solution.py:323
  28.1 3.9 %collective-permute-done.1 = bf16[384,256]{1,0:T(8,128)(2,1)S(1)} collective-permute-done((bf16[384,256]{1,0:T(8,128)(2,1)S(1)}, bf16[384,256]{1,0:T(8,128)(2,1)S(1)}, u32[]{:S(2)}, u32[]{:S(2)}) %collective-permute-start.1) | collective-permute-done | bytes 196640 | tf_op jit(solution)/shard_map/ppermute | solution.py:323
  32.0 1.0 pad_maximum_fusion.rest_0_
  33.0 3.2 %pack_tokens.1 = (bf16[3,128,1024]{2,1,0:T(8,128)(2,1)}, bf16[3,128,1024]{2,1,0:T(8,128)(2,1)}) custom-call(s32[3]{0:T(128)} %pad_add_fusion.place, bf16[128,4096]{1,0:T(8,128)(2,1)} %bitcast.21, bf16[128,4096]{1,0:T(8,128)(2,1)} %bitcast.25, bf16[4,384,256]{2,1,0:T(8,128)(2,1)} %pad_maximum_fusion.rest_0_, ...), custom_call_target="tpu_custom_call" | custom-call | bytes 4194304 | tf_op jit(solution)/shard_map/pack_tokens/pallas_call | solution.py:108
  36.2 4.3 %collective-permute-start.4 = (bf16[3,128,1024]{2,1,0:T(8,128)(2,1)}, bf16[3,128,1024]{2,1,0:T(8,128)(2,1)S(1)}, u32[]{:S(2)}, u32[]{:S(2)}) collective-permute-start(bf16[3,128,1024]{2,1,0:T(8,128)(2,1)} %get-tuple-element.14), channel_id=1, source_target_pairs={{0,128},{128,256},{256,384},{384,0},{1,129},{129,257},{257,385},{3... | collective-permute-start | bytes 2359304 | tf_op jit(solution)/shard_map/ppermute | solution.py:319
  40.5 3.1 %collective-permute-start.5 = (bf16[3,128,1024]{2,1,0:T(8,128)(2,1)}, bf16[3,128,1024]{2,1,0:T(8,128)(2,1)}, u32[]{:S(2)}, u32[]{:S(2)}) collective-permute-start(bf16[3,128,1024]{2,1,0:T(8,128)(2,1)} %get-tuple-element.15), channel_id=1, source_target_pairs={{0,384},{128,0},{256,128},{384,256},{1,385},{129,1},{257,129},{385... | collective-permute-start | bytes 2359304 | tf_op jit(solution)/shard_map/ppermute | solution.py:319
  43.6 2.1 %collective-permute-start.11 = (bf16[4,384,256]{2,1,0:T(8,128)(2,1)}, bf16[4,384,256]{2,1,0:T(8,128)(2,1)}, u32[]{:S(2)}, u32[]{:S(2)}) collective-permute-start(bf16[4,384,256]{2,1,0:T(8,128)(2,1)} %pad_maximum_fusion.rest_0_), channel_id=1, source_target_pairs={{0,8},{8,16},{16,24},{24,0},{1,9},{9,17},{17,25},{25,1},{2,10},{10... | collective-permute-start | bytes 2359304 | tf_op jit(solution)/shard_map/ppermute | solution.py:327
  45.8 4.1 %collective-permute-start.10 = (bf16[4,384,256]{2,1,0:T(8,128)(2,1)}, bf16[4,384,256]{2,1,0:T(8,128)(2,1)}, u32[]{:S(2)}, u32[]{:S(2)}) collective-permute-start(bf16[4,384,256]{2,1,0:T(8,128)(2,1)} %pad_maximum_fusion.rest_0_), channel_id=1, source_target_pairs={{0,16},{8,24},{16,0},{24,8},{1,17},{9,25},{17,1},{25,9},{2,18},{10... | collective-permute-start | bytes 2359304 | tf_op jit(solution)/shard_map/ppermute | solution.py:327
  49.8 1.9 %collective-permute-start.9 = (bf16[4,384,256]{2,1,0:T(8,128)(2,1)}, bf16[4,384,256]{2,1,0:T(8,128)(2,1)}, u32[]{:S(2)}, u32[]{:S(2)}) collective-permute-start(bf16[4,384,256]{2,1,0:T(8,128)(2,1)} %pad_maximum_fusion.rest_0_), channel_id=1, source_target_pairs={{0,24},{8,0},{16,8},{24,16},{1,25},{9,1},{17,9},{25,17},{2,26},{10... | collective-permute-start | bytes 2359304 | tf_op jit(solution)/shard_map/ppermute | solution.py:327
  51.7 1.7 %delta_staged.1 = f32[16,4096]{1,0:T(8,128)} custom-call(f32[16,4096]{1,0:T(8,128)} %bitcast.32, bf16[4,2,128,512]{3,2,1,0:T(8,128)(2,1)} %collective-permute-done.rest_1_.beside.after), custom_call_target="tpu_custom_call" | custom-call | bytes 524288 | tf_op jit(solution)/shard_map/delta_staged/pallas_call | solution.py:165
  53.4 19.4 %all-to-all-start = ((f32[64,8,128]{2,1,0:T(8,128)}), f32[64,8,128]{2,1,0:T(8,128)}, u32[]{:S(2)}, u32[]{:S(2)}) async-start(f32[64,8,128]{2,1,0:T(8,128)} %bitcast.31), calls=%async_computation | async-start | bytes 524288 | tf_op jit(solution)/shard_map/all_to_all | solution.py:360
  72.8 0.0 collective-permute-done.4.ahead
  72.9 0.0 collective-permute-done.5.back
  72.9 0.9 copy-done
  73.8 1.8 %onward.1 = (bf16[1,128,1024]{2,1,0:T(8,128)(2,1)}, bf16[1,128,1024]{2,1,0:T(8,128)(2,1)}) custom-call(bf16[3,128,1024]{2,1,0:T(8,128)(2,1)} %copy-done, bf16[3,128,1024]{2,1,0:T(8,128)(2,1)} %collective-permute-done.5.back), custom_call_target="tpu_custom_call" | custom-call | bytes 104857600 | tf_op jit(solution)/shard_map/onward/pallas_call | solution.py:126
  75.6 3.3 %collective-permute-start.6 = (bf16[1,128,1024]{2,1,0:T(8,128)(2,1)}, bf16[1,128,1024]{2,1,0:T(8,128)(2,1)S(1)}, u32[]{:S(2)}, u32[]{:S(2)}) collective-permute-start(bf16[1,128,1024]{2,1,0:T(8,128)(2,1)} %get-tuple-element.16.rest_0_), channel_id=1, source_target_pairs={{0,128},{128,256},{256,384},{384,0},{1,129},{129,257},{257,385},{3... | collective-permute-start | bytes 786440 | tf_op jit(solution)/shard_map/ppermute | solution.py:319
  78.9 4.1 %collective-permute-start.7 = (bf16[1,128,1024]{2,1,0:T(8,128)(2,1)}, bf16[1,128,1024]{2,1,0:T(8,128)(2,1)S(1)}, u32[]{:S(2)}, u32[]{:S(2)}) collective-permute-start(bf16[1,128,1024]{2,1,0:T(8,128)(2,1)} %get-tuple-element.17.rest_1_), channel_id=1, source_target_pairs={{0,384},{128,0},{256,128},{384,256},{1,385},{129,1},{257,129},{385... | collective-permute-start | bytes 786440 | tf_op jit(solution)/shard_map/ppermute | solution.py:319
  83.0 11.6 %all-to-all-done.parts = f32[64,8,128]{2,1,0:T(8,128)} async-done(((f32[64,8,128]{2,1,0:T(8,128)}), f32[64,8,128]{2,1,0:T(8,128)}, u32[]{:S(2)}, u32[]{:S(2)}) %all-to-all-start) | async-done | bytes 262176 | tf_op jit(solution)/shard_map/all_to_all | solution.py:360
  94.6 1.7 %mean_tile.1 = f32[64,8,128]{2,1,0:T(8,128)} custom-call(f32[64,8,128]{2,1,0:T(8,128)} %all-to-all-done.parts, bf16[1,128,1024]{2,1,0:T(8,128)(2,1)} %get-tuple-element.16.rest_0_, bf16[1,128,1024]{2,1,0:T(8,128)(2,1)} %get-tuple-element.17.rest_1_), custom_call_target="tpu_custom_call" | custom-call | flops 65536 | bytes 524288 | tf_op jit(solution)/shard_map/mean_tile/pallas_call | solution.py:343
  96.3 12.9 %all-to-all-start.1 = ((f32[64,8,128]{2,1,0:T(8,128)}), f32[64,8,128]{2,1,0:T(8,128)S(1)}, u32[]{:S(2)}, u32[]{:S(2)}) async-start(f32[64,8,128]{2,1,0:T(8,128)} %mean_tile.1), calls=%async_computation.1 | async-start | bytes 524288 | tf_op jit(solution)/shard_map/all_to_all | solution.py:361
  109.3 0.0 collective-permute-done.10.rest_2_
  109.3 0.0 collective-permute-done.9.rest_1_
  109.3 0.0 collective-permute-done.7.far_dy.rest_5_
  109.3 0.7 copy-done.2
  110.0 0.7 copy-done.3
  110.7 5.4 %hidden_sums.1 = (f32[3,128,256]{2,1,0:T(8,128)}, f32[3,128,256]{2,1,0:T(8,128)}) custom-call(s32[3]{0:T(128)} %pad_add_fusion.place, bf16[128,4096]{1,0:T(8,128)(2,1)} %bitcast.22, bf16[128,4096]{1,0:T(8,128)(2,1)} %bitcast.26, bf16[4,2,128,512]{3,2,1,0:T(8,128)(2,1)} %collective-permute-done.rest_1_.beside.after, ...), custom_call_target="tpu_custom_call" | custom-call | flops 805306368 | bytes 6291456 | tf_op jit(solution)/shard_map/hidden_sums/pallas_call | solution.py:222
  116.1 3.4 %collective-permute-start.12 = (f32[3,128,256]{2,1,0:T(8,128)}, f32[3,128,256]{2,1,0:T(8,128)S(1)}, u32[]{:S(2)}, u32[]{:S(2)}) collective-permute-start(f32[3,128,256]{2,1,0:T(8,128)} %get-tuple-element.19), channel_id=1, source_target_pairs={{0,64},{64,0},{1,65},{65,1},{2,66},{66,2},{3,67},{67,3},{4,68},{68... | collective-permute-start | bytes 1179656 | tf_op jit(solution)/shard_map/ppermute | solution.py:331
  119.5 0.7 all-to-all-done.1
  120.2 0.8 collective-permute-done.12.arrived_ref
  121.1 0.7 copy-done.6
  121.8 2.1 %activation.1 = bf16[4,3,128,256]{3,2,1,0:T(8,128)(2,1)} custom-call(f32[3,128,256]{2,1,0:T(8,128)} %get-tuple-element.18.mine_ref, f32[3,128,256]{2,1,0:T(8,128)} %copy-done.6, f32[16,4096]{1,0:T(8,128)} %bitcast.28), custom_call_target="tpu_custom_call" | custom-call | flops 655360 | bytes 1048576 | tf_op jit(solution)/shard_map/activation/pallas_call | solution.py:256
  123.9 5.9 %all-to-all-start.2 = ((bf16[4,3,128,256]{3,2,1,0:T(8,128)(2,1)}), bf16[4,3,128,256]{3,2,1,0:T(8,128)(2,1)S(1)}, u32[]{:S(2)}, u32[]{:S(2)}) async-start(bf16[4,3,128,256]{3,2,1,0:T(8,128)(2,1)} %activation.1), calls=%async_computation.2 | async-start | bytes 1572864 | tf_op jit(solution)/shard_map/all_to_all | solution.py:392
  129.8 2.9 %repack_tokens.1 = bf16[3,2,128,512]{3,2,1,0:T(8,128)(2,1)} custom-call(s32[3]{0:T(128)} %pad_add_fusion.place, bf16[3,128,1024]{2,1,0:T(8,128)(2,1)} %copy-done, bf16[3,128,1024]{2,1,0:T(8,128)(2,1)} %collective-permute-done.5.back, bf16[1,128,1024]{2,1,0:T(8,128)(2,1)} %copy-done.2, bf16[1,128,1024]{2,1,0:T(8,128)(2,1)} %copy-done.3), custom_call_target="tpu_custom_call" | custom-call | bytes 209715200 | tf_op jit(solution)/shard_map/repack_tokens/pallas_call | solution.py:147
  132.7 2.6 %collective-permute-start.8 = (bf16[3,2,128,512]{3,2,1,0:T(8,128)(2,1)}, bf16[3,2,128,512]{3,2,1,0:T(8,128)(2,1)}, u32[]{:S(2)}, u32[]{:S(2)}) collective-permute-start(bf16[3,2,128,512]{3,2,1,0:T(8,128)(2,1)} %repack_tokens.1), channel_id=1, source_target_pairs={{0,64},{64,0},{1,65},{65,1},{2,66},{66,2},{3,67},{67,3},{4,68},{68... | collective-permute-start | bytes 2359304 | tf_op jit(solution)/shard_map/ppermute | solution.py:331
  135.3 16.2 %all-to-all-done.2.rest_0_ = bf16[4,3,128,256]{3,2,1,0:T(8,128)(2,1)S(1)} async-done(((bf16[4,3,128,256]{3,2,1,0:T(8,128)(2,1)}), bf16[4,3,128,256]{3,2,1,0:T(8,128)(2,1)S(1)}, u32[]{:S(2)}, u32[]{:S(2)}) %all-to-all-start.2) | async-done | bytes 786464 | tf_op jit(solution)/shard_map/all_to_all | solution.py:392
  151.4 3.3 %collective-permute-start.13 = (bf16[4,3,128,256]{3,2,1,0:T(8,128)(2,1)S(1)}, bf16[4,3,128,256]{3,2,1,0:T(8,128)(2,1)}, u32[]{:S(2)}, u32[]{:S(2)}) collective-permute-start(bf16[4,3,128,256]{3,2,1,0:T(8,128)(2,1)S(1)} %all-to-all-done.2.rest_0_), channel_id=1, source_target_pairs={{0,64},{64,0},{1,65},{65,1},{2,66},{66,2},{3,67},{67,3},{4,68},{68... | collective-permute-start | bytes 2359304 | tf_op jit(solution)/shard_map/ppermute | solution.py:331
  154.7 2.0 %multiply_subtract_fusion = (f32[16,4096]{1,0:T(8,128)}, f32[16,4096]{1,0:T(8,128)}) fusion(f32[16,4096]{1,0:T(8,128)} %param.14, f32[16,4096]{1,0:T(8,128)} %bitcast.29, f32[16,4096]{1,0:T(8,128)} %param.15), kind=kLoop, calls=%fused_computation.1 | loop fusion | flops 393216 | bytes 1310720 | tf_op jit(solution)/shard_map/sub | solution.py:388
  156.7 0.1 collective-permute-done.13.rest_1_
  156.8 4.7 %weight_grads.1 = (bf16[1,512,256]{2,1,0:T(8,128)(2,1)}, bf16[1,512,256]{2,1,0:T(8,128)(2,1)}, bf16[1,256,512]{2,1,0:T(8,128)(2,1)}) custom-call(s32[3]{0:T(128)} %pad_add_fusion.place, bf16[128,4096]{1,0:T(8,128)(2,1)} %bitcast.23, bf16[128,4096]{1,0:T(8,128)(2,1)} %bitcast.27, bf16[4,2,128,512]{3,2,1,0:T(8,128)(2,1)} %collective-permute-done.rest_1_.beside.after, ...), custom_call_target="tpu_custom_call" | custom-call | flops 805306368 | bytes 5242880 | tf_op jit(solution)/shard_map/weight_grads/pallas_call | solution.py:297
  (13 shorter events, 0.0 us)
Async XLA Ops:
  3.5 5.7 %copy-start.5 = (bf16[384,256]{1,0:T(8,128)(2,1)S(1)}, bf16[384,256]{1,0:T(8,128)(2,1)}, u32[]{:S(2)}) copy-start(bf16[384,256]{1,0:T(8,128)(2,1)} %weight_share.1.after) | copy-start | bytes 589828
  6.7 26.3 %collective-permute-start = (bf16[4,2,128,512]{3,2,1,0:T(8,128)(2,1)}, bf16[4,2,128,512]{3,2,1,0:T(8,128)(2,1)}, u32[]{:S(2)}, u32[]{:S(2)}) collective-permute-start(bf16[4,2,128,512]{3,2,1,0:T(8,128)(2,1)} %tokens_beside.1), channel_id=1, source_target_pairs={{0,64},{64,0},{1,65},{65,1},{2,66},{66,2},{3,67},{67,3},{4,68},{68... | collective-permute-start | bytes 3145736 | tf_op jit(solution)/shard_map/ppermute | solution.py:331
  9.3 16.7 %collective-permute-start.3 = (bf16[384,256]{1,0:T(8,128)(2,1)S(1)}, bf16[384,256]{1,0:T(8,128)(2,1)S(1)}, u32[]{:S(2)}, u32[]{:S(2)}) collective-permute-start(bf16[384,256]{1,0:T(8,128)(2,1)S(1)} %copy-done.5), channel_id=1, source_target_pairs={{0,128},{128,256},{256,384},{384,0},{1,129},{129,257},{257,385},{3... | collective-permute-start | bytes 589832 | tf_op jit(solution)/shard_map/ppermute | solution.py:323
  13.5 14.6 %collective-permute-start.2 = (bf16[384,256]{1,0:T(8,128)(2,1)S(1)}, bf16[384,256]{1,0:T(8,128)(2,1)S(1)}, u32[]{:S(2)}, u32[]{:S(2)}) collective-permute-start(bf16[384,256]{1,0:T(8,128)(2,1)S(1)} %copy-done.5), channel_id=1, source_target_pairs={{0,256},{128,384},{256,0},{384,128},{1,257},{129,385},{257,1},{385... | collective-permute-start | bytes 589832 | tf_op jit(solution)/shard_map/ppermute | solution.py:323
  18.3 13.7 %collective-permute-start.1 = (bf16[384,256]{1,0:T(8,128)(2,1)S(1)}, bf16[384,256]{1,0:T(8,128)(2,1)S(1)}, u32[]{:S(2)}, u32[]{:S(2)}) collective-permute-start(bf16[384,256]{1,0:T(8,128)(2,1)S(1)} %copy-done.5), channel_id=1, source_target_pairs={{0,384},{128,0},{256,128},{384,256},{1,385},{129,1},{257,129},{385... | collective-permute-start | bytes 589832 | tf_op jit(solution)/shard_map/ppermute | solution.py:323
  36.2 36.6 %collective-permute-start.4 = (bf16[3,128,1024]{2,1,0:T(8,128)(2,1)}, bf16[3,128,1024]{2,1,0:T(8,128)(2,1)S(1)}, u32[]{:S(2)}, u32[]{:S(2)}) collective-permute-start(bf16[3,128,1024]{2,1,0:T(8,128)(2,1)} %get-tuple-element.14), channel_id=1, source_target_pairs={{0,128},{128,256},{256,384},{384,0},{1,129},{129,257},{257,385},{3... | collective-permute-start | bytes 2359304 | tf_op jit(solution)/shard_map/ppermute | solution.py:319
  40.5 32.4 %collective-permute-start.5 = (bf16[3,128,1024]{2,1,0:T(8,128)(2,1)}, bf16[3,128,1024]{2,1,0:T(8,128)(2,1)}, u32[]{:S(2)}, u32[]{:S(2)}) collective-permute-start(bf16[3,128,1024]{2,1,0:T(8,128)(2,1)} %get-tuple-element.15), channel_id=1, source_target_pairs={{0,384},{128,0},{256,128},{384,256},{1,385},{129,1},{257,129},{385... | collective-permute-start | bytes 2359304 | tf_op jit(solution)/shard_map/ppermute | solution.py:319
  43.6 65.6 %collective-permute-start.11 = (bf16[4,384,256]{2,1,0:T(8,128)(2,1)}, bf16[4,384,256]{2,1,0:T(8,128)(2,1)}, u32[]{:S(2)}, u32[]{:S(2)}) collective-permute-start(bf16[4,384,256]{2,1,0:T(8,128)(2,1)} %pad_maximum_fusion.rest_0_), channel_id=1, source_target_pairs={{0,8},{8,16},{16,24},{24,0},{1,9},{9,17},{17,25},{25,1},{2,10},{10... | collective-permute-start | bytes 2359304 | tf_op jit(solution)/shard_map/ppermute | solution.py:327
  45.8 63.5 %collective-permute-start.10 = (bf16[4,384,256]{2,1,0:T(8,128)(2,1)}, bf16[4,384,256]{2,1,0:T(8,128)(2,1)}, u32[]{:S(2)}, u32[]{:S(2)}) collective-permute-start(bf16[4,384,256]{2,1,0:T(8,128)(2,1)} %pad_maximum_fusion.rest_0_), channel_id=1, source_target_pairs={{0,16},{8,24},{16,0},{24,8},{1,17},{9,25},{17,1},{25,9},{2,18},{10... | collective-permute-start | bytes 2359304 | tf_op jit(solution)/shard_map/ppermute | solution.py:327
  49.8 59.5 %collective-permute-start.9 = (bf16[4,384,256]{2,1,0:T(8,128)(2,1)}, bf16[4,384,256]{2,1,0:T(8,128)(2,1)}, u32[]{:S(2)}, u32[]{:S(2)}) collective-permute-start(bf16[4,384,256]{2,1,0:T(8,128)(2,1)} %pad_maximum_fusion.rest_0_), channel_id=1, source_target_pairs={{0,24},{8,0},{16,8},{24,16},{1,25},{9,1},{17,9},{25,17},{2,26},{10... | collective-permute-start | bytes 2359304 | tf_op jit(solution)/shard_map/ppermute | solution.py:327
  53.4 41.1 %all-to-all-start = ((f32[64,8,128]{2,1,0:T(8,128)}), f32[64,8,128]{2,1,0:T(8,128)}, u32[]{:S(2)}, u32[]{:S(2)}) async-start(f32[64,8,128]{2,1,0:T(8,128)} %bitcast.31), calls=%async_computation | async-start | bytes 524288 | tf_op jit(solution)/shard_map/all_to_all | solution.py:360
  72.9 0.9 copy-start
  75.6 33.7 %collective-permute-start.6 = (bf16[1,128,1024]{2,1,0:T(8,128)(2,1)}, bf16[1,128,1024]{2,1,0:T(8,128)(2,1)S(1)}, u32[]{:S(2)}, u32[]{:S(2)}) collective-permute-start(bf16[1,128,1024]{2,1,0:T(8,128)(2,1)} %get-tuple-element.16.rest_0_), channel_id=1, source_target_pairs={{0,128},{128,256},{256,384},{384,0},{1,129},{129,257},{257,385},{3... | collective-permute-start | bytes 786440 | tf_op jit(solution)/shard_map/ppermute | solution.py:319
  78.9 30.4 %collective-permute-start.7 = (bf16[1,128,1024]{2,1,0:T(8,128)(2,1)}, bf16[1,128,1024]{2,1,0:T(8,128)(2,1)S(1)}, u32[]{:S(2)}, u32[]{:S(2)}) collective-permute-start(bf16[1,128,1024]{2,1,0:T(8,128)(2,1)} %get-tuple-element.17.rest_1_), channel_id=1, source_target_pairs={{0,384},{128,0},{256,128},{384,256},{1,385},{129,1},{257,129},{385... | collective-permute-start | bytes 786440 | tf_op jit(solution)/shard_map/ppermute | solution.py:319
  96.3 23.9 %all-to-all-start.1 = ((f32[64,8,128]{2,1,0:T(8,128)}), f32[64,8,128]{2,1,0:T(8,128)S(1)}, u32[]{:S(2)}, u32[]{:S(2)}) async-start(f32[64,8,128]{2,1,0:T(8,128)} %mean_tile.1), calls=%async_computation.1 | async-start | bytes 524288 | tf_op jit(solution)/shard_map/all_to_all | solution.py:361
  109.3 0.7 copy-start.2
  110.0 0.7 copy-start.3
  116.1 4.9 %collective-permute-start.12 = (f32[3,128,256]{2,1,0:T(8,128)}, f32[3,128,256]{2,1,0:T(8,128)S(1)}, u32[]{:S(2)}, u32[]{:S(2)}) collective-permute-start(f32[3,128,256]{2,1,0:T(8,128)} %get-tuple-element.19), channel_id=1, source_target_pairs={{0,64},{64,0},{1,65},{65,1},{2,66},{66,2},{3,67},{67,3},{4,68},{68... | collective-permute-start | bytes 1179656 | tf_op jit(solution)/shard_map/ppermute | solution.py:331
  120.2 0.8 copy-start.4
  121.0 0.7 copy-start.6
  123.9 27.5 %all-to-all-start.2 = ((bf16[4,3,128,256]{3,2,1,0:T(8,128)(2,1)}), bf16[4,3,128,256]{3,2,1,0:T(8,128)(2,1)S(1)}, u32[]{:S(2)}, u32[]{:S(2)}) async-start(bf16[4,3,128,256]{3,2,1,0:T(8,128)(2,1)} %activation.1), calls=%async_computation.2 | async-start | bytes 1572864 | tf_op jit(solution)/shard_map/all_to_all | solution.py:392
  132.7 24.0 %collective-permute-start.8 = (bf16[3,2,128,512]{3,2,1,0:T(8,128)(2,1)}, bf16[3,2,128,512]{3,2,1,0:T(8,128)(2,1)}, u32[]{:S(2)}, u32[]{:S(2)}) collective-permute-start(bf16[3,2,128,512]{3,2,1,0:T(8,128)(2,1)} %repack_tokens.1), channel_id=1, source_target_pairs={{0,64},{64,0},{1,65},{65,1},{2,66},{66,2},{3,67},{67,3},{4,68},{68... | collective-permute-start | bytes 2359304 | tf_op jit(solution)/shard_map/ppermute | solution.py:331
  151.4 5.3 %copy-start.1 = (bf16[4,3,128,256]{3,2,1,0:T(8,128)(2,1)}, bf16[4,3,128,256]{3,2,1,0:T(8,128)(2,1)S(1)}, u32[]{:S(2)}) copy-start(bf16[4,3,128,256]{3,2,1,0:T(8,128)(2,1)S(1)} %all-to-all-done.2.rest_0_) | copy-start | bytes 2359300
  151.4 5.3 %collective-permute-start.13 = (bf16[4,3,128,256]{3,2,1,0:T(8,128)(2,1)S(1)}, bf16[4,3,128,256]{3,2,1,0:T(8,128)(2,1)}, u32[]{:S(2)}, u32[]{:S(2)}) collective-permute-start(bf16[4,3,128,256]{3,2,1,0:T(8,128)(2,1)S(1)} %all-to-all-done.2.rest_0_), channel_id=1, source_target_pairs={{0,64},{64,0},{1,65},{65,1},{2,66},{66,2},{3,67},{67,3},{4,68},{68... | collective-permute-start | bytes 2359304 | tf_op jit(solution)/shard_map/ppermute | solution.py:331

commit v9 on v6

--- a/solution.py
+++ b/solution.py
@@ -23,12 +23,20 @@
 SMEM = pl.BlockSpec(memory_space=pltpu.SMEM)
 
 
-def run_copies(copies, sems):
+def start_copies(copies, sems):
     started = [pltpu.make_async_copy(src, dst, sems.at[i]) for i, (src, dst) in enumerate(copies)]
     for copy in started:
         copy.start()
+    return started
+
+
+def wait_copies(started):
     for copy in started:
         copy.wait()
+
+
+def run_copies(copies, sems):
+    wait_copies(start_copies(copies, sems))
 
 
 def columns(base):
@@ -179,42 +187,43 @@
     mine, theirs, xs, dys, gates, ups, downs, sems = rest[parts + waited :]
     gate_rows, down_rows = HALF // parts, HID // parts
     cut = 2 * gate_rows
-    copies = []
+    to_gate, to_up, to_down = [], [], []
     for shift in range(CHIPS):
         chip = lax.rem(place[2] + shift, CHIPS)
         own = columns(chip * WIDE + place[0] * HALF)
-        copies += [
-            (x.at[:, own], xs.at[shift, :ROWS]),
-            (dy.at[:, own], dys.at[shift, :ROWS]),
-            (beside.at[chip, 0], xs.at[shift, ROWS:]),
-            (beside.at[chip, 1], dys.at[shift, ROWS:]),
-        ]
+        to_gate += [(x.at[:, own], xs.at[shift, :ROWS]), (beside.at[chip, 0], xs.at[shift, ROWS:])]
+        to_down += [(dy.at[:, own], dys.at[shift, :ROWS]), (beside.at[chip, 1], dys.at[shift, ROWS:])]
     for shift, ref in enumerate(weights):
         part = lax.rem(place[1] + shift, parts)
-        to_gate = pl.ds(pl.multiple_of(part * gate_rows, gate_rows), gate_rows)
-        to_down = pl.ds(pl.multiple_of(part * down_rows, down_rows), down_rows)
-        copies += [
-            (ref.at[:, pl.ds(0, gate_rows)], gates.at[:, to_gate]),
-            (ref.at[:, pl.ds(gate_rows, gate_rows)], ups.at[:, to_gate]),
-            (ref.at[:, pl.ds(cut, down_rows)], downs.at[:, 0, to_down]),
-            (ref.at[:, pl.ds(cut + down_rows, down_rows)], downs.at[:, 1, to_down]),
+        gate_at = pl.ds(pl.multiple_of(part * gate_rows, gate_rows), gate_rows)
+        down_at = pl.ds(pl.multiple_of(part * down_rows, down_rows), down_rows)
+        to_gate.append((ref.at[:, pl.ds(0, gate_rows)], gates.at[:, gate_at]))
+        to_up.append((ref.at[:, pl.ds(gate_rows, gate_rows)], ups.at[:, gate_at]))
+        to_down += [
+            (ref.at[:, pl.ds(cut, down_rows)], downs.at[:, 0, down_at]),
+            (ref.at[:, pl.ds(cut + down_rows, down_rows)], downs.at[:, 1, down_at]),
         ]
-    run_copies(copies, sems)
-    gate = up = dh = 0.0
-    for chip in range(CHIPS):
-        a, b = xs[chip], dys[chip]
-        gate += jnp.dot(a, gates[chip], preferred_element_type=F32)
-        up += jnp.dot(a, ups[chip], preferred_element_type=F32)
-        for h in range(2):
-            dh += lax.dot_general(
-                b[:, HID * h : HID * (h + 1)],
-                downs[chip, h],
-                (((1,), (1,)), ((), ())),
-                preferred_element_type=F32,
-            )
-    for i, value in enumerate((gate, up, dh)):
+    started = start_copies(to_gate + to_up + to_down, sems)
+    first, second = len(to_gate), len(to_gate) + len(to_up)
+
+    def put(i, value):
         mine[i] = value[:ROWS]
         theirs[i] = value[ROWS:]
+
+    wait_copies(started[:first])
+    put(0, sum(jnp.dot(xs[i], gates[i], preferred_element_type=F32) for i in range(CHIPS)))
+    wait_copies(started[first:second])
+    put(1, sum(jnp.dot(xs[i], ups[i], preferred_element_type=F32) for i in range(CHIPS)))
+    wait_copies(started[second:])
+    wide = (((1,), (1,)), ((), ()))
+    put(
+        2,
+        sum(
+            lax.dot_general(dys[i, :, HID * h : HID * (h + 1)], downs[i, h], wide, preferred_element_type=F32)
+            for i in range(CHIPS)
+            for h in range(2)
+        ),
+    )
 
 
 def hidden_sums(place, x, dy, beside, weights, after):
@@ -280,15 +289,18 @@
     ]
     there = [(beside.at[chip, 0], beside.at[chip, 1])]
     there += [(swapped.at[i, 0], swapped.at[i, 1]) for i in range(CHIPS - 1)]
-    copies = []
+    early, late = [], []
     for i, (a, b) in enumerate(here + there):
         rows = pl.ds(i * ROWS, ROWS)
         source = lax.rem(chip + 2 * CHIPS - i, CHIPS)
-        copies += [(a, xs.at[rows]), (b, dys.at[rows]), (acts[i // CHIPS].at[source], hs.at[:, rows])]
-    run_copies(copies, sems)
+        early += [(acts[i // CHIPS].at[source], hs.at[:, rows]), (a, xs.at[rows])]
+        late.append((b, dys.at[rows]))
+    started = start_copies(early + late, sems)
     tall = (((0,), (0,)), ((), ()))
+    wait_copies(started[: len(early)])
     gg[0] = lax.dot_general(xs[...], hs[0], tall, preferred_element_type=F32).astype(BF16)
     gu[0] = lax.dot_general(xs[...], hs[1], tall, preferred_element_type=F32).astype(BF16)
+    wait_copies(started[len(early) :])
     gd[0] = lax.dot_general(hs[2], dys[...], tall, preferred_element_type=F32).astype(BF16)
 
 

time: 153 us -> 152 us (level)
  no operation moved by 1% of the time
where the time goes in v9:
time: 152 us; the launch traced here: 151 us
  starting transfers between devices  71.8 us (47%)
  waiting for transfers between devices  44.9 us (30%)
  Pallas kernels  26.9 us (18%)
  other arithmetic  4.51 us (3%)
  local copies, waits for them, and re-layouts  2.21 us (1%)
    ppermute x4, waiting for transfers between devices, to_shift(): lax.ppermute(value, 'yh', [(i, (i + shift) % CHIPS) for i in range(CHIPS)])  21.3 us
    all_to_all x1, waiting for transfers between devices, on_device(): acts = lax.all_to_all(acts, 'yh', 0, 0, tiled=True)  16.6 us
    ppermute x4, starting transfers between devices, to_shift(): lax.ppermute(value, 'yh', [(i, (i + shift) % CHIPS) for i in range(CHIPS)])  15.2 us
    ppermute x4, starting transfers between devices, other_core(): return lax.ppermute(value, 'core', [(0, 1), (1, 0)])  13.2 us
    ppermute x3, starting transfers between devices, from_shift(): lax.ppermute(value, 'yh', [(i, (i - shift) % CHIPS) for i in range(CHIPS)])  12.7 us
    ppermute x3, starting transfers between devices, from_x(): lax.ppermute(value, 'x', [(i, (i - shift) % size) for i in range(size)])  9.04 us
    all_to_all x1, starting transfers between devices, share_of_sum(): lax.all_to_all(tiles, everyone, 0, 0, tiled=True)  8.24 us
    all_to_all x1, starting transfers between devices, whole_mean(): lax.all_to_all(jnp.broadcast_to(part / count, (count, 8, 128)), everyone,...  7.88 us
  transfers between devices with their start and end apart: 17, of which 8 were waited for; matrix products, arithmetic and copies ran while one was open for 3% of the time, Pallas kernels for 10%

profile of v9, /device:TPU:459, one launch (start us, length us, event | category | flops | bytes accessed | tf_op | source)
XLA Modules:
  0.0 151.3 jit_solution(14275660480133546881)
XLA Ops:
  0.6 0.6 pad_add_fusion.place
  1.3 2.2 %weight_share.1.after = bf16[384,256]{1,0:T(8,128)(2,1)} custom-call(s32[3]{0:T(128)} %pad_add_fusion.place, bf16[512,256]{1,0:T(8,128)(2,1)} %gate.1, bf16[512,256]{1,0:T(8,128)(2,1)} %up.1, bf16[256,512]{1,0:T(8,128)(2,1)} %down.1), custom_call_target="tpu_custom_call" | custom-call | bytes 262144 | tf_op jit(solution)/shard_map/weight_share/pallas_call | solution.py:65
  3.5 0.0 copy-start.4
  3.5 3.1 %tokens_beside.1 = bf16[4,2,128,512]{3,2,1,0:T(8,128)(2,1)} custom-call(s32[3]{0:T(128)} %pad_add_fusion.place, bf16[128,4096]{1,0:T(8,128)(2,1)} %bitcast.20, bf16[128,4096]{1,0:T(8,128)(2,1)} %bitcast.24, bf16[384,256]{1,0:T(8,128)(2,1)} %weight_share.1.after), custom_call_target="tpu_custom_call" | custom-call | bytes 2097152 | tf_op jit(solution)/shard_map/tokens_beside/pallas_call | solution.py:87
  6.6 2.6 %collective-permute-start = (bf16[4,2,128,512]{3,2,1,0:T(8,128)(2,1)}, bf16[4,2,128,512]{3,2,1,0:T(8,128)(2,1)}, u32[]{:S(2)}, u32[]{:S(2)}) collective-permute-start(bf16[4,2,128,512]{3,2,1,0:T(8,128)(2,1)} %tokens_beside.1), channel_id=1, source_target_pairs={{0,64},{64,0},{1,65},{65,1},{2,66},{66,2},{3,67},{67,3},{4,68},{68... | collective-permute-start | bytes 3145736 | tf_op jit(solution)/shard_map/ppermute | solution.py:343
  9.2 5.0 %collective-permute-start.1 = (bf16[384,256]{1,0:T(8,128)(2,1)S(1)}, bf16[384,256]{1,0:T(8,128)(2,1)S(1)}, u32[]{:S(2)}, u32[]{:S(2)}) collective-permute-start(bf16[384,256]{1,0:T(8,128)(2,1)S(1)} %copy-done.4), channel_id=1, source_target_pairs={{0,384},{128,0},{256,128},{384,256},{1,385},{129,1},{257,129},{385... | collective-permute-start | bytes 589832 | tf_op jit(solution)/shard_map/ppermute | solution.py:335
  14.2 4.4 %collective-permute-start.2 = (bf16[384,256]{1,0:T(8,128)(2,1)S(1)}, bf16[384,256]{1,0:T(8,128)(2,1)S(1)}, u32[]{:S(2)}, u32[]{:S(2)}) collective-permute-start(bf16[384,256]{1,0:T(8,128)(2,1)S(1)} %copy-done.4), channel_id=1, source_target_pairs={{0,256},{128,384},{256,0},{384,128},{1,257},{129,385},{257,1},{385... | collective-permute-start | bytes 589832 | tf_op jit(solution)/shard_map/ppermute | solution.py:335
  18.7 3.3 %collective-permute-start.3 = (bf16[384,256]{1,0:T(8,128)(2,1)S(1)}, bf16[384,256]{1,0:T(8,128)(2,1)S(1)}, u32[]{:S(2)}, u32[]{:S(2)}) collective-permute-start(bf16[384,256]{1,0:T(8,128)(2,1)S(1)} %copy-done.4), channel_id=1, source_target_pairs={{0,128},{128,256},{256,384},{384,0},{1,129},{129,257},{257,385},{3... | collective-permute-start | bytes 589832 | tf_op jit(solution)/shard_map/ppermute | solution.py:335
  22.0 0.0 collective-permute-done.rest_1_.beside.after
  22.0 1.7 %delta_staged.1 = f32[16,4096]{1,0:T(8,128)} custom-call(f32[16,4096]{1,0:T(8,128)} %bitcast.30, bf16[4,2,128,512]{3,2,1,0:T(8,128)(2,1)} %collective-permute-done.rest_1_.beside.after), custom_call_target="tpu_custom_call" | custom-call | bytes 524288 | tf_op jit(solution)/shard_map/delta_staged/pallas_call | solution.py:173
  23.7 8.2 %all-to-all-start = ((f32[64,8,128]{2,1,0:T(8,128)}), f32[64,8,128]{2,1,0:T(8,128)}, u32[]{:S(2)}, u32[]{:S(2)}) async-start(f32[64,8,128]{2,1,0:T(8,128)} %bitcast.29), calls=%async_computation | async-start | bytes 524288 | tf_op jit(solution)/shard_map/all_to_all | solution.py:351
  31.9 0.0 collective-permute-done.1
  31.9 2.5 %collective-permute-done.2 = bf16[384,256]{1,0:T(8,128)(2,1)S(1)} collective-permute-done((bf16[384,256]{1,0:T(8,128)(2,1)S(1)}, bf16[384,256]{1,0:T(8,128)(2,1)S(1)}, u32[]{:S(2)}, u32[]{:S(2)}) %collective-permute-start.2) | collective-permute-done | bytes 196640 | tf_op jit(solution)/shard_map/ppermute | solution.py:335
  34.5 2.5 %collective-permute-done.3 = bf16[384,256]{1,0:T(8,128)(2,1)S(1)} collective-permute-done((bf16[384,256]{1,0:T(8,128)(2,1)S(1)}, bf16[384,256]{1,0:T(8,128)(2,1)S(1)}, u32[]{:S(2)}, u32[]{:S(2)}) %collective-permute-start.3) | collective-permute-done | bytes 196640 | tf_op jit(solution)/shard_map/ppermute | solution.py:335
  37.0 1.0 pad_maximum_fusion.rest_0_
  38.0 3.2 %pack_tokens.1 = (bf16[3,128,1024]{2,1,0:T(8,128)(2,1)}, bf16[3,128,1024]{2,1,0:T(8,128)(2,1)}) custom-call(s32[3]{0:T(128)} %pad_add_fusion.place, bf16[128,4096]{1,0:T(8,128)(2,1)} %bitcast.21, bf16[128,4096]{1,0:T(8,128)(2,1)} %bitcast.25, bf16[4,384,256]{2,1,0:T(8,128)(2,1)} %pad_maximum_fusion.rest_0_, ...), custom_call_target="tpu_custom_call" | custom-call | bytes 4194304 | tf_op jit(solution)/shard_map/pack_tokens/pallas_call | solution.py:116
  41.2 4.0 %collective-permute-start.4 = (bf16[3,128,1024]{2,1,0:T(8,128)(2,1)}, bf16[3,128,1024]{2,1,0:T(8,128)(2,1)S(1)}, u32[]{:S(2)}, u32[]{:S(2)}) collective-permute-start(bf16[3,128,1024]{2,1,0:T(8,128)(2,1)} %get-tuple-element.14), channel_id=1, source_target_pairs={{0,128},{128,256},{256,384},{384,0},{1,129},{129,257},{257,385},{3... | collective-permute-start | bytes 2359304 | tf_op jit(solution)/shard_map/ppermute | solution.py:331
  45.2 3.7 %collective-permute-start.5 = (bf16[3,128,1024]{2,1,0:T(8,128)(2,1)}, bf16[3,128,1024]{2,1,0:T(8,128)(2,1)}, u32[]{:S(2)}, u32[]{:S(2)}) collective-permute-start(bf16[3,128,1024]{2,1,0:T(8,128)(2,1)} %get-tuple-element.15), channel_id=1, source_target_pairs={{0,384},{128,0},{256,128},{384,256},{1,385},{129,1},{257,129},{385... | collective-permute-start | bytes 2359304 | tf_op jit(solution)/shard_map/ppermute | solution.py:331
  48.9 3.8 %collective-permute-start.10 = (bf16[4,384,256]{2,1,0:T(8,128)(2,1)}, bf16[4,384,256]{2,1,0:T(8,128)(2,1)}, u32[]{:S(2)}, u32[]{:S(2)}) collective-permute-start(bf16[4,384,256]{2,1,0:T(8,128)(2,1)} %pad_maximum_fusion.rest_0_), channel_id=1, source_target_pairs={{0,16},{8,24},{16,0},{24,8},{1,17},{9,25},{17,1},{25,9},{2,18},{10... | collective-permute-start | bytes 2359304 | tf_op jit(solution)/shard_map/ppermute | solution.py:339
  52.7 1.9 %collective-permute-start.11 = (bf16[4,384,256]{2,1,0:T(8,128)(2,1)}, bf16[4,384,256]{2,1,0:T(8,128)(2,1)}, u32[]{:S(2)}, u32[]{:S(2)}) collective-permute-start(bf16[4,384,256]{2,1,0:T(8,128)(2,1)} %pad_maximum_fusion.rest_0_), channel_id=1, source_target_pairs={{0,8},{8,16},{16,24},{24,0},{1,9},{9,17},{17,25},{25,1},{2,10},{10... | collective-permute-start | bytes 2359304 | tf_op jit(solution)/shard_map/ppermute | solution.py:339
  54.6 3.4 %collective-permute-start.9 = (bf16[4,384,256]{2,1,0:T(8,128)(2,1)}, bf16[4,384,256]{2,1,0:T(8,128)(2,1)}, u32[]{:S(2)}, u32[]{:S(2)}) collective-permute-start(bf16[4,384,256]{2,1,0:T(8,128)(2,1)} %pad_maximum_fusion.rest_0_), channel_id=1, source_target_pairs={{0,24},{8,0},{16,8},{24,16},{1,25},{9,1},{17,9},{25,17},{2,26},{10... | collective-permute-start | bytes 2359304 | tf_op jit(solution)/shard_map/ppermute | solution.py:339
  58.0 0.0 all-to-all-done
  58.0 1.0 reduce_sum.9
  59.0 0.7 broadcast_in_dim.2
  59.7 7.9 %all-to-all-start.1 = ((f32[64,8,128]{2,1,0:T(8,128)}), f32[64,8,128]{2,1,0:T(8,128)}, u32[]{:S(2)}, u32[]{:S(2)}) async-start(f32[64,8,128]{2,1,0:T(8,128)} %broadcast_in_dim.2), calls=%async_computation.1 | async-start | bytes 524288 | tf_op jit(solution)/shard_map/all_to_all | solution.py:358
  67.6 10.2 %collective-permute-done.4.ahead = bf16[3,128,1024]{2,1,0:T(8,128)(2,1)S(1)} collective-permute-done((bf16[3,128,1024]{2,1,0:T(8,128)(2,1)}, bf16[3,128,1024]{2,1,0:T(8,128)(2,1)S(1)}, u32[]{:S(2)}, u32[]{:S(2)}) %collective-permute-start.4) | collective-permute-done | bytes 786464 | tf_op jit(solution)/shard_map/ppermute | solution.py:331
  77.8 5.3 %collective-permute-done.5.back = bf16[3,128,1024]{2,1,0:T(8,128)(2,1)} collective-permute-done((bf16[3,128,1024]{2,1,0:T(8,128)(2,1)}, bf16[3,128,1024]{2,1,0:T(8,128)(2,1)}, u32[]{:S(2)}, u32[]{:S(2)}) %collective-permute-start.5) | collective-permute-done | bytes 786464 | tf_op jit(solution)/shard_map/ppermute | solution.py:331
  83.2 1.8 %onward.1 = (bf16[1,128,1024]{2,1,0:T(8,128)(2,1)}, bf16[1,128,1024]{2,1,0:T(8,128)(2,1)}) custom-call(bf16[3,128,1024]{2,1,0:T(8,128)(2,1)} %copy-done, bf16[3,128,1024]{2,1,0:T(8,128)(2,1)} %collective-permute-done.5.back), custom_call_target="tpu_custom_call" | custom-call | bytes 104857600 | tf_op jit(solution)/shard_map/onward/pallas_call | solution.py:134
  85.0 2.2 %collective-permute-start.6 = (bf16[1,128,1024]{2,1,0:T(8,128)(2,1)}, bf16[1,128,1024]{2,1,0:T(8,128)(2,1)S(1)}, u32[]{:S(2)}, u32[]{:S(2)}) collective-permute-start(bf16[1,128,1024]{2,1,0:T(8,128)(2,1)} %get-tuple-element.16), channel_id=1, source_target_pairs={{0,128},{128,256},{256,384},{384,0},{1,129},{129,257},{257,385},{3... | collective-permute-start | bytes 786440 | tf_op jit(solution)/shard_map/ppermute | solution.py:331
  87.2 0.0 copy-start.6
  87.2 5.4 %collective-permute-start.7 = (bf16[1,128,1024]{2,1,0:T(8,128)(2,1)}, bf16[1,128,1024]{2,1,0:T(8,128)(2,1)S(1)}, u32[]{:S(2)}, u32[]{:S(2)}) collective-permute-start(bf16[1,128,1024]{2,1,0:T(8,128)(2,1)} %get-tuple-element.17), channel_id=1, source_target_pairs={{0,384},{128,0},{256,128},{384,256},{1,385},{129,1},{257,129},{385... | collective-permute-start | bytes 786440 | tf_op jit(solution)/shard_map/ppermute | solution.py:331
  92.6 0.0 collective-permute-done.11.rest_3_
  92.6 3.9 %collective-permute-done.6.far_x.rest_4_ = bf16[1,128,1024]{2,1,0:T(8,128)(2,1)S(1)} collective-permute-done((bf16[1,128,1024]{2,1,0:T(8,128)(2,1)}, bf16[1,128,1024]{2,1,0:T(8,128)(2,1)S(1)}, u32[]{:S(2)}, u32[]{:S(2)}) %collective-permute-start.6) | collective-permute-done | bytes 262176 | tf_op jit(solution)/shard_map/ppermute | solution.py:331
  96.4 1.9 %collective-permute-done.7.far_dy.rest_5_ = bf16[1,128,1024]{2,1,0:T(8,128)(2,1)S(1)} collective-permute-done((bf16[1,128,1024]{2,1,0:T(8,128)(2,1)}, bf16[1,128,1024]{2,1,0:T(8,128)(2,1)S(1)}, u32[]{:S(2)}, u32[]{:S(2)}) %collective-permute-start.7) | collective-permute-done | bytes 262176 | tf_op jit(solution)/shard_map/ppermute | solution.py:331
  98.3 0.7 copy-done.3
  99.0 5.3 %hidden_sums.1 = (f32[3,128,256]{2,1,0:T(8,128)}, f32[3,128,256]{2,1,0:T(8,128)}) custom-call(s32[3]{0:T(128)} %pad_add_fusion.place, bf16[128,4096]{1,0:T(8,128)(2,1)} %bitcast.22, bf16[128,4096]{1,0:T(8,128)(2,1)} %bitcast.26, bf16[4,2,128,512]{3,2,1,0:T(8,128)(2,1)} %collective-permute-done.rest_1_.beside.after, ...), custom_call_target="tpu_custom_call" | custom-call | flops 805306368 | bytes 6291456 | tf_op jit(solution)/shard_map/hidden_sums/pallas_call | solution.py:231
  104.3 5.8 %collective-permute-start.12 = (f32[3,128,256]{2,1,0:T(8,128)}, f32[3,128,256]{2,1,0:T(8,128)S(1)}, u32[]{:S(2)}, u32[]{:S(2)}) collective-permute-start(f32[3,128,256]{2,1,0:T(8,128)} %get-tuple-element.19), channel_id=1, source_target_pairs={{0,64},{64,0},{1,65},{65,1},{2,66},{66,2},{3,67},{67,3},{4,68},{68... | collective-permute-start | bytes 1179656 | tf_op jit(solution)/shard_map/ppermute | solution.py:343
  110.1 1.9 %multiply_subtract_fusion = (f32[16,4096]{1,0:T(8,128)}, f32[16,4096]{1,0:T(8,128)}) fusion(f32[16,4096]{1,0:T(8,128)S(1)} %copy-done.6, f32[16,4096]{1,0:T(8,128)} %bitcast.15, f32[16,4096]{1,0:T(8,128)} %param.15), kind=kLoop, calls=%fused_computation.1 | loop fusion | flops 393216 | bytes 1310720 | tf_op jit(solution)/shard_map/sub | solution.py:384
  112.0 0.0 collective-permute-done.12.arrived_ref
  112.0 0.8 copy-done.5
  112.8 2.1 %activation.1 = bf16[4,3,128,256]{3,2,1,0:T(8,128)(2,1)} custom-call(f32[3,128,256]{2,1,0:T(8,128)} %get-tuple-element.18.mine_ref, f32[3,128,256]{2,1,0:T(8,128)} %copy-done.5, f32[16,4096]{1,0:T(8,128)} %get-tuple-element.23.after), custom_call_target="tpu_custom_call" | custom-call | flops 655360 | bytes 1048576 | tf_op jit(solution)/shard_map/activation/pallas_call | solution.py:265
  114.9 5.5 %all-to-all-start.2 = ((bf16[4,3,128,256]{3,2,1,0:T(8,128)(2,1)}), bf16[4,3,128,256]{3,2,1,0:T(8,128)(2,1)S(1)}, u32[]{:S(2)}, u32[]{:S(2)}) async-start(bf16[4,3,128,256]{3,2,1,0:T(8,128)(2,1)} %activation.1), calls=%async_computation.2 | async-start | bytes 1572864 | tf_op jit(solution)/shard_map/all_to_all | solution.py:388
  120.4 2.8 %repack_tokens.1 = bf16[3,2,128,512]{3,2,1,0:T(8,128)(2,1)} custom-call(s32[3]{0:T(128)} %pad_add_fusion.place, bf16[3,128,1024]{2,1,0:T(8,128)(2,1)} %copy-done, bf16[3,128,1024]{2,1,0:T(8,128)(2,1)} %collective-permute-done.5.back, bf16[1,128,1024]{2,1,0:T(8,128)(2,1)} %copy-done.2, bf16[1,128,1024]{2,1,0:T(8,128)(2,1)} %copy-done.3), custom_call_target="tpu_custom_call" | custom-call | bytes 209715200 | tf_op jit(solution)/shard_map/repack_tokens/pallas_call | solution.py:155
  123.2 2.2 %collective-permute-start.8 = (bf16[3,2,128,512]{3,2,1,0:T(8,128)(2,1)}, bf16[3,2,128,512]{3,2,1,0:T(8,128)(2,1)}, u32[]{:S(2)}, u32[]{:S(2)}) collective-permute-start(bf16[3,2,128,512]{3,2,1,0:T(8,128)(2,1)} %repack_tokens.1), channel_id=1, source_target_pairs={{0,64},{64,0},{1,65},{65,1},{2,66},{66,2},{3,67},{67,3},{4,68},{68... | collective-permute-start | bytes 2359304 | tf_op jit(solution)/shard_map/ppermute | solution.py:343
  125.4 16.6 %all-to-all-done.2.rest_0_ = bf16[4,3,128,256]{3,2,1,0:T(8,128)(2,1)S(1)} async-done(((bf16[4,3,128,256]{3,2,1,0:T(8,128)(2,1)}), bf16[4,3,128,256]{3,2,1,0:T(8,128)(2,1)S(1)}, u32[]{:S(2)}, u32[]{:S(2)}) %all-to-all-start.2) | async-done | bytes 786464 | tf_op jit(solution)/shard_map/all_to_all | solution.py:388
  142.0 2.7 %collective-permute-start.13 = (bf16[4,3,128,256]{3,2,1,0:T(8,128)(2,1)S(1)}, bf16[4,3,128,256]{3,2,1,0:T(8,128)(2,1)}, u32[]{:S(2)}, u32[]{:S(2)}) collective-permute-start(bf16[4,3,128,256]{3,2,1,0:T(8,128)(2,1)S(1)} %all-to-all-done.2.rest_0_), channel_id=1, source_target_pairs={{0,64},{64,0},{1,65},{65,1},{2,66},{66,2},{3,67},{67,3},{4,68},{68... | collective-permute-start | bytes 2359304 | tf_op jit(solution)/shard_map/ppermute | solution.py:343
  144.7 2.0 %collective-permute-done.13.rest_1_ = bf16[4,3,128,256]{3,2,1,0:T(8,128)(2,1)} collective-permute-done((bf16[4,3,128,256]{3,2,1,0:T(8,128)(2,1)S(1)}, bf16[4,3,128,256]{3,2,1,0:T(8,128)(2,1)}, u32[]{:S(2)}, u32[]{:S(2)}) %collective-permute-start.13) | collective-permute-done | bytes 786464 | tf_op jit(solution)/shard_map/ppermute | solution.py:343
  146.7 4.6 %weight_grads.1 = (bf16[1,512,256]{2,1,0:T(8,128)(2,1)}, bf16[1,512,256]{2,1,0:T(8,128)(2,1)}, bf16[1,256,512]{2,1,0:T(8,128)(2,1)}) custom-call(s32[3]{0:T(128)} %pad_add_fusion.place, bf16[128,4096]{1,0:T(8,128)(2,1)} %bitcast.23, bf16[128,4096]{1,0:T(8,128)(2,1)} %bitcast.27, bf16[4,2,128,512]{3,2,1,0:T(8,128)(2,1)} %collective-permute-done.rest_1_.beside.after, ...), custom_call_target="tpu_custom_call" | custom-call | flops 805306368 | bytes 5242880 | tf_op jit(solution)/shard_map/weight_grads/pallas_call | solution.py:309
  (15 shorter events, 0.0 us)
Async XLA Ops:
  3.5 5.7 %copy-start.4 = (bf16[384,256]{1,0:T(8,128)(2,1)S(1)}, bf16[384,256]{1,0:T(8,128)(2,1)}, u32[]{:S(2)}) copy-start(bf16[384,256]{1,0:T(8,128)(2,1)} %weight_share.1.after) | copy-start | bytes 589828
  6.6 15.4 %collective-permute-start = (bf16[4,2,128,512]{3,2,1,0:T(8,128)(2,1)}, bf16[4,2,128,512]{3,2,1,0:T(8,128)(2,1)}, u32[]{:S(2)}, u32[]{:S(2)}) collective-permute-start(bf16[4,2,128,512]{3,2,1,0:T(8,128)(2,1)} %tokens_beside.1), channel_id=1, source_target_pairs={{0,64},{64,0},{1,65},{65,1},{2,66},{66,2},{3,67},{67,3},{4,68},{68... | collective-permute-start | bytes 3145736 | tf_op jit(solution)/shard_map/ppermute | solution.py:343
  9.2 22.7 %collective-permute-start.1 = (bf16[384,256]{1,0:T(8,128)(2,1)S(1)}, bf16[384,256]{1,0:T(8,128)(2,1)S(1)}, u32[]{:S(2)}, u32[]{:S(2)}) collective-permute-start(bf16[384,256]{1,0:T(8,128)(2,1)S(1)} %copy-done.4), channel_id=1, source_target_pairs={{0,384},{128,0},{256,128},{384,256},{1,385},{129,1},{257,129},{385... | collective-permute-start | bytes 589832 | tf_op jit(solution)/shard_map/ppermute | solution.py:335
  14.2 20.2 %collective-permute-start.2 = (bf16[384,256]{1,0:T(8,128)(2,1)S(1)}, bf16[384,256]{1,0:T(8,128)(2,1)S(1)}, u32[]{:S(2)}, u32[]{:S(2)}) collective-permute-start(bf16[384,256]{1,0:T(8,128)(2,1)S(1)} %copy-done.4), channel_id=1, source_target_pairs={{0,256},{128,384},{256,0},{384,128},{1,257},{129,385},{257,1},{385... | collective-permute-start | bytes 589832 | tf_op jit(solution)/shard_map/ppermute | solution.py:335
  18.7 18.3 %collective-permute-start.3 = (bf16[384,256]{1,0:T(8,128)(2,1)S(1)}, bf16[384,256]{1,0:T(8,128)(2,1)S(1)}, u32[]{:S(2)}, u32[]{:S(2)}) collective-permute-start(bf16[384,256]{1,0:T(8,128)(2,1)S(1)} %copy-done.4), channel_id=1, source_target_pairs={{0,128},{128,256},{256,384},{384,0},{1,129},{129,257},{257,385},{3... | collective-permute-start | bytes 589832 | tf_op jit(solution)/shard_map/ppermute | solution.py:335
  23.7 34.3 %all-to-all-start = ((f32[64,8,128]{2,1,0:T(8,128)}), f32[64,8,128]{2,1,0:T(8,128)}, u32[]{:S(2)}, u32[]{:S(2)}) async-start(f32[64,8,128]{2,1,0:T(8,128)} %bitcast.29), calls=%async_computation | async-start | bytes 524288 | tf_op jit(solution)/shard_map/all_to_all | solution.py:351
  41.2 36.6 %collective-permute-start.4 = (bf16[3,128,1024]{2,1,0:T(8,128)(2,1)}, bf16[3,128,1024]{2,1,0:T(8,128)(2,1)S(1)}, u32[]{:S(2)}, u32[]{:S(2)}) collective-permute-start(bf16[3,128,1024]{2,1,0:T(8,128)(2,1)} %get-tuple-element.14), channel_id=1, source_target_pairs={{0,128},{128,256},{256,384},{384,0},{1,129},{129,257},{257,385},{3... | collective-permute-start | bytes 2359304 | tf_op jit(solution)/shard_map/ppermute | solution.py:331
  45.2 38.0 %collective-permute-start.5 = (bf16[3,128,1024]{2,1,0:T(8,128)(2,1)}, bf16[3,128,1024]{2,1,0:T(8,128)(2,1)}, u32[]{:S(2)}, u32[]{:S(2)}) collective-permute-start(bf16[3,128,1024]{2,1,0:T(8,128)(2,1)} %get-tuple-element.15), channel_id=1, source_target_pairs={{0,384},{128,0},{256,128},{384,256},{1,385},{129,1},{257,129},{385... | collective-permute-start | bytes 2359304 | tf_op jit(solution)/shard_map/ppermute | solution.py:331
  48.9 43.6 %collective-permute-start.10 = (bf16[4,384,256]{2,1,0:T(8,128)(2,1)}, bf16[4,384,256]{2,1,0:T(8,128)(2,1)}, u32[]{:S(2)}, u32[]{:S(2)}) collective-permute-start(bf16[4,384,256]{2,1,0:T(8,128)(2,1)} %pad_maximum_fusion.rest_0_), channel_id=1, source_target_pairs={{0,16},{8,24},{16,0},{24,8},{1,17},{9,25},{17,1},{25,9},{2,18},{10... | collective-permute-start | bytes 2359304 | tf_op jit(solution)/shard_map/ppermute | solution.py:339
  52.7 39.9 %collective-permute-start.11 = (bf16[4,384,256]{2,1,0:T(8,128)(2,1)}, bf16[4,384,256]{2,1,0:T(8,128)(2,1)}, u32[]{:S(2)}, u32[]{:S(2)}) collective-permute-start(bf16[4,384,256]{2,1,0:T(8,128)(2,1)} %pad_maximum_fusion.rest_0_), channel_id=1, source_target_pairs={{0,8},{8,16},{16,24},{24,0},{1,9},{9,17},{17,25},{25,1},{2,10},{10... | collective-permute-start | bytes 2359304 | tf_op jit(solution)/shard_map/ppermute | solution.py:339
  54.6 38.0 %collective-permute-start.9 = (bf16[4,384,256]{2,1,0:T(8,128)(2,1)}, bf16[4,384,256]{2,1,0:T(8,128)(2,1)}, u32[]{:S(2)}, u32[]{:S(2)}) collective-permute-start(bf16[4,384,256]{2,1,0:T(8,128)(2,1)} %pad_maximum_fusion.rest_0_), channel_id=1, source_target_pairs={{0,24},{8,0},{16,8},{24,16},{1,25},{9,1},{17,9},{25,17},{2,26},{10... | collective-permute-start | bytes 2359304 | tf_op jit(solution)/shard_map/ppermute | solution.py:339
  59.7 50.4 %all-to-all-start.1 = ((f32[64,8,128]{2,1,0:T(8,128)}), f32[64,8,128]{2,1,0:T(8,128)}, u32[]{:S(2)}, u32[]{:S(2)}) async-start(f32[64,8,128]{2,1,0:T(8,128)} %broadcast_in_dim.2), calls=%async_computation.1 | async-start | bytes 524288 | tf_op jit(solution)/shard_map/all_to_all | solution.py:358
  77.8 5.3 %copy-start = (bf16[3,128,1024]{2,1,0:T(8,128)(2,1)}, bf16[3,128,1024]{2,1,0:T(8,128)(2,1)S(1)}, u32[]{:S(2)}) copy-start(bf16[3,128,1024]{2,1,0:T(8,128)(2,1)S(1)} %collective-permute-done.4.ahead) | copy-start | bytes 2359300
  85.0 11.4 %collective-permute-start.6 = (bf16[1,128,1024]{2,1,0:T(8,128)(2,1)}, bf16[1,128,1024]{2,1,0:T(8,128)(2,1)S(1)}, u32[]{:S(2)}, u32[]{:S(2)}) collective-permute-start(bf16[1,128,1024]{2,1,0:T(8,128)(2,1)} %get-tuple-element.16), channel_id=1, source_target_pairs={{0,128},{128,256},{256,384},{384,0},{1,129},{129,257},{257,385},{3... | collective-permute-start | bytes 786440 | tf_op jit(solution)/shard_map/ppermute | solution.py:331
  87.2 23.0 %copy-start.6 = (f32[16,4096]{1,0:T(8,128)S(1)}, f32[16,4096]{1,0:T(8,128)}, u32[]{:S(2)}) copy-start(f32[16,4096]{1,0:T(8,128)} %param.14) | copy-start | bytes 786436
  87.2 11.2 %collective-permute-start.7 = (bf16[1,128,1024]{2,1,0:T(8,128)(2,1)}, bf16[1,128,1024]{2,1,0:T(8,128)(2,1)S(1)}, u32[]{:S(2)}, u32[]{:S(2)}) collective-permute-start(bf16[1,128,1024]{2,1,0:T(8,128)(2,1)} %get-tuple-element.17), channel_id=1, source_target_pairs={{0,384},{128,0},{256,128},{384,256},{1,385},{129,1},{257,129},{385... | collective-permute-start | bytes 786440 | tf_op jit(solution)/shard_map/ppermute | solution.py:331
  96.4 1.9 %copy-start.2 = (bf16[1,128,1024]{2,1,0:T(8,128)(2,1)}, bf16[1,128,1024]{2,1,0:T(8,128)(2,1)S(1)}, u32[]{:S(2)}) copy-start(bf16[1,128,1024]{2,1,0:T(8,128)(2,1)S(1)} %collective-permute-done.6.far_x.rest_4_) | copy-start | bytes 786436
  98.3 0.7 copy-start.3
  104.3 7.7 %collective-permute-start.12 = (f32[3,128,256]{2,1,0:T(8,128)}, f32[3,128,256]{2,1,0:T(8,128)S(1)}, u32[]{:S(2)}, u32[]{:S(2)}) collective-permute-start(f32[3,128,256]{2,1,0:T(8,128)} %get-tuple-element.19), channel_id=1, source_target_pairs={{0,64},{64,0},{1,65},{65,1},{2,66},{66,2},{3,67},{67,3},{4,68},{68... | collective-permute-start | bytes 1179656 | tf_op jit(solution)/shard_map/ppermute | solution.py:343
  112.0 0.8 copy-start.5
  114.9 27.1 %all-to-all-start.2 = ((bf16[4,3,128,256]{3,2,1,0:T(8,128)(2,1)}), bf16[4,3,128,256]{3,2,1,0:T(8,128)(2,1)S(1)}, u32[]{:S(2)}, u32[]{:S(2)}) async-start(bf16[4,3,128,256]{3,2,1,0:T(8,128)(2,1)} %activation.1), calls=%async_computation.2 | async-start | bytes 1572864 | tf_op jit(solution)/shard_map/all_to_all | solution.py:388
  123.2 21.4 %collective-permute-start.8 = (bf16[3,2,128,512]{3,2,1,0:T(8,128)(2,1)}, bf16[3,2,128,512]{3,2,1,0:T(8,128)(2,1)}, u32[]{:S(2)}, u32[]{:S(2)}) collective-permute-start(bf16[3,2,128,512]{3,2,1,0:T(8,128)(2,1)} %repack_tokens.1), channel_id=1, source_target_pairs={{0,64},{64,0},{1,65},{65,1},{2,66},{66,2},{3,67},{67,3},{4,68},{68... | collective-permute-start | bytes 2359304 | tf_op jit(solution)/shard_map/ppermute | solution.py:343
  142.0 4.7 %copy-start.1 = (bf16[4,3,128,256]{3,2,1,0:T(8,128)(2,1)}, bf16[4,3,128,256]{3,2,1,0:T(8,128)(2,1)S(1)}, u32[]{:S(2)}) copy-start(bf16[4,3,128,256]{3,2,1,0:T(8,128)(2,1)S(1)} %all-to-all-done.2.rest_0_) | copy-start | bytes 2359300
  142.0 4.7 %collective-permute-start.13 = (bf16[4,3,128,256]{3,2,1,0:T(8,128)(2,1)S(1)}, bf16[4,3,128,256]{3,2,1,0:T(8,128)(2,1)}, u32[]{:S(2)}, u32[]{:S(2)}) collective-permute-start(bf16[4,3,128,256]{3,2,1,0:T(8,128)(2,1)S(1)} %all-to-all-done.2.rest_0_), channel_id=1, source_target_pairs={{0,64},{64,0},{1,65},{65,1},{2,66},{66,2},{3,67},{67,3},{4,68},{68... | collective-permute-start | bytes 2359304 | tf_op jit(solution)/shard_map/ppermute | solution.py:343

commit v10 on v9

--- a/solution.py
+++ b/solution.py
@@ -72,28 +72,6 @@
         cost_estimate=pl.CostEstimate(flops=0, bytes_accessed=1 << 18, transcendentals=0),
         name="weight_share",
     )(place, gate, up, down)
-
-
-def beside_kernel(place, x, dy, after, out, sems):
-    del after
-    copies = []
-    for i in range(CHIPS):
-        other = columns(i * WIDE + (1 - place[0]) * HALF)
-        copies += [(x.at[:, other], out.at[i, 0]), (dy.at[:, other], out.at[i, 1])]
-    run_copies(copies, sems)
-
-
-def for_beside(place, x, dy, after):
-    return pl.pallas_call(
-        beside_kernel,
-        out_shape=jax.ShapeDtypeStruct((CHIPS, 2, ROWS, HALF), BF16),
-        in_specs=[SMEM] + [ANY] * 3,
-        out_specs=VMEM,
-        scratch_shapes=[pltpu.SemaphoreType.DMA((8,))],
-        compiler_params=pltpu.CompilerParams(vmem_limit_bytes=VMEM_LIMIT),
-        cost_estimate=pl.CostEstimate(flops=0, bytes_accessed=2 << 20, transcendentals=0),
-        name="tokens_beside",
-    )(place, x, dy, after)
 
 
 def pack_kernel(waited, place, x, dy, *rest):
@@ -182,7 +160,7 @@
     )(delta, after)
 
 
-def hidden_kernel(parts, waited, place, x, dy, beside, *rest):
+def hidden_kernel(parts, waited, place, x, dy, beside_x, beside_dy, *rest):
     weights = rest[:parts]
     mine, theirs, xs, dys, gates, ups, downs, sems = rest[parts + waited :]
     gate_rows, down_rows = HALF // parts, HID // parts
@@ -191,8 +169,8 @@
     for shift in range(CHIPS):
         chip = lax.rem(place[2] + shift, CHIPS)
         own = columns(chip * WIDE + place[0] * HALF)
-        to_gate += [(x.at[:, own], xs.at[shift, :ROWS]), (beside.at[chip, 0], xs.at[shift, ROWS:])]
-        to_down += [(dy.at[:, own], dys.at[shift, :ROWS]), (beside.at[chip, 1], dys.at[shift, ROWS:])]
+        to_gate += [(x.at[:, own], xs.at[shift, :ROWS]), (beside_x.at[:, own], xs.at[shift, ROWS:])]
+        to_down += [(dy.at[:, own], dys.at[shift, :ROWS]), (beside_dy.at[:, own], dys.at[shift, ROWS:])]
     for shift, ref in enumerate(weights):
         part = lax.rem(place[1] + shift, parts)
         gate_at = pl.ds(pl.multiple_of(part * gate_rows, gate_rows), gate_rows)
@@ -231,7 +209,7 @@
     return pl.pallas_call(
         functools.partial(hidden_kernel, len(weights), len(after)),
         out_shape=(out, out),
-        in_specs=[SMEM] + [ANY] * (3 + len(weights) + len(after)),
+        in_specs=[SMEM] + [ANY] * (4 + len(weights) + len(after)),
         out_specs=(VMEM, VMEM),
         scratch_shapes=[
             pltpu.VMEM((CHIPS, 2 * ROWS, HALF), BF16),
@@ -244,7 +222,7 @@
         compiler_params=pltpu.CompilerParams(vmem_limit_bytes=VMEM_LIMIT),
         cost_estimate=pl.CostEstimate(flops=6 * 256 * 2048 * 256, bytes_accessed=6 << 20, transcendentals=0),
         name="hidden_sums",
-    )(place, x, dy, beside, *weights, *after)
+    )(place, x, dy, *beside, *weights, *after)
 
 
 def activation_kernel(mine_ref, arrived_ref, after, out, mine, arrived, sems):
@@ -278,7 +256,7 @@
     )(mine, arrived, after)
 
 
-def grads_kernel(place, x, dy, beside, ahead, back, far_x, far_dy, swapped, *rest):
+def grads_kernel(place, x, dy, beside_x, beside_dy, ahead, back, far_x, far_dy, swapped, *rest):
     acts, (gg, gu, gd, xs, dys, hs, sems) = rest[:2], rest[2:]
     core, chip = place[0], place[2]
     half, own = columns(core * HALF), columns(chip * WIDE + core * HALF)
@@ -287,7 +265,7 @@
         (a.at[:, half], b.at[:, half])
         for a, b in ((ahead.at[0], ahead.at[1]), (far_x.at[0], far_dy.at[0]), (back.at[0], back.at[1]))
     ]
-    there = [(beside.at[chip, 0], beside.at[chip, 1])]
+    there = [(beside_x.at[:, own], beside_dy.at[:, own])]
     there += [(swapped.at[i, 0], swapped.at[i, 1]) for i in range(CHIPS - 1)]
     early, late = [], []
     for i, (a, b) in enumerate(here + there):
@@ -313,7 +291,7 @@
             jax.ShapeDtypeStruct((1, HALF, HID), BF16),
             jax.ShapeDtypeStruct((1, HID, HALF), BF16),
         ),
-        in_specs=[SMEM] + [ANY] * (8 + len(acts)),
+        in_specs=[SMEM] + [ANY] * (9 + len(acts)),
         out_specs=(VMEM,) * 3,
         scratch_shapes=[
             pltpu.VMEM((tokens, HALF), BF16),
@@ -324,7 +302,7 @@
         compiler_params=pltpu.CompilerParams(vmem_limit_bytes=VMEM_LIMIT),
         cost_estimate=pl.CostEstimate(flops=6 * 1024 * 512 * 256, bytes_accessed=5 << 20, transcendentals=0),
         name="weight_grads",
-    )(place, x, dy, beside, *arrived, swapped, *acts)
+    )(place, x, dy, *beside, *arrived, swapped, *acts)
 
 
 def to_shift(value, shift):
@@ -369,9 +347,9 @@
     shares = jnp.stack([share] + [shares[shift] for shift in (1, 2, 3)])
     weights = [shares] + [from_x(shares, shift, parts) for shift in range(1, parts)]
 
-    beside = other_core(for_beside(place, x, dy, share))
-    part = share_of_sum(staged(delta[0], beside))
-    ahead, back = pack(place, x, dy, (shares, beside))
+    beside = (other_core(x), other_core(dy))
+    part = share_of_sum(staged(delta[0], beside[0]))
+    ahead, back = pack(place, x, dy, (shares, *beside))
     ahead, back = to_shift(ahead, 1), to_shift(back, 3)
     far_x, far_dy = onward(ahead, back)
     far_x, far_dy = to_shift(far_x, 1), to_shift(far_dy, 3)

time: 152 us -> 151 us (level)
  Pallas kernels: 26.9 us -> 23.8 us
  starting transfers between devices: 71.8 us -> 73.7 us
    pallas_call x1 -> x0, Pallas kernels: 3.11 us -> none  [for_beside(): pl.pallas_call(beside_kernel, out_shape=jax.ShapeDtypeStruct((CHIPS, 2, R...]
    ppermute x4 -> x5, starting transfers between devices: 13.2 us -> 15 us  [other_core(): return lax.ppermute(value, 'core', [(0, 1), (1, 0)])]
  transfers between devices with their start and end apart: 17 -> 18, of which waited for: 8 -> 9; matrix products, arithmetic and copies ran while one was open for 3% -> 3% of each run, Pallas kernels for 10% -> 11%
where the time goes in v10:
time: 151 us; the launch traced here: 150 us
  starting transfers between devices  73.7 us (49%)
  waiting for transfers between devices  45.1 us (30%)
  Pallas kernels  23.8 us (16%)
  other arithmetic  4.45 us (3%)
  local copies, waits for them, and re-layouts  2.22 us (1%)
    ppermute x4, waiting for transfers between devices, to_shift(): lax.ppermute(value, 'yh', [(i, (i + shift) % CHIPS) for i in range(CHIPS)])  21.3 us
    all_to_all x1, waiting for transfers between devices, on_device(): acts = lax.all_to_all(acts, 'yh', 0, 0, tiled=True)  16.5 us
    ppermute x4, starting transfers between devices, to_shift(): lax.ppermute(value, 'yh', [(i, (i + shift) % CHIPS) for i in range(CHIPS)])  15.1 us
    ppermute x5, starting transfers between devices, other_core(): return lax.ppermute(value, 'core', [(0, 1), (1, 0)])  15 us
    ppermute x3, starting transfers between devices, from_shift(): lax.ppermute(value, 'yh', [(i, (i - shift) % CHIPS) for i in range(CHIPS)])  12.7 us
    ppermute x3, starting transfers between devices, from_x(): lax.ppermute(value, 'x', [(i, (i - shift) % size) for i in range(size)])  9.66 us
    all_to_all x1, starting transfers between devices, share_of_sum(): lax.all_to_all(tiles, everyone, 0, 0, tiled=True)  8.37 us
    all_to_all x1, starting transfers between devices, whole_mean(): lax.all_to_all(jnp.broadcast_to(part / count, (count, 8, 128)), everyone,...  7.27 us
  transfers between devices with their start and end apart: 18, of which 9 were waited for; matrix products, arithmetic and copies ran while one was open for 3% of the time, Pallas kernels for 11%

profile of v10, /device:TPU:459, one launch (start us, length us, event | category | flops | bytes accessed | tf_op | source)
XLA Modules:
  0.0 150.2 jit_solution(4839165927332936962)
XLA Ops:
  0.6 2.6 %collective-permute-start = (bf16[128,4096]{1,0:T(8,128)(2,1)}, bf16[128,4096]{1,0:T(8,128)(2,1)}, u32[]{:S(2)}, u32[]{:S(2)}) collective-permute-start(bf16[128,4096]{1,0:T(8,128)(2,1)} %bitcast.20), channel_id=1, source_target_pairs={{0,64},{64,0},{1,65},{65,1},{2,66},{66,2},{3,67},{67,3},{4,68},{68... | collective-permute-start | bytes 3145736 | tf_op jit(solution)/shard_map/ppermute | solution.py:321
  3.2 1.9 %collective-permute-start.1 = (bf16[128,4096]{1,0:T(8,128)(2,1)}, bf16[128,4096]{1,0:T(8,128)(2,1)}, u32[]{:S(2)}, u32[]{:S(2)}) collective-permute-start(bf16[128,4096]{1,0:T(8,128)(2,1)} %bitcast.24), channel_id=1, source_target_pairs={{0,64},{64,0},{1,65},{65,1},{2,66},{66,2},{3,67},{67,3},{4,68},{68... | collective-permute-start | bytes 3145736 | tf_op jit(solution)/shard_map/ppermute | solution.py:321
  5.2 0.6 pad_add_fusion.place
  5.7 2.2 %weight_share.1 = bf16[384,256]{1,0:T(8,128)(2,1)} custom-call(s32[3]{0:T(128)} %pad_add_fusion.place, bf16[512,256]{1,0:T(8,128)(2,1)} %gate.1, bf16[512,256]{1,0:T(8,128)(2,1)} %up.1, bf16[256,512]{1,0:T(8,128)(2,1)} %down.1), custom_call_target="tpu_custom_call" | custom-call | bytes 262144 | tf_op jit(solution)/shard_map/weight_share/pallas_call | solution.py:65
  8.0 5.0 %collective-permute-start.2 = (bf16[384,256]{1,0:T(8,128)(2,1)}, bf16[384,256]{1,0:T(8,128)(2,1)S(1)}, u32[]{:S(2)}, u32[]{:S(2)}) collective-permute-start(bf16[384,256]{1,0:T(8,128)(2,1)} %weight_share.1), channel_id=1, source_target_pairs={{0,384},{128,0},{256,128},{384,256},{1,385},{129,1},{257,129},{385... | collective-permute-start | bytes 589832 | tf_op jit(solution)/shard_map/ppermute | solution.py:313
  13.0 4.4 %collective-permute-start.3 = (bf16[384,256]{1,0:T(8,128)(2,1)}, bf16[384,256]{1,0:T(8,128)(2,1)S(1)}, u32[]{:S(2)}, u32[]{:S(2)}) collective-permute-start(bf16[384,256]{1,0:T(8,128)(2,1)} %weight_share.1), channel_id=1, source_target_pairs={{0,256},{128,384},{256,0},{384,128},{1,257},{129,385},{257,1},{385... | collective-permute-start | bytes 589832 | tf_op jit(solution)/shard_map/ppermute | solution.py:313
  17.4 3.3 %collective-permute-start.4 = (bf16[384,256]{1,0:T(8,128)(2,1)}, bf16[384,256]{1,0:T(8,128)(2,1)S(1)}, u32[]{:S(2)}, u32[]{:S(2)}) collective-permute-start(bf16[384,256]{1,0:T(8,128)(2,1)} %weight_share.1), channel_id=1, source_target_pairs={{0,128},{128,256},{256,384},{384,0},{1,129},{129,257},{257,385},{3... | collective-permute-start | bytes 589832 | tf_op jit(solution)/shard_map/ppermute | solution.py:313
  20.7 0.0 collective-permute-done.rest_1_.beside_x.after
  20.7 1.7 %delta_staged.1 = f32[16,4096]{1,0:T(8,128)} custom-call(f32[16,4096]{1,0:T(8,128)} %bitcast.30, bf16[128,4096]{1,0:T(8,128)(2,1)} %collective-permute-done.rest_1_.beside_x.after), custom_call_target="tpu_custom_call" | custom-call | bytes 524288 | tf_op jit(solution)/shard_map/delta_staged/pallas_call | solution.py:151
  22.4 0.0 copy-start.4
  22.4 8.4 %all-to-all-start = ((f32[64,8,128]{2,1,0:T(8,128)}), f32[64,8,128]{2,1,0:T(8,128)}, u32[]{:S(2)}, u32[]{:S(2)}) async-start(f32[64,8,128]{2,1,0:T(8,128)} %bitcast.28), calls=%async_computation | async-start | bytes 524288 | tf_op jit(solution)/shard_map/all_to_all | solution.py:329
  30.8 0.0 collective-permute-done.2
  30.8 2.6 %collective-permute-done.3 = bf16[384,256]{1,0:T(8,128)(2,1)S(1)} collective-permute-done((bf16[384,256]{1,0:T(8,128)(2,1)}, bf16[384,256]{1,0:T(8,128)(2,1)S(1)}, u32[]{:S(2)}, u32[]{:S(2)}) %collective-permute-start.3) | collective-permute-done | bytes 196640 | tf_op jit(solution)/shard_map/ppermute | solution.py:313
  33.5 2.5 %collective-permute-done.4 = bf16[384,256]{1,0:T(8,128)(2,1)S(1)} collective-permute-done((bf16[384,256]{1,0:T(8,128)(2,1)}, bf16[384,256]{1,0:T(8,128)(2,1)S(1)}, u32[]{:S(2)}, u32[]{:S(2)}) %collective-permute-start.4) | collective-permute-done | bytes 196640 | tf_op jit(solution)/shard_map/ppermute | solution.py:313
  35.9 1.0 pad_maximum_fusion.rest_0_
  36.9 0.0 collective-permute-done.1.rest_2_.beside_dy
  36.9 3.2 %pack_tokens.1 = (bf16[3,128,1024]{2,1,0:T(8,128)(2,1)}, bf16[3,128,1024]{2,1,0:T(8,128)(2,1)}) custom-call(s32[3]{0:T(128)} %pad_add_fusion.place, bf16[128,4096]{1,0:T(8,128)(2,1)} %bitcast.21, bf16[128,4096]{1,0:T(8,128)(2,1)} %bitcast.25, bf16[4,384,256]{2,1,0:T(8,128)(2,1)} %pad_maximum_fusion.rest_0_, ...), custom_call_target="tpu_custom_call" | custom-call | bytes 4194304 | tf_op jit(solution)/shard_map/pack_tokens/pallas_call | solution.py:94
  40.2 4.0 %collective-permute-start.5 = (bf16[3,128,1024]{2,1,0:T(8,128)(2,1)}, bf16[3,128,1024]{2,1,0:T(8,128)(2,1)S(1)}, u32[]{:S(2)}, u32[]{:S(2)}) collective-permute-start(bf16[3,128,1024]{2,1,0:T(8,128)(2,1)} %get-tuple-element.14), channel_id=1, source_target_pairs={{0,128},{128,256},{256,384},{384,0},{1,129},{129,257},{257,385},{3... | collective-permute-start | bytes 2359304 | tf_op jit(solution)/shard_map/ppermute | solution.py:309
  44.1 3.6 %collective-permute-start.6 = (bf16[3,128,1024]{2,1,0:T(8,128)(2,1)}, bf16[3,128,1024]{2,1,0:T(8,128)(2,1)}, u32[]{:S(2)}, u32[]{:S(2)}) collective-permute-start(bf16[3,128,1024]{2,1,0:T(8,128)(2,1)} %get-tuple-element.15), channel_id=1, source_target_pairs={{0,384},{128,0},{256,128},{384,256},{1,385},{129,1},{257,129},{385... | collective-permute-start | bytes 2359304 | tf_op jit(solution)/shard_map/ppermute | solution.py:309
  47.8 2.2 %collective-permute-start.10 = (bf16[4,384,256]{2,1,0:T(8,128)(2,1)}, bf16[4,384,256]{2,1,0:T(8,128)(2,1)}, u32[]{:S(2)}, u32[]{:S(2)}) collective-permute-start(bf16[4,384,256]{2,1,0:T(8,128)(2,1)} %pad_maximum_fusion.rest_0_), channel_id=1, source_target_pairs={{0,24},{8,0},{16,8},{24,16},{1,25},{9,1},{17,9},{25,17},{2,26},{10... | collective-permute-start | bytes 2359304 | tf_op jit(solution)/shard_map/ppermute | solution.py:317
  49.9 4.0 %collective-permute-start.11 = (bf16[4,384,256]{2,1,0:T(8,128)(2,1)}, bf16[4,384,256]{2,1,0:T(8,128)(2,1)}, u32[]{:S(2)}, u32[]{:S(2)}) collective-permute-start(bf16[4,384,256]{2,1,0:T(8,128)(2,1)} %pad_maximum_fusion.rest_0_), channel_id=1, source_target_pairs={{0,16},{8,24},{16,0},{24,8},{1,17},{9,25},{17,1},{25,9},{2,18},{10... | collective-permute-start | bytes 2359304 | tf_op jit(solution)/shard_map/ppermute | solution.py:317
  54.0 3.4 %collective-permute-start.12 = (bf16[4,384,256]{2,1,0:T(8,128)(2,1)}, bf16[4,384,256]{2,1,0:T(8,128)(2,1)}, u32[]{:S(2)}, u32[]{:S(2)}) collective-permute-start(bf16[4,384,256]{2,1,0:T(8,128)(2,1)} %pad_maximum_fusion.rest_0_), channel_id=1, source_target_pairs={{0,8},{8,16},{16,24},{24,0},{1,9},{9,17},{17,25},{25,1},{2,10},{10... | collective-permute-start | bytes 2359304 | tf_op jit(solution)/shard_map/ppermute | solution.py:317
  57.4 0.0 all-to-all-done
  57.4 1.0 reduce_sum.9
  58.5 0.7 broadcast_in_dim.2
  59.2 7.3 %all-to-all-start.1 = ((f32[64,8,128]{2,1,0:T(8,128)}), f32[64,8,128]{2,1,0:T(8,128)}, u32[]{:S(2)}, u32[]{:S(2)}) async-start(f32[64,8,128]{2,1,0:T(8,128)} %broadcast_in_dim.2), calls=%async_computation.1 | async-start | bytes 524288 | tf_op jit(solution)/shard_map/all_to_all | solution.py:336
  66.5 10.3 %collective-permute-done.5.ahead = bf16[3,128,1024]{2,1,0:T(8,128)(2,1)S(1)} collective-permute-done((bf16[3,128,1024]{2,1,0:T(8,128)(2,1)}, bf16[3,128,1024]{2,1,0:T(8,128)(2,1)S(1)}, u32[]{:S(2)}, u32[]{:S(2)}) %collective-permute-start.5) | collective-permute-done | bytes 786464 | tf_op jit(solution)/shard_map/ppermute | solution.py:309
  76.8 5.3 %collective-permute-done.6.back = bf16[3,128,1024]{2,1,0:T(8,128)(2,1)} collective-permute-done((bf16[3,128,1024]{2,1,0:T(8,128)(2,1)}, bf16[3,128,1024]{2,1,0:T(8,128)(2,1)}, u32[]{:S(2)}, u32[]{:S(2)}) %collective-permute-start.6) | collective-permute-done | bytes 786464 | tf_op jit(solution)/shard_map/ppermute | solution.py:309
  82.1 1.8 %onward.1 = (bf16[1,128,1024]{2,1,0:T(8,128)(2,1)}, bf16[1,128,1024]{2,1,0:T(8,128)(2,1)}) custom-call(bf16[3,128,1024]{2,1,0:T(8,128)(2,1)} %copy-done, bf16[3,128,1024]{2,1,0:T(8,128)(2,1)} %collective-permute-done.6.back), custom_call_target="tpu_custom_call" | custom-call | bytes 104857600 | tf_op jit(solution)/shard_map/onward/pallas_call | solution.py:112
  84.0 2.2 %collective-permute-start.7 = (bf16[1,128,1024]{2,1,0:T(8,128)(2,1)}, bf16[1,128,1024]{2,1,0:T(8,128)(2,1)S(1)}, u32[]{:S(2)}, u32[]{:S(2)}) collective-permute-start(bf16[1,128,1024]{2,1,0:T(8,128)(2,1)} %get-tuple-element.16), channel_id=1, source_target_pairs={{0,128},{128,256},{256,384},{384,0},{1,129},{129,257},{257,385},{3... | collective-permute-start | bytes 786440 | tf_op jit(solution)/shard_map/ppermute | solution.py:309
  86.1 0.0 copy-start.6
  86.1 5.4 %collective-permute-start.8 = (bf16[1,128,1024]{2,1,0:T(8,128)(2,1)}, bf16[1,128,1024]{2,1,0:T(8,128)(2,1)S(1)}, u32[]{:S(2)}, u32[]{:S(2)}) collective-permute-start(bf16[1,128,1024]{2,1,0:T(8,128)(2,1)} %get-tuple-element.17), channel_id=1, source_target_pairs={{0,384},{128,0},{256,128},{384,256},{1,385},{129,1},{257,129},{385... | collective-permute-start | bytes 786440 | tf_op jit(solution)/shard_map/ppermute | solution.py:309
  91.5 0.1 collective-permute-done.12.rest_3_
  91.7 3.8 %collective-permute-done.7.far_x.rest_4_ = bf16[1,128,1024]{2,1,0:T(8,128)(2,1)S(1)} collective-permute-done((bf16[1,128,1024]{2,1,0:T(8,128)(2,1)}, bf16[1,128,1024]{2,1,0:T(8,128)(2,1)S(1)}, u32[]{:S(2)}, u32[]{:S(2)}) %collective-permute-start.7) | collective-permute-done | bytes 262176 | tf_op jit(solution)/shard_map/ppermute | solution.py:309
  95.4 1.9 %collective-permute-done.8.far_dy.rest_5_ = bf16[1,128,1024]{2,1,0:T(8,128)(2,1)S(1)} collective-permute-done((bf16[1,128,1024]{2,1,0:T(8,128)(2,1)}, bf16[1,128,1024]{2,1,0:T(8,128)(2,1)S(1)}, u32[]{:S(2)}, u32[]{:S(2)}) %collective-permute-start.8) | collective-permute-done | bytes 262176 | tf_op jit(solution)/shard_map/ppermute | solution.py:309
  97.3 0.7 copy-done.3
  98.0 5.3 %hidden_sums.1 = (f32[3,128,256]{2,1,0:T(8,128)}, f32[3,128,256]{2,1,0:T(8,128)}) custom-call(s32[3]{0:T(128)} %pad_add_fusion.place, bf16[128,4096]{1,0:T(8,128)(2,1)} %bitcast.22, bf16[128,4096]{1,0:T(8,128)(2,1)} %bitcast.26, bf16[128,4096]{1,0:T(8,128)(2,1)} %collective-permute-done.rest_1_.beside_x.after, ...), custom_call_target="tpu_custom_call" | custom-call | flops 805306368 | bytes 6291456 | tf_op jit(solution)/shard_map/hidden_sums/pallas_call | solution.py:209
  103.3 5.7 %collective-permute-start.13 = (f32[3,128,256]{2,1,0:T(8,128)}, f32[3,128,256]{2,1,0:T(8,128)S(1)}, u32[]{:S(2)}, u32[]{:S(2)}) collective-permute-start(f32[3,128,256]{2,1,0:T(8,128)} %get-tuple-element.19), channel_id=1, source_target_pairs={{0,64},{64,0},{1,65},{65,1},{2,66},{66,2},{3,67},{67,3},{4,68},{68... | collective-permute-start | bytes 1179656 | tf_op jit(solution)/shard_map/ppermute | solution.py:321
  109.1 1.9 %multiply_subtract_fusion = (f32[16,4096]{1,0:T(8,128)}, f32[16,4096]{1,0:T(8,128)}) fusion(f32[16,4096]{1,0:T(8,128)S(1)} %copy-done.6, f32[16,4096]{1,0:T(8,128)} %bitcast.15, f32[16,4096]{1,0:T(8,128)} %param.15), kind=kLoop, calls=%fused_computation.1 | loop fusion | flops 393216 | bytes 1310720 | tf_op jit(solution)/shard_map/sub | solution.py:362
  111.0 0.8 copy-done.5
  111.7 2.1 %activation.1 = bf16[4,3,128,256]{3,2,1,0:T(8,128)(2,1)} custom-call(f32[3,128,256]{2,1,0:T(8,128)} %get-tuple-element.18.mine_ref, f32[3,128,256]{2,1,0:T(8,128)} %copy-done.5, f32[16,4096]{1,0:T(8,128)} %get-tuple-element.23.after), custom_call_target="tpu_custom_call" | custom-call | flops 655360 | bytes 1048576 | tf_op jit(solution)/shard_map/activation/pallas_call | solution.py:243
  113.9 5.5 %all-to-all-start.2 = ((bf16[4,3,128,256]{3,2,1,0:T(8,128)(2,1)}), bf16[4,3,128,256]{3,2,1,0:T(8,128)(2,1)S(1)}, u32[]{:S(2)}, u32[]{:S(2)}) async-start(bf16[4,3,128,256]{3,2,1,0:T(8,128)(2,1)} %activation.1), calls=%async_computation.2 | async-start | bytes 1572864 | tf_op jit(solution)/shard_map/all_to_all | solution.py:366
  119.4 2.8 %repack_tokens.1 = bf16[3,2,128,512]{3,2,1,0:T(8,128)(2,1)} custom-call(s32[3]{0:T(128)} %pad_add_fusion.place, bf16[3,128,1024]{2,1,0:T(8,128)(2,1)} %copy-done, bf16[3,128,1024]{2,1,0:T(8,128)(2,1)} %collective-permute-done.6.back, bf16[1,128,1024]{2,1,0:T(8,128)(2,1)} %copy-done.2, bf16[1,128,1024]{2,1,0:T(8,128)(2,1)} %copy-done.3), custom_call_target="tpu_custom_call" | custom-call | bytes 209715200 | tf_op jit(solution)/shard_map/repack_tokens/pallas_call | solution.py:133
  122.2 2.2 %collective-permute-start.9 = (bf16[3,2,128,512]{3,2,1,0:T(8,128)(2,1)}, bf16[3,2,128,512]{3,2,1,0:T(8,128)(2,1)}, u32[]{:S(2)}, u32[]{:S(2)}) collective-permute-start(bf16[3,2,128,512]{3,2,1,0:T(8,128)(2,1)} %repack_tokens.1), channel_id=1, source_target_pairs={{0,64},{64,0},{1,65},{65,1},{2,66},{66,2},{3,67},{67,3},{4,68},{68... | collective-permute-start | bytes 2359304 | tf_op jit(solution)/shard_map/ppermute | solution.py:321
  124.4 16.5 %all-to-all-done.2.rest_0_ = bf16[4,3,128,256]{3,2,1,0:T(8,128)(2,1)S(1)} async-done(((bf16[4,3,128,256]{3,2,1,0:T(8,128)(2,1)}), bf16[4,3,128,256]{3,2,1,0:T(8,128)(2,1)S(1)}, u32[]{:S(2)}, u32[]{:S(2)}) %all-to-all-start.2) | async-done | bytes 786464 | tf_op jit(solution)/shard_map/all_to_all | solution.py:366
  140.9 2.6 %collective-permute-start.14 = (bf16[4,3,128,256]{3,2,1,0:T(8,128)(2,1)S(1)}, bf16[4,3,128,256]{3,2,1,0:T(8,128)(2,1)}, u32[]{:S(2)}, u32[]{:S(2)}) collective-permute-start(bf16[4,3,128,256]{3,2,1,0:T(8,128)(2,1)S(1)} %all-to-all-done.2.rest_0_), channel_id=1, source_target_pairs={{0,64},{64,0},{1,65},{65,1},{2,66},{66,2},{3,67},{67,3},{4,68},{68... | collective-permute-start | bytes 2359304 | tf_op jit(solution)/shard_map/ppermute | solution.py:321
  143.6 2.0 %collective-permute-done.14.rest_1_ = bf16[4,3,128,256]{3,2,1,0:T(8,128)(2,1)} collective-permute-done((bf16[4,3,128,256]{3,2,1,0:T(8,128)(2,1)S(1)}, bf16[4,3,128,256]{3,2,1,0:T(8,128)(2,1)}, u32[]{:S(2)}, u32[]{:S(2)}) %collective-permute-start.14) | collective-permute-done | bytes 786464 | tf_op jit(solution)/shard_map/ppermute | solution.py:321
  145.6 4.6 %weight_grads.1 = (bf16[1,512,256]{2,1,0:T(8,128)(2,1)}, bf16[1,512,256]{2,1,0:T(8,128)(2,1)}, bf16[1,256,512]{2,1,0:T(8,128)(2,1)}) custom-call(s32[3]{0:T(128)} %pad_add_fusion.place, bf16[128,4096]{1,0:T(8,128)(2,1)} %bitcast.23, bf16[128,4096]{1,0:T(8,128)(2,1)} %bitcast.27, bf16[128,4096]{1,0:T(8,128)(2,1)} %collective-permute-done.rest_1_.beside_x.after, ...), custom_call_target="tpu_custom_call" | custom-call | flops 805306368 | bytes 5242880 | tf_op jit(solution)/shard_map/weight_grads/pallas_call | solution.py:287
  (16 shorter events, 0.0 us)
Async XLA Ops:
  0.6 20.1 %collective-permute-start = (bf16[128,4096]{1,0:T(8,128)(2,1)}, bf16[128,4096]{1,0:T(8,128)(2,1)}, u32[]{:S(2)}, u32[]{:S(2)}) collective-permute-start(bf16[128,4096]{1,0:T(8,128)(2,1)} %bitcast.20), channel_id=1, source_target_pairs={{0,64},{64,0},{1,65},{65,1},{2,66},{66,2},{3,67},{67,3},{4,68},{68... | collective-permute-start | bytes 3145736 | tf_op jit(solution)/shard_map/ppermute | solution.py:321
  3.2 33.7 %collective-permute-start.1 = (bf16[128,4096]{1,0:T(8,128)(2,1)}, bf16[128,4096]{1,0:T(8,128)(2,1)}, u32[]{:S(2)}, u32[]{:S(2)}) collective-permute-start(bf16[128,4096]{1,0:T(8,128)(2,1)} %bitcast.24), channel_id=1, source_target_pairs={{0,64},{64,0},{1,65},{65,1},{2,66},{66,2},{3,67},{67,3},{4,68},{68... | collective-permute-start | bytes 3145736 | tf_op jit(solution)/shard_map/ppermute | solution.py:321
  8.0 22.8 %collective-permute-start.2 = (bf16[384,256]{1,0:T(8,128)(2,1)}, bf16[384,256]{1,0:T(8,128)(2,1)S(1)}, u32[]{:S(2)}, u32[]{:S(2)}) collective-permute-start(bf16[384,256]{1,0:T(8,128)(2,1)} %weight_share.1), channel_id=1, source_target_pairs={{0,384},{128,0},{256,128},{384,256},{1,385},{129,1},{257,129},{385... | collective-permute-start | bytes 589832 | tf_op jit(solution)/shard_map/ppermute | solution.py:313
  13.0 20.5 %collective-permute-start.3 = (bf16[384,256]{1,0:T(8,128)(2,1)}, bf16[384,256]{1,0:T(8,128)(2,1)S(1)}, u32[]{:S(2)}, u32[]{:S(2)}) collective-permute-start(bf16[384,256]{1,0:T(8,128)(2,1)} %weight_share.1), channel_id=1, source_target_pairs={{0,256},{128,384},{256,0},{384,128},{1,257},{129,385},{257,1},{385... | collective-permute-start | bytes 589832 | tf_op jit(solution)/shard_map/ppermute | solution.py:313
  17.4 18.5 %collective-permute-start.4 = (bf16[384,256]{1,0:T(8,128)(2,1)}, bf16[384,256]{1,0:T(8,128)(2,1)S(1)}, u32[]{:S(2)}, u32[]{:S(2)}) collective-permute-start(bf16[384,256]{1,0:T(8,128)(2,1)} %weight_share.1), channel_id=1, source_target_pairs={{0,128},{128,256},{256,384},{384,0},{1,129},{129,257},{257,385},{3... | collective-permute-start | bytes 589832 | tf_op jit(solution)/shard_map/ppermute | solution.py:313
  22.4 13.5 %copy-start.4 = (bf16[384,256]{1,0:T(8,128)(2,1)S(1)}, bf16[384,256]{1,0:T(8,128)(2,1)}, u32[]{:S(2)}) copy-start(bf16[384,256]{1,0:T(8,128)(2,1)} %weight_share.1) | copy-start | bytes 589828
  22.4 35.0 %all-to-all-start = ((f32[64,8,128]{2,1,0:T(8,128)}), f32[64,8,128]{2,1,0:T(8,128)}, u32[]{:S(2)}, u32[]{:S(2)}) async-start(f32[64,8,128]{2,1,0:T(8,128)} %bitcast.28), calls=%async_computation | async-start | bytes 524288 | tf_op jit(solution)/shard_map/all_to_all | solution.py:329
  40.2 36.6 %collective-permute-start.5 = (bf16[3,128,1024]{2,1,0:T(8,128)(2,1)}, bf16[3,128,1024]{2,1,0:T(8,128)(2,1)S(1)}, u32[]{:S(2)}, u32[]{:S(2)}) collective-permute-start(bf16[3,128,1024]{2,1,0:T(8,128)(2,1)} %get-tuple-element.14), channel_id=1, source_target_pairs={{0,128},{128,256},{256,384},{384,0},{1,129},{129,257},{257,385},{3... | collective-permute-start | bytes 2359304 | tf_op jit(solution)/shard_map/ppermute | solution.py:309
  44.1 38.0 %collective-permute-start.6 = (bf16[3,128,1024]{2,1,0:T(8,128)(2,1)}, bf16[3,128,1024]{2,1,0:T(8,128)(2,1)}, u32[]{:S(2)}, u32[]{:S(2)}) collective-permute-start(bf16[3,128,1024]{2,1,0:T(8,128)(2,1)} %get-tuple-element.15), channel_id=1, source_target_pairs={{0,384},{128,0},{256,128},{384,256},{1,385},{129,1},{257,129},{385... | collective-permute-start | bytes 2359304 | tf_op jit(solution)/shard_map/ppermute | solution.py:309
  47.8 43.7 %collective-permute-start.10 = (bf16[4,384,256]{2,1,0:T(8,128)(2,1)}, bf16[4,384,256]{2,1,0:T(8,128)(2,1)}, u32[]{:S(2)}, u32[]{:S(2)}) collective-permute-start(bf16[4,384,256]{2,1,0:T(8,128)(2,1)} %pad_maximum_fusion.rest_0_), channel_id=1, source_target_pairs={{0,24},{8,0},{16,8},{24,16},{1,25},{9,1},{17,9},{25,17},{2,26},{10... | collective-permute-start | bytes 2359304 | tf_op jit(solution)/shard_map/ppermute | solution.py:317
  49.9 41.6 %collective-permute-start.11 = (bf16[4,384,256]{2,1,0:T(8,128)(2,1)}, bf16[4,384,256]{2,1,0:T(8,128)(2,1)}, u32[]{:S(2)}, u32[]{:S(2)}) collective-permute-start(bf16[4,384,256]{2,1,0:T(8,128)(2,1)} %pad_maximum_fusion.rest_0_), channel_id=1, source_target_pairs={{0,16},{8,24},{16,0},{24,8},{1,17},{9,25},{17,1},{25,9},{2,18},{10... | collective-permute-start | bytes 2359304 | tf_op jit(solution)/shard_map/ppermute | solution.py:317
  54.0 37.7 %collective-permute-start.12 = (bf16[4,384,256]{2,1,0:T(8,128)(2,1)}, bf16[4,384,256]{2,1,0:T(8,128)(2,1)}, u32[]{:S(2)}, u32[]{:S(2)}) collective-permute-start(bf16[4,384,256]{2,1,0:T(8,128)(2,1)} %pad_maximum_fusion.rest_0_), channel_id=1, source_target_pairs={{0,8},{8,16},{16,24},{24,0},{1,9},{9,17},{17,25},{25,1},{2,10},{10... | collective-permute-start | bytes 2359304 | tf_op jit(solution)/shard_map/ppermute | solution.py:317
  59.2 49.9 %all-to-all-start.1 = ((f32[64,8,128]{2,1,0:T(8,128)}), f32[64,8,128]{2,1,0:T(8,128)}, u32[]{:S(2)}, u32[]{:S(2)}) async-start(f32[64,8,128]{2,1,0:T(8,128)} %broadcast_in_dim.2), calls=%async_computation.1 | async-start | bytes 524288 | tf_op jit(solution)/shard_map/all_to_all | solution.py:336
  76.8 5.3 %copy-start = (bf16[3,128,1024]{2,1,0:T(8,128)(2,1)}, bf16[3,128,1024]{2,1,0:T(8,128)(2,1)S(1)}, u32[]{:S(2)}) copy-start(bf16[3,128,1024]{2,1,0:T(8,128)(2,1)S(1)} %collective-permute-done.5.ahead) | copy-start | bytes 2359300
  84.0 11.5 %collective-permute-start.7 = (bf16[1,128,1024]{2,1,0:T(8,128)(2,1)}, bf16[1,128,1024]{2,1,0:T(8,128)(2,1)S(1)}, u32[]{:S(2)}, u32[]{:S(2)}) collective-permute-start(bf16[1,128,1024]{2,1,0:T(8,128)(2,1)} %get-tuple-element.16), channel_id=1, source_target_pairs={{0,128},{128,256},{256,384},{384,0},{1,129},{129,257},{257,385},{3... | collective-permute-start | bytes 786440 | tf_op jit(solution)/shard_map/ppermute | solution.py:309
  86.1 23.0 %copy-start.6 = (f32[16,4096]{1,0:T(8,128)S(1)}, f32[16,4096]{1,0:T(8,128)}, u32[]{:S(2)}) copy-start(f32[16,4096]{1,0:T(8,128)} %param.14) | copy-start | bytes 786436
  86.1 11.2 %collective-permute-start.8 = (bf16[1,128,1024]{2,1,0:T(8,128)(2,1)}, bf16[1,128,1024]{2,1,0:T(8,128)(2,1)S(1)}, u32[]{:S(2)}, u32[]{:S(2)}) collective-permute-start(bf16[1,128,1024]{2,1,0:T(8,128)(2,1)} %get-tuple-element.17), channel_id=1, source_target_pairs={{0,384},{128,0},{256,128},{384,256},{1,385},{129,1},{257,129},{385... | collective-permute-start | bytes 786440 | tf_op jit(solution)/shard_map/ppermute | solution.py:309
  95.4 1.9 %copy-start.2 = (bf16[1,128,1024]{2,1,0:T(8,128)(2,1)}, bf16[1,128,1024]{2,1,0:T(8,128)(2,1)S(1)}, u32[]{:S(2)}) copy-start(bf16[1,128,1024]{2,1,0:T(8,128)(2,1)S(1)} %collective-permute-done.7.far_x.rest_4_) | copy-start | bytes 786436
  97.3 0.7 copy-start.3
  103.3 7.6 %collective-permute-start.13 = (f32[3,128,256]{2,1,0:T(8,128)}, f32[3,128,256]{2,1,0:T(8,128)S(1)}, u32[]{:S(2)}, u32[]{:S(2)}) collective-permute-start(f32[3,128,256]{2,1,0:T(8,128)} %get-tuple-element.19), channel_id=1, source_target_pairs={{0,64},{64,0},{1,65},{65,1},{2,66},{66,2},{3,67},{67,3},{4,68},{68... | collective-permute-start | bytes 1179656 | tf_op jit(solution)/shard_map/ppermute | solution.py:321
  111.0 0.8 copy-start.5
  113.9 27.1 %all-to-all-start.2 = ((bf16[4,3,128,256]{3,2,1,0:T(8,128)(2,1)}), bf16[4,3,128,256]{3,2,1,0:T(8,128)(2,1)S(1)}, u32[]{:S(2)}, u32[]{:S(2)}) async-start(bf16[4,3,128,256]{3,2,1,0:T(8,128)(2,1)} %activation.1), calls=%async_computation.2 | async-start | bytes 1572864 | tf_op jit(solution)/shard_map/all_to_all | solution.py:366
  122.2 21.4 %collective-permute-start.9 = (bf16[3,2,128,512]{3,2,1,0:T(8,128)(2,1)}, bf16[3,2,128,512]{3,2,1,0:T(8,128)(2,1)}, u32[]{:S(2)}, u32[]{:S(2)}) collective-permute-start(bf16[3,2,128,512]{3,2,1,0:T(8,128)(2,1)} %repack_tokens.1), channel_id=1, source_target_pairs={{0,64},{64,0},{1,65},{65,1},{2,66},{66,2},{3,67},{67,3},{4,68},{68... | collective-permute-start | bytes 2359304 | tf_op jit(solution)/shard_map/ppermute | solution.py:321
  140.9 4.6 %copy-start.1 = (bf16[4,3,128,256]{3,2,1,0:T(8,128)(2,1)}, bf16[4,3,128,256]{3,2,1,0:T(8,128)(2,1)S(1)}, u32[]{:S(2)}) copy-start(bf16[4,3,128,256]{3,2,1,0:T(8,128)(2,1)S(1)} %all-to-all-done.2.rest_0_) | copy-start | bytes 2359300
  140.9 4.6 %collective-permute-start.14 = (bf16[4,3,128,256]{3,2,1,0:T(8,128)(2,1)S(1)}, bf16[4,3,128,256]{3,2,1,0:T(8,128)(2,1)}, u32[]{:S(2)}, u32[]{:S(2)}) collective-permute-start(bf16[4,3,128,256]{3,2,1,0:T(8,128)(2,1)S(1)} %all-to-all-done.2.rest_0_), channel_id=1, source_target_pairs={{0,64},{64,0},{1,65},{65,1},{2,66},{66,2},{3,67},{67,3},{4,68},{68... | collective-permute-start | bytes 2359304 | tf_op jit(solution)/shard_map/ppermute | solution.py:321
